TPU v7x, 256 devices: a whole 4x4x8 slice. The times are simulated.
256 devices in a mesh: caption: 16 (over y_lo, z), replica: 16 (over x, y_hi, core).
Axes of the slice: x: 4, y: 4 (y_hi: 2, y_lo: 2; y = y_hi * 2 + y_lo), z: 8, core: 2. Of those that a mesh axis runs over, the one named last changes fastest.
Arguments:
- caption_feats: bfloat16 [16, 2048, 1152], P('replica', 'caption')
- text_head: bfloat16 [1152, 1152], replicated, may hold values from -0.1875 to 0.1875
- image_pool: bfloat16 [16, 2048, 1152], P('caption', 'replica')
- image_head: bfloat16 [1152, 1152], replicated, may hold values from -0.1875 to 0.1875
- image_owner: int32 [16, 1536, 1], P(None, 'caption'), may hold values from 0 to 15; in each aligned block of 96 rows (0 to 95, 96 to 191, ..., all dimensions but the last counted through in order) at most 12 rows name the same one
- image_slot: int32 [16, 1536], P(None, 'caption'), may hold values from 0 to 127
- caption_image: int32 [16, 2048], P('replica', 'caption'), may hold values from 0 to 95
- logit_scale: float32 [1], replicated, may hold values from 90 to 130
- logit_bias: float32 [1], replicated, may hold values from -14 to -10
Outputs:
- text_feat_grad: bfloat16 [16, 2048, 1152], P('replica', 'caption')
- pool_grad: bfloat16 [16, 2048, 1152], P('caption', 'replica')
- head_grads: float32 [2304, 1152], P(('caption', 'replica'))
Inputs may be any that keep to these rules, and one draw needn't show every extreme that they name: `image_owner`: among the 96 images of one device (aligned blocks of rows in group order), at most 12 have the same owner, and in every draw some owner holds exactly 12 images of some device.
All inputs are finite; a program needn't handle non-finite values.
Results may differ from a plain program's by a relative error of at most 0.0083.
Values may be sent and summed in bfloat16 or wider, within the bound.
No kernel may reach another device: no remote copies, remote signals or barrier semaphores. Data moves between devices by JAX's collectives and lax.ppermute only.
A program may use at most 128 MiB of HBM per device.

v0:
```python
import jax
import jax.numpy as jnp
from jax import lax
from jax.sharding import PartitionSpec as P


def passed_along(block, axis, distance):
    devices = range(lax.axis_size(axis))
    route = [((i - distance) % len(devices), i) for i in devices]
    return lax.ppermute(block, axis, route)


def project_rows(features, head_matrix):
    projected = jnp.dot(features, head_matrix, preferred_element_type=jnp.float32)
    norm_rows = jnp.sqrt(jnp.sum(projected * projected, axis=-1, keepdims=True) + 1e-06)
    return (projected / norm_rows, norm_rows)


def pull_back(unit_rows, norm_rows, gradient):
    radial = jnp.sum(unit_rows * gradient, axis=-1, keepdims=True)
    return ((gradient - unit_rows * radial) / norm_rows).astype(jnp.bfloat16)


def score_weights(moving, resident, temper, offset):
    logits = (
        jnp.einsum("te,ie->ti", moving, resident, preferred_element_type=jnp.float32) * temper
        + offset
    )
    return jax.nn.sigmoid(logits).astype(jnp.bfloat16)


def per_device(
    caption_feats,
    text_head,
    image_pool,
    image_head,
    image_owner,
    image_slot,
    caption_image,
    logit_scale,
    logit_bias,
):
    temper = logit_scale[0]
    offset = logit_bias[0]
    captions = caption_feats[0]
    pool_rows = image_pool[0]
    owners_all = image_owner[:, :, 0]
    targets = caption_image[0]
    rank_count = lax.axis_size("replica")
    cycle_size = lax.axis_size("caption")
    image_count = owners_all.shape[1]
    capacity = 2 * image_count // rank_count
    my_rank = lax.axis_index("replica")
    is_owned = (owners_all == my_rank).astype(jnp.int32)
    places = jnp.where(is_owned == 1, jnp.cumsum(is_owned, axis=1) - 1, capacity)
    requesters = jnp.arange(rank_count, dtype=jnp.int32)[:, None]
    slot_table = (
        jnp.zeros((rank_count, capacity + 1), jnp.int32)
        .at[requesters, places]
        .set(image_slot)[:, :capacity]
    )
    outgoing = pool_rows[slot_table]
    arrived = lax.all_to_all(outgoing, "replica", split_axis=0, concat_axis=0, tiled=True)
    my_owners = lax.dynamic_index_in_dim(owners_all, my_rank, 0, keepdims=False)
    owner_hits = (my_owners[:, None] == jnp.arange(rank_count, dtype=jnp.int32)[None, :]).astype(
        jnp.int32
    )
    my_places = jnp.sum((jnp.cumsum(owner_hits, axis=0) - 1) * owner_hits, axis=1)
    image_feats = arrived[my_owners, my_places]
    text_unit, text_norm = project_rows(captions, text_head)
    image_unit, image_norm = project_rows(image_feats, image_head)
    text_emb = text_unit.astype(jnp.bfloat16)
    image_emb = image_unit.astype(jnp.bfloat16)

    def cycle_turn(turn_index, cycle_state):
        moving, carried, image_total = cycle_state
        moving = passed_along(moving, "caption", 1)
        carried = passed_along(carried, "caption", 1)
        weights = score_weights(moving, image_emb, temper, offset)
        toward = temper * jnp.dot(weights, image_emb, preferred_element_type=jnp.float32)
        returned = temper * jnp.einsum(
            "ti,te->ie", weights, moving, preferred_element_type=jnp.float32
        )
        return (moving, carried + toward, image_total + returned)

    start_state = (
        text_emb,
        jnp.zeros(text_unit.shape, jnp.float32),
        jnp.zeros(image_unit.shape, jnp.float32),
    )
    final_state = lax.fori_loop(0, cycle_size, cycle_turn, start_state)
    text_grad = final_state[1]
    image_grad = final_state[2]
    text_grad = text_grad - temper * image_emb[targets].astype(jnp.float32)
    target_hits = (targets[None, :] == jnp.arange(image_count, dtype=jnp.int32)[:, None]).astype(
        jnp.bfloat16
    )
    image_grad = image_grad - temper * jnp.dot(
        target_hits, text_emb, preferred_element_type=jnp.float32
    )
    text_proj_grad = pull_back(text_unit, text_norm, text_grad)
    image_proj_grad = pull_back(image_unit, image_norm, image_grad)
    text_feat_grad = jnp.einsum(
        "te,de->td", text_proj_grad, text_head, preferred_element_type=jnp.float32
    ).astype(jnp.bfloat16)
    image_feat_grad = jnp.einsum(
        "ie,de->id", image_proj_grad, image_head, preferred_element_type=jnp.float32
    ).astype(jnp.bfloat16)
    send_back = jnp.zeros(arrived.shape, jnp.bfloat16).at[my_owners, my_places].set(image_feat_grad)
    received = lax.all_to_all(send_back, "replica", split_axis=0, concat_axis=0, tiled=True)
    pool_hits = (
        jnp.arange(pool_rows.shape[0], dtype=jnp.int32)[:, None] == slot_table.reshape(-1)[None, :]
    ).astype(jnp.bfloat16)
    pool_grad = jnp.dot(
        pool_hits, received.reshape(-1, received.shape[-1]), preferred_element_type=jnp.float32
    ).astype(jnp.bfloat16)
    depth_rows = captions.shape[1]
    emb_width = text_head.shape[1]
    span_cols = min(
        2 * depth_rows // (cycle_size * rank_count) * lax.axis_size(("caption", "replica")) // 2
        + 1,
        depth_rows,
    )
    text_part = jnp.einsum(
        "td,te->de", captions, text_proj_grad, preferred_element_type=jnp.float32
    )
    image_part = jnp.einsum(
        "td,te->de", image_feats, image_proj_grad, preferred_element_type=jnp.float32
    )
    stacked = jnp.stack([text_part, image_part], axis=1).reshape(2 * span_cols, emb_width)
    head_share = lax.psum_scatter(stacked, ("caption", "replica"), scatter_dimension=0, tiled=True)
    return (text_feat_grad[None], pool_grad[None], head_share)


def solution(mesh):
    in_specs = (
        P("replica", "caption", None),
        P(),
        P("caption", "replica", None),
        P(),
        P(None, "caption", None),
        P(None, "caption"),
        P("replica", "caption"),
        P(),
        P(),
    )
    out_specs = (
        P("replica", "caption", None),
        P("caption", "replica", None),
        P(("caption", "replica"), None),
    )
    return jax.shard_map(
        per_device, mesh=mesh, in_specs=in_specs, out_specs=out_specs, check_vma=False
    )
```

profile of v0, /device:TPU:1, one launch (start us, length us, event | category | flops | bytes accessed | tf_op | source)
XLA Modules:
  0.0 747.0 jit_solution(10258642000287413393)
XLA Ops:
  16.2 6.2 scatter_custom_fusion.1
  24.6 8.4 %all-to-all-start = ((bf16[16,12,1152]{2,1,0:T(8,128)(2,1)}), bf16[16,12,1152]{2,1,0:T(8,128)(2,1)}, u32[]{:S(2)}, u32[]{:S(2)}) async-start(bf16[16,12,1152]{2,1,0:T(8,128)(2,1)} %reshape.117), calls=%async_computation | async-start | bytes 1179648 | tf_op jit(solution)/shard_map/all_to_all | solution.py:63
  39.6 5.3 all-to-all-done
  52.4 345.6 %while.15 = (s32[]{:T(128)}, bf16[128,1152]{1,0:T(8,128)(2,1)}, f32[128,1152]{1,0:T(8,128)}, f32[96,1152]{1,0:T(8,128)}, f32[]{:T(128)}, /*index=5*/bf16[96,1152]{1,0:T(8,128)(2,1)S(1)}, f32[]{:T(128)}, s32[]{:T(128)}, s32[]{:T(128)}) while((s32[]{:T(128)}, bf16[128,1152]{1,0:T(8,128)(2,1)}, f32[128,1152]{1,0:T(8,128)}, ...), condition=%wide.region_7.8_spmd.clone, body=%wide.region_6.7_spmd.clone.sunk | while | flops 85782528 | bytes 8478920 | solution.py:91
  56.8 7.6 %collective-permute-done = bf16[128,1152]{1,0:T(8,128)(2,1)S(1)} collective-permute-done((bf16[128,1152]{1,0:T(8,128)(2,1)}, bf16[128,1152]{1,0:T(8,128)(2,1)S(1)}, u32[]{:S(2)}, u32[]{:S(2)}) %collective-permute-start) | collective-permute-done | bytes 294944 | tf_op jit(solution)/shard_map/while/body/eval_jaxpr/ppermute | solution.py:10
  68.3 8.8 %collective-permute-done.1 = f32[128,1152]{1,0:T(8,128)} collective-permute-done((f32[128,1152]{1,0:T(8,128)}, f32[128,1152]{1,0:T(8,128)}, u32[]{:S(2)}, u32[]{:S(2)}) %collective-permute-start.1) | collective-permute-done | bytes 589856 | tf_op jit(solution)/shard_map/while/body/eval_jaxpr/ppermute | solution.py:10
  81.9 6.7 collective-permute-done
  93.6 7.8 %collective-permute-done.1 = f32[128,1152]{1,0:T(8,128)} collective-permute-done((f32[128,1152]{1,0:T(8,128)}, f32[128,1152]{1,0:T(8,128)}, u32[]{:S(2)}, u32[]{:S(2)}) %collective-permute-start.1) | collective-permute-done | bytes 589856 | tf_op jit(solution)/shard_map/while/body/eval_jaxpr/ppermute | solution.py:10
  106.1 6.0 collective-permute-done
  117.0 7.7 %collective-permute-done.1 = f32[128,1152]{1,0:T(8,128)} collective-permute-done((f32[128,1152]{1,0:T(8,128)}, f32[128,1152]{1,0:T(8,128)}, u32[]{:S(2)}, u32[]{:S(2)}) %collective-permute-start.1) | collective-permute-done | bytes 589856 | tf_op jit(solution)/shard_map/while/body/eval_jaxpr/ppermute | solution.py:10
  129.4 6.0 collective-permute-done
  140.3 6.7 collective-permute-done.1
  151.8 6.0 collective-permute-done
  162.7 5.8 collective-permute-done.1
  173.2 6.0 collective-permute-done
  184.1 4.8 collective-permute-done.1
  193.6 6.0 collective-permute-done
  213.0 6.6 collective-permute-done
  263.9 7.3 collective-permute-done.1
  286.8 7.3 collective-permute-done.1
  309.7 7.0 collective-permute-done.1
  321.7 5.7 collective-permute-done
  332.3 5.1 collective-permute-done.1
  342.1 6.0 collective-permute-done
  361.7 6.1 collective-permute-done
  409.0 4.8 pad_maximum_fusion
  413.8 16.0 %copy.71 = f32[1152,2,1152]{2,1,0:T(2,128)} copy(f32[1152,2,1152]{2,0,1:T(8,128)S(1)} %pad_maximum_fusion) | data formatting | bytes 21233664 | tf_op jit(solution)/shard_map/stack | solution.py:130
  429.8 13.4 %reshape.111 = f32[2304,1152]{1,0:T(8,128)} reshape(f32[1152,2,1152]{2,1,0:T(2,128)} %copy.71) | data formatting | bytes 21233664 | tf_op jit(solution)/shard_map/reshape | solution.py:130
  447.7 14.8 %scatter_fusion = bf16[16,12,1152]{2,0,1:T(8,128)(2,1)} fusion(bf16[16,12,1152]{2,0,1:T(8,128)(2,1)} %broadcast_in_dim.52, s32[96]{0:T(128)S(1)} %get-tuple-element.81, bf16[96,1152]{1,0:T(8,128)(2,1)} %convolution_convert_fusion.2), kind=kCustom, calls=%fused_computation.3 | custom fusion | bytes 664320 | tf_op jit(solution)/shard_map/scatter | solution.py:109
  464.4 21.7 %all-to-all-start.1 = ((bf16[16,12,1152]{2,1,0:T(8,128)(2,1)}), bf16[16,12,1152]{2,1,0:T(8,128)(2,1)}, u32[]{:S(2)}, u32[]{:S(2)}) async-start(bf16[16,12,1152]{2,1,0:T(8,128)(2,1)} %copy.70), calls=%async_computation.1 | async-start | bytes 1179648 | tf_op jit(solution)/shard_map/all_to_all | solution.py:110
  489.0 10.1 %all-to-all-done.1 = bf16[16,12,1152]{2,1,0:T(8,128)(2,1)} async-done(((bf16[16,12,1152]{2,1,0:T(8,128)(2,1)}), bf16[16,12,1152]{2,1,0:T(8,128)(2,1)}, u32[]{:S(2)}, u32[]{:S(2)}) %all-to-all-start.1) | async-done | bytes 442400 | tf_op jit(solution)/shard_map/all_to_all | solution.py:110
  501.2 237.4 %all-reduce.3.cloned.1.call-done = f32[2304,1152]{1,0:T(8,128)} async-done(((f32[2304,1152]{1,0:T(8,128)}), f32[2304,1152]{1,0:T(8,128)}) %all-reduce.3.cloned.1.call-update) | async-done | bytes 10616848
  (204 shorter events, 256.8 us)
Async XLA Ops:
  24.6 20.2 %all-to-all-start = ((bf16[16,12,1152]{2,1,0:T(8,128)(2,1)}), bf16[16,12,1152]{2,1,0:T(8,128)(2,1)}, u32[]{:S(2)}, u32[]{:S(2)}) async-start(bf16[16,12,1152]{2,1,0:T(8,128)(2,1)} %reshape.117), calls=%async_computation | async-start | bytes 1179648 | tf_op jit(solution)/shard_map/all_to_all | solution.py:63
  33.1 705.6 %all-reduce.3.cloned.1.call-start = ((), (), s32[]{:S(2)}) async-start(), calls=%async_computation.2 | async-start | bytes 21233664
  52.6 11.8 %collective-permute-start = (bf16[128,1152]{1,0:T(8,128)(2,1)}, bf16[128,1152]{1,0:T(8,128)(2,1)S(1)}, u32[]{:S(2)}, u32[]{:S(2)}) collective-permute-start(bf16[128,1152]{1,0:T(8,128)(2,1)} %get-tuple-element.144), channel_id=1, source_target_pairs={{240,0},{0,16},{16,32},{32,48},{48,64},{64,80},{80,96},{96,112},{1... | collective-permute-start | bytes 884744 | tf_op jit(solution)/shard_map/while/body/eval_jaxpr/ppermute | solution.py:10
  55.2 22.0 %collective-permute-start.1 = (f32[128,1152]{1,0:T(8,128)}, f32[128,1152]{1,0:T(8,128)}, u32[]{:S(2)}, u32[]{:S(2)}) collective-permute-start(f32[128,1152]{1,0:T(8,128)} %broadcast_select_fusion.3), channel_id=1, source_target_pairs={{240,0},{0,16},{16,32},{32,48},{48,64},{64,80},{80,96},{96,112},{1... | collective-permute-start | bytes 1769480 | tf_op jit(solution)/shard_map/while/body/eval_jaxpr/ppermute | solution.py:10
  80.0 8.7 %collective-permute-start = (bf16[128,1152]{1,0:T(8,128)(2,1)}, bf16[128,1152]{1,0:T(8,128)(2,1)S(1)}, u32[]{:S(2)}, u32[]{:S(2)}) collective-permute-start(bf16[128,1152]{1,0:T(8,128)(2,1)} %get-tuple-element.144), channel_id=1, source_target_pairs={{240,0},{0,16},{16,32},{32,48},{48,64},{64,80},{80,96},{96,112},{1... | collective-permute-start | bytes 884744 | tf_op jit(solution)/shard_map/while/body/eval_jaxpr/ppermute | solution.py:10
  81.9 19.5 %collective-permute-start.1 = (f32[128,1152]{1,0:T(8,128)}, f32[128,1152]{1,0:T(8,128)}, u32[]{:S(2)}, u32[]{:S(2)}) collective-permute-start(f32[128,1152]{1,0:T(8,128)} %broadcast_select_fusion.3), channel_id=1, source_target_pairs={{240,0},{0,16},{16,32},{32,48},{48,64},{64,80},{80,96},{96,112},{1... | collective-permute-start | bytes 1769480 | tf_op jit(solution)/shard_map/while/body/eval_jaxpr/ppermute | solution.py:10
  104.2 7.9 %collective-permute-start = (bf16[128,1152]{1,0:T(8,128)(2,1)}, bf16[128,1152]{1,0:T(8,128)(2,1)S(1)}, u32[]{:S(2)}, u32[]{:S(2)}) collective-permute-start(bf16[128,1152]{1,0:T(8,128)(2,1)} %get-tuple-element.144), channel_id=1, source_target_pairs={{240,0},{0,16},{16,32},{32,48},{48,64},{64,80},{80,96},{96,112},{1... | collective-permute-start | bytes 884744 | tf_op jit(solution)/shard_map/while/body/eval_jaxpr/ppermute | solution.py:10
  106.1 18.6 %collective-permute-start.1 = (f32[128,1152]{1,0:T(8,128)}, f32[128,1152]{1,0:T(8,128)}, u32[]{:S(2)}, u32[]{:S(2)}) collective-permute-start(f32[128,1152]{1,0:T(8,128)} %broadcast_select_fusion.3), channel_id=1, source_target_pairs={{240,0},{0,16},{16,32},{32,48},{48,64},{64,80},{80,96},{96,112},{1... | collective-permute-start | bytes 1769480 | tf_op jit(solution)/shard_map/while/body/eval_jaxpr/ppermute | solution.py:10
  127.5 7.9 %collective-permute-start = (bf16[128,1152]{1,0:T(8,128)(2,1)}, bf16[128,1152]{1,0:T(8,128)(2,1)S(1)}, u32[]{:S(2)}, u32[]{:S(2)}) collective-permute-start(bf16[128,1152]{1,0:T(8,128)(2,1)} %get-tuple-element.144), channel_id=1, source_target_pairs={{240,0},{0,16},{16,32},{32,48},{48,64},{64,80},{80,96},{96,112},{1... | collective-permute-start | bytes 884744 | tf_op jit(solution)/shard_map/while/body/eval_jaxpr/ppermute | solution.py:10
  129.4 17.6 %collective-permute-start.1 = (f32[128,1152]{1,0:T(8,128)}, f32[128,1152]{1,0:T(8,128)}, u32[]{:S(2)}, u32[]{:S(2)}) collective-permute-start(f32[128,1152]{1,0:T(8,128)} %broadcast_select_fusion.3), channel_id=1, source_target_pairs={{240,0},{0,16},{16,32},{32,48},{48,64},{64,80},{80,96},{96,112},{1... | collective-permute-start | bytes 1769480 | tf_op jit(solution)/shard_map/while/body/eval_jaxpr/ppermute | solution.py:10
  149.8 7.9 %collective-permute-start = (bf16[128,1152]{1,0:T(8,128)(2,1)}, bf16[128,1152]{1,0:T(8,128)(2,1)S(1)}, u32[]{:S(2)}, u32[]{:S(2)}) collective-permute-start(bf16[128,1152]{1,0:T(8,128)(2,1)} %get-tuple-element.144), channel_id=1, source_target_pairs={{240,0},{0,16},{16,32},{32,48},{48,64},{64,80},{80,96},{96,112},{1... | collective-permute-start | bytes 884744 | tf_op jit(solution)/shard_map/while/body/eval_jaxpr/ppermute | solution.py:10
  151.8 16.7 %collective-permute-start.1 = (f32[128,1152]{1,0:T(8,128)}, f32[128,1152]{1,0:T(8,128)}, u32[]{:S(2)}, u32[]{:S(2)}) collective-permute-start(f32[128,1152]{1,0:T(8,128)} %broadcast_select_fusion.3), channel_id=1, source_target_pairs={{240,0},{0,16},{16,32},{32,48},{48,64},{64,80},{80,96},{96,112},{1... | collective-permute-start | bytes 1769480 | tf_op jit(solution)/shard_map/while/body/eval_jaxpr/ppermute | solution.py:10
  171.3 7.9 %collective-permute-start = (bf16[128,1152]{1,0:T(8,128)(2,1)}, bf16[128,1152]{1,0:T(8,128)(2,1)S(1)}, u32[]{:S(2)}, u32[]{:S(2)}) collective-permute-start(bf16[128,1152]{1,0:T(8,128)(2,1)} %get-tuple-element.144), channel_id=1, source_target_pairs={{240,0},{0,16},{16,32},{32,48},{48,64},{64,80},{80,96},{96,112},{1... | collective-permute-start | bytes 884744 | tf_op jit(solution)/shard_map/while/body/eval_jaxpr/ppermute | solution.py:10
  173.2 15.7 %collective-permute-start.1 = (f32[128,1152]{1,0:T(8,128)}, f32[128,1152]{1,0:T(8,128)}, u32[]{:S(2)}, u32[]{:S(2)}) collective-permute-start(f32[128,1152]{1,0:T(8,128)} %broadcast_select_fusion.3), channel_id=1, source_target_pairs={{240,0},{0,16},{16,32},{32,48},{48,64},{64,80},{80,96},{96,112},{1... | collective-permute-start | bytes 1769480 | tf_op jit(solution)/shard_map/while/body/eval_jaxpr/ppermute | solution.py:10
  191.7 7.9 %collective-permute-start = (bf16[128,1152]{1,0:T(8,128)(2,1)}, bf16[128,1152]{1,0:T(8,128)(2,1)S(1)}, u32[]{:S(2)}, u32[]{:S(2)}) collective-permute-start(bf16[128,1152]{1,0:T(8,128)(2,1)} %get-tuple-element.144), channel_id=1, source_target_pairs={{240,0},{0,16},{16,32},{32,48},{48,64},{64,80},{80,96},{96,112},{1... | collective-permute-start | bytes 884744 | tf_op jit(solution)/shard_map/while/body/eval_jaxpr/ppermute | solution.py:10
  193.6 14.7 %collective-permute-start.1 = (f32[128,1152]{1,0:T(8,128)}, f32[128,1152]{1,0:T(8,128)}, u32[]{:S(2)}, u32[]{:S(2)}) collective-permute-start(f32[128,1152]{1,0:T(8,128)} %broadcast_select_fusion.3), channel_id=1, source_target_pairs={{240,0},{0,16},{16,32},{32,48},{48,64},{64,80},{80,96},{96,112},{1... | collective-permute-start | bytes 1769480 | tf_op jit(solution)/shard_map/while/body/eval_jaxpr/ppermute | solution.py:10
  211.1 8.5 %collective-permute-start = (bf16[128,1152]{1,0:T(8,128)(2,1)}, bf16[128,1152]{1,0:T(8,128)(2,1)S(1)}, u32[]{:S(2)}, u32[]{:S(2)}) collective-permute-start(bf16[128,1152]{1,0:T(8,128)(2,1)} %get-tuple-element.144), channel_id=1, source_target_pairs={{240,0},{0,16},{16,32},{32,48},{48,64},{64,80},{80,96},{96,112},{1... | collective-permute-start | bytes 884744 | tf_op jit(solution)/shard_map/while/body/eval_jaxpr/ppermute | solution.py:10
  213.0 14.9 %collective-permute-start.1 = (f32[128,1152]{1,0:T(8,128)}, f32[128,1152]{1,0:T(8,128)}, u32[]{:S(2)}, u32[]{:S(2)}) collective-permute-start(f32[128,1152]{1,0:T(8,128)} %broadcast_select_fusion.3), channel_id=1, source_target_pairs={{240,0},{0,16},{16,32},{32,48},{48,64},{64,80},{80,96},{96,112},{1... | collective-permute-start | bytes 1769480 | tf_op jit(solution)/shard_map/while/body/eval_jaxpr/ppermute | solution.py:10
  230.7 8.4 %collective-permute-start = (bf16[128,1152]{1,0:T(8,128)(2,1)}, bf16[128,1152]{1,0:T(8,128)(2,1)S(1)}, u32[]{:S(2)}, u32[]{:S(2)}) collective-permute-start(bf16[128,1152]{1,0:T(8,128)(2,1)} %get-tuple-element.144), channel_id=1, source_target_pairs={{240,0},{0,16},{16,32},{32,48},{48,64},{64,80},{80,96},{96,112},{1... | collective-permute-start | bytes 884744 | tf_op jit(solution)/shard_map/while/body/eval_jaxpr/ppermute | solution.py:10
  232.6 14.2 %collective-permute-start.1 = (f32[128,1152]{1,0:T(8,128)}, f32[128,1152]{1,0:T(8,128)}, u32[]{:S(2)}, u32[]{:S(2)}) collective-permute-start(f32[128,1152]{1,0:T(8,128)} %broadcast_select_fusion.3), channel_id=1, source_target_pairs={{240,0},{0,16},{16,32},{32,48},{48,64},{64,80},{80,96},{96,112},{1... | collective-permute-start | bytes 1769480 | tf_op jit(solution)/shard_map/while/body/eval_jaxpr/ppermute | solution.py:10
  249.6 9.3 %collective-permute-start = (bf16[128,1152]{1,0:T(8,128)(2,1)}, bf16[128,1152]{1,0:T(8,128)(2,1)S(1)}, u32[]{:S(2)}, u32[]{:S(2)}) collective-permute-start(bf16[128,1152]{1,0:T(8,128)(2,1)} %get-tuple-element.144), channel_id=1, source_target_pairs={{240,0},{0,16},{16,32},{32,48},{48,64},{64,80},{80,96},{96,112},{1... | collective-permute-start | bytes 884744 | tf_op jit(solution)/shard_map/while/body/eval_jaxpr/ppermute | solution.py:10
  255.9 15.2 %collective-permute-start.1 = (f32[128,1152]{1,0:T(8,128)}, f32[128,1152]{1,0:T(8,128)}, u32[]{:S(2)}, u32[]{:S(2)}) collective-permute-start(f32[128,1152]{1,0:T(8,128)} %broadcast_select_fusion.3), channel_id=1, source_target_pairs={{240,0},{0,16},{16,32},{32,48},{48,64},{64,80},{80,96},{96,112},{1... | collective-permute-start | bytes 1769480 | tf_op jit(solution)/shard_map/while/body/eval_jaxpr/ppermute | solution.py:10
  274.0 7.9 %collective-permute-start = (bf16[128,1152]{1,0:T(8,128)(2,1)}, bf16[128,1152]{1,0:T(8,128)(2,1)S(1)}, u32[]{:S(2)}, u32[]{:S(2)}) collective-permute-start(bf16[128,1152]{1,0:T(8,128)(2,1)} %get-tuple-element.144), channel_id=1, source_target_pairs={{240,0},{0,16},{16,32},{32,48},{48,64},{64,80},{80,96},{96,112},{1... | collective-permute-start | bytes 884744 | tf_op jit(solution)/shard_map/while/body/eval_jaxpr/ppermute | solution.py:10
  278.4 15.6 %collective-permute-start.1 = (f32[128,1152]{1,0:T(8,128)}, f32[128,1152]{1,0:T(8,128)}, u32[]{:S(2)}, u32[]{:S(2)}) collective-permute-start(f32[128,1152]{1,0:T(8,128)} %broadcast_select_fusion.3), channel_id=1, source_target_pairs={{240,0},{0,16},{16,32},{32,48},{48,64},{64,80},{80,96},{96,112},{1... | collective-permute-start | bytes 1769480 | tf_op jit(solution)/shard_map/while/body/eval_jaxpr/ppermute | solution.py:10
  301.0 15.7 %collective-permute-start.1 = (f32[128,1152]{1,0:T(8,128)}, f32[128,1152]{1,0:T(8,128)}, u32[]{:S(2)}, u32[]{:S(2)}) collective-permute-start(f32[128,1152]{1,0:T(8,128)} %broadcast_select_fusion.3), channel_id=1, source_target_pairs={{240,0},{0,16},{16,32},{32,48},{48,64},{64,80},{80,96},{96,112},{1... | collective-permute-start | bytes 1769480 | tf_op jit(solution)/shard_map/while/body/eval_jaxpr/ppermute | solution.py:10
  321.7 15.7 %collective-permute-start.1 = (f32[128,1152]{1,0:T(8,128)}, f32[128,1152]{1,0:T(8,128)}, u32[]{:S(2)}, u32[]{:S(2)}) collective-permute-start(f32[128,1152]{1,0:T(8,128)} %broadcast_select_fusion.3), channel_id=1, source_target_pairs={{240,0},{0,16},{16,32},{32,48},{48,64},{64,80},{80,96},{96,112},{1... | collective-permute-start | bytes 1769480 | tf_op jit(solution)/shard_map/while/body/eval_jaxpr/ppermute | solution.py:10
  342.1 15.0 %collective-permute-start.1 = (f32[128,1152]{1,0:T(8,128)}, f32[128,1152]{1,0:T(8,128)}, u32[]{:S(2)}, u32[]{:S(2)}) collective-permute-start(f32[128,1152]{1,0:T(8,128)} %broadcast_select_fusion.3), channel_id=1, source_target_pairs={{240,0},{0,16},{16,32},{32,48},{48,64},{64,80},{80,96},{96,112},{1... | collective-permute-start | bytes 1769480 | tf_op jit(solution)/shard_map/while/body/eval_jaxpr/ppermute | solution.py:10
  359.8 8.0 %collective-permute-start = (bf16[128,1152]{1,0:T(8,128)(2,1)}, bf16[128,1152]{1,0:T(8,128)(2,1)S(1)}, u32[]{:S(2)}, u32[]{:S(2)}) collective-permute-start(bf16[128,1152]{1,0:T(8,128)(2,1)} %get-tuple-element.144), channel_id=1, source_target_pairs={{240,0},{0,16},{16,32},{32,48},{48,64},{64,80},{80,96},{96,112},{1... | collective-permute-start | bytes 884744 | tf_op jit(solution)/shard_map/while/body/eval_jaxpr/ppermute | solution.py:10
  361.7 14.2 %collective-permute-start.1 = (f32[128,1152]{1,0:T(8,128)}, f32[128,1152]{1,0:T(8,128)}, u32[]{:S(2)}, u32[]{:S(2)}) collective-permute-start(f32[128,1152]{1,0:T(8,128)} %broadcast_select_fusion.3), channel_id=1, source_target_pairs={{240,0},{0,16},{16,32},{32,48},{48,64},{64,80},{80,96},{96,112},{1... | collective-permute-start | bytes 1769480 | tf_op jit(solution)/shard_map/while/body/eval_jaxpr/ppermute | solution.py:10
  378.7 8.7 %collective-permute-start = (bf16[128,1152]{1,0:T(8,128)(2,1)}, bf16[128,1152]{1,0:T(8,128)(2,1)S(1)}, u32[]{:S(2)}, u32[]{:S(2)}) collective-permute-start(bf16[128,1152]{1,0:T(8,128)(2,1)} %get-tuple-element.144), channel_id=1, source_target_pairs={{240,0},{0,16},{16,32},{32,48},{48,64},{64,80},{80,96},{96,112},{1... | collective-permute-start | bytes 884744 | tf_op jit(solution)/shard_map/while/body/eval_jaxpr/ppermute | solution.py:10
  380.6 14.6 %collective-permute-start.1 = (f32[128,1152]{1,0:T(8,128)}, f32[128,1152]{1,0:T(8,128)}, u32[]{:S(2)}, u32[]{:S(2)}) collective-permute-start(f32[128,1152]{1,0:T(8,128)} %broadcast_select_fusion.3), channel_id=1, source_target_pairs={{240,0},{0,16},{16,32},{32,48},{48,64},{64,80},{80,96},{96,112},{1... | collective-permute-start | bytes 1769480 | tf_op jit(solution)/shard_map/while/body/eval_jaxpr/ppermute | solution.py:10
  464.4 34.6 %all-to-all-start.1 = ((bf16[16,12,1152]{2,1,0:T(8,128)(2,1)}), bf16[16,12,1152]{2,1,0:T(8,128)(2,1)}, u32[]{:S(2)}, u32[]{:S(2)}) async-start(bf16[16,12,1152]{2,1,0:T(8,128)(2,1)} %copy.70), calls=%async_computation.1 | async-start | bytes 1179648 | tf_op jit(solution)/shard_map/all_to_all | solution.py:110
  (17 other events, 114.1 us)
Sparse Core Ops, SparseCore 0:
  443.4 295.2 all-reduce.2
where the time goes:
time: 752 us; the launch traced here: 747 us
  waiting for transfers between devices  423 us (56%)
  matrix products  132 us (18%)
  local copies, waits for them, and re-layouts  82.4 us (11%)
  starting transfers between devices  53.2 us (7%)
  other arithmetic  41 us (5%)
  between operations  15 us (2%)
    unnamed x2, waiting for transfers between devices  237 us
    ppermute x32, waiting for transfers between devices, passed_along(): return lax.ppermute(block, axis, route)  170 us
    dot_general x16, matrix products, cycle_turn(): jnp.dot(weights, image_emb, preferred_element_type=jnp.float32)  44.9 us
    dot_general x16, matrix products, cycle_turn(): jnp.einsum('ti,te->ie', weights, moving, preferred_element_type=jnp.float32)  41.4 us
    while x16, other arithmetic  29.5 us
    dot_general x16, matrix products, score_weights(): jnp.einsum('te,ie->ti', moving, resident, preferred_element_type=jnp.floa...  24.8 us
    ppermute x32, starting transfers between devices, passed_along(): return lax.ppermute(block, axis, route)  23 us
    all_to_all x1, starting transfers between devices, per_device(): lax.all_to_all(send_back, 'replica', split_axis=0, concat_axis=0, tiled=T...  21.7 us
  transfers between devices with their start and end apart: 35, of which 35 were waited for; matrix products, arithmetic and copies ran while one was open for 18% of the time, Pallas kernels for 0%

commit v1 on v0

v1 whole, which is shorter than its diff:
```python
import jax
import jax.numpy as jnp
from jax import lax
from jax.sharding import Mesh
from jax.sharding import PartitionSpec as P

BF = jnp.bfloat16
F32 = jnp.float32
CAP_AXES = ("ylo", "z")
REP_AXES = ("x", "yhi", "core")
SLOTS = 12


def shifted(block, axis, distance):
    size = lax.axis_size(axis)
    return lax.ppermute(block, axis, [(i, (i + distance) % size) for i in range(size)])


def gathered_along_z(block):
    half = block.shape[0] // 2
    up, down, found = block, block, [block]
    for _ in range(3):
        up, down = shifted(up, "z", 1), shifted(down, "z", -1)
        found += [up, down]
    return found + [shifted(up[:half], "z", 1), shifted(down[half:], "z", -1)]


def project_rows(features, head_matrix):
    projected = jnp.dot(features, head_matrix, preferred_element_type=F32)
    norm_rows = jnp.sqrt(jnp.sum(projected * projected, axis=-1, keepdims=True) + 1e-06)
    return projected / norm_rows, norm_rows


def pull_back(unit_rows, norm_rows, gradient):
    radial = jnp.sum(unit_rows * gradient, axis=-1, keepdims=True)
    return ((gradient - unit_rows * radial) / norm_rows).astype(BF)


def pair_sums(resident, blocks, temper, offset):
    moving = jnp.concatenate(blocks, axis=0)
    logits = (
        lax.dot_general(resident, moving, (((1,), (1,)), ((), ())), preferred_element_type=F32)
        * temper
        + offset
    )
    weights = jax.nn.sigmoid(logits).astype(BF)
    return jnp.dot(weights, moving, preferred_element_type=F32)


def per_device(
    caption_feats,
    text_head,
    image_pool,
    image_head,
    image_owner,
    image_slot,
    caption_image,
    logit_scale,
    logit_bias,
):
    temper = logit_scale[0]
    offset = logit_bias[0]
    captions = caption_feats[0]
    pool = image_pool[0]
    owners = image_owner[:, :, 0]
    targets = caption_image[0]
    groups, images = owners.shape
    width = pool.shape[1]
    rank = lax.axis_index(REP_AXES)
    core = lax.axis_index("core")

    text_unit, text_norm = project_rows(captions, text_head)
    text_emb = text_unit.astype(BF)
    pool_unit, pool_norm = project_rows(pool, image_head)
    pool_emb = pool_unit.astype(BF)

    ids = jnp.arange(images, dtype=jnp.int32)
    owned = owners == rank
    earlier = (ids[:, None] < ids[None, :]).astype(BF)
    place = jnp.dot(owned.astype(BF), earlier, preferred_element_type=F32).astype(jnp.int32)
    wanted = jnp.arange(SLOTS, dtype=jnp.int32)[None, :, None]
    slot_table = jnp.max(
        jnp.where(owned[:, None, :] & (place[:, None, :] == wanted), image_slot[:, None, :], -1),
        axis=2,
    )
    select = (
        slot_table.reshape(-1)[:, None] == jnp.arange(pool.shape[0], dtype=jnp.int32)[None, :]
    ).astype(BF)
    mine = lax.dynamic_index_in_dim(owners, rank, 0, keepdims=False)
    my_place = jnp.sum(
        ((mine[:, None] == mine[None, :]) & (ids[None, :] < ids[:, None])).astype(jnp.int32), axis=1
    )
    hit = (
        (mine * SLOTS + my_place)[:, None]
        == jnp.arange(groups * SLOTS, dtype=jnp.int32)[None, :]
    ).astype(BF)

    outgoing = jnp.dot(select, pool_emb, preferred_element_type=F32).astype(BF)
    arrived = lax.all_to_all(
        outgoing.reshape(groups, SLOTS, width), REP_AXES, 0, 0, tiled=True
    ).reshape(groups * SLOTS, width)
    image_emb = jnp.dot(hit, arrived, preferred_element_type=F32).astype(BF)

    other_text = shifted(text_emb, "ylo", 1)
    text_blocks = gathered_along_z(text_emb)
    other_image = shifted(image_emb, "ylo", 1)
    image_blocks = gathered_along_z(image_emb)

    first = core == 0
    my_kind = jnp.where(first, captions, pool)
    its_kind = shifted(jnp.where(first, pool, captions), "core", 1)
    kind_feats = jnp.stack([jnp.where(first, my_kind, its_kind), jnp.where(first, its_kind, my_kind)])
    kind_feats = lax.all_gather(kind_feats.reshape(-1, width), "x", axis=0, tiled=True)

    target_hits = (targets[None, :] == ids[:, None]).astype(BF)
    image_sums = pair_sums(
        jnp.concatenate([image_emb, other_image]), text_blocks, temper, offset
    )
    image_rest = shifted(image_sums[images:].astype(BF), "ylo", 1)
    matched = jnp.dot(target_hits, text_emb, preferred_element_type=F32)
    image_grad = temper * (image_sums[:images] + image_rest.astype(F32) - matched)

    captions_here = captions.shape[0]
    text_sums = pair_sums(jnp.concatenate([text_emb, other_text]), image_blocks, temper, offset)
    text_rest = shifted(text_sums[captions_here:].astype(BF), "ylo", 1)
    positive = lax.dot_general(
        target_hits, image_emb, (((0,), (0,)), ((), ())), preferred_element_type=F32
    )
    text_grad = temper * (text_sums[:captions_here] + text_rest.astype(F32) - positive)

    send_back = lax.dot_general(
        hit, image_grad.astype(BF), (((0,), (0,)), ((), ())), preferred_element_type=F32
    ).astype(BF)
    received = lax.all_to_all(
        send_back.reshape(groups, SLOTS, width), REP_AXES, 0, 0, tiled=True
    ).reshape(groups * SLOTS, width)
    pool_emb_grad = lax.dot_general(
        select, received, (((0,), (0,)), ((), ())), preferred_element_type=F32
    )

    text_proj_grad = pull_back(text_unit, text_norm, text_grad)
    pool_proj_grad = pull_back(pool_unit, pool_norm, pool_emb_grad)
    back = (((1,), (1,)), ((), ()))
    text_feat_grad = lax.dot_general(
        text_proj_grad, text_head, back, preferred_element_type=F32
    ).astype(BF)
    pool_grad = lax.dot_general(
        pool_proj_grad, image_head, back, preferred_element_type=F32
    ).astype(BF)

    four = lax.axis_size("x")
    strip = width // four
    by_strip = jnp.stack(
        [
            text_proj_grad.T.reshape(four, strip, -1),
            pool_proj_grad.T.reshape(four, strip, -1),
        ],
        axis=1,
    ).reshape(2 * four, strip, -1)
    strips = lax.all_to_all(by_strip, ("x", "core"), 0, 0, tiled=True)
    kind_feats = kind_feats.reshape(2 * four, -1, width)
    part = lax.dot_general(
        kind_feats, strips, (((0, 1), (0, 2)), ((), ())), preferred_element_type=F32
    ).astype(BF)
    part = part.reshape(2, 8, four, 2, 9, strip).transpose(0, 1, 3, 2, 4, 5)
    part = lax.all_to_all(
        part.reshape(32, 9 * four, strip), ("ylo", "z", "yhi"), 0, 0, tiled=True
    )
    rows = jnp.sum(part.astype(F32), axis=0).reshape(four, 9, strip)
    rows = jnp.stack([rows[:, :5], rows[:, 4:]], axis=1).reshape(2 * four, 5, strip)
    rows = lax.all_to_all(rows, ("x", "core"), 0, 0, tiled=True)
    rows = rows.reshape(four, 2, 5, strip).transpose(2, 1, 0, 3).reshape(10, width)
    head_share = jnp.where(first, rows[:9], rows[1:])
    return text_feat_grad[None], pool_grad[None], head_share


def solution(mesh):
    fine = Mesh(mesh.devices.reshape(2, 8, 4, 2, 2), CAP_AXES + REP_AXES)
    in_specs = (
        P(REP_AXES, CAP_AXES, None),
        P(),
        P(CAP_AXES, REP_AXES, None),
        P(),
        P(None, CAP_AXES, None),
        P(None, CAP_AXES),
        P(REP_AXES, CAP_AXES),
        P(),
        P(),
    )
    out_specs = (
        P(REP_AXES, CAP_AXES, None),
        P(CAP_AXES, REP_AXES, None),
        P(CAP_AXES + REP_AXES, None),
    )
    return jax.shard_map(
        per_device, mesh=fine, in_specs=in_specs, out_specs=out_specs, check_vma=False
    )
```

time: 752 us -> 234 us (0.31)
  waiting for transfers between devices: 423 us -> 57.4 us
  matrix products: 132 us -> 30.7 us
  local copies, waits for them, and re-layouts: 82.4 us -> 46.2 us
  other arithmetic: 41 us -> 12.1 us
  blocking collectives: 0 us -> 14.9 us
    unnamed x2 -> x1, waiting for transfers between devices: 237 us -> 0.02 us
    ppermute x32 -> x21, waiting for transfers between devices: 170 us -> 24.1 us  [shifted(): lax.ppermute(block, axis, [(i, (i + distance) % size) for i in range(size)])]
    dot_general x56 -> x13, matrix products: 132 us -> 30.7 us  [the longest x2 9.75 us: pair_sums(): return jnp.dot(weights, moving, preferred_element_type=F32)]
    while x16 -> x0, other arithmetic: 29.5 us -> none
    all_to_all x2 -> x4, waiting for transfers between devices: 15.4 us -> 33.3 us  [the longest x1 23.3 us: per_device(): lax.all_to_all(part.reshape(32, 9 * four, strip), ('ylo', 'z', 'yhi'), 0,...]
    another operation x2, local copies, waits for them, and re-layouts: 17.5 us -> 0.05 us  [the longest x1 0.04 us: per_device(): jnp.stack([text_proj_grad.T.reshape(four, strip, -1), pool_proj_grad.T.re...]
    scatter x3 -> x0, local copies, waits for them, and re-layouts: 16.8 us -> none  [the longest x2 16.7 us: per_device(): jnp.zeros(arrived.shape, jnp.bfloat16).at[my_owners, my_places]]
    all_to_all x0 -> x1, blocking collectives: none -> 14.9 us  [per_device(): strips = lax.all_to_all(by_strip, ('x', 'core'), 0, 0, tiled=True)]
  transfers between devices with their start and end apart: 35 -> 26, of which waited for: 35 -> 9; matrix products, arithmetic and copies ran while one was open for 18% -> 27% of each run, Pallas kernels for 0% -> 0%
where the time goes in v1:
time: 234 us; the launch traced here: 232 us
  waiting for transfers between devices  57.4 us (25%)
  starting transfers between devices  55.3 us (24%)
  local copies, waits for them, and re-layouts  46.2 us (20%)
  matrix products  30.7 us (13%)
  between operations  15.8 us (7%)
  blocking collectives  14.9 us (6%)
  other arithmetic  12.1 us (5%)
    ppermute x21, waiting for transfers between devices, shifted(): lax.ppermute(block, axis, [(i, (i + distance) % size) for i in range(size)])  24.1 us
    all_to_all x1, waiting for transfers between devices, per_device(): lax.all_to_all(part.reshape(32, 9 * four, strip), ('ylo', 'z', 'yhi'), 0,...  23.3 us
    ppermute x21, starting transfers between devices, shifted(): lax.ppermute(block, axis, [(i, (i + distance) % size) for i in range(size)])  21.9 us
    unnamed x47, local copies, waits for them, and re-layouts  18.6 us
    all_to_all x1, blocking collectives, per_device(): strips = lax.all_to_all(by_strip, ('x', 'core'), 0, 0, tiled=True)  14.9 us
    all_to_all x1, starting transfers between devices, per_device(): lax.all_to_all(send_back.reshape(groups, SLOTS, width), REP_AXES, 0, 0, t...  12.7 us
    dot_general x2, matrix products, pair_sums(): return jnp.dot(weights, moving, preferred_element_type=F32)  9.75 us
    all_to_all x1, waiting for transfers between devices, per_device(): lax.all_to_all(send_back.reshape(groups, SLOTS, width), REP_AXES, 0, 0, t...  8.61 us
  transfers between devices with their start and end apart: 26, of which 9 were waited for; matrix products, arithmetic and copies ran while one was open for 27% of the time, Pallas kernels for 0%

profile of v1, /device:TPU:1, one launch (start us, length us, event | category | flops | bytes accessed | tf_op | source)
XLA Modules:
  0.0 232.4 jit_solution(2678045798743832902)
XLA Ops:
  12.0 2.5 %collective-permute-start.11 = (bf16[128,1152]{1,0:T(8,128)(2,1)}, bf16[128,1152]{1,0:T(8,128)(2,1)}, u32[]{:S(2)}, u32[]{:S(2)}) collective-permute-start(bf16[128,1152]{1,0:T(8,128)(2,1)} %get-tuple-element.4), channel_id=1, source_target_pairs={{0,16},{16,32},{32,48},{48,64},{64,80},{80,96},{96,112},{112,0},{1... | collective-permute-start | bytes 884744 | tf_op jit(solution)/shard_map/ppermute | solution.py:16
  14.5 3.9 %collective-permute-start.12 = (bf16[128,1152]{1,0:T(8,128)(2,1)}, bf16[128,1152]{1,0:T(8,128)(2,1)}, u32[]{:S(2)}, u32[]{:S(2)}) collective-permute-start(bf16[128,1152]{1,0:T(8,128)(2,1)} %get-tuple-element.4), channel_id=1, source_target_pairs={{0,112},{16,0},{32,16},{48,32},{64,48},{80,64},{96,80},{112,96},{1... | collective-permute-start | bytes 884744 | tf_op jit(solution)/shard_map/ppermute | solution.py:16
  20.4 2.4 %multiply_reduce_fusion.2 = (f32[128]{0:T(128)S(1)}, f32[128,1152]{1,0:T(8,128)S(1)}) fusion(bf16[1152,1152]{1,0:T(8,128)(2,1)} %param.12, bf16[1,128,1152]{2,1,0:T(8,128)(2,1)S(1)} %copy-done.1), kind=kOutput, calls=%fused_computation.40 | convolution fusion | flops 340033408 | bytes 3539456 | tf_op jit(solution)/shard_map/dot_general | solution.py:29
  24.8 1.9 reshape.82
  26.8 7.9 %all-to-all-start = ((bf16[16,12,1152]{2,1,0:T(8,128)(2,1)}), bf16[16,12,1152]{2,1,0:T(8,128)(2,1)}, u32[]{:S(2)}, u32[]{:S(2)}) async-start(bf16[16,12,1152]{2,1,0:T(8,128)(2,1)} %reshape.82), calls=%async_computation | async-start | bytes 1179648 | tf_op jit(solution)/shard_map/all_to_all | solution.py:99
  41.6 2.7 %collective-permute-start.14 = (bf16[128,1152]{1,0:T(8,128)(2,1)}, bf16[128,1152]{1,0:T(8,128)(2,1)}, u32[]{:S(2)}, u32[]{:S(2)}) collective-permute-start(bf16[128,1152]{1,0:T(8,128)(2,1)} %collective-permute-done.12), channel_id=1, source_target_pairs={{0,112},{16,0},{32,16},{48,32},{64,48},{80,64},{96,80},{112,96},{1... | collective-permute-start | bytes 884744 | tf_op jit(solution)/shard_map/ppermute | solution.py:16
  47.6 1.9 reshape.83
  51.3 2.4 %collective-permute-start.2 = (bf16[96,1152]{1,0:T(8,128)(2,1)S(1)}, bf16[96,1152]{1,0:T(8,128)(2,1)S(1)}, u32[]{:S(2)}, u32[]{:S(2)}) collective-permute-start(bf16[96,1152]{1,0:T(8,128)(2,1)S(1)} %get-tuple-element.12), channel_id=1, source_target_pairs={{0,112},{16,0},{32,16},{48,32},{64,48},{80,64},{96,80},{112,96},{1... | collective-permute-start | bytes 663560 | tf_op jit(solution)/shard_map/ppermute | solution.py:16
  60.0 9.0 %collective-permute-done.3 = bf16[96,1152]{1,0:T(8,128)(2,1)} collective-permute-done((bf16[96,1152]{1,0:T(8,128)(2,1)S(1)}, bf16[96,1152]{1,0:T(8,128)(2,1)}, u32[]{:S(2)}, u32[]{:S(2)}) %collective-permute-start.3) | collective-permute-done | bytes 221216 | tf_op jit(solution)/shard_map/ppermute | solution.py:16
  69.9 4.2 %collective-permute-done.4 = bf16[96,1152]{1,0:T(8,128)(2,1)} collective-permute-done((bf16[96,1152]{1,0:T(8,128)(2,1)S(1)}, bf16[96,1152]{1,0:T(8,128)(2,1)}, u32[]{:S(2)}, u32[]{:S(2)}) %collective-permute-start.4) | collective-permute-done | bytes 221216 | tf_op jit(solution)/shard_map/ppermute | solution.py:16
  75.1 2.7 %collective-permute-start.6 = (bf16[96,1152]{1,0:T(8,128)(2,1)}, bf16[96,1152]{1,0:T(8,128)(2,1)}, u32[]{:S(2)}, u32[]{:S(2)}) collective-permute-start(bf16[96,1152]{1,0:T(8,128)(2,1)} %collective-permute-done.4), channel_id=1, source_target_pairs={{0,112},{16,0},{32,16},{48,32},{64,48},{80,64},{96,80},{112,96},{1... | collective-permute-start | bytes 663560 | tf_op jit(solution)/shard_map/ppermute | solution.py:16
  79.4 6.3 %collective-permute-done.17 = bf16[64,1152]{1,0:T(8,128)(2,1)S(1)} collective-permute-done((bf16[64,1152]{1,0:T(8,128)(2,1)S(1)}, bf16[64,1152]{1,0:T(8,128)(2,1)S(1)}, u32[]{:S(2)}, u32[]{:S(2)}) %collective-permute-start.17) | collective-permute-done | bytes 147488 | tf_op jit(solution)/shard_map/ppermute | solution.py:16
  86.3 3.3 %collective-permute-done.18 = bf16[64,1152]{1,0:T(8,128)(2,1)S(1)} collective-permute-done((bf16[64,1152]{1,0:T(8,128)(2,1)S(1)}, bf16[64,1152]{1,0:T(8,128)(2,1)S(1)}, u32[]{:S(2)}, u32[]{:S(2)}) %collective-permute-start.18) | collective-permute-done | bytes 147488 | tf_op jit(solution)/shard_map/ppermute | solution.py:16
  91.0 5.0 %fusion.16 = f32[192,1152]{1,0:T(8,128)} fusion(bf16[1024,1152]{1,0:T(8,128)(2,1)} %constant_dynamic-update-slice_fusion.9, bf16[96,1152]{1,0:T(8,128)(2,1)} %copy-done.14, bf16[96,1152]{1,0:T(8,128)(2,1)} %copy-done.5, f32[]{:T(128)} %bitcast.84, f32[]{:T(128)} %bitcast.81), kind=kOutput, calls=%fused_computation.26 | convolution fusion | flops 908034048 | bytes 3686408 | tf_op jit(solution)/shard_map/dot_general | solution.py:47
  99.9 2.7 %collective-permute-start.8 = (bf16[48,1152]{1,0:T(8,128)(2,1)S(1)}, bf16[48,1152]{1,0:T(8,128)(2,1)S(1)}, u32[]{:S(2)}, u32[]{:S(2)}) collective-permute-start(bf16[48,1152]{1,0:T(8,128)(2,1)S(1)} %slice.51), channel_id=1, source_target_pairs={{0,112},{16,0},{32,16},{48,32},{64,48},{80,64},{96,80},{112,96},{1... | collective-permute-start | bytes 331784 | tf_op jit(solution)/shard_map/ppermute | solution.py:16
  106.3 4.7 %fusion.15 = f32[256,1152]{1,0:T(8,128)} fusion(bf16[768,1152]{1,0:T(8,128)(2,1)} %constant_dynamic-update-slice_fusion, bf16[128,1152]{1,0:T(8,128)(2,1)} %collective-permute-done, bf16[128,1152]{1,0:T(8,128)(2,1)} %get-tuple-element.4, f32[]{:T(128)} %bitcast.83, f32[]{:T(128)} %bitcast.79), kind=kOutput, calls=%fused_computation.25 | convolution fusion | flops 908328960 | bytes 3538952 | tf_op jit(solution)/shard_map/dot_general | solution.py:47
  111.1 1.8 slice.85
  113.2 2.3 %convolution_convert_fusion = bf16[192,1152]{1,0:T(8,128)(2,1)} fusion(f32[192,1152]{1,0:T(8,128)} %fusion.16, bf16[96,1152]{1,0:T(8,128)(2,1)} %collective-permute-done.19, f32[]{:T(128)} %bitcast.80, bf16[128,1152]{1,0:T(8,128)(2,1)} %get-tuple-element.4, s32[96]{0:T(128)S(1)} %multiply_add_fusion, s32[128]{0:T(128)S(1)} %bitcast.97), kind=kOutput, calls=%fused_computation.2 | convolution fusion | flops 71583744 | bytes 1402240 | tf_op jit(solution)/shard_map/dot_general | solution.py:131
  115.5 1.9 reshape.84
  117.5 12.7 %all-to-all-start.1 = ((bf16[16,12,1152]{2,1,0:T(8,128)(2,1)}), bf16[16,12,1152]{2,1,0:T(8,128)(2,1)}, u32[]{:S(2)}, u32[]{:S(2)}) async-start(bf16[16,12,1152]{2,1,0:T(8,128)(2,1)} %reshape.84), calls=%async_computation.1 | async-start | bytes 1179648 | tf_op jit(solution)/shard_map/all_to_all | solution.py:134
  133.4 8.6 %all-to-all-done.1 = bf16[16,12,1152]{2,1,0:T(8,128)(2,1)} async-done(((bf16[16,12,1152]{2,1,0:T(8,128)(2,1)}), bf16[16,12,1152]{2,1,0:T(8,128)(2,1)}, u32[]{:S(2)}, u32[]{:S(2)}) %all-to-all-start.1) | async-done | bytes 442400 | tf_op jit(solution)/shard_map/all_to_all | solution.py:134
  142.0 1.9 reshape.85
  148.8 14.9 %all_to_all.25 = bf16[8,288,128]{2,1,0:T(8,128)(2,1)} all-to-all(bf16[8,288,128]{2,1,0:T(8,128)(2,1)S(1)} %bitcast.89), channel_id=1, replica_groups=mesh['ylo'=2,'z'=8,'x'=4,'yhi'=2,'core'=2] {'x','core'}, dimensions={0} | all-to-all | bytes 1179648 | tf_op jit(solution)/shard_map/all_to_all | solution.py:160
  163.8 3.6 %fusion = bf16[1152,288]{0,1:T(8,128)(2,1)} fusion(bf16[8,288,128]{2,1,0:T(8,128)(2,1)} %all_to_all.25, bf16[8,128,1152]{2,1,0:T(8,128)(2,1)} %bitcast.99), kind=kOutput, calls=%fused_computation.1 | convolution fusion | flops 679809024 | bytes 3612672 | tf_op jit(solution)/shard_map/dot_general | solution.py:162
  167.4 2.3 %copy.50 = bf16[1152,288]{1,0:T(8,128)(2,1)} copy(bf16[1152,288]{0,1:T(8,128)(2,1)} %fusion) | data formatting | bytes 1327104 | tf_op jit(solution)/shard_map/convert_element_type | solution.py:164
  169.7 3.0 %reshape.89 = bf16[2,8,4,2,9,288]{5,4,3,2,1,0:T(8,128)(2,1)} reshape(bf16[1152,288]{1,0:T(8,128)(2,1)} %copy.50) | data formatting | bytes 1327104 | tf_op jit(solution)/shard_map/reshape | solution.py:165
  172.8 2.8 %copy.57 = bf16[2,8,2,4,9,288]{5,4,3,2,1,0:T(8,128)(2,1)} copy(bf16[2,8,2,4,9,288]{5,4,2,3,1,0:T(8,128)(2,1)} %bitcast.85) | data formatting | bytes 1327104 | tf_op jit(solution)/shard_map/reshape | solution.py:167
  175.6 3.2 %reshape.96 = bf16[32,36,288]{2,1,0:T(8,128)(2,1)} reshape(bf16[2,8,2,4,9,288]{5,4,3,2,1,0:T(8,128)(2,1)} %copy.57) | data formatting | bytes 1327104 | tf_op jit(solution)/shard_map/reshape | solution.py:167
  178.8 6.5 %all-to-all-start.3 = ((bf16[32,36,288]{2,1,0:T(8,128)(2,1)}), bf16[32,36,288]{2,1,0:T(8,128)(2,1)}, u32[]{:S(2)}, u32[]{:S(2)}) async-start(bf16[32,36,288]{2,1,0:T(8,128)(2,1)} %reshape.96), calls=%async_computation.3 | async-start | bytes 1966080 | tf_op jit(solution)/shard_map/all_to_all | solution.py:166
  186.9 23.3 %all-to-all-done.3 = bf16[32,36,288]{2,1,0:T(8,128)(2,1)} async-done(((bf16[32,36,288]{2,1,0:T(8,128)(2,1)}), bf16[32,36,288]{2,1,0:T(8,128)(2,1)}, u32[]{:S(2)}, u32[]{:S(2)}) %all-to-all-start.3) | async-done | bytes 663584 | tf_op jit(solution)/shard_map/all_to_all | solution.py:166
  212.3 6.3 %all-to-all-start.4 = ((f32[8,1,1440]{2,1,0:T(1,128)}), f32[8,1,1440]{2,1,0:T(1,128)S(1)}, u32[]{:S(2)}, u32[]{:S(2)}) async-start(f32[8,1,1440]{2,1,0:T(1,128)} %reshape.97), calls=%async_computation.4 | async-start | bytes 98304 | tf_op jit(solution)/shard_map/all_to_all | solution.py:171
  218.6 3.4 %fusion.2 = bf16[1,128,1152]{2,1,0:T(8,128)(2,1)} fusion(bf16[128,1152]{1,0:T(8,128)(2,1)S(1)} %divide_convert_fusion, bf16[1152,1152]{1,0:T(8,128)(2,1)} %param.12), kind=kOutput, calls=%fused_computation.8 | convolution fusion | flops 339886080 | bytes 3244032 | tf_op jit(solution)/shard_map/dot_general | solution.py:147
  (128 shorter events, 54.3 us)
Async XLA Ops:
  7.2 12.6 %copy-start.7 = (s32[16,96,1]{1,2,0:T(1,128)S(1)}, s32[16,96,1]{1,2,0:T(1,128)}, u32[]{:S(2)}) copy-start(s32[16,96,1]{1,2,0:T(1,128)} %param.13) | copy-start | bytes 18436
  7.2 12.7 %copy-start.8 = (s32[16,96]{1,0:T(8,128)S(1)}, s32[16,96]{1,0:T(8,128)}, u32[]{:S(2)}) copy-start(s32[16,96]{1,0:T(8,128)} %param.14) | copy-start | bytes 18436
  7.2 13.2 %copy-start.1 = (bf16[1,128,1152]{2,1,0:T(8,128)(2,1)S(1)}, bf16[1,128,1152]{2,1,0:T(8,128)(2,1)}, u32[]{:S(2)}) copy-start(bf16[1,128,1152]{2,1,0:T(8,128)(2,1)} %param.11) | copy-start | bytes 884740
  12.0 29.4 %collective-permute-start.11 = (bf16[128,1152]{1,0:T(8,128)(2,1)}, bf16[128,1152]{1,0:T(8,128)(2,1)}, u32[]{:S(2)}, u32[]{:S(2)}) collective-permute-start(bf16[128,1152]{1,0:T(8,128)(2,1)} %get-tuple-element.4), channel_id=1, source_target_pairs={{0,16},{16,32},{32,48},{48,64},{64,80},{80,96},{96,112},{112,0},{1... | collective-permute-start | bytes 884744 | tf_op jit(solution)/shard_map/ppermute | solution.py:16
  14.5 27.0 %collective-permute-start.12 = (bf16[128,1152]{1,0:T(8,128)(2,1)}, bf16[128,1152]{1,0:T(8,128)(2,1)}, u32[]{:S(2)}, u32[]{:S(2)}) collective-permute-start(bf16[128,1152]{1,0:T(8,128)(2,1)} %get-tuple-element.4), channel_id=1, source_target_pairs={{0,112},{16,0},{32,16},{48,32},{64,48},{80,64},{96,80},{112,96},{1... | collective-permute-start | bytes 884744 | tf_op jit(solution)/shard_map/ppermute | solution.py:16
  18.5 87.9 %collective-permute-start = (bf16[128,1152]{1,0:T(8,128)(2,1)}, bf16[128,1152]{1,0:T(8,128)(2,1)}, u32[]{:S(2)}, u32[]{:S(2)}) collective-permute-start(bf16[128,1152]{1,0:T(8,128)(2,1)} %get-tuple-element.4), channel_id=1, source_target_pairs={{0,128},{128,0},{1,129},{129,1},{2,130},{130,2},{3,131},{131,3},{4... | collective-permute-start | bytes 884744 | tf_op jit(solution)/shard_map/ppermute | solution.py:16
  26.8 20.8 %all-to-all-start = ((bf16[16,12,1152]{2,1,0:T(8,128)(2,1)}), bf16[16,12,1152]{2,1,0:T(8,128)(2,1)}, u32[]{:S(2)}, u32[]{:S(2)}) async-start(bf16[16,12,1152]{2,1,0:T(8,128)(2,1)} %reshape.82), calls=%async_computation | async-start | bytes 1179648 | tf_op jit(solution)/shard_map/all_to_all | solution.py:99
  34.7 129.1 %all-gather.2.cloned.1.call-start = ((), (), s32[]{:S(2)}) async-start(), calls=%async_computation.5 | async-start | bytes 2949120 | tf_op jit(solution)/shard_map/all_gather | solution.py:113
  36.4 3.0 %collective-permute-start.20 = (bf16[128,1152]{1,0:T(8,128)(2,1)}, bf16[128,1152]{1,0:T(8,128)(2,1)}, u32[]{:S(2)}, u32[]{:S(2)}) collective-permute-start(bf16[128,1152]{1,0:T(8,128)(2,1)} %bitcast_select_fusion), channel_id=1, source_target_pairs={{0,1},{1,0},{2,3},{3,2},{4,5},{5,4},{6,7},{7,6},{8,9},{9,8},{10,11... | collective-permute-start | bytes 884744 | tf_op jit(solution)/shard_map/ppermute | solution.py:16
  41.5 9.8 %collective-permute-start.13 = (bf16[128,1152]{1,0:T(8,128)(2,1)}, bf16[128,1152]{1,0:T(8,128)(2,1)}, u32[]{:S(2)}, u32[]{:S(2)}) collective-permute-start(bf16[128,1152]{1,0:T(8,128)(2,1)} %collective-permute-done.11), channel_id=1, source_target_pairs={{0,16},{16,32},{32,48},{48,64},{64,80},{80,96},{96,112},{112,0},{1... | collective-permute-start | bytes 884744 | tf_op jit(solution)/shard_map/ppermute | solution.py:16
  41.6 13.8 %collective-permute-start.14 = (bf16[128,1152]{1,0:T(8,128)(2,1)}, bf16[128,1152]{1,0:T(8,128)(2,1)}, u32[]{:S(2)}, u32[]{:S(2)}) collective-permute-start(bf16[128,1152]{1,0:T(8,128)(2,1)} %collective-permute-done.12), channel_id=1, source_target_pairs={{0,112},{16,0},{32,16},{48,32},{64,48},{80,64},{96,80},{112,96},{1... | collective-permute-start | bytes 884744 | tf_op jit(solution)/shard_map/ppermute | solution.py:16
  50.8 28.5 %copy-start.5 = (bf16[96,1152]{1,0:T(8,128)(2,1)}, bf16[96,1152]{1,0:T(8,128)(2,1)S(1)}, u32[]{:S(2)}) copy-start(bf16[96,1152]{1,0:T(8,128)(2,1)S(1)} %get-tuple-element.12) | copy-start | bytes 663556
  50.8 39.5 %collective-permute-start.10 = (bf16[96,1152]{1,0:T(8,128)(2,1)S(1)}, bf16[96,1152]{1,0:T(8,128)(2,1)S(1)}, u32[]{:S(2)}, u32[]{:S(2)}) collective-permute-start(bf16[96,1152]{1,0:T(8,128)(2,1)S(1)} %get-tuple-element.12), channel_id=1, source_target_pairs={{0,128},{128,0},{1,129},{129,1},{2,130},{130,2},{3,131},{131,3},{4... | collective-permute-start | bytes 663560 | tf_op jit(solution)/shard_map/ppermute | solution.py:16
  50.9 7.2 %collective-permute-start.1 = (bf16[96,1152]{1,0:T(8,128)(2,1)S(1)}, bf16[96,1152]{1,0:T(8,128)(2,1)S(1)}, u32[]{:S(2)}, u32[]{:S(2)}) collective-permute-start(bf16[96,1152]{1,0:T(8,128)(2,1)S(1)} %get-tuple-element.12), channel_id=1, source_target_pairs={{0,16},{16,32},{32,48},{48,64},{64,80},{80,96},{96,112},{112,0},{1... | collective-permute-start | bytes 663560 | tf_op jit(solution)/shard_map/ppermute | solution.py:16
  51.3 8.5 %collective-permute-start.2 = (bf16[96,1152]{1,0:T(8,128)(2,1)S(1)}, bf16[96,1152]{1,0:T(8,128)(2,1)S(1)}, u32[]{:S(2)}, u32[]{:S(2)}) collective-permute-start(bf16[96,1152]{1,0:T(8,128)(2,1)S(1)} %get-tuple-element.12), channel_id=1, source_target_pairs={{0,112},{16,0},{32,16},{48,32},{64,48},{80,64},{96,80},{112,96},{1... | collective-permute-start | bytes 663560 | tf_op jit(solution)/shard_map/ppermute | solution.py:16
  55.4 19.7 %collective-permute-start.15 = (bf16[128,1152]{1,0:T(8,128)(2,1)}, bf16[128,1152]{1,0:T(8,128)(2,1)S(1)}, u32[]{:S(2)}, u32[]{:S(2)}) collective-permute-start(bf16[128,1152]{1,0:T(8,128)(2,1)} %collective-permute-done.13), channel_id=1, source_target_pairs={{0,16},{16,32},{32,48},{48,64},{64,80},{80,96},{96,112},{112,0},{1... | collective-permute-start | bytes 884744 | tf_op jit(solution)/shard_map/ppermute | solution.py:16
  58.2 20.4 %collective-permute-start.16 = (bf16[128,1152]{1,0:T(8,128)(2,1)}, bf16[128,1152]{1,0:T(8,128)(2,1)S(1)}, u32[]{:S(2)}, u32[]{:S(2)}) collective-permute-start(bf16[128,1152]{1,0:T(8,128)(2,1)} %collective-permute-done.14), channel_id=1, source_target_pairs={{0,112},{16,0},{32,16},{48,32},{64,48},{80,64},{96,80},{112,96},{1... | collective-permute-start | bytes 884744 | tf_op jit(solution)/shard_map/ppermute | solution.py:16
  59.9 9.1 %collective-permute-start.3 = (bf16[96,1152]{1,0:T(8,128)(2,1)S(1)}, bf16[96,1152]{1,0:T(8,128)(2,1)}, u32[]{:S(2)}, u32[]{:S(2)}) collective-permute-start(bf16[96,1152]{1,0:T(8,128)(2,1)S(1)} %collective-permute-done.1), channel_id=1, source_target_pairs={{0,16},{16,32},{32,48},{48,64},{64,80},{80,96},{96,112},{112,0},{1... | collective-permute-start | bytes 663560 | tf_op jit(solution)/shard_map/ppermute | solution.py:16
  68.9 5.2 %collective-permute-start.4 = (bf16[96,1152]{1,0:T(8,128)(2,1)S(1)}, bf16[96,1152]{1,0:T(8,128)(2,1)}, u32[]{:S(2)}, u32[]{:S(2)}) collective-permute-start(bf16[96,1152]{1,0:T(8,128)(2,1)S(1)} %collective-permute-done.2), channel_id=1, source_target_pairs={{0,112},{16,0},{32,16},{48,32},{64,48},{80,64},{96,80},{112,96},{1... | collective-permute-start | bytes 663560 | tf_op jit(solution)/shard_map/ppermute | solution.py:16
  74.1 24.8 %collective-permute-start.5 = (bf16[96,1152]{1,0:T(8,128)(2,1)}, bf16[96,1152]{1,0:T(8,128)(2,1)S(1)}, u32[]{:S(2)}, u32[]{:S(2)}) collective-permute-start(bf16[96,1152]{1,0:T(8,128)(2,1)} %collective-permute-done.3), channel_id=1, source_target_pairs={{0,16},{16,32},{32,48},{48,64},{64,80},{80,96},{96,112},{112,0},{1... | collective-permute-start | bytes 663560 | tf_op jit(solution)/shard_map/ppermute | solution.py:16
  75.1 15.2 %copy-start.6 = (bf16[768,1152]{1,0:T(8,128)(2,1)}, bf16[768,1152]{1,0:T(8,128)(2,1)S(1)}, u32[]{:S(2)}) copy-start(bf16[768,1152]{1,0:T(8,128)(2,1)S(1)} %constant_dynamic-update-slice_fusion.4) | copy-start | bytes 5308420
  75.1 23.9 %collective-permute-start.6 = (bf16[96,1152]{1,0:T(8,128)(2,1)}, bf16[96,1152]{1,0:T(8,128)(2,1)}, u32[]{:S(2)}, u32[]{:S(2)}) collective-permute-start(bf16[96,1152]{1,0:T(8,128)(2,1)} %collective-permute-done.4), channel_id=1, source_target_pairs={{0,112},{16,0},{32,16},{48,32},{64,48},{80,64},{96,80},{112,96},{1... | collective-permute-start | bytes 663560 | tf_op jit(solution)/shard_map/ppermute | solution.py:16
  78.6 7.0 %collective-permute-start.17 = (bf16[64,1152]{1,0:T(8,128)(2,1)S(1)}, bf16[64,1152]{1,0:T(8,128)(2,1)S(1)}, u32[]{:S(2)}, u32[]{:S(2)}) collective-permute-start(bf16[64,1152]{1,0:T(8,128)(2,1)S(1)} %slice.54), channel_id=1, source_target_pairs={{0,16},{16,32},{32,48},{48,64},{64,80},{80,96},{96,112},{112,0},{1... | collective-permute-start | bytes 442376 | tf_op jit(solution)/shard_map/ppermute | solution.py:16
  85.6 4.0 %collective-permute-start.18 = (bf16[64,1152]{1,0:T(8,128)(2,1)S(1)}, bf16[64,1152]{1,0:T(8,128)(2,1)S(1)}, u32[]{:S(2)}, u32[]{:S(2)}) collective-permute-start(bf16[64,1152]{1,0:T(8,128)(2,1)S(1)} %slice.55), channel_id=1, source_target_pairs={{0,112},{16,0},{32,16},{48,32},{64,48},{80,64},{96,80},{112,96},{1... | collective-permute-start | bytes 442376 | tf_op jit(solution)/shard_map/ppermute | solution.py:16
  97.7 15.5 %collective-permute-start.19 = (bf16[96,1152]{1,0:T(8,128)(2,1)}, bf16[96,1152]{1,0:T(8,128)(2,1)}, u32[]{:S(2)}, u32[]{:S(2)}) collective-permute-start(bf16[96,1152]{1,0:T(8,128)(2,1)} %slice.86), channel_id=1, source_target_pairs={{0,128},{128,0},{1,129},{129,1},{2,130},{130,2},{3,131},{131,3},{4... | collective-permute-start | bytes 663560 | tf_op jit(solution)/shard_map/ppermute | solution.py:16
  98.9 6.1 %collective-permute-start.7 = (bf16[48,1152]{1,0:T(8,128)(2,1)S(1)}, bf16[48,1152]{1,0:T(8,128)(2,1)S(1)}, u32[]{:S(2)}, u32[]{:S(2)}) collective-permute-start(bf16[48,1152]{1,0:T(8,128)(2,1)S(1)} %slice.50), channel_id=1, source_target_pairs={{0,16},{16,32},{32,48},{48,64},{64,80},{80,96},{96,112},{112,0},{1... | collective-permute-start | bytes 331784 | tf_op jit(solution)/shard_map/ppermute | solution.py:16
  99.9 5.7 %collective-permute-start.8 = (bf16[48,1152]{1,0:T(8,128)(2,1)S(1)}, bf16[48,1152]{1,0:T(8,128)(2,1)S(1)}, u32[]{:S(2)}, u32[]{:S(2)}) collective-permute-start(bf16[48,1152]{1,0:T(8,128)(2,1)S(1)} %slice.51), channel_id=1, source_target_pairs={{0,112},{16,0},{32,16},{48,32},{64,48},{80,64},{96,80},{112,96},{1... | collective-permute-start | bytes 331784 | tf_op jit(solution)/shard_map/ppermute | solution.py:16
  111.1 19.2 %copy-start.10 = (f32[128]{0:T(128)S(1)}, f32[128]{0:T(128)}, u32[]{:S(2)}) copy-start(f32[128]{0:T(128)} %copy-done.9) | copy-start | bytes 1540
  112.9 17.4 %collective-permute-start.9 = (bf16[128,1152]{1,0:T(8,128)(2,1)}, bf16[128,1152]{1,0:T(8,128)(2,1)S(1)}, u32[]{:S(2)}, u32[]{:S(2)}) collective-permute-start(bf16[128,1152]{1,0:T(8,128)(2,1)} %slice.85), channel_id=1, source_target_pairs={{0,128},{128,0},{1,129},{129,1},{2,130},{130,2},{3,131},{131,3},{4... | collective-permute-start | bytes 884744 | tf_op jit(solution)/shard_map/ppermute | solution.py:16
  117.5 24.5 %all-to-all-start.1 = ((bf16[16,12,1152]{2,1,0:T(8,128)(2,1)}), bf16[16,12,1152]{2,1,0:T(8,128)(2,1)}, u32[]{:S(2)}, u32[]{:S(2)}) async-start(bf16[16,12,1152]{2,1,0:T(8,128)(2,1)} %reshape.84), calls=%async_computation.1 | async-start | bytes 1179648 | tf_op jit(solution)/shard_map/all_to_all | solution.py:134
  178.8 31.4 %all-to-all-start.3 = ((bf16[32,36,288]{2,1,0:T(8,128)(2,1)}), bf16[32,36,288]{2,1,0:T(8,128)(2,1)}, u32[]{:S(2)}, u32[]{:S(2)}) async-start(bf16[32,36,288]{2,1,0:T(8,128)(2,1)} %reshape.96), calls=%async_computation.3 | async-start | bytes 1966080 | tf_op jit(solution)/shard_map/all_to_all | solution.py:166
  212.3 11.1 %all-to-all-start.4 = ((f32[8,1,1440]{2,1,0:T(1,128)}), f32[8,1,1440]{2,1,0:T(1,128)S(1)}, u32[]{:S(2)}, u32[]{:S(2)}) async-start(f32[8,1,1440]{2,1,0:T(1,128)} %reshape.97), calls=%async_computation.4 | async-start | bytes 98304 | tf_op jit(solution)/shard_map/all_to_all | solution.py:171
  (9 other events, 30.6 us)
Sparse Core Ops, SparseCore 0:
  41.6 35.5 all-gather.1

commit v2 on v1

v2 whole, which is shorter than its diff:
```python
import jax
import jax.numpy as jnp
from jax import lax
from jax.experimental import pallas as pl
from jax.experimental.pallas import tpu as pltpu
from jax.sharding import Mesh
from jax.sharding import PartitionSpec as P

BF = jnp.bfloat16
F32 = jnp.float32
CAP_AXES = ("ylo", "z")
REP_AXES = ("x", "yhi", "core")
SLOTS = 16
VMEM = pl.BlockSpec(memory_space=pltpu.VMEM)
SMEM = pl.BlockSpec(memory_space=pltpu.SMEM)


def shifted(block, axis, distance):
    size = lax.axis_size(axis)
    return lax.ppermute(block, axis, [(i, (i + distance) % size) for i in range(size)])


def gathered_along_z(block):
    half = block.shape[0] // 2
    up, down, found = block, block, [block]
    for _ in range(3):
        up, down = shifted(up, "z", 1), shifted(down, "z", -1)
        found += [up, down]
    return found + [shifted(up[:half], "z", 1), shifted(down[half:], "z", -1)]


def call(body, outs, name, specs, *args):
    shapes = [jax.ShapeDtypeStruct(shape, dtype) for shape, dtype in outs]
    return pl.pallas_call(
        body,
        out_shape=shapes,
        in_specs=specs,
        out_specs=[VMEM] * len(shapes),
        compiler_params=pltpu.CompilerParams(vmem_limit_bytes=40 * 2**20),
        name=name,
    )(*args)


def dot(a, b, left=1, right=0):
    return lax.dot_general(a, b, (((left,), (right,)), ((), ())), preferred_element_type=F32)


def iota(shape, dim):
    return lax.broadcasted_iota(jnp.int32, shape, dim)


def one_hot(condition):
    return jnp.where(condition, 1.0, 0.0).astype(BF)


def project(features, head):
    projected = dot(features, head)
    norm = jnp.sqrt(jnp.sum(projected * projected, axis=-1, keepdims=True) + 1e-06)
    return projected / norm, norm


def pull_back(unit, norm, gradient):
    radial = jnp.sum(unit * gradient, axis=-1, keepdims=True)
    return (gradient - unit * radial) / norm


def text_front(feats_ref, head_ref, unit_ref, norm_ref, emb_ref):
    unit, norm = project(feats_ref[...], head_ref[...])
    unit_ref[...] = unit
    norm_ref[...] = norm
    emb_ref[...] = unit.astype(BF)


def pool_front(
    rank_ref, feats_ref, head_ref, owners_ref, slots_ref,
    unit_ref, norm_ref, out_ref, select_ref, hit_ref, hit_t_ref,
):
    rank = rank_ref[0]
    owners = owners_ref[...]
    groups, images = owners.shape
    rows = groups * SLOTS
    unit, norm = project(feats_ref[...], head_ref[...])
    unit_ref[...] = unit
    norm_ref[...] = norm

    row, lane = iota((images, images), 0), iota((images, images), 1)
    owned = owners == rank
    place = dot(one_hot(owned), one_hot(row < lane))
    code = jnp.where(owned, place, -1.0)
    spread = one_hot(lax.div(iota((rows, groups), 0), SLOTS) == iota((rows, groups), 1))
    code_rows = dot(spread, code.astype(BF))
    slot_rows = dot(spread, slots_ref[...].astype(F32).astype(BF))
    at = lax.rem(iota((rows, images), 0), SLOTS).astype(F32)
    slot = jnp.sum(jnp.where(code_rows == at, slot_rows + 1.0, 0.0), axis=1, keepdims=True) - 1.0
    pool_rows = unit.shape[0]
    select = one_hot(slot == iota((rows, pool_rows), 1).astype(F32))
    select_ref[...] = select
    out_ref[...] = dot(select, unit.astype(BF)).astype(BF).reshape(out_ref.shape)

    mine = jnp.sum(
        jnp.where(iota((groups, images), 0) == rank, owners.astype(F32), 0.0), axis=0, keepdims=True
    )
    mine_t = jnp.sum(jnp.where(row == lane, mine, 0.0), axis=1, keepdims=True)
    same = mine == mine_t
    spot_t = mine_t * SLOTS + jnp.sum(jnp.where(same & (lane < row), 1.0, 0.0), axis=1, keepdims=True)
    spot = mine * SLOTS + jnp.sum(jnp.where(same & (row < lane), 1.0, 0.0), axis=0, keepdims=True)
    hit_ref[...] = one_hot(spot_t == iota((images, rows), 1).astype(F32))
    hit_t_ref[...] = one_hot(spot == iota((rows, images), 0).astype(F32))


def pair_sums(scale_ref, bias_ref, own_ref, other_ref, hits_ref, partners_ref, *refs):
    *block_refs, mine_ref, rest_ref = refs
    resident = jnp.concatenate([own_ref[...], other_ref[...]], axis=0)
    total = jnp.zeros(resident.shape, F32)
    for i in range(0, len(block_refs) - 1, 2):
        moving = jnp.concatenate([block_refs[i][...], block_refs[i + 1][...]], axis=0)
        logits = dot(resident, moving, 1, 1) * scale_ref[0] + bias_ref[0]
        total += dot(jax.nn.sigmoid(logits).astype(BF), moving)
    if len(block_refs) % 2:
        moving = block_refs[-1][...]
        logits = dot(resident, moving, 1, 1) * scale_ref[0] + bias_ref[0]
        total += dot(jax.nn.sigmoid(logits).astype(BF), moving)
    own_rows = own_ref.shape[0]
    mine_ref[...] = total[:own_rows] - dot(hits_ref[...], partners_ref[...])
    rest_ref[...] = total[own_rows:].astype(BF)


def image_back(scale_ref, mine_ref, rest_ref, hit_t_ref, out_ref):
    gradient = (scale_ref[0] * (mine_ref[...] + rest_ref[...].astype(F32))).astype(BF)
    out_ref[...] = dot(hit_t_ref[...], gradient).astype(BF).reshape(out_ref.shape)


def text_back(scale_ref, mine_ref, rest_ref, unit_ref, norm_ref, grad_ref):
    gradient = scale_ref[0] * (mine_ref[...] + rest_ref[...].astype(F32))
    grad_ref[...] = pull_back(unit_ref[...], norm_ref[...], gradient).astype(BF)


def pool_back(received_ref, select_ref, unit_ref, norm_ref, text_ref, grad_ref, strips_ref):
    received = received_ref[...].reshape(select_ref.shape[0], -1)
    choose = select_ref[...].astype(F32).T.astype(BF)
    gradient = pull_back(unit_ref[...], norm_ref[...], dot(choose, received))
    grad_ref[...] = gradient.astype(BF)
    columns, _, strip, rows = strips_ref.shape
    turned = text_ref[...].astype(F32).T.astype(BF)
    strips_ref[:, 0] = turned.reshape(columns, strip, rows)
    turned = gradient.T.astype(BF)
    strips_ref[:, 1] = turned.reshape(columns, strip, rows)


def head_terms(feats_ref, strips_ref, out_ref):
    sources, strip, _ = strips_ref.shape
    grads = jnp.concatenate([strips_ref[i] for i in range(sources)], axis=1)
    terms = dot(grads, feats_ref[...])
    pieces, rows, lanes = out_ref.shape
    extra = strip - lanes
    piece = terms.shape[1] // pieces
    main = terms[:lanes].T
    blank = jnp.zeros((extra, lanes - piece), F32)
    below = jnp.zeros((rows - extra - piece, lanes), F32)
    for i in range(pieces):
        left = jnp.concatenate([terms[lanes:, i * piece : (i + 1) * piece], blank], axis=1)
        block = jnp.concatenate([left, main[i * piece : (i + 1) * piece], below], axis=0)
        out_ref[i] = block.astype(BF)


def head_sums(terms_ref, out_ref):
    pieces, rows, lanes = terms_ref.shape
    total = terms_ref[0].astype(F32)
    for i in range(1, pieces):
        total += terms_ref[i].astype(F32)
    places = out_ref.shape[0] // 2
    extra = out_ref.shape[2] - lanes
    left = total[:16].T
    left = jnp.concatenate([left[:, :16], jnp.zeros((lanes, extra - 16), F32)], axis=1)
    full = jnp.concatenate([total[16:], left[: rows - 16]], axis=1)
    for i in range(places):
        out_ref[2 * i] = full[9 * i : 9 * i + 8]
        out_ref[2 * i + 1] = full[9 * i + 4 : 9 * i + 12]


def per_device(
    caption_feats,
    text_head,
    image_pool,
    image_head,
    image_owner,
    image_slot,
    caption_image,
    logit_scale,
    logit_bias,
):
    captions = caption_feats[0]
    pool = image_pool[0]
    owners = image_owner[:, :, 0]
    targets = caption_image[0]
    groups, images = owners.shape
    texts, width = captions.shape
    pool_rows = pool.shape[0]
    rank = lax.axis_index(REP_AXES)[None]
    first = lax.axis_index("core") == 0

    text_unit, text_norm, text_emb = call(
        text_front,
        [((texts, width), F32), ((texts, 1), F32), ((texts, width), BF)],
        "text_front",
        [VMEM, VMEM],
        captions,
        text_head,
    )
    pool_unit, pool_norm, outgoing, select, hit, hit_t = call(
        pool_front,
        [
            ((pool_rows, width), F32),
            ((pool_rows, 1), F32),
            ((groups, SLOTS, width), BF),
            ((groups * SLOTS, pool_rows), BF),
            ((images, groups * SLOTS), BF),
            ((groups * SLOTS, images), BF),
        ],
        "pool_front",
        [SMEM, VMEM, VMEM, VMEM, VMEM],
        rank,
        pool,
        image_head,
        owners,
        image_slot,
    )
    other_text = shifted(text_emb, "ylo", 1)
    text_blocks = gathered_along_z(text_emb)
    arrived = lax.all_to_all(outgoing, REP_AXES, 0, 0, tiled=True)
    image_emb = dot(hit, arrived.reshape(groups * SLOTS, width)).astype(BF)
    other_image = shifted(image_emb, "ylo", 1)
    image_blocks = gathered_along_z(image_emb)

    my_kind = jnp.where(first, captions, pool)
    its_kind = shifted(jnp.where(first, pool, captions), "core", 1)
    kinds = jnp.stack([jnp.where(first, my_kind, its_kind), jnp.where(first, its_kind, my_kind)])
    kinds = lax.all_gather(kinds.reshape(-1, width), ("x", "yhi"), axis=0, tiled=True)

    ids = jnp.arange(images, dtype=jnp.int32)
    hits = one_hot(targets[None, :] == ids[:, None])
    hits_t = one_hot(targets[:, None] == ids[None, :])
    image_mine, image_rest = call(
        pair_sums,
        [((images, width), F32), ((images, width), BF)],
        "image_sums",
        [SMEM, SMEM] + [VMEM] * (4 + len(text_blocks)),
        logit_scale, logit_bias, image_emb, other_image, hits, text_emb, *text_blocks,
    )
    image_rest = shifted(image_rest, "ylo", 1)
    (send_back,) = call(
        image_back,
        [((groups, SLOTS, width), BF)],
        "image_back",
        [SMEM, VMEM, VMEM, VMEM],
        logit_scale, image_mine, image_rest, hit_t,
    )
    received = lax.all_to_all(send_back, REP_AXES, 0, 0, tiled=True)

    text_mine, text_rest = call(
        pair_sums,
        [((texts, width), F32), ((texts, width), BF)],
        "text_sums",
        [SMEM, SMEM] + [VMEM] * (4 + len(image_blocks)),
        logit_scale, logit_bias, text_emb, other_text, hits_t, image_emb, *image_blocks,
    )
    text_rest = shifted(text_rest, "ylo", 1)
    (text_grad,) = call(
        text_back,
        [((texts, width), BF)],
        "text_back",
        [SMEM, VMEM, VMEM, VMEM, VMEM],
        logit_scale, text_mine, text_rest, text_unit, text_norm,
    )
    columns = groups // 2
    strip = width // columns
    pool_proj_grad, strips = call(
        pool_back,
        [((pool_rows, width), BF), ((columns, 2, strip, texts), BF)],
        "pool_back",
        [VMEM] * 5,
        received, select, pool_unit, pool_norm, text_grad,
    )
    strips = lax.all_to_all(strips.reshape(groups, strip, texts), REP_AXES, 0, 0, tiled=True)
    text_feat_grad = dot(text_grad, text_head, 1, 1).astype(BF)
    pool_grad = dot(pool_proj_grad, image_head, 1, 1).astype(BF)

    (terms,) = call(
        head_terms, [((16, 96, 128), BF)], "head_terms", [VMEM, VMEM], kinds, strips
    )
    terms = lax.all_to_all(terms, CAP_AXES, 0, 0, tiled=True)
    (rows,) = call(head_sums, [((groups, 8, 256), F32)], "head_sums", [VMEM], terms)
    rows = lax.all_to_all(rows, REP_AXES, 0, 0, tiled=True)
    rows = rows.reshape(columns, 2, 8, 256)[:, :, :5, :strip].transpose(2, 1, 0, 3)
    rows = rows.reshape(10, width)
    head_share = jnp.where(first, rows[:9], rows[1:])
    return text_feat_grad[None], pool_grad[None], head_share


def solution(mesh):
    fine = Mesh(mesh.devices.reshape(2, 8, 4, 2, 2), CAP_AXES + REP_AXES)
    in_specs = (
        P(REP_AXES, CAP_AXES, None),
        P(),
        P(CAP_AXES, REP_AXES, None),
        P(),
        P(None, CAP_AXES, None),
        P(None, CAP_AXES),
        P(REP_AXES, CAP_AXES),
        P(),
        P(),
    )
    out_specs = (
        P(REP_AXES, CAP_AXES, None),
        P(CAP_AXES, REP_AXES, None),
        P(CAP_AXES + REP_AXES, None),
    )
    return jax.shard_map(
        per_device, mesh=fine, in_specs=in_specs, out_specs=out_specs, check_vma=False
    )
```

time: 234 us -> 189 us (0.81)
  local copies, waits for them, and re-layouts: 46.2 us -> 19.6 us
  matrix products: 30.7 us -> 6.45 us
  Pallas kernels: 0 us -> 13.5 us
  waiting for transfers between devices: 57.4 us -> 46 us
  other arithmetic: 12.1 us -> 4.7 us
  blocking collectives: 14.9 us -> 21 us
  starting transfers between devices: 55.3 us -> 60.9 us
    dot_general x13 -> x3, matrix products: 30.7 us -> 6.45 us  [dot(): lax.dot_general(a, b, (((left,), (right,)), ((), ())), preferred_element_...]
    all_to_all x4, waiting for transfers between devices: 33.3 us -> 16 us  [the longest x1 9.47 us: per_device(): terms = lax.all_to_all(terms, CAP_AXES, 0, 0, tiled=True)]
    reshape x11 -> x1, local copies, waits for them, and re-layouts: 16.9 us -> 0.1 us  [per_device(): rows = rows.reshape(10, width)]
    pallas_call x0 -> x9, Pallas kernels: none -> 13.5 us  [call(): pl.pallas_call(body, out_shape=shapes, in_specs=specs, out_specs=[VMEM] *...]
    ppermute x21, starting transfers between devices: 21.9 us -> 30.9 us  [shifted(): lax.ppermute(block, axis, [(i, (i + distance) % size) for i in range(size)])]
    all_to_all x1, blocking collectives: 14.9 us -> 21 us  [per_device(): lax.all_to_all(strips.reshape(groups, strip, texts), REP_AXES, 0, 0, tile...]
    ppermute x21, waiting for transfers between devices: 24.1 us -> 30 us  [shifted(): lax.ppermute(block, axis, [(i, (i + distance) % size) for i in range(size)])]
    slice x2 -> x0, local copies, waits for them, and re-layouts: 3.53 us -> none  [the longest x1 1.81 us: per_device(): text_rest = shifted(text_sums[captions_here:].astype(BF), 'ylo', 1)]
  transfers between devices with their start and end apart: 26 -> 26, of which waited for: 9 -> 11; matrix products, arithmetic and copies ran while one was open for 27% -> 5% of each run, Pallas kernels for 0% -> 6%
where the time goes in v2:
time: 189 us; the launch traced here: 188 us
  starting transfers between devices  60.9 us (32%)
  waiting for transfers between devices  46 us (24%)
  blocking collectives  21 us (11%)
  local copies, waits for them, and re-layouts  19.6 us (10%)
  between operations  15.7 us (8%)
  Pallas kernels  13.5 us (7%)
  matrix products  6.45 us (3%)
  other arithmetic  4.7 us (2%)
    ppermute x21, starting transfers between devices, shifted(): lax.ppermute(block, axis, [(i, (i + distance) % size) for i in range(size)])  30.9 us
    ppermute x21, waiting for transfers between devices, shifted(): lax.ppermute(block, axis, [(i, (i + distance) % size) for i in range(size)])  30 us
    all_to_all x1, blocking collectives, per_device(): lax.all_to_all(strips.reshape(groups, strip, texts), REP_AXES, 0, 0, tile...  21 us
    unnamed x62, local copies, waits for them, and re-layouts  17.5 us
    pallas_call x9, Pallas kernels, call(): pl.pallas_call(body, out_shape=shapes, in_specs=specs, out_specs=[VMEM] *...  13.5 us
    all_to_all x1, starting transfers between devices, per_device(): received = lax.all_to_all(send_back, REP_AXES, 0, 0, tiled=True)  9.92 us
    all_to_all x1, waiting for transfers between devices, per_device(): terms = lax.all_to_all(terms, CAP_AXES, 0, 0, tiled=True)  9.47 us
    all_to_all x1, starting transfers between devices, per_device(): arrived = lax.all_to_all(outgoing, REP_AXES, 0, 0, tiled=True)  7.6 us
  transfers between devices with their start and end apart: 26, of which 11 were waited for; matrix products, arithmetic and copies ran while one was open for 5% of the time, Pallas kernels for 6%

profile of v2, /device:TPU:1, one launch (start us, length us, event | category | flops | bytes accessed | tf_op | source)
XLA Modules:
  0.0 187.9 jit_solution(3753188328580034450)
XLA Ops:
  7.2 1.2 broadcast_select_fusion
  8.5 3.3 %collective-permute-start.20 = (bf16[128,1152]{1,0:T(8,128)(2,1)S(1)}, bf16[128,1152]{1,0:T(8,128)(2,1)S(1)}, u32[]{:S(2)}, u32[]{:S(2)}) collective-permute-start(bf16[128,1152]{1,0:T(8,128)(2,1)S(1)} %broadcast_select_fusion), channel_id=1, source_target_pairs={{0,1},{1,0},{2,3},{3,2},{4,5},{5,4},{6,7},{7,6},{8,9},{9,8},{10,11... | collective-permute-start | bytes 884744 | tf_op jit(solution)/shard_map/ppermute | solution.py:20
  17.3 3.8 %collective-permute-start.12 = (bf16[128,1152]{1,0:T(8,128)(2,1)S(1)}, bf16[128,1152]{1,0:T(8,128)(2,1)}, u32[]{:S(2)}, u32[]{:S(2)}) collective-permute-start(bf16[128,1152]{1,0:T(8,128)(2,1)S(1)} %get-tuple-element.18.own_ref.partners_ref.refs_0_), channel_id=1, source_target_pairs={{0,112},{16,0},{32,16},{48,32},{64,48},{80,64},{96,80},{112,96},{1... | collective-permute-start | bytes 884744 | tf_op jit(solution)/shard_map/ppermute | solution.py:20
  21.2 1.7 copy-done.1
  28.2 7.6 %all-to-all-start = ((bf16[16,16,1152]{2,1,0:T(8,128)(2,1)}), bf16[16,16,1152]{2,1,0:T(8,128)(2,1)}, u32[]{:S(2)}, u32[]{:S(2)}) async-start(bf16[16,16,1152]{2,1,0:T(8,128)(2,1)} %copy-done.9), calls=%async_computation | async-start | bytes 1179648 | tf_op jit(solution)/shard_map/all_to_all | solution.py:230
  36.6 2.7 %collective-permute-start.14 = (bf16[128,1152]{1,0:T(8,128)(2,1)}, bf16[128,1152]{1,0:T(8,128)(2,1)}, u32[]{:S(2)}, u32[]{:S(2)}) collective-permute-start(bf16[128,1152]{1,0:T(8,128)(2,1)} %collective-permute-done.12.refs_2_), channel_id=1, source_target_pairs={{0,112},{16,0},{32,16},{48,32},{64,48},{80,64},{96,80},{112,96},{1... | collective-permute-start | bytes 884744 | tf_op jit(solution)/shard_map/ppermute | solution.py:20
  39.3 6.4 %collective-permute-done.13.refs_3_ = bf16[128,1152]{1,0:T(8,128)(2,1)} collective-permute-done((bf16[128,1152]{1,0:T(8,128)(2,1)S(1)}, bf16[128,1152]{1,0:T(8,128)(2,1)}, u32[]{:S(2)}, u32[]{:S(2)}) %collective-permute-start.13) | collective-permute-done | bytes 294944 | tf_op jit(solution)/shard_map/ppermute | solution.py:20
  45.7 3.3 %collective-permute-start.16 = (bf16[128,1152]{1,0:T(8,128)(2,1)}, bf16[128,1152]{1,0:T(8,128)(2,1)}, u32[]{:S(2)}, u32[]{:S(2)}) collective-permute-start(bf16[128,1152]{1,0:T(8,128)(2,1)} %collective-permute-done.14.refs_4_), channel_id=1, source_target_pairs={{0,112},{16,0},{32,16},{48,32},{64,48},{80,64},{96,80},{112,96},{1... | collective-permute-start | bytes 884744 | tf_op jit(solution)/shard_map/ppermute | solution.py:20
  48.9 2.3 %all-to-all-done = bf16[16,16,1152]{2,1,0:T(8,128)(2,1)} async-done(((bf16[16,16,1152]{2,1,0:T(8,128)(2,1)}), bf16[16,16,1152]{2,1,0:T(8,128)(2,1)}, u32[]{:S(2)}, u32[]{:S(2)}) %all-to-all-start) | async-done | bytes 589856 | tf_op jit(solution)/shard_map/all_to_all | solution.py:230
  51.2 1.3 convolution_convert_fusion.2.partners_ref.refs_0_.own_ref
  52.6 2.7 %collective-permute-start.2 = (bf16[96,1152]{1,0:T(8,128)(2,1)S(1)}, bf16[96,1152]{1,0:T(8,128)(2,1)S(1)}, u32[]{:S(2)}, u32[]{:S(2)}) collective-permute-start(bf16[96,1152]{1,0:T(8,128)(2,1)S(1)} %convolution_convert_fusion.2.partners_ref.refs_0_.own_ref), channel_id=1, source_target_pairs={{0,112},{16,0},{32,16},{48,32},{64,48},{80,64},{96,80},{112,96},{1... | collective-permute-start | bytes 663560 | tf_op jit(solution)/shard_map/ppermute | solution.py:20
  57.4 3.0 %collective-permute-done.1.refs_1_ = bf16[96,1152]{1,0:T(8,128)(2,1)S(1)} collective-permute-done((bf16[96,1152]{1,0:T(8,128)(2,1)S(1)}, bf16[96,1152]{1,0:T(8,128)(2,1)S(1)}, u32[]{:S(2)}, u32[]{:S(2)}) %collective-permute-start.1) | collective-permute-done | bytes 221216 | tf_op jit(solution)/shard_map/ppermute | solution.py:20
  60.4 2.7 %collective-permute-start.4 = (bf16[96,1152]{1,0:T(8,128)(2,1)S(1)}, bf16[96,1152]{1,0:T(8,128)(2,1)}, u32[]{:S(2)}, u32[]{:S(2)}) collective-permute-start(bf16[96,1152]{1,0:T(8,128)(2,1)S(1)} %collective-permute-done.2.refs_2_), channel_id=1, source_target_pairs={{0,112},{16,0},{32,16},{48,32},{64,48},{80,64},{96,80},{112,96},{1... | collective-permute-start | bytes 663560 | tf_op jit(solution)/shard_map/ppermute | solution.py:20
  64.1 2.9 %collective-permute-start.18 = (bf16[64,1152]{1,0:T(8,128)(2,1)S(1)}, bf16[64,1152]{1,0:T(8,128)(2,1)S(1)}, u32[]{:S(2)}, u32[]{:S(2)}) collective-permute-start(bf16[64,1152]{1,0:T(8,128)(2,1)S(1)} %slice.31), channel_id=1, source_target_pairs={{0,112},{16,0},{32,16},{48,32},{64,48},{80,64},{96,80},{112,96},{1... | collective-permute-start | bytes 442376 | tf_op jit(solution)/shard_map/ppermute | solution.py:20
  67.8 2.7 %collective-permute-done.17.refs_7_ = bf16[64,1152]{1,0:T(8,128)(2,1)S(1)} collective-permute-done((bf16[64,1152]{1,0:T(8,128)(2,1)S(1)}, bf16[64,1152]{1,0:T(8,128)(2,1)S(1)}, u32[]{:S(2)}, u32[]{:S(2)}) %collective-permute-start.17) | collective-permute-done | bytes 147488 | tf_op jit(solution)/shard_map/ppermute | solution.py:20
  71.5 3.7 %image_sums.1 = (f32[96,1152]{1,0:T(8,128)S(1)}, bf16[96,1152]{1,0:T(8,128)(2,1)S(1)}) custom-call(f32[1]{0:T(128)S(6)} %copy.13.scale_ref, f32[1]{0:T(128)S(6)} %copy.14.bias_ref, bf16[96,1152]{1,0:T(8,128)(2,1)S(1)} %convolution_convert_fusion.2.partners_ref.refs_0_.own_ref, bf16[96,1152]{1,0:T(8,128)(2,1)S(1)} %collective-permute-done.10.other_ref, ...), custom_call_target="tpu_custom_call" | custom-call | tf_op jit(solution)/shard_map/image_sums/pallas_call | solution.py:34
  77.0 2.1 %collective-permute-start.6 = (bf16[96,1152]{1,0:T(8,128)(2,1)}, bf16[96,1152]{1,0:T(8,128)(2,1)}, u32[]{:S(2)}, u32[]{:S(2)}) collective-permute-start(bf16[96,1152]{1,0:T(8,128)(2,1)} %collective-permute-done.4.refs_4_), channel_id=1, source_target_pairs={{0,112},{16,0},{32,16},{48,32},{64,48},{80,64},{96,80},{112,96},{1... | collective-permute-start | bytes 663560 | tf_op jit(solution)/shard_map/ppermute | solution.py:20
  79.8 6.9 %collective-permute-done.19.rest_ref = bf16[96,1152]{1,0:T(8,128)(2,1)S(1)} collective-permute-done((bf16[96,1152]{1,0:T(8,128)(2,1)S(1)}, bf16[96,1152]{1,0:T(8,128)(2,1)S(1)}, u32[]{:S(2)}, u32[]{:S(2)}) %collective-permute-start.19) | collective-permute-done | bytes 221216 | tf_op jit(solution)/shard_map/ppermute | solution.py:20
  87.9 9.9 %all-to-all-start.1 = ((bf16[16,16,1152]{2,1,0:T(8,128)(2,1)}), bf16[16,16,1152]{2,1,0:T(8,128)(2,1)}, u32[]{:S(2)}, u32[]{:S(2)}) async-start(bf16[16,16,1152]{2,1,0:T(8,128)(2,1)} %copy-done.5), calls=%async_computation.1 | async-start | bytes 1179648 | tf_op jit(solution)/shard_map/all_to_all | solution.py:258
  98.9 3.4 %collective-permute-start.8 = (bf16[48,1152]{1,0:T(8,128)(2,1)S(1)}, bf16[48,1152]{1,0:T(8,128)(2,1)S(1)}, u32[]{:S(2)}, u32[]{:S(2)}) collective-permute-start(bf16[48,1152]{1,0:T(8,128)(2,1)S(1)} %slice.29), channel_id=1, source_target_pairs={{0,112},{16,0},{32,16},{48,32},{64,48},{80,64},{96,80},{112,96},{1... | collective-permute-start | bytes 331784 | tf_op jit(solution)/shard_map/ppermute | solution.py:20
  102.5 2.2 %collective-permute-done.7.refs_7_ = bf16[48,1152]{1,0:T(8,128)(2,1)S(1)} collective-permute-done((bf16[48,1152]{1,0:T(8,128)(2,1)S(1)}, bf16[48,1152]{1,0:T(8,128)(2,1)S(1)}, u32[]{:S(2)}, u32[]{:S(2)}) %collective-permute-start.7) | collective-permute-done | bytes 110624 | tf_op jit(solution)/shard_map/ppermute | solution.py:20
  106.8 4.0 %text_sums.1 = (f32[128,1152]{1,0:T(8,128)S(1)}, bf16[128,1152]{1,0:T(8,128)(2,1)S(1)}) custom-call(f32[1]{0:T(128)S(6)} %copy.13.scale_ref, f32[1]{0:T(128)S(6)} %copy.14.bias_ref, bf16[128,1152]{1,0:T(8,128)(2,1)S(1)} %get-tuple-element.18.own_ref.partners_ref.refs_0_, bf16[128,1152]{1,0:T(8,128)(2,1)} %collective-permute-done.other_ref, ...), custom_call_target="tpu_custom_call" | custom-call | tf_op jit(solution)/shard_map/text_sums/pallas_call | solution.py:34
  111.3 7.3 %collective-permute-done.9.rest_ref = bf16[128,1152]{1,0:T(8,128)(2,1)S(1)} collective-permute-done((bf16[128,1152]{1,0:T(8,128)(2,1)S(1)}, bf16[128,1152]{1,0:T(8,128)(2,1)S(1)}, u32[]{:S(2)}, u32[]{:S(2)}) %collective-permute-start.9) | collective-permute-done | bytes 294944 | tf_op jit(solution)/shard_map/ppermute | solution.py:20
  120.8 1.6 pool_back.1
  123.1 21.0 %all_to_all.25.strips_ref = bf16[16,144,128]{2,1,0:T(8,128)(2,1)S(1)} all-to-all(bf16[16,144,128]{2,1,0:T(8,128)(2,1)S(1)} %bitcast.35), channel_id=1, replica_groups=mesh['ylo'=2,'z'=8,'x'=4,'yhi'=2,'core'=2] {'x','yhi','core'}, dimensions={0} | all-to-all | bytes 1179648 | tf_op jit(solution)/shard_map/all_to_all | solution.py:284
  144.1 2.3 %copy-done.2 = bf16[2048,1152]{1,0:T(8,128)(2,1)S(1)} copy-done((bf16[2048,1152]{1,0:T(8,128)(2,1)S(1)}, bf16[2048,1152]{1,0:T(8,128)(2,1)}, u32[]{:S(2)}) %copy-start.2) | copy-done | bytes 4718616
  148.2 6.6 %all-to-all-start.3 = ((bf16[16,96,128]{2,1,0:T(8,128)(2,1)}), bf16[16,96,128]{2,1,0:T(8,128)(2,1)S(1)}, u32[]{:S(2)}, u32[]{:S(2)}) async-start(bf16[16,96,128]{2,1,0:T(8,128)(2,1)} %copy-done.6), calls=%async_computation.3 | async-start | bytes 786432 | tf_op jit(solution)/shard_map/all_to_all | solution.py:291
  154.8 1.6 fusion
  156.4 9.5 %all-to-all-done.3.terms_ref = bf16[16,96,128]{2,1,0:T(8,128)(2,1)S(1)} async-done(((bf16[16,96,128]{2,1,0:T(8,128)(2,1)}), bf16[16,96,128]{2,1,0:T(8,128)(2,1)S(1)}, u32[]{:S(2)}, u32[]{:S(2)}) %all-to-all-start.3) | async-done | bytes 393248 | tf_op jit(solution)/shard_map/all_to_all | solution.py:291
  166.7 5.9 %all-to-all-start.4 = ((f32[16,8,256]{2,1,0:T(8,128)}), f32[16,8,256]{2,1,0:T(8,128)S(1)}, u32[]{:S(2)}, u32[]{:S(2)}) async-start(f32[16,8,256]{2,1,0:T(8,128)} %head_sums.1), calls=%async_computation.4 | async-start | bytes 262144 | tf_op jit(solution)/shard_map/all_to_all | solution.py:293
  172.5 3.5 %fusion.1 = bf16[1,128,1152]{2,1,0:T(8,128)(2,1)} fusion(bf16[128,1152]{1,0:T(8,128)(2,1)} %copy-done.12, bf16[1152,1152]{1,0:T(8,128)(2,1)} %head_ref.3), kind=kOutput, calls=%fused_computation.4 | convolution fusion | flops 339886080 | bytes 3244032 | tf_op jit(solution)/shard_map/dot_general | solution.py:45
  176.0 4.2 %all-to-all-done.4 = f32[16,8,256]{2,1,0:T(8,128)S(1)} async-done(((f32[16,8,256]{2,1,0:T(8,128)}), f32[16,8,256]{2,1,0:T(8,128)S(1)}, u32[]{:S(2)}, u32[]{:S(2)}) %all-to-all-start.4) | async-done | bytes 131104 | tf_op jit(solution)/shard_map/all_to_all | solution.py:293
  (109 shorter events, 28.8 us)
Async XLA Ops:
  7.2 136.9 %all-gather.2.cloned.1.call-start = ((), (), s32[]{:S(2)}) async-start(), calls=%async_computation.5 | async-start | bytes 5308416 | tf_op jit(solution)/shard_map/all_gather | solution.py:238
  8.5 4.5 %collective-permute-start.20 = (bf16[128,1152]{1,0:T(8,128)(2,1)S(1)}, bf16[128,1152]{1,0:T(8,128)(2,1)S(1)}, u32[]{:S(2)}, u32[]{:S(2)}) collective-permute-start(bf16[128,1152]{1,0:T(8,128)(2,1)S(1)} %broadcast_select_fusion), channel_id=1, source_target_pairs={{0,1},{1,0},{2,3},{3,2},{4,5},{5,4},{6,7},{7,6},{8,9},{9,8},{10,11... | collective-permute-start | bytes 884744 | tf_op jit(solution)/shard_map/ppermute | solution.py:20
  17.3 18.5 %collective-permute-start.11 = (bf16[128,1152]{1,0:T(8,128)(2,1)S(1)}, bf16[128,1152]{1,0:T(8,128)(2,1)S(1)}, u32[]{:S(2)}, u32[]{:S(2)}) collective-permute-start(bf16[128,1152]{1,0:T(8,128)(2,1)S(1)} %get-tuple-element.18.own_ref.partners_ref.refs_0_), channel_id=1, source_target_pairs={{0,16},{16,32},{32,48},{48,64},{64,80},{80,96},{96,112},{112,0},{1... | collective-permute-start | bytes 884744 | tf_op jit(solution)/shard_map/ppermute | solution.py:20
  17.3 19.3 %collective-permute-start.12 = (bf16[128,1152]{1,0:T(8,128)(2,1)S(1)}, bf16[128,1152]{1,0:T(8,128)(2,1)}, u32[]{:S(2)}, u32[]{:S(2)}) collective-permute-start(bf16[128,1152]{1,0:T(8,128)(2,1)S(1)} %get-tuple-element.18.own_ref.partners_ref.refs_0_), channel_id=1, source_target_pairs={{0,112},{16,0},{32,16},{48,32},{64,48},{80,64},{96,80},{112,96},{1... | collective-permute-start | bytes 884744 | tf_op jit(solution)/shard_map/ppermute | solution.py:20
  28.2 23.0 %all-to-all-start = ((bf16[16,16,1152]{2,1,0:T(8,128)(2,1)}), bf16[16,16,1152]{2,1,0:T(8,128)(2,1)}, u32[]{:S(2)}, u32[]{:S(2)}) async-start(bf16[16,16,1152]{2,1,0:T(8,128)(2,1)} %copy-done.9), calls=%async_computation | async-start | bytes 1179648 | tf_op jit(solution)/shard_map/all_to_all | solution.py:230
  35.8 9.9 %collective-permute-start.13 = (bf16[128,1152]{1,0:T(8,128)(2,1)S(1)}, bf16[128,1152]{1,0:T(8,128)(2,1)}, u32[]{:S(2)}, u32[]{:S(2)}) collective-permute-start(bf16[128,1152]{1,0:T(8,128)(2,1)S(1)} %collective-permute-done.11.refs_1_), channel_id=1, source_target_pairs={{0,16},{16,32},{32,48},{48,64},{64,80},{80,96},{96,112},{112,0},{1... | collective-permute-start | bytes 884744 | tf_op jit(solution)/shard_map/ppermute | solution.py:20
  36.6 9.0 %collective-permute-start.14 = (bf16[128,1152]{1,0:T(8,128)(2,1)}, bf16[128,1152]{1,0:T(8,128)(2,1)}, u32[]{:S(2)}, u32[]{:S(2)}) collective-permute-start(bf16[128,1152]{1,0:T(8,128)(2,1)} %collective-permute-done.12.refs_2_), channel_id=1, source_target_pairs={{0,112},{16,0},{32,16},{48,32},{64,48},{80,64},{96,80},{112,96},{1... | collective-permute-start | bytes 884744 | tf_op jit(solution)/shard_map/ppermute | solution.py:20
  45.6 41.1 %copy-start.26 = (bf16[256,96]{1,0:T(8,128)(2,1)S(1)}, bf16[256,96]{1,0:T(8,128)(2,1)}, u32[]{:S(2)}) copy-start(bf16[256,96]{1,0:T(8,128)(2,1)} %copy-done.25) | copy-start | bytes 147460
  45.6 17.4 %collective-permute-start.15 = (bf16[128,1152]{1,0:T(8,128)(2,1)}, bf16[128,1152]{1,0:T(8,128)(2,1)S(1)}, u32[]{:S(2)}, u32[]{:S(2)}) collective-permute-start(bf16[128,1152]{1,0:T(8,128)(2,1)} %collective-permute-done.13.refs_3_), channel_id=1, source_target_pairs={{0,16},{16,32},{32,48},{48,64},{64,80},{80,96},{96,112},{112,0},{1... | collective-permute-start | bytes 884744 | tf_op jit(solution)/shard_map/ppermute | solution.py:20
  45.7 17.6 %collective-permute-start.16 = (bf16[128,1152]{1,0:T(8,128)(2,1)}, bf16[128,1152]{1,0:T(8,128)(2,1)}, u32[]{:S(2)}, u32[]{:S(2)}) collective-permute-start(bf16[128,1152]{1,0:T(8,128)(2,1)} %collective-permute-done.14.refs_4_), channel_id=1, source_target_pairs={{0,112},{16,0},{32,16},{48,32},{64,48},{80,64},{96,80},{112,96},{1... | collective-permute-start | bytes 884744 | tf_op jit(solution)/shard_map/ppermute | solution.py:20
  52.5 7.8 %collective-permute-start.1 = (bf16[96,1152]{1,0:T(8,128)(2,1)S(1)}, bf16[96,1152]{1,0:T(8,128)(2,1)S(1)}, u32[]{:S(2)}, u32[]{:S(2)}) collective-permute-start(bf16[96,1152]{1,0:T(8,128)(2,1)S(1)} %convolution_convert_fusion.2.partners_ref.refs_0_.own_ref), channel_id=1, source_target_pairs={{0,16},{16,32},{32,48},{48,64},{64,80},{80,96},{96,112},{112,0},{1... | collective-permute-start | bytes 663560 | tf_op jit(solution)/shard_map/ppermute | solution.py:20
  52.6 7.8 %collective-permute-start.2 = (bf16[96,1152]{1,0:T(8,128)(2,1)S(1)}, bf16[96,1152]{1,0:T(8,128)(2,1)S(1)}, u32[]{:S(2)}, u32[]{:S(2)}) collective-permute-start(bf16[96,1152]{1,0:T(8,128)(2,1)S(1)} %convolution_convert_fusion.2.partners_ref.refs_0_.own_ref), channel_id=1, source_target_pairs={{0,112},{16,0},{32,16},{48,32},{64,48},{80,64},{96,80},{112,96},{1... | collective-permute-start | bytes 663560 | tf_op jit(solution)/shard_map/ppermute | solution.py:20
  56.6 11.2 %collective-permute-start.10 = (bf16[96,1152]{1,0:T(8,128)(2,1)S(1)}, bf16[96,1152]{1,0:T(8,128)(2,1)S(1)}, u32[]{:S(2)}, u32[]{:S(2)}) collective-permute-start(bf16[96,1152]{1,0:T(8,128)(2,1)S(1)} %convolution_convert_fusion.2.partners_ref.refs_0_.own_ref), channel_id=1, source_target_pairs={{0,128},{128,0},{1,129},{129,1},{2,130},{130,2},{3,131},{131,3},{4... | collective-permute-start | bytes 663560 | tf_op jit(solution)/shard_map/ppermute | solution.py:20
  60.4 26.3 %copy-start.15 = (bf16[96,1152]{1,0:T(8,128)(2,1)}, bf16[96,1152]{1,0:T(8,128)(2,1)S(1)}, u32[]{:S(2)}) copy-start(bf16[96,1152]{1,0:T(8,128)(2,1)S(1)} %collective-permute-done.1.refs_1_) | copy-start | bytes 663556
  60.4 15.7 %collective-permute-start.3 = (bf16[96,1152]{1,0:T(8,128)(2,1)S(1)}, bf16[96,1152]{1,0:T(8,128)(2,1)}, u32[]{:S(2)}, u32[]{:S(2)}) collective-permute-start(bf16[96,1152]{1,0:T(8,128)(2,1)S(1)} %collective-permute-done.1.refs_1_), channel_id=1, source_target_pairs={{0,16},{16,32},{32,48},{48,64},{64,80},{80,96},{96,112},{112,0},{1... | collective-permute-start | bytes 663560 | tf_op jit(solution)/shard_map/ppermute | solution.py:20
  60.4 26.3 %copy-start.17 = (bf16[96,1152]{1,0:T(8,128)(2,1)}, bf16[96,1152]{1,0:T(8,128)(2,1)S(1)}, u32[]{:S(2)}) copy-start(bf16[96,1152]{1,0:T(8,128)(2,1)S(1)} %collective-permute-done.2.refs_2_) | copy-start | bytes 663556
  60.4 16.6 %collective-permute-start.4 = (bf16[96,1152]{1,0:T(8,128)(2,1)S(1)}, bf16[96,1152]{1,0:T(8,128)(2,1)}, u32[]{:S(2)}, u32[]{:S(2)}) collective-permute-start(bf16[96,1152]{1,0:T(8,128)(2,1)S(1)} %collective-permute-done.2.refs_2_), channel_id=1, source_target_pairs={{0,112},{16,0},{32,16},{48,32},{64,48},{80,64},{96,80},{112,96},{1... | collective-permute-start | bytes 663560 | tf_op jit(solution)/shard_map/ppermute | solution.py:20
  63.1 7.4 %collective-permute-start.17 = (bf16[64,1152]{1,0:T(8,128)(2,1)S(1)}, bf16[64,1152]{1,0:T(8,128)(2,1)S(1)}, u32[]{:S(2)}, u32[]{:S(2)}) collective-permute-start(bf16[64,1152]{1,0:T(8,128)(2,1)S(1)} %slice.30), channel_id=1, source_target_pairs={{0,16},{16,32},{32,48},{48,64},{64,80},{80,96},{96,112},{112,0},{1... | collective-permute-start | bytes 442376 | tf_op jit(solution)/shard_map/ppermute | solution.py:20
  64.1 6.4 %collective-permute-start.18 = (bf16[64,1152]{1,0:T(8,128)(2,1)S(1)}, bf16[64,1152]{1,0:T(8,128)(2,1)S(1)}, u32[]{:S(2)}, u32[]{:S(2)}) collective-permute-start(bf16[64,1152]{1,0:T(8,128)(2,1)S(1)} %slice.31), channel_id=1, source_target_pairs={{0,112},{16,0},{32,16},{48,32},{64,48},{80,64},{96,80},{112,96},{1... | collective-permute-start | bytes 442376 | tf_op jit(solution)/shard_map/ppermute | solution.py:20
  67.0 35.3 %copy-start.30 = (s32[1,128]{1,0:T(1,128)S(1)}, s32[1,128]{1,0:T(1,128)}, u32[]{:S(2)}) copy-start(s32[1,128]{1,0:T(1,128)} %param.15) | copy-start | bytes 1540
  75.2 11.5 %collective-permute-start.19 = (bf16[96,1152]{1,0:T(8,128)(2,1)S(1)}, bf16[96,1152]{1,0:T(8,128)(2,1)S(1)}, u32[]{:S(2)}, u32[]{:S(2)}) collective-permute-start(bf16[96,1152]{1,0:T(8,128)(2,1)S(1)} %get-tuple-element.26), channel_id=1, source_target_pairs={{0,128},{128,0},{1,129},{129,1},{2,130},{130,2},{3,131},{131,3},{4... | collective-permute-start | bytes 663560 | tf_op jit(solution)/shard_map/ppermute | solution.py:20
  76.1 21.7 %collective-permute-start.5 = (bf16[96,1152]{1,0:T(8,128)(2,1)}, bf16[96,1152]{1,0:T(8,128)(2,1)S(1)}, u32[]{:S(2)}, u32[]{:S(2)}) collective-permute-start(bf16[96,1152]{1,0:T(8,128)(2,1)} %collective-permute-done.3.refs_3_), channel_id=1, source_target_pairs={{0,16},{16,32},{32,48},{48,64},{64,80},{80,96},{96,112},{112,0},{1... | collective-permute-start | bytes 663560 | tf_op jit(solution)/shard_map/ppermute | solution.py:20
  77.0 21.0 %collective-permute-start.6 = (bf16[96,1152]{1,0:T(8,128)(2,1)}, bf16[96,1152]{1,0:T(8,128)(2,1)}, u32[]{:S(2)}, u32[]{:S(2)}) collective-permute-start(bf16[96,1152]{1,0:T(8,128)(2,1)} %collective-permute-done.4.refs_4_), channel_id=1, source_target_pairs={{0,112},{16,0},{32,16},{48,32},{64,48},{80,64},{96,80},{112,96},{1... | collective-permute-start | bytes 663560 | tf_op jit(solution)/shard_map/ppermute | solution.py:20
  79.1 23.4 %collective-permute-start = (bf16[128,1152]{1,0:T(8,128)(2,1)S(1)}, bf16[128,1152]{1,0:T(8,128)(2,1)}, u32[]{:S(2)}, u32[]{:S(2)}) collective-permute-start(bf16[128,1152]{1,0:T(8,128)(2,1)S(1)} %get-tuple-element.18.own_ref.partners_ref.refs_0_), channel_id=1, source_target_pairs={{0,128},{128,0},{1,129},{129,1},{2,130},{130,2},{3,131},{131,3},{4... | collective-permute-start | bytes 884744 | tf_op jit(solution)/shard_map/ppermute | solution.py:20
  86.7 31.8 %copy-start.20 = (f32[128,1]{1,0:T(8,128)S(1)}, f32[128,1]{1,0:T(8,128)}, u32[]{:S(2)}) copy-start(f32[128,1]{1,0:T(8,128)} %copy-done.19) | copy-start | bytes 1540
  87.9 30.9 %copy-start.22 = (f32[128,1]{1,0:T(8,128)S(1)}, f32[128,1]{1,0:T(8,128)}, u32[]{:S(2)}) copy-start(f32[128,1]{1,0:T(8,128)} %copy-done.21) | copy-start | bytes 1540
  87.9 30.9 %all-to-all-start.1 = ((bf16[16,16,1152]{2,1,0:T(8,128)(2,1)}), bf16[16,16,1152]{2,1,0:T(8,128)(2,1)}, u32[]{:S(2)}, u32[]{:S(2)}) async-start(bf16[16,16,1152]{2,1,0:T(8,128)(2,1)} %copy-done.5), calls=%async_computation.1 | async-start | bytes 1179648 | tf_op jit(solution)/shard_map/all_to_all | solution.py:258
  97.9 6.8 %collective-permute-start.7 = (bf16[48,1152]{1,0:T(8,128)(2,1)S(1)}, bf16[48,1152]{1,0:T(8,128)(2,1)S(1)}, u32[]{:S(2)}, u32[]{:S(2)}) collective-permute-start(bf16[48,1152]{1,0:T(8,128)(2,1)S(1)} %slice.28), channel_id=1, source_target_pairs={{0,16},{16,32},{32,48},{48,64},{64,80},{80,96},{96,112},{112,0},{1... | collective-permute-start | bytes 331784 | tf_op jit(solution)/shard_map/ppermute | solution.py:20
  98.9 6.0 %collective-permute-start.8 = (bf16[48,1152]{1,0:T(8,128)(2,1)S(1)}, bf16[48,1152]{1,0:T(8,128)(2,1)S(1)}, u32[]{:S(2)}, u32[]{:S(2)}) collective-permute-start(bf16[48,1152]{1,0:T(8,128)(2,1)S(1)} %slice.29), channel_id=1, source_target_pairs={{0,112},{16,0},{32,16},{48,32},{64,48},{80,64},{96,80},{112,96},{1... | collective-permute-start | bytes 331784 | tf_op jit(solution)/shard_map/ppermute | solution.py:20
  110.8 7.8 %collective-permute-start.9 = (bf16[128,1152]{1,0:T(8,128)(2,1)S(1)}, bf16[128,1152]{1,0:T(8,128)(2,1)S(1)}, u32[]{:S(2)}, u32[]{:S(2)}) collective-permute-start(bf16[128,1152]{1,0:T(8,128)(2,1)S(1)} %get-tuple-element.22), channel_id=1, source_target_pairs={{0,128},{128,0},{1,129},{129,1},{2,130},{130,2},{3,131},{131,3},{4... | collective-permute-start | bytes 884744 | tf_op jit(solution)/shard_map/ppermute | solution.py:20
  148.2 17.7 %all-to-all-start.3 = ((bf16[16,96,128]{2,1,0:T(8,128)(2,1)}), bf16[16,96,128]{2,1,0:T(8,128)(2,1)S(1)}, u32[]{:S(2)}, u32[]{:S(2)}) async-start(bf16[16,96,128]{2,1,0:T(8,128)(2,1)} %copy-done.6), calls=%async_computation.3 | async-start | bytes 786432 | tf_op jit(solution)/shard_map/all_to_all | solution.py:291
  166.7 13.6 %all-to-all-start.4 = ((f32[16,8,256]{2,1,0:T(8,128)}), f32[16,8,256]{2,1,0:T(8,128)S(1)}, u32[]{:S(2)}, u32[]{:S(2)}) async-start(f32[16,8,256]{2,1,0:T(8,128)} %head_sums.1), calls=%async_computation.4 | async-start | bytes 262144 | tf_op jit(solution)/shard_map/all_to_all | solution.py:293
  (25 other events, 75.0 us)
Sparse Core Ops, SparseCore 0:
  15.2 101.2 all-gather.1

commit v3 on v2

v3 whole, which is shorter than its diff:
```python
import functools

import jax
import jax.numpy as jnp
from jax import lax
from jax.experimental import pallas as pl
from jax.experimental.pallas import tpu as pltpu
from jax.sharding import Mesh
from jax.sharding import PartitionSpec as P

BF = jnp.bfloat16
F32 = jnp.float32
CAP_AXES = ("ylo", "z")
REP_AXES = ("x", "yhi", "core")
SLOTS = 16
ANY = pl.BlockSpec(memory_space=pl.ANY)
SMEM = pl.BlockSpec(memory_space=pltpu.SMEM)


def shifted(block, axis, distance):
    size = lax.axis_size(axis)
    return lax.ppermute(block, axis, [(i, (i + distance) % size) for i in range(size)])


def gathered_along_z(block):
    half = block.shape[0] // 2
    up, down, found = block, block, [block]
    for _ in range(3):
        up, down = shifted(up, "z", 1), shifted(down, "z", -1)
        found += [up, down]
    return found + [shifted(up[:half], "z", 1), shifted(down[half:], "z", -1)]


def call(body, outs, name, scalars, arrays):
    shapes = [jax.ShapeDtypeStruct(shape, dtype) for shape, dtype in outs]
    count, total = len(arrays), len(arrays) + len(outs)

    def kernel(*refs):
        head = refs[: len(scalars)]
        far = refs[len(scalars) : len(scalars) + total]
        near = refs[len(scalars) + total : -1]
        sems = refs[-1]
        copies = [
            pltpu.make_async_copy(far[i], near[i], sems.at[i])
            if i < count
            else pltpu.make_async_copy(near[i], far[i], sems.at[i])
            for i in range(total)
        ]
        for i in range(count):
            copies[i].start()
        for i in range(count):
            copies[i].wait()
        body(*head, *near)
        for i in range(count, total):
            copies[i].start()
        for i in range(count, total):
            copies[i].wait()

    everything = [(a.shape, a.dtype) for a in arrays] + list(outs)
    return pl.pallas_call(
        kernel,
        out_shape=shapes,
        in_specs=[SMEM] * len(scalars) + [ANY] * count,
        out_specs=[ANY] * len(outs),
        scratch_shapes=[pltpu.VMEM(s, d) for s, d in everything]
        + [pltpu.SemaphoreType.DMA((total,))],
        compiler_params=pltpu.CompilerParams(vmem_limit_bytes=48 * 2**20),
        name=name,
    )(*scalars, *arrays)


def dot(a, b, left=1, right=0):
    return lax.dot_general(a, b, (((left,), (right,)), ((), ())), preferred_element_type=F32)


def iota(shape, dim):
    return lax.broadcasted_iota(jnp.int32, shape, dim)


def one_hot(condition):
    return jnp.where(condition, 1.0, 0.0).astype(BF)


def project(features, head):
    projected = dot(features, head)
    norm = jnp.sqrt(jnp.sum(projected * projected, axis=-1, keepdims=True) + 1e-06)
    return projected / norm, norm


def pull_back(unit, norm, gradient):
    radial = jnp.sum(unit * gradient, axis=-1, keepdims=True)
    return (gradient - unit * radial) / norm


def text_front(feats_ref, head_ref, unit_ref, norm_ref, emb_ref):
    unit, norm = project(feats_ref[...], head_ref[...])
    unit_ref[...] = unit
    norm_ref[...] = norm
    emb_ref[...] = unit.astype(BF)


def pool_front(
    place_ref, feats_ref, head_ref, owners_ref, slots_ref, captions_ref,
    unit_ref, norm_ref, out_ref, select_ref, hit_ref, hit_t_ref, keep_ref, give_ref,
):
    rank = place_ref[0]
    owners = owners_ref[...]
    groups, images = owners.shape
    rows = groups * SLOTS
    unit, norm = project(feats_ref[...], head_ref[...])
    unit_ref[...] = unit
    norm_ref[...] = norm

    row, lane = iota((images, images), 0), iota((images, images), 1)
    owned = owners == rank
    place = dot(one_hot(owned), one_hot(row < lane))
    code = jnp.where(owned, place, -1.0)
    spread = one_hot(lax.div(iota((rows, groups), 0), SLOTS) == iota((rows, groups), 1))
    code_rows = dot(spread, code.astype(BF))
    slot_rows = dot(spread, slots_ref[...].astype(F32).astype(BF))
    at = lax.rem(iota((rows, images), 0), SLOTS).astype(F32)
    slot = jnp.sum(jnp.where(code_rows == at, slot_rows + 1.0, 0.0), axis=1, keepdims=True) - 1.0
    pool_rows = unit.shape[0]
    select = one_hot(slot == iota((rows, pool_rows), 1).astype(F32))
    select_ref[...] = select
    out_ref[...] = dot(select, unit.astype(BF)).astype(BF).reshape(out_ref.shape)

    mine = jnp.sum(
        jnp.where(iota((groups, images), 0) == rank, owners.astype(F32), 0.0), axis=0, keepdims=True
    )
    mine_t = jnp.sum(jnp.where(row == lane, mine, 0.0), axis=1, keepdims=True)
    same = mine == mine_t
    spot_t = mine_t * SLOTS + jnp.sum(jnp.where(same & (lane < row), 1.0, 0.0), axis=1, keepdims=True)
    spot = mine * SLOTS + jnp.sum(jnp.where(same & (row < lane), 1.0, 0.0), axis=0, keepdims=True)
    hit_ref[...] = one_hot(spot_t == iota((images, rows), 1).astype(F32))
    hit_t_ref[...] = one_hot(spot == iota((rows, images), 0).astype(F32))

    @pl.when(place_ref[1] == 0)
    def _():
        keep_ref[...] = captions_ref[...]
        give_ref[...] = feats_ref[...]

    @pl.when(place_ref[1] != 0)
    def _():
        keep_ref[...] = feats_ref[...]
        give_ref[...] = captions_ref[...]


def arrive(arrived_ref, hit_ref, keep_ref, given_ref, far_ref, emb_ref, four_ref):
    arrived = arrived_ref[...].reshape(hit_ref.shape[1], -1)
    emb_ref[...] = dot(hit_ref[...], arrived).astype(BF)
    rows = keep_ref.shape[0]
    four_ref[:rows] = keep_ref[...]
    four_ref[rows : 2 * rows] = given_ref[...]
    four_ref[2 * rows :] = far_ref[...]


def pair_sums(turned, scale_ref, bias_ref, own_ref, other_ref, targets_ref, partners_ref, *refs):
    *block_refs, mine_ref, rest_ref = refs
    resident = jnp.concatenate([own_ref[...], other_ref[...]], axis=0)
    total = jnp.zeros(resident.shape, F32)
    groups = [block_refs[:1]] + [block_refs[i : i + 2] for i in range(1, len(block_refs), 2)]
    for group in groups:
        moving = jnp.concatenate([ref[...] for ref in group], axis=0)
        logits = dot(resident, moving, 1, 1) * scale_ref[0] + bias_ref[0]
        total += dot(jax.nn.sigmoid(logits).astype(BF), moving)
    own_rows, partner_rows = own_ref.shape[0], partners_ref.shape[0]
    images, texts = (partner_rows, own_rows) if turned else (own_rows, partner_rows)
    hits = jnp.where(targets_ref[...] == iota((images, texts), 0), 1.0, 0.0)
    hits = hits.T if turned else hits
    mine_ref[...] = total[:own_rows] - dot(hits.astype(BF), partners_ref[...])
    rest_ref[...] = total[own_rows:].astype(BF)


def image_back(scale_ref, mine_ref, rest_ref, hit_t_ref, out_ref):
    gradient = (scale_ref[0] * (mine_ref[...] + rest_ref[...].astype(F32))).astype(BF)
    out_ref[...] = dot(hit_t_ref[...], gradient).astype(BF).reshape(out_ref.shape)


def text_back(scale_ref, mine_ref, rest_ref, unit_ref, norm_ref, grad_ref):
    gradient = scale_ref[0] * (mine_ref[...] + rest_ref[...].astype(F32))
    grad_ref[...] = pull_back(unit_ref[...], norm_ref[...], gradient).astype(BF)


def pool_back(received_ref, select_ref, unit_ref, norm_ref, text_ref, grad_ref, strips_ref):
    received = received_ref[...].reshape(select_ref.shape[0], -1)
    choose = select_ref[...].astype(F32).T.astype(BF)
    gradient = pull_back(unit_ref[...], norm_ref[...], dot(choose, received))
    grad_ref[...] = gradient.astype(BF)
    columns, _, strip, rows = strips_ref.shape
    turned = text_ref[...].astype(F32).T.astype(BF)
    strips_ref[:, 0] = turned.reshape(columns, strip, rows)
    turned = gradient.T.astype(BF)
    strips_ref[:, 1] = turned.reshape(columns, strip, rows)


def head_terms(place_ref, strips_ref, home_ref, up_ref, down_ref, far_up_ref, far_down_ref, out_ref):
    x, yhi, core = place_ref[2], place_ref[3], place_ref[1]
    _, strip, lanes = strips_ref.shape
    extra = strip - lanes

    def grads(along, across):
        blocks = []
        for dy in across:
            for dc in range(2):
                source = lax.rem(x + along, 4) * 4 + lax.rem(yhi + dy, 2) * 2 + lax.rem(core + dc, 2)
                blocks.append(strips_ref[source])
        block = jnp.concatenate(blocks, axis=1)
        return jnp.concatenate([block[:lanes]] + [block[lanes:]] * (lanes // extra), axis=0)

    terms = dot(grads(0, (0, 1)), home_ref[...])
    terms += dot(grads(3, (0, 1)), up_ref[...])
    terms += dot(grads(1, (0, 1)), down_ref[...])
    terms += dot(grads(2, (0,)), far_up_ref[...])
    terms += dot(grads(2, (1,)), far_down_ref[...])
    turned = terms.T
    turned = jnp.concatenate([turned, jnp.zeros((8, 2 * lanes), F32)], axis=0)
    row, lane = iota((8, lanes), 0), iota((8, lanes), 1)
    diagonal = (lax.div(lane, extra) == row) & (row < 5)
    for pair in range(out_ref.shape[0]):
        halves = []
        for start in (9 * pair, 9 * pair + 4):
            last = jnp.where(diagonal, turned[start : start + 8, lanes:], 0.0)
            last = jnp.sum(last, axis=0, keepdims=True)
            main = turned[start : start + 8, :lanes]
            halves.append(jnp.where(row < 5, main, jnp.where(row == 5, last, 0.0)))
        out_ref[pair] = jnp.concatenate(halves, axis=0).astype(BF)


def head_sums(place_ref, terms_ref, out_ref):
    core = place_ref[1]
    lanes = terms_ref.shape[2]
    extra = out_ref.shape[1] // 8 - lanes
    row, lane = iota((16, lanes), 0), iota((16, lanes), 1)
    diagonal = lax.div(lane, extra) == lax.rem(row, 8)
    fold = jnp.where(lax.rem(iota((lanes, extra), 0), extra) == iota((lanes, extra), 1), 1.0, 0.0)
    strips = []
    for k in range(8):
        total = terms_ref[k].astype(F32)
        for i in range(1, 16):
            total += terms_ref[8 * i + k].astype(F32)
        last = jnp.where(row < 8, total[5:6], total[13:14])
        last = jnp.where(diagonal, last, 0.0)
        last = jnp.dot(last, fold, preferred_element_type=F32, precision=lax.Precision.HIGHEST)
        strips += [total, last]
    rows = jnp.concatenate(strips, axis=1)
    to, source = iota((16, 16), 0), iota((16, 16), 1)
    order = jnp.where(2 * lax.rem(source, 8) + lax.div(source, 8) == to + core, 1.0, 0.0)
    rows = jnp.dot(order, rows, preferred_element_type=F32, precision=lax.Precision.HIGHEST)
    out_ref[...] = rows[: out_ref.shape[0]]


def per_device(
    caption_feats,
    text_head,
    image_pool,
    image_head,
    image_owner,
    image_slot,
    caption_image,
    logit_scale,
    logit_bias,
):
    captions = caption_feats[0]
    pool = image_pool[0]
    owners = image_owner[:, :, 0]
    groups, images = owners.shape
    texts, width = captions.shape
    pool_rows = pool.shape[0]
    place = jnp.stack([lax.axis_index(REP_AXES)] + [lax.axis_index(a) for a in ("core", "x", "yhi")])

    text_unit, text_norm, text_emb = call(
        text_front,
        [((texts, width), F32), ((texts, 1), F32), ((texts, width), BF)],
        "text_front", [], [captions, text_head],
    )
    pool_unit, pool_norm, outgoing, select, hit, hit_t, keep, give = call(
        pool_front,
        [
            ((pool_rows, width), F32),
            ((pool_rows, 1), F32),
            ((groups, SLOTS, width), BF),
            ((groups * SLOTS, pool_rows), BF),
            ((images, groups * SLOTS), BF),
            ((groups * SLOTS, images), BF),
            ((texts, width), BF),
            ((texts, width), BF),
        ],
        "pool_front", [place], [pool, image_head, owners, image_slot, captions],
    )
    other_text = shifted(text_emb, "ylo", 1)
    text_blocks = gathered_along_z(text_emb)
    arrived = lax.all_to_all(outgoing, REP_AXES, 0, 0, tiled=True)
    given = shifted(give, "core", 1)
    far = shifted(jnp.concatenate([keep, given]), "yhi", 1)
    image_emb, four = call(
        arrive, [((images, width), BF), ((4 * texts, width), BF)], "arrive", [],
        [arrived, hit, keep, given, far],
    )
    other_image = shifted(image_emb, "ylo", 1)
    image_blocks = gathered_along_z(image_emb)
    up, down = shifted(four, "x", 1), shifted(four, "x", -1)
    far_up, far_down = shifted(up[: 2 * texts], "x", 1), shifted(down[2 * texts :], "x", -1)

    scalars = [logit_scale, logit_bias]
    image_mine, image_rest = call(
        functools.partial(pair_sums, False),
        [((images, width), F32), ((images, width), BF)],
        "image_sums", scalars, [image_emb, other_image, caption_image, text_emb, *text_blocks],
    )
    image_rest = shifted(image_rest, "ylo", 1)
    (send_back,) = call(
        image_back, [((groups, SLOTS, width), BF)], "image_back", scalars[:1],
        [image_mine, image_rest, hit_t],
    )
    received = lax.all_to_all(send_back, REP_AXES, 0, 0, tiled=True)

    text_mine, text_rest = call(
        functools.partial(pair_sums, True),
        [((texts, width), F32), ((texts, width), BF)],
        "text_sums", scalars, [text_emb, other_text, caption_image, image_emb, *image_blocks],
    )
    text_rest = shifted(text_rest, "ylo", 1)
    (text_grad,) = call(
        text_back, [((texts, width), BF)], "text_back", scalars[:1],
        [text_mine, text_rest, text_unit, text_norm],
    )
    columns = groups // 2
    strip = width // columns
    pool_proj_grad, strips = call(
        pool_back,
        [((pool_rows, width), BF), ((columns, 2, strip, texts), BF)],
        "pool_back", [], [received, select, pool_unit, pool_norm, text_grad],
    )
    strips = lax.all_to_all(strips.reshape(groups, strip, texts), REP_AXES, 0, 0, tiled=True)
    text_feat_grad = dot(text_grad, text_head, 1, 1).astype(BF)
    pool_grad = dot(pool_proj_grad, image_head, 1, 1).astype(BF)

    (terms,) = call(
        head_terms, [((128, 16, 128), BF)], "head_terms", [place],
        [strips, four, up, down, far_up, far_down],
    )
    terms = lax.all_to_all(terms.reshape(256, 8, 128), CAP_AXES + REP_AXES, 0, 0, tiled=True)
    (head_share,) = call(
        head_sums, [((9, width), F32)], "head_sums", [place], [terms.reshape(128, 16, 128)]
    )
    return text_feat_grad[None], pool_grad[None], head_share


def solution(mesh):
    fine = Mesh(mesh.devices.reshape(2, 8, 4, 2, 2), CAP_AXES + REP_AXES)
    in_specs = (
        P(REP_AXES, CAP_AXES, None),
        P(),
        P(CAP_AXES, REP_AXES, None),
        P(),
        P(None, CAP_AXES, None),
        P(None, CAP_AXES),
        P(REP_AXES, CAP_AXES),
        P(),
        P(),
    )
    out_specs = (
        P(REP_AXES, CAP_AXES, None),
        P(CAP_AXES, REP_AXES, None),
        P(CAP_AXES + REP_AXES, None),
    )
    return jax.shard_map(
        per_device, mesh=fine, in_specs=in_specs, out_specs=out_specs, check_vma=False
    )
```

time: 189 us -> 180 us (0.952)
  Pallas kernels: 13.5 us -> 27.2 us
  between operations: 15.7 us -> 2.61 us
  waiting for transfers between devices: 46 us -> 39.3 us
  other arithmetic: 4.7 us -> 0.97 us
  matrix products: 6.45 us -> 3.25 us
  starting transfers between devices: 60.9 us -> 63.3 us
  local copies, waits for them, and re-layouts: 19.6 us -> 21.7 us
    pallas_call x9 -> x10, Pallas kernels: 13.5 us -> 27.2 us  [call(): pl.pallas_call(kernel, out_shape=shapes, in_specs=[SMEM] * len(scalars) +...]
    ppermute x21 -> x26, waiting for transfers between devices: 30 us -> 20.8 us  [shifted(): lax.ppermute(block, axis, [(i, (i + distance) % size) for i in range(size)])]
    ppermute x21 -> x26, starting transfers between devices: 30.9 us -> 36.3 us  [shifted(): lax.ppermute(block, axis, [(i, (i + distance) % size) for i in range(size)])]
    all_to_all x2 -> x1, starting transfers between devices: 12.4 us -> 8.63 us  [per_device(): lax.all_to_all(terms.reshape(256, 8, 128), CAP_AXES + REP_AXES, 0, 0, til...]
    all_to_all x2 -> x1, waiting for transfers between devices: 13.7 us -> 17.4 us  [per_device(): lax.all_to_all(terms.reshape(256, 8, 128), CAP_AXES + REP_AXES, 0, 0, til...]
    dot_general x3 -> x2, matrix products: 6.45 us -> 3.25 us  [dot(): lax.dot_general(a, b, (((left,), (right,)), ((), ())), preferred_element_...]
    another operation x2 -> x1, other arithmetic: 2 us -> 0.08 us  [per_device(): jnp.stack([lax.axis_index(REP_AXES)] + [lax.axis_index(a) for a in ('core...]
    slice x0 -> x2, local copies, waits for them, and re-layouts: none -> 1.92 us  [the longest x1 0.96 us: per_device(): up[:2 * texts]]
  transfers between devices with their start and end apart: 26 -> 29, of which waited for: 11 -> 10; matrix products, arithmetic and copies ran while one was open for 5% -> 5% of each run, Pallas kernels for 6% -> 10%
where the time goes in v3:
time: 180 us; the launch traced here: 179 us
  starting transfers between devices  63.3 us (35%)
  waiting for transfers between devices  39.3 us (22%)
  Pallas kernels  27.2 us (15%)
  local copies, waits for them, and re-layouts  21.7 us (12%)
  blocking collectives  21.1 us (12%)
  matrix products  3.25 us (2%)
  between operations  2.61 us (1%)
    ppermute x26, starting transfers between devices, shifted(): lax.ppermute(block, axis, [(i, (i + distance) % size) for i in range(size)])  36.3 us
    pallas_call x10, Pallas kernels, call(): pl.pallas_call(kernel, out_shape=shapes, in_specs=[SMEM] * len(scalars) +...  27.2 us
    all_to_all x1, blocking collectives, per_device(): lax.all_to_all(strips.reshape(groups, strip, texts), REP_AXES, 0, 0, tile...  21.1 us
    ppermute x26, waiting for transfers between devices, shifted(): lax.ppermute(block, axis, [(i, (i + distance) % size) for i in range(size)])  20.8 us
    all_to_all x1, waiting for transfers between devices, per_device(): lax.all_to_all(terms.reshape(256, 8, 128), CAP_AXES + REP_AXES, 0, 0, til...  17.4 us
    unnamed x92, local copies, waits for them, and re-layouts  17.2 us
    all_to_all x1, starting transfers between devices, per_device(): received = lax.all_to_all(send_back, REP_AXES, 0, 0, tiled=True)  10.3 us
    all_to_all x1, starting transfers between devices, per_device(): lax.all_to_all(terms.reshape(256, 8, 128), CAP_AXES + REP_AXES, 0, 0, til...  8.63 us
  transfers between devices with their start and end apart: 29, of which 10 were waited for; matrix products, arithmetic and copies ran while one was open for 5% of the time, Pallas kernels for 10%

profile of v3, /device:TPU:1, one launch (start us, length us, event | category | flops | bytes accessed | tf_op | source)
XLA Modules:
  0.0 179.4 jit_solution(10138184334734517211)
XLA Ops:
  0.6 1.7 copy-done
  6.2 2.5 %collective-permute-start.13 = (bf16[128,1152]{1,0:T(8,128)(2,1)S(1)}, bf16[128,1152]{1,0:T(8,128)(2,1)S(1)}, u32[]{:S(2)}, u32[]{:S(2)}) collective-permute-start(bf16[128,1152]{1,0:T(8,128)(2,1)S(1)} %get-tuple-element.22.refs_2_.refs_5_.refs_6_), channel_id=1, source_target_pairs={{0,16},{16,32},{32,48},{48,64},{64,80},{80,96},{96,112},{112,0},{1... | collective-permute-start | bytes 884744 | tf_op jit(solution)/shard_map/ppermute | solution.py:22
  9.7 2.9 %pool_front.1 = (f32[128,1152]{1,0:T(8,128)S(1)}, f32[128,1]{1,0:T(8,128)S(1)}, bf16[16,16,1152]{2,1,0:T(8,128)(2,1)S(1)}, bf16[256,128]{1,0:T(8,128)(2,1)S(1)},...) custom-call(s32[4]{0:T(128)S(1)} %pad_add_fusion.refs_0_, ...), custom_call_target="tpu_custom_call" | custom-call | tf_op jit(solution)/shard_map/pool_front/pallas_call | solution.py:60
  14.5 3.7 %collective-permute-start.14 = (bf16[128,1152]{1,0:T(8,128)(2,1)S(1)}, bf16[128,1152]{1,0:T(8,128)(2,1)S(1)}, u32[]{:S(2)}, u32[]{:S(2)}) collective-permute-start(bf16[128,1152]{1,0:T(8,128)(2,1)S(1)} %get-tuple-element.22.refs_2_.refs_5_.refs_6_), channel_id=1, source_target_pairs={{0,112},{16,0},{32,16},{48,32},{64,48},{80,64},{96,80},{112,96},{1... | collective-permute-start | bytes 884744 | tf_op jit(solution)/shard_map/ppermute | solution.py:22
  20.2 2.9 %collective-permute-start.2 = (bf16[256,1152]{1,0:T(8,128)(2,1)}, bf16[256,1152]{1,0:T(8,128)(2,1)S(1)}, u32[]{:S(2)}, u32[]{:S(2)}) collective-permute-start(bf16[256,1152]{1,0:T(8,128)(2,1)} %pad_maximum_fusion), channel_id=1, source_target_pairs={{0,2},{2,0},{1,3},{3,1},{4,6},{6,4},{5,7},{7,5},{8,10},{10,8},{9,1... | collective-permute-start | bytes 1769480 | tf_op jit(solution)/shard_map/ppermute | solution.py:22
  24.5 3.4 %collective-permute-start.16 = (bf16[128,1152]{1,0:T(8,128)(2,1)S(1)}, bf16[128,1152]{1,0:T(8,128)(2,1)}, u32[]{:S(2)}, u32[]{:S(2)}) collective-permute-start(bf16[128,1152]{1,0:T(8,128)(2,1)S(1)} %collective-permute-done.14.refs_8_), channel_id=1, source_target_pairs={{0,112},{16,0},{32,16},{48,32},{64,48},{80,64},{96,80},{112,96},{1... | collective-permute-start | bytes 884744 | tf_op jit(solution)/shard_map/ppermute | solution.py:22
  28.0 8.1 %all-to-all-start = ((bf16[16,16,1152]{2,1,0:T(8,128)(2,1)}), bf16[16,16,1152]{2,1,0:T(8,128)(2,1)S(1)}, u32[]{:S(2)}, u32[]{:S(2)}) async-start(bf16[16,16,1152]{2,1,0:T(8,128)(2,1)} %copy-done.15), calls=%async_computation | async-start | bytes 1179648 | tf_op jit(solution)/shard_map/all_to_all | solution.py:293
  36.2 2.7 %collective-permute-start.18 = (bf16[128,1152]{1,0:T(8,128)(2,1)}, bf16[128,1152]{1,0:T(8,128)(2,1)S(1)}, u32[]{:S(2)}, u32[]{:S(2)}) collective-permute-start(bf16[128,1152]{1,0:T(8,128)(2,1)} %collective-permute-done.16.refs_10_), channel_id=1, source_target_pairs={{0,112},{16,0},{32,16},{48,32},{64,48},{80,64},{96,80},{112,96},{1... | collective-permute-start | bytes 884744 | tf_op jit(solution)/shard_map/ppermute | solution.py:22
  38.9 7.1 %collective-permute-done.17.refs_11_ = bf16[128,1152]{1,0:T(8,128)(2,1)S(1)} collective-permute-done((bf16[128,1152]{1,0:T(8,128)(2,1)S(1)}, bf16[128,1152]{1,0:T(8,128)(2,1)S(1)}, u32[]{:S(2)}, u32[]{:S(2)}) %collective-permute-start.17) | collective-permute-done | bytes 294944 | tf_op jit(solution)/shard_map/ppermute | solution.py:22
  49.5 2.1 %arrive.1 = (bf16[96,1152]{1,0:T(8,128)(2,1)S(1)}, bf16[512,1152]{1,0:T(8,128)(2,1)}) custom-call(bf16[16,16,1152]{2,1,0:T(8,128)(2,1)S(1)} %all-to-all-done.refs_0_, bf16[96,256]{1,0:T(8,128)(2,1)S(1)} %copy-done.40, bf16[128,1152]{1,0:T(8,128)(2,1)S(1)} %copy-done.12, bf16[128,1152]{1,0:T(8,128)(2,1)S(1)} %collective-permute-done.1.refs_3_, ...), custom_call_target="tpu_custom_call" | custom-call | tf_op jit(solution)/shard_map/arrive/pallas_call | solution.py:60
  52.1 2.3 %collective-permute-start.23 = (bf16[512,1152]{1,0:T(8,128)(2,1)}, bf16[512,1152]{1,0:T(8,128)(2,1)S(1)}, u32[]{:S(2)}, u32[]{:S(2)}) collective-permute-start(bf16[512,1152]{1,0:T(8,128)(2,1)} %get-tuple-element.40.refs_2_), channel_id=1, source_target_pairs={{0,12},{4,0},{8,4},{12,8},{1,13},{5,1},{9,5},{13,9},{2,14},{6,2},{... | collective-permute-start | bytes 3538952 | tf_op jit(solution)/shard_map/ppermute | solution.py:22
  54.4 1.7 collective-permute-start.20
  56.1 2.7 %collective-permute-start.4 = (bf16[96,1152]{1,0:T(8,128)(2,1)S(1)}, bf16[96,1152]{1,0:T(8,128)(2,1)S(1)}, u32[]{:S(2)}, u32[]{:S(2)}) collective-permute-start(bf16[96,1152]{1,0:T(8,128)(2,1)S(1)} %get-tuple-element.27.refs_5_.refs_6_.refs_2_), channel_id=1, source_target_pairs={{0,112},{16,0},{32,16},{48,32},{64,48},{80,64},{96,80},{112,96},{1... | collective-permute-start | bytes 663560 | tf_op jit(solution)/shard_map/ppermute | solution.py:22
  59.2 3.2 %collective-permute-done.3.refs_7_ = bf16[96,1152]{1,0:T(8,128)(2,1)S(1)} collective-permute-done((bf16[96,1152]{1,0:T(8,128)(2,1)S(1)}, bf16[96,1152]{1,0:T(8,128)(2,1)S(1)}, u32[]{:S(2)}, u32[]{:S(2)}) %collective-permute-start.3) | collective-permute-done | bytes 221216 | tf_op jit(solution)/shard_map/ppermute | solution.py:22
  63.3 3.4 %collective-permute-start.6 = (bf16[96,1152]{1,0:T(8,128)(2,1)S(1)}, bf16[96,1152]{1,0:T(8,128)(2,1)}, u32[]{:S(2)}, u32[]{:S(2)}) collective-permute-start(bf16[96,1152]{1,0:T(8,128)(2,1)S(1)} %collective-permute-done.4.refs_8_), channel_id=1, source_target_pairs={{0,112},{16,0},{32,16},{48,32},{64,48},{80,64},{96,80},{112,96},{1... | collective-permute-start | bytes 663560 | tf_op jit(solution)/shard_map/ppermute | solution.py:22
  71.0 4.8 %image_sums.1 = (f32[96,1152]{1,0:T(8,128)S(1)}, bf16[96,1152]{1,0:T(8,128)(2,1)S(1)}) custom-call(f32[1]{0:T(128)S(6)} %copy.12.refs_0_, f32[1]{0:T(128)S(6)} %copy.13.refs_1_, bf16[96,1152]{1,0:T(8,128)(2,1)S(1)} %get-tuple-element.27.refs_5_.refs_6_.refs_2_, bf16[96,1152]{1,0:T(8,128)(2,1)S(1)} %collective-permute-done.12.refs_3_, ...), custom_call_target="tpu_custom_call" | custom-call | tf_op jit(solution)/shard_map/image_sums/pallas_call | solution.py:60
  76.3 2.7 %collective-permute-start.8 = (bf16[96,1152]{1,0:T(8,128)(2,1)}, bf16[96,1152]{1,0:T(8,128)(2,1)}, u32[]{:S(2)}, u32[]{:S(2)}) collective-permute-start(bf16[96,1152]{1,0:T(8,128)(2,1)} %collective-permute-done.6.refs_10_), channel_id=1, source_target_pairs={{0,112},{16,0},{32,16},{48,32},{64,48},{80,64},{96,80},{112,96},{1... | collective-permute-start | bytes 663560 | tf_op jit(solution)/shard_map/ppermute | solution.py:22
  79.0 2.0 %collective-permute-done.21.refs_2_ = bf16[96,1152]{1,0:T(8,128)(2,1)S(1)} collective-permute-done((bf16[96,1152]{1,0:T(8,128)(2,1)S(1)}, bf16[96,1152]{1,0:T(8,128)(2,1)S(1)}, u32[]{:S(2)}, u32[]{:S(2)}) %collective-permute-start.21) | collective-permute-done | bytes 221216 | tf_op jit(solution)/shard_map/ppermute | solution.py:22
  83.3 10.3 %all-to-all-start.1 = ((bf16[16,16,1152]{2,1,0:T(8,128)(2,1)}), bf16[16,16,1152]{2,1,0:T(8,128)(2,1)S(1)}, u32[]{:S(2)}, u32[]{:S(2)}) async-start(bf16[16,16,1152]{2,1,0:T(8,128)(2,1)} %copy-done.8), calls=%async_computation.1 | async-start | bytes 1179648 | tf_op jit(solution)/shard_map/all_to_all | solution.py:316
  95.6 2.8 %collective-permute-start.10 = (bf16[48,1152]{1,0:T(8,128)(2,1)S(1)}, bf16[48,1152]{1,0:T(8,128)(2,1)S(1)}, u32[]{:S(2)}, u32[]{:S(2)}) collective-permute-start(bf16[48,1152]{1,0:T(8,128)(2,1)S(1)} %slice.25), channel_id=1, source_target_pairs={{0,112},{16,0},{32,16},{48,32},{64,48},{80,64},{96,80},{112,96},{1... | collective-permute-start | bytes 331784 | tf_op jit(solution)/shard_map/ppermute | solution.py:22
  98.3 2.1 %collective-permute-done.9.refs_13_ = bf16[48,1152]{1,0:T(8,128)(2,1)S(1)} collective-permute-done((bf16[48,1152]{1,0:T(8,128)(2,1)S(1)}, bf16[48,1152]{1,0:T(8,128)(2,1)S(1)}, u32[]{:S(2)}, u32[]{:S(2)}) %collective-permute-start.9) | collective-permute-done | bytes 110624 | tf_op jit(solution)/shard_map/ppermute | solution.py:22
  102.4 5.6 %text_sums.1 = (f32[128,1152]{1,0:T(8,128)S(1)}, bf16[128,1152]{1,0:T(8,128)(2,1)S(1)}) custom-call(f32[1]{0:T(128)S(6)} %copy.12.refs_0_, f32[1]{0:T(128)S(6)} %copy.13.refs_1_, bf16[128,1152]{1,0:T(8,128)(2,1)S(1)} %get-tuple-element.22.refs_2_.refs_5_.refs_6_, bf16[128,1152]{1,0:T(8,128)(2,1)} %collective-permute-done.refs_3_, s32[1,128]{1,0:T(1,128)S(1)} %copy-done.45, ...), custom_call_target="tpu_custom_call" | custom-call | tf_op jit(solution)/shard_map/text_sums/pallas_call | solution.py:60
  111.1 1.6 collective-permute-start.25
  112.7 2.8 %collective-permute-done.11.refs_2_ = bf16[128,1152]{1,0:T(8,128)(2,1)S(1)} collective-permute-done((bf16[128,1152]{1,0:T(8,128)(2,1)S(1)}, bf16[128,1152]{1,0:T(8,128)(2,1)S(1)}, u32[]{:S(2)}, u32[]{:S(2)}) %collective-permute-start.11) | collective-permute-done | bytes 294944 | tf_op jit(solution)/shard_map/ppermute | solution.py:22
  118.7 21.1 %all_to_all.20.refs_1_ = bf16[16,144,128]{2,1,0:T(8,128)(2,1)S(1)} all-to-all(bf16[16,144,128]{2,1,0:T(8,128)(2,1)S(1)} %bitcast.21), channel_id=1, replica_groups=mesh['ylo'=2,'z'=8,'x'=4,'yhi'=2,'core'=2] {'x','yhi','core'}, dimensions={0} | all-to-all | bytes 1179648 | tf_op jit(solution)/shard_map/all_to_all | solution.py:335
  139.8 1.4 copy-done.5
  142.5 5.3 %head_terms.1 = bf16[128,16,128]{2,1,0:T(8,128)(2,1)} custom-call(s32[4]{0:T(128)S(1)} %copy-done.44, bf16[16,144,128]{2,1,0:T(8,128)(2,1)S(1)} %all_to_all.20.refs_1_, bf16[512,1152]{1,0:T(8,128)(2,1)} %get-tuple-element.40.refs_2_, bf16[512,1152]{1,0:T(8,128)(2,1)S(1)} %copy-done.5, bf16[512,1152]{1,0:T(8,128)(2,1)S(1)} %copy-done.7, ...), custom_call_target="tpu_custom_call" | custom-call | tf_op jit(solution)/shard_map/head_terms/pallas_call | solution.py:60
  147.8 8.6 %all-to-all-start.3 = ((bf16[256,8,128]{2,1,0:T(8,128)(2,1)}), bf16[256,8,128]{2,1,0:T(8,128)(2,1)S(1)}, u32[]{:S(2)}, u32[]{:S(2)}) async-start(bf16[256,8,128]{2,1,0:T(8,128)(2,1)} %bitcast.10), calls=%async_computation.3 | async-start | bytes 1048576 | tf_op jit(solution)/shard_map/all_to_all | solution.py:343
  156.5 1.6 fusion
  158.2 1.6 fusion.1
  159.8 17.4 %all-to-all-done.3 = bf16[256,8,128]{2,1,0:T(8,128)(2,1)S(1)} async-done(((bf16[256,8,128]{2,1,0:T(8,128)(2,1)}), bf16[256,8,128]{2,1,0:T(8,128)(2,1)S(1)}, u32[]{:S(2)}, u32[]{:S(2)}) %all-to-all-start.3) | async-done | bytes 524320 | tf_op jit(solution)/shard_map/all_to_all | solution.py:343
  177.2 2.0 %head_sums.1 = f32[9,1152]{1,0:T(8,128)} custom-call(s32[4]{0:T(128)S(1)} %copy-done.44, bf16[128,16,128]{2,1,0:T(8,128)(2,1)S(1)} %bitcast.18), custom_call_target="tpu_custom_call" | custom-call | tf_op jit(solution)/shard_map/head_sums/pallas_call | solution.py:60
  (139 shorter events, 32.8 us)
Async XLA Ops:
  6.2 13.1 %collective-permute-start.13 = (bf16[128,1152]{1,0:T(8,128)(2,1)S(1)}, bf16[128,1152]{1,0:T(8,128)(2,1)S(1)}, u32[]{:S(2)}, u32[]{:S(2)}) collective-permute-start(bf16[128,1152]{1,0:T(8,128)(2,1)S(1)} %get-tuple-element.22.refs_2_.refs_5_.refs_6_), channel_id=1, source_target_pairs={{0,16},{16,32},{32,48},{48,64},{64,80},{80,96},{96,112},{112,0},{1... | collective-permute-start | bytes 884744 | tf_op jit(solution)/shard_map/ppermute | solution.py:22
  13.5 54.6 %copy-start.45 = (s32[1,128]{1,0:T(1,128)S(1)}, s32[1,128]{1,0:T(1,128)}, u32[]{:S(2)}) copy-start(s32[1,128]{1,0:T(1,128)} %refs_4_.5) | copy-start | bytes 1540
  13.5 5.8 %collective-permute-start.1 = (bf16[128,1152]{1,0:T(8,128)(2,1)S(1)}, bf16[128,1152]{1,0:T(8,128)(2,1)S(1)}, u32[]{:S(2)}, u32[]{:S(2)}) collective-permute-start(bf16[128,1152]{1,0:T(8,128)(2,1)S(1)} %get-tuple-element.26), channel_id=1, source_target_pairs={{0,1},{1,0},{2,3},{3,2},{4,5},{5,4},{6,7},{7,6},{8,9},{9,8},{10,11... | collective-permute-start | bytes 884744 | tf_op jit(solution)/shard_map/ppermute | solution.py:22
  14.5 10.0 %collective-permute-start.14 = (bf16[128,1152]{1,0:T(8,128)(2,1)S(1)}, bf16[128,1152]{1,0:T(8,128)(2,1)S(1)}, u32[]{:S(2)}, u32[]{:S(2)}) collective-permute-start(bf16[128,1152]{1,0:T(8,128)(2,1)S(1)} %get-tuple-element.22.refs_2_.refs_5_.refs_6_), channel_id=1, source_target_pairs={{0,112},{16,0},{32,16},{48,32},{64,48},{80,64},{96,80},{112,96},{1... | collective-permute-start | bytes 884744 | tf_op jit(solution)/shard_map/ppermute | solution.py:22
  19.3 16.8 %collective-permute-start.15 = (bf16[128,1152]{1,0:T(8,128)(2,1)S(1)}, bf16[128,1152]{1,0:T(8,128)(2,1)S(1)}, u32[]{:S(2)}, u32[]{:S(2)}) collective-permute-start(bf16[128,1152]{1,0:T(8,128)(2,1)S(1)} %collective-permute-done.13.refs_7_), channel_id=1, source_target_pairs={{0,16},{16,32},{32,48},{48,64},{64,80},{80,96},{96,112},{112,0},{1... | collective-permute-start | bytes 884744 | tf_op jit(solution)/shard_map/ppermute | solution.py:22
  20.2 27.5 %collective-permute-start.2 = (bf16[256,1152]{1,0:T(8,128)(2,1)}, bf16[256,1152]{1,0:T(8,128)(2,1)S(1)}, u32[]{:S(2)}, u32[]{:S(2)}) collective-permute-start(bf16[256,1152]{1,0:T(8,128)(2,1)} %pad_maximum_fusion), channel_id=1, source_target_pairs={{0,2},{2,0},{1,3},{3,1},{4,6},{6,4},{5,7},{7,5},{8,10},{10,8},{9,1... | collective-permute-start | bytes 1769480 | tf_op jit(solution)/shard_map/ppermute | solution.py:22
  24.5 11.7 %collective-permute-start.16 = (bf16[128,1152]{1,0:T(8,128)(2,1)S(1)}, bf16[128,1152]{1,0:T(8,128)(2,1)}, u32[]{:S(2)}, u32[]{:S(2)}) collective-permute-start(bf16[128,1152]{1,0:T(8,128)(2,1)S(1)} %collective-permute-done.14.refs_8_), channel_id=1, source_target_pairs={{0,112},{16,0},{32,16},{48,32},{64,48},{80,64},{96,80},{112,96},{1... | collective-permute-start | bytes 884744 | tf_op jit(solution)/shard_map/ppermute | solution.py:22
  28.0 19.8 %all-to-all-start = ((bf16[16,16,1152]{2,1,0:T(8,128)(2,1)}), bf16[16,16,1152]{2,1,0:T(8,128)(2,1)S(1)}, u32[]{:S(2)}, u32[]{:S(2)}) async-start(bf16[16,16,1152]{2,1,0:T(8,128)(2,1)} %copy-done.15), calls=%async_computation | async-start | bytes 1179648 | tf_op jit(solution)/shard_map/all_to_all | solution.py:293
  36.1 9.9 %collective-permute-start.17 = (bf16[128,1152]{1,0:T(8,128)(2,1)S(1)}, bf16[128,1152]{1,0:T(8,128)(2,1)S(1)}, u32[]{:S(2)}, u32[]{:S(2)}) collective-permute-start(bf16[128,1152]{1,0:T(8,128)(2,1)S(1)} %collective-permute-done.15.refs_9_), channel_id=1, source_target_pairs={{0,16},{16,32},{32,48},{48,64},{64,80},{80,96},{96,112},{112,0},{1... | collective-permute-start | bytes 884744 | tf_op jit(solution)/shard_map/ppermute | solution.py:22
  36.2 18.2 %collective-permute-start.18 = (bf16[128,1152]{1,0:T(8,128)(2,1)}, bf16[128,1152]{1,0:T(8,128)(2,1)S(1)}, u32[]{:S(2)}, u32[]{:S(2)}) collective-permute-start(bf16[128,1152]{1,0:T(8,128)(2,1)} %collective-permute-done.16.refs_10_), channel_id=1, source_target_pairs={{0,112},{16,0},{32,16},{48,32},{64,48},{80,64},{96,80},{112,96},{1... | collective-permute-start | bytes 884744 | tf_op jit(solution)/shard_map/ppermute | solution.py:22
  46.0 35.4 %copy-start.38 = (bf16[256,96]{1,0:T(8,128)(2,1)S(1)}, bf16[256,96]{1,0:T(8,128)(2,1)}, u32[]{:S(2)}) copy-start(bf16[256,96]{1,0:T(8,128)(2,1)} %copy-done.37) | copy-start | bytes 147460
  46.6 9.4 %collective-permute-start.19 = (bf16[64,1152]{1,0:T(8,128)(2,1)}, bf16[64,1152]{1,0:T(8,128)(2,1)}, u32[]{:S(2)}, u32[]{:S(2)}) collective-permute-start(bf16[64,1152]{1,0:T(8,128)(2,1)} %slice.26), channel_id=1, source_target_pairs={{0,16},{16,32},{32,48},{48,64},{64,80},{80,96},{96,112},{112,0},{1... | collective-permute-start | bytes 442376 | tf_op jit(solution)/shard_map/ppermute | solution.py:22
  51.6 56.4 %collective-permute-start.22 = (bf16[512,1152]{1,0:T(8,128)(2,1)}, bf16[512,1152]{1,0:T(8,128)(2,1)S(1)}, u32[]{:S(2)}, u32[]{:S(2)}) collective-permute-start(bf16[512,1152]{1,0:T(8,128)(2,1)} %get-tuple-element.40.refs_2_), channel_id=1, source_target_pairs={{0,4},{4,8},{8,12},{12,0},{1,5},{5,9},{9,13},{13,1},{2,6},{6,10},{... | collective-permute-start | bytes 3538952 | tf_op jit(solution)/shard_map/ppermute | solution.py:22
  52.1 58.0 %collective-permute-start.23 = (bf16[512,1152]{1,0:T(8,128)(2,1)}, bf16[512,1152]{1,0:T(8,128)(2,1)S(1)}, u32[]{:S(2)}, u32[]{:S(2)}) collective-permute-start(bf16[512,1152]{1,0:T(8,128)(2,1)} %get-tuple-element.40.refs_2_), channel_id=1, source_target_pairs={{0,12},{4,0},{8,4},{12,8},{1,13},{5,1},{9,5},{13,9},{2,14},{6,2},{... | collective-permute-start | bytes 3538952 | tf_op jit(solution)/shard_map/ppermute | solution.py:22
  54.4 4.4 %collective-permute-start.20 = (bf16[64,1152]{1,0:T(8,128)(2,1)S(1)}, bf16[64,1152]{1,0:T(8,128)(2,1)S(1)}, u32[]{:S(2)}, u32[]{:S(2)}) collective-permute-start(bf16[64,1152]{1,0:T(8,128)(2,1)S(1)} %slice.27), channel_id=1, source_target_pairs={{0,112},{16,0},{32,16},{48,32},{64,48},{80,64},{96,80},{112,96},{1... | collective-permute-start | bytes 442376 | tf_op jit(solution)/shard_map/ppermute | solution.py:22
  56.1 6.3 %collective-permute-start.3 = (bf16[96,1152]{1,0:T(8,128)(2,1)S(1)}, bf16[96,1152]{1,0:T(8,128)(2,1)S(1)}, u32[]{:S(2)}, u32[]{:S(2)}) collective-permute-start(bf16[96,1152]{1,0:T(8,128)(2,1)S(1)} %get-tuple-element.27.refs_5_.refs_6_.refs_2_), channel_id=1, source_target_pairs={{0,16},{16,32},{32,48},{48,64},{64,80},{80,96},{96,112},{112,0},{1... | collective-permute-start | bytes 663560 | tf_op jit(solution)/shard_map/ppermute | solution.py:22
  56.1 7.3 %collective-permute-start.4 = (bf16[96,1152]{1,0:T(8,128)(2,1)S(1)}, bf16[96,1152]{1,0:T(8,128)(2,1)S(1)}, u32[]{:S(2)}, u32[]{:S(2)}) collective-permute-start(bf16[96,1152]{1,0:T(8,128)(2,1)S(1)} %get-tuple-element.27.refs_5_.refs_6_.refs_2_), channel_id=1, source_target_pairs={{0,112},{16,0},{32,16},{48,32},{64,48},{80,64},{96,80},{112,96},{1... | collective-permute-start | bytes 663560 | tf_op jit(solution)/shard_map/ppermute | solution.py:22
  58.8 9.3 %collective-permute-start.12 = (bf16[96,1152]{1,0:T(8,128)(2,1)S(1)}, bf16[96,1152]{1,0:T(8,128)(2,1)S(1)}, u32[]{:S(2)}, u32[]{:S(2)}) collective-permute-start(bf16[96,1152]{1,0:T(8,128)(2,1)S(1)} %get-tuple-element.27.refs_5_.refs_6_.refs_2_), channel_id=1, source_target_pairs={{0,128},{128,0},{1,129},{129,1},{2,130},{130,2},{3,131},{131,3},{4... | collective-permute-start | bytes 663560 | tf_op jit(solution)/shard_map/ppermute | solution.py:22
  62.4 13.9 %collective-permute-start.5 = (bf16[96,1152]{1,0:T(8,128)(2,1)S(1)}, bf16[96,1152]{1,0:T(8,128)(2,1)}, u32[]{:S(2)}, u32[]{:S(2)}) collective-permute-start(bf16[96,1152]{1,0:T(8,128)(2,1)S(1)} %collective-permute-done.3.refs_7_), channel_id=1, source_target_pairs={{0,16},{16,32},{32,48},{48,64},{64,80},{80,96},{96,112},{112,0},{1... | collective-permute-start | bytes 663560 | tf_op jit(solution)/shard_map/ppermute | solution.py:22
  63.3 13.0 %collective-permute-start.6 = (bf16[96,1152]{1,0:T(8,128)(2,1)S(1)}, bf16[96,1152]{1,0:T(8,128)(2,1)}, u32[]{:S(2)}, u32[]{:S(2)}) collective-permute-start(bf16[96,1152]{1,0:T(8,128)(2,1)S(1)} %collective-permute-done.4.refs_8_), channel_id=1, source_target_pairs={{0,112},{16,0},{32,16},{48,32},{64,48},{80,64},{96,80},{112,96},{1... | collective-permute-start | bytes 663560 | tf_op jit(solution)/shard_map/ppermute | solution.py:22
  75.8 5.2 %collective-permute-start.21 = (bf16[96,1152]{1,0:T(8,128)(2,1)S(1)}, bf16[96,1152]{1,0:T(8,128)(2,1)S(1)}, u32[]{:S(2)}, u32[]{:S(2)}) collective-permute-start(bf16[96,1152]{1,0:T(8,128)(2,1)S(1)} %get-tuple-element.33), channel_id=1, source_target_pairs={{0,128},{128,0},{1,129},{129,1},{2,130},{130,2},{3,131},{131,3},{4... | collective-permute-start | bytes 663560 | tf_op jit(solution)/shard_map/ppermute | solution.py:22
  76.3 17.3 %collective-permute-start.7 = (bf16[96,1152]{1,0:T(8,128)(2,1)}, bf16[96,1152]{1,0:T(8,128)(2,1)}, u32[]{:S(2)}, u32[]{:S(2)}) collective-permute-start(bf16[96,1152]{1,0:T(8,128)(2,1)} %collective-permute-done.5.refs_9_), channel_id=1, source_target_pairs={{0,16},{16,32},{32,48},{48,64},{64,80},{80,96},{96,112},{112,0},{1... | collective-permute-start | bytes 663560 | tf_op jit(solution)/shard_map/ppermute | solution.py:22
  76.3 18.4 %collective-permute-start.8 = (bf16[96,1152]{1,0:T(8,128)(2,1)}, bf16[96,1152]{1,0:T(8,128)(2,1)}, u32[]{:S(2)}, u32[]{:S(2)}) collective-permute-start(bf16[96,1152]{1,0:T(8,128)(2,1)} %collective-permute-done.6.refs_10_), channel_id=1, source_target_pairs={{0,112},{16,0},{32,16},{48,32},{64,48},{80,64},{96,80},{112,96},{1... | collective-permute-start | bytes 663560 | tf_op jit(solution)/shard_map/ppermute | solution.py:22
  81.0 17.4 %collective-permute-start = (bf16[128,1152]{1,0:T(8,128)(2,1)S(1)}, bf16[128,1152]{1,0:T(8,128)(2,1)}, u32[]{:S(2)}, u32[]{:S(2)}) collective-permute-start(bf16[128,1152]{1,0:T(8,128)(2,1)S(1)} %get-tuple-element.22.refs_2_.refs_5_.refs_6_), channel_id=1, source_target_pairs={{0,128},{128,0},{1,129},{129,1},{2,130},{130,2},{3,131},{131,3},{4... | collective-permute-start | bytes 884744 | tf_op jit(solution)/shard_map/ppermute | solution.py:22
  83.3 32.2 %copy-start.32 = (f32[128,1]{1,0:T(8,128)S(1)}, f32[128,1]{1,0:T(8,128)}, u32[]{:S(2)}) copy-start(f32[128,1]{1,0:T(8,128)} %copy-done.31) | copy-start | bytes 1540
  83.3 33.0 %all-to-all-start.1 = ((bf16[16,16,1152]{2,1,0:T(8,128)(2,1)}), bf16[16,16,1152]{2,1,0:T(8,128)(2,1)S(1)}, u32[]{:S(2)}, u32[]{:S(2)}) async-start(bf16[16,16,1152]{2,1,0:T(8,128)(2,1)} %copy-done.8), calls=%async_computation.1 | async-start | bytes 1179648 | tf_op jit(solution)/shard_map/all_to_all | solution.py:316
  94.6 5.9 %collective-permute-start.9 = (bf16[48,1152]{1,0:T(8,128)(2,1)S(1)}, bf16[48,1152]{1,0:T(8,128)(2,1)S(1)}, u32[]{:S(2)}, u32[]{:S(2)}) collective-permute-start(bf16[48,1152]{1,0:T(8,128)(2,1)S(1)} %slice.24), channel_id=1, source_target_pairs={{0,16},{16,32},{32,48},{48,64},{64,80},{80,96},{96,112},{112,0},{1... | collective-permute-start | bytes 331784 | tf_op jit(solution)/shard_map/ppermute | solution.py:22
  95.6 4.9 %collective-permute-start.10 = (bf16[48,1152]{1,0:T(8,128)(2,1)S(1)}, bf16[48,1152]{1,0:T(8,128)(2,1)S(1)}, u32[]{:S(2)}, u32[]{:S(2)}) collective-permute-start(bf16[48,1152]{1,0:T(8,128)(2,1)S(1)} %slice.25), channel_id=1, source_target_pairs={{0,112},{16,0},{32,16},{48,32},{64,48},{80,64},{96,80},{112,96},{1... | collective-permute-start | bytes 331784 | tf_op jit(solution)/shard_map/ppermute | solution.py:22
  108.0 7.6 %collective-permute-start.11 = (bf16[128,1152]{1,0:T(8,128)(2,1)S(1)}, bf16[128,1152]{1,0:T(8,128)(2,1)S(1)}, u32[]{:S(2)}, u32[]{:S(2)}) collective-permute-start(bf16[128,1152]{1,0:T(8,128)(2,1)S(1)} %get-tuple-element.29), channel_id=1, source_target_pairs={{0,128},{128,0},{1,129},{129,1},{2,130},{130,2},{3,131},{131,3},{4... | collective-permute-start | bytes 884744 | tf_op jit(solution)/shard_map/ppermute | solution.py:22
  109.0 30.7 %collective-permute-start.24 = (bf16[256,1152]{1,0:T(8,128)(2,1)}, bf16[256,1152]{1,0:T(8,128)(2,1)}, u32[]{:S(2)}, u32[]{:S(2)}) collective-permute-start(bf16[256,1152]{1,0:T(8,128)(2,1)} %slice.28), channel_id=1, source_target_pairs={{0,4},{4,8},{8,12},{12,0},{1,5},{5,9},{9,13},{13,1},{2,6},{6,10},{... | collective-permute-start | bytes 1769480 | tf_op jit(solution)/shard_map/ppermute | solution.py:22
  111.1 28.7 %collective-permute-start.25 = (bf16[256,1152]{1,0:T(8,128)(2,1)}, bf16[256,1152]{1,0:T(8,128)(2,1)}, u32[]{:S(2)}, u32[]{:S(2)}) collective-permute-start(bf16[256,1152]{1,0:T(8,128)(2,1)} %slice.29), channel_id=1, source_target_pairs={{0,12},{4,0},{8,4},{12,8},{1,13},{5,1},{9,5},{13,9},{2,14},{6,2},{... | collective-permute-start | bytes 1769480 | tf_op jit(solution)/shard_map/ppermute | solution.py:22
  147.8 29.4 %all-to-all-start.3 = ((bf16[256,8,128]{2,1,0:T(8,128)(2,1)}), bf16[256,8,128]{2,1,0:T(8,128)(2,1)S(1)}, u32[]{:S(2)}, u32[]{:S(2)}) async-start(bf16[256,8,128]{2,1,0:T(8,128)(2,1)} %bitcast.10), calls=%async_computation.3 | async-start | bytes 1048576 | tf_op jit(solution)/shard_map/all_to_all | solution.py:343
  (43 other events, 360.1 us)

commit v4 on v3

--- a/solution.py
+++ b/solution.py
@@ -13,7 +13,7 @@
 CAP_AXES = ("ylo", "z")
 REP_AXES = ("x", "yhi", "core")
 SLOTS = 16
-ANY = pl.BlockSpec(memory_space=pl.ANY)
+FAR = pl.BlockSpec(memory_space=pltpu.HBM)
 SMEM = pl.BlockSpec(memory_space=pltpu.SMEM)
 
 
@@ -22,13 +22,12 @@
     return lax.ppermute(block, axis, [(i, (i + distance) % size) for i in range(size)])
 
 
-def gathered_along_z(block):
-    half = block.shape[0] // 2
-    up, down, found = block, block, [block]
+def gathered_along_z(block, way):
+    ahead, behind, found = block, block, [block]
     for _ in range(3):
-        up, down = shifted(up, "z", 1), shifted(down, "z", -1)
-        found += [up, down]
-    return found + [shifted(up[:half], "z", 1), shifted(down[half:], "z", -1)]
+        ahead, behind = shifted(ahead, "z", way), shifted(behind, "z", -way)
+        found += [ahead, behind]
+    return found + [shifted(ahead, "z", way)]
 
 
 def call(body, outs, name, scalars, arrays):
@@ -60,11 +59,11 @@
     return pl.pallas_call(
         kernel,
         out_shape=shapes,
-        in_specs=[SMEM] * len(scalars) + [ANY] * count,
-        out_specs=[ANY] * len(outs),
+        in_specs=[SMEM] * len(scalars) + [FAR] * count,
+        out_specs=[FAR] * len(outs),
         scratch_shapes=[pltpu.VMEM(s, d) for s, d in everything]
         + [pltpu.SemaphoreType.DMA((total,))],
-        compiler_params=pltpu.CompilerParams(vmem_limit_bytes=48 * 2**20),
+        compiler_params=pltpu.CompilerParams(vmem_limit_bytes=64 * 2**20),
         name=name,
     )(*scalars, *arrays)
 
@@ -92,7 +91,7 @@
     return (gradient - unit * radial) / norm
 
 
-def text_front(feats_ref, head_ref, unit_ref, norm_ref, emb_ref):
+def text_front(feats_ref, head_ref, after_ref, unit_ref, norm_ref, emb_ref):
     unit, norm = project(feats_ref[...], head_ref[...])
     unit_ref[...] = unit
     norm_ref[...] = norm
@@ -100,8 +99,7 @@
 
 
 def pool_front(
-    place_ref, feats_ref, head_ref, owners_ref, slots_ref, captions_ref,
-    unit_ref, norm_ref, out_ref, select_ref, hit_ref, hit_t_ref, keep_ref, give_ref,
+    place_ref, feats_ref, head_ref, owners_ref, slots_ref, unit_ref, norm_ref, out_ref, select_ref
 ):
     rank = place_ref[0]
     owners = owners_ref[...]
@@ -125,34 +123,47 @@
     select_ref[...] = select
     out_ref[...] = dot(select, unit.astype(BF)).astype(BF).reshape(out_ref.shape)
 
+
+def requested(place_ref, owners_ref, turned):
+    owners = owners_ref[...]
+    groups, images = owners.shape
+    row, lane = iota((images, images), 0), iota((images, images), 1)
     mine = jnp.sum(
-        jnp.where(iota((groups, images), 0) == rank, owners.astype(F32), 0.0), axis=0, keepdims=True
+        jnp.where(iota((groups, images), 0) == place_ref[0], owners.astype(F32), 0.0),
+        axis=0,
+        keepdims=True,
     )
     mine_t = jnp.sum(jnp.where(row == lane, mine, 0.0), axis=1, keepdims=True)
     same = mine == mine_t
-    spot_t = mine_t * SLOTS + jnp.sum(jnp.where(same & (lane < row), 1.0, 0.0), axis=1, keepdims=True)
-    spot = mine * SLOTS + jnp.sum(jnp.where(same & (row < lane), 1.0, 0.0), axis=0, keepdims=True)
-    hit_ref[...] = one_hot(spot_t == iota((images, rows), 1).astype(F32))
-    hit_t_ref[...] = one_hot(spot == iota((rows, images), 0).astype(F32))
+    if turned:
+        before = jnp.sum(jnp.where(same & (row < lane), 1.0, 0.0), axis=0, keepdims=True)
+        rows = iota((groups * SLOTS, images), 0)
+        return one_hot(mine * SLOTS + before == rows.astype(F32))
+    before = jnp.sum(jnp.where(same & (lane < row), 1.0, 0.0), axis=1, keepdims=True)
+    return one_hot(mine_t * SLOTS + before == iota((images, groups * SLOTS), 1).astype(F32))
+
+
+def arrive(place_ref, arrived_ref, owners_ref, captions_ref, pool_ref, emb_ref, keep_ref, give_ref):
+    hit = requested(place_ref, owners_ref, False)
+    emb_ref[...] = dot(hit, arrived_ref[...].reshape(hit.shape[1], -1)).astype(BF)
 
     @pl.when(place_ref[1] == 0)
     def _():
         keep_ref[...] = captions_ref[...]
-        give_ref[...] = feats_ref[...]
+        give_ref[...] = pool_ref[...]
 
     @pl.when(place_ref[1] != 0)
     def _():
-        keep_ref[...] = feats_ref[...]
+        keep_ref[...] = pool_ref[...]
         give_ref[...] = captions_ref[...]
 
 
-def arrive(arrived_ref, hit_ref, keep_ref, given_ref, far_ref, emb_ref, four_ref):
-    arrived = arrived_ref[...].reshape(hit_ref.shape[1], -1)
-    emb_ref[...] = dot(hit_ref[...], arrived).astype(BF)
-    rows = keep_ref.shape[0]
-    four_ref[:rows] = keep_ref[...]
-    four_ref[rows : 2 * rows] = given_ref[...]
-    four_ref[2 * rows :] = far_ref[...]
+def joined(a_ref, b_ref, c_ref, d_ref, ab_ref, cd_ref):
+    rows = a_ref.shape[0]
+    ab_ref[:rows] = a_ref[...]
+    ab_ref[rows:] = b_ref[...]
+    cd_ref[:rows] = c_ref[...]
+    cd_ref[rows:] = d_ref[...]
 
 
 def pair_sums(turned, scale_ref, bias_ref, own_ref, other_ref, targets_ref, partners_ref, *refs):
@@ -172,9 +183,9 @@
     rest_ref[...] = total[own_rows:].astype(BF)
 
 
-def image_back(scale_ref, mine_ref, rest_ref, hit_t_ref, out_ref):
+def image_back(place_ref, scale_ref, mine_ref, rest_ref, owners_ref, out_ref):
     gradient = (scale_ref[0] * (mine_ref[...] + rest_ref[...].astype(F32))).astype(BF)
-    out_ref[...] = dot(hit_t_ref[...], gradient).astype(BF).reshape(out_ref.shape)
+    out_ref[...] = dot(requested(place_ref, owners_ref, True), gradient).astype(BF).reshape(out_ref.shape)
 
 
 def text_back(scale_ref, mine_ref, rest_ref, unit_ref, norm_ref, grad_ref):
@@ -194,25 +205,21 @@
     strips_ref[:, 1] = turned.reshape(columns, strip, rows)
 
 
-def head_terms(place_ref, strips_ref, home_ref, up_ref, down_ref, far_up_ref, far_down_ref, out_ref):
+def head_terms(place_ref, strips_ref, *refs):
     x, yhi, core = place_ref[2], place_ref[3], place_ref[1]
+    *feats_refs, out_ref = refs
     _, strip, lanes = strips_ref.shape
     extra = strip - lanes
-
-    def grads(along, across):
+    terms = jnp.zeros((2 * lanes, feats_refs[0].shape[1]), F32)
+    for i, feats_ref in enumerate(feats_refs):
+        along, across = (0, 3, 1, 2)[i // 2], i % 2
         blocks = []
-        for dy in across:
-            for dc in range(2):
-                source = lax.rem(x + along, 4) * 4 + lax.rem(yhi + dy, 2) * 2 + lax.rem(core + dc, 2)
-                blocks.append(strips_ref[source])
+        for dc in range(2):
+            source = lax.rem(x + along, 4) * 4 + lax.rem(yhi + across, 2) * 2 + lax.rem(core + dc, 2)
+            blocks.append(strips_ref[source])
         block = jnp.concatenate(blocks, axis=1)
-        return jnp.concatenate([block[:lanes]] + [block[lanes:]] * (lanes // extra), axis=0)
-
-    terms = dot(grads(0, (0, 1)), home_ref[...])
-    terms += dot(grads(3, (0, 1)), up_ref[...])
-    terms += dot(grads(1, (0, 1)), down_ref[...])
-    terms += dot(grads(2, (0,)), far_up_ref[...])
-    terms += dot(grads(2, (1,)), far_down_ref[...])
+        block = jnp.concatenate([block[:lanes]] + [block[lanes:]] * (lanes // extra), axis=0)
+        terms += dot(block, feats_ref[...])
     turned = terms.T
     turned = jnp.concatenate([turned, jnp.zeros((8, 2 * lanes), F32)], axis=0)
     row, lane = iota((8, lanes), 0), iota((8, lanes), 1)
@@ -269,38 +276,41 @@
     pool_rows = pool.shape[0]
     place = jnp.stack([lax.axis_index(REP_AXES)] + [lax.axis_index(a) for a in ("core", "x", "yhi")])
 
-    text_unit, text_norm, text_emb = call(
-        text_front,
-        [((texts, width), F32), ((texts, 1), F32), ((texts, width), BF)],
-        "text_front", [], [captions, text_head],
-    )
-    pool_unit, pool_norm, outgoing, select, hit, hit_t, keep, give = call(
+    pool_unit, pool_norm, outgoing, select = call(
         pool_front,
         [
             ((pool_rows, width), F32),
             ((pool_rows, 1), F32),
             ((groups, SLOTS, width), BF),
             ((groups * SLOTS, pool_rows), BF),
-            ((images, groups * SLOTS), BF),
-            ((groups * SLOTS, images), BF),
-            ((texts, width), BF),
-            ((texts, width), BF),
         ],
-        "pool_front", [place], [pool, image_head, owners, image_slot, captions],
+        "pool_front", [place], [pool, image_head, owners, image_slot],
+    )
+    arrived = lax.all_to_all(outgoing, REP_AXES, 0, 0, tiled=True)
+    text_unit, text_norm, text_emb = call(
+        text_front,
+        [((texts, width), F32), ((texts, 1), F32), ((texts, width), BF)],
+        "text_front", [], [captions, text_head, pool_norm],
     )
     other_text = shifted(text_emb, "ylo", 1)
-    text_blocks = gathered_along_z(text_emb)
-    arrived = lax.all_to_all(outgoing, REP_AXES, 0, 0, tiled=True)
+    text_blocks = gathered_along_z(text_emb, 1)
+    image_emb, keep, give = call(
+        arrive, [((images, width), BF), ((texts, width), BF), ((texts, width), BF)],
+        "arrive", [place], [arrived, owners, captions, pool],
+    )
+    other_image = shifted(image_emb, "ylo", 1)
+    image_blocks = gathered_along_z(image_emb, -1)
+
     given = shifted(give, "core", 1)
-    far = shifted(jnp.concatenate([keep, given]), "yhi", 1)
-    image_emb, four = call(
-        arrive, [((images, width), BF), ((4 * texts, width), BF)], "arrive", [],
-        [arrived, hit, keep, given, far],
-    )
-    other_image = shifted(image_emb, "ylo", 1)
-    image_blocks = gathered_along_z(image_emb)
-    up, down = shifted(four, "x", 1), shifted(four, "x", -1)
-    far_up, far_down = shifted(up[: 2 * texts], "x", 1), shifted(down[2 * texts :], "x", -1)
+    far_keep = shifted(keep, "yhi", 1)
+    far_given = lax.ppermute(give, ("yhi", "core"), [(i, 3 - i) for i in range(4)])
+    home, far = call(
+        joined, [((2 * texts, width), BF)] * 2, "joined", [], [keep, given, far_keep, far_given]
+    )
+    feats = [home, far]
+    feats += [shifted(home, "x", 1), shifted(far, "x", 1)]
+    feats += [shifted(home, "x", -1), shifted(far, "x", -1)]
+    feats += [shifted(feats[2], "x", 1), shifted(feats[5], "x", -1)]
 
     scalars = [logit_scale, logit_bias]
     image_mine, image_rest = call(
@@ -310,8 +320,8 @@
     )
     image_rest = shifted(image_rest, "ylo", 1)
     (send_back,) = call(
-        image_back, [((groups, SLOTS, width), BF)], "image_back", scalars[:1],
-        [image_mine, image_rest, hit_t],
+        image_back, [((groups, SLOTS, width), BF)], "image_back",
+        [place, logit_scale], [image_mine, image_rest, owners],
     )
     received = lax.all_to_all(send_back, REP_AXES, 0, 0, tiled=True)
 
@@ -338,7 +348,7 @@
 
     (terms,) = call(
         head_terms, [((128, 16, 128), BF)], "head_terms", [place],
-        [strips, four, up, down, far_up, far_down],
+        [strips, *feats],
     )
     terms = lax.all_to_all(terms.reshape(256, 8, 128), CAP_AXES + REP_AXES, 0, 0, tiled=True)
     (head_share,) = call(

time: 180 us -> 177 us (0.983)
  blocking collectives: 21.1 us -> 0 us
  local copies, waits for them, and re-layouts: 21.7 us -> 0.75 us
  starting transfers between devices: 63.3 us -> 79.2 us
  Pallas kernels: 27.2 us -> 41.8 us
  waiting for transfers between devices: 39.3 us -> 46.8 us
  matrix products: 3.25 us -> 5.11 us
    all_to_all x1 -> x0, blocking collectives: 21.1 us -> none  [per_device(): lax.all_to_all(strips.reshape(groups, strip, texts), REP_AXES, 0, 0, tile...]
    unnamed x92 -> x6, local copies, waits for them, and re-layouts: 17.2 us -> 0.75 us
    pallas_call x10 -> x11, Pallas kernels: 27.2 us -> 41.8 us  [call(): pl.pallas_call(kernel, out_shape=shapes, in_specs=[SMEM] * len(scalars) +...]
    all_to_all x0 -> x1, waiting for transfers between devices: none -> 10.9 us  [per_device(): lax.all_to_all(strips.reshape(groups, strip, texts), REP_AXES, 0, 0, tile...]
    all_to_all x0 -> x1, starting transfers between devices: none -> 8.54 us  [per_device(): lax.all_to_all(strips.reshape(groups, strip, texts), REP_AXES, 0, 0, tile...]
    ppermute x26, starting transfers between devices: 36.3 us -> 42 us  [shifted(): lax.ppermute(block, axis, [(i, (i + distance) % size) for i in range(size)])]
    slice x6 -> x0, local copies, waits for them, and re-layouts: 4.48 us -> none  [the longest x4 2.56 us: gathered_along_z(): return found + [shifted(up[:half], 'z', 1), shifted(down[half:], 'z', -1)]]
    ppermute x0 -> x1, starting transfers between devices: none -> 4.13 us  [per_device(): lax.ppermute(give, ('yhi', 'core'), [(i, 3 - i) for i in range(4)])]
  transfers between devices with their start and end apart: 29 -> 31, of which waited for: 10 -> 10; matrix products, arithmetic and copies ran while one was open for 5% -> 3% of each run, Pallas kernels for 10% -> 14%
where the time goes in v4:
time: 177 us
  starting transfers between devices  79.2 us (45%)
  waiting for transfers between devices  46.8 us (26%)
  Pallas kernels  41.8 us (24%)
  matrix products  5.11 us (3%)
  between operations  2.29 us (1%)
    ppermute x26, starting transfers between devices, shifted(): lax.ppermute(block, axis, [(i, (i + distance) % size) for i in range(size)])  42 us
    pallas_call x11, Pallas kernels, call(): pl.pallas_call(kernel, out_shape=shapes, in_specs=[SMEM] * len(scalars) +...  41.8 us
    ppermute x26, waiting for transfers between devices, shifted(): lax.ppermute(block, axis, [(i, (i + distance) % size) for i in range(size)])  20.7 us
    all_to_all x1, waiting for transfers between devices, per_device(): lax.all_to_all(terms.reshape(256, 8, 128), CAP_AXES + REP_AXES, 0, 0, til...  14.8 us
    all_to_all x1, waiting for transfers between devices, per_device(): lax.all_to_all(strips.reshape(groups, strip, texts), REP_AXES, 0, 0, tile...  10.9 us
    all_to_all x1, starting transfers between devices, per_device(): lax.all_to_all(terms.reshape(256, 8, 128), CAP_AXES + REP_AXES, 0, 0, til...  9.81 us
    all_to_all x1, starting transfers between devices, per_device(): lax.all_to_all(strips.reshape(groups, strip, texts), REP_AXES, 0, 0, tile...  8.54 us
    all_to_all x1, starting transfers between devices, per_device(): arrived = lax.all_to_all(outgoing, REP_AXES, 0, 0, tiled=True)  7.9 us
  transfers between devices with their start and end apart: 31, of which 10 were waited for; matrix products, arithmetic and copies ran while one was open for 3% of the time, Pallas kernels for 14%

profile of v4, /device:TPU:1, one launch (start us, length us, event | category | flops | bytes accessed | tf_op | source)
XLA Modules:
  0.0 176.6 jit_solution(14117394615566373243)
XLA Ops:
  1.3 4.5 %pool_front.1 = (f32[128,1152]{1,0:T(8,128)}, f32[128,1]{1,0:T(8,128)}, bf16[16,16,1152]{2,1,0:T(8,128)(2,1)}, bf16[256,128]{1,0:T(8,128)(2,1)}) custom-call(s32[4]{0:T(128)} %pad_add_fusion.refs_0_, bf16[128,1152]{1,0:T(8,128)(2,1)} %bitcast.21, bf16[1152,1152]{1,0:T(8,128)(2,1)} %refs_2_.1, s32[16,96]{1,0:T(8,128)} %bitcast.24, s32[16,96]{1,0:T(8,128)} %refs_4_.3), custom_call_target="tpu_custom_call" | custom-call | tf_op jit(solution)/shard_map/pool_front/pallas_call | solution.py:59
  5.9 3.6 %text_front.1 = (f32[128,1152]{1,0:T(8,128)}, f32[128,1]{1,0:T(8,128)}, bf16[128,1152]{1,0:T(8,128)(2,1)}) custom-call(bf16[128,1152]{1,0:T(8,128)(2,1)} %bitcast.19, bf16[1152,1152]{1,0:T(8,128)(2,1)} %refs_1_.4, f32[128,1]{1,0:T(8,128)} %get-tuple-element.21.refs_2_.refs_3_), custom_call_target="tpu_custom_call" | custom-call | tf_op jit(solution)/shard_map/text_front/pallas_call | solution.py:59
  9.4 2.5 %collective-permute-start.10 = (bf16[128,1152]{1,0:T(8,128)(2,1)}, bf16[128,1152]{1,0:T(8,128)(2,1)S(1)}, u32[]{:S(2)}, u32[]{:S(2)}) collective-permute-start(bf16[128,1152]{1,0:T(8,128)(2,1)} %get-tuple-element.22.refs_2_.refs_5_.refs_6_), channel_id=1, source_target_pairs={{0,16},{16,32},{32,48},{48,64},{64,80},{80,96},{96,112},{112,0},{1... | collective-permute-start | bytes 884744 | tf_op jit(solution)/shard_map/ppermute | solution.py:22
  12.0 7.9 %all-to-all-start = ((bf16[16,16,1152]{2,1,0:T(8,128)(2,1)}), bf16[16,16,1152]{2,1,0:T(8,128)(2,1)}, u32[]{:S(2)}, u32[]{:S(2)}) async-start(bf16[16,16,1152]{2,1,0:T(8,128)(2,1)} %get-tuple-element.23), calls=%async_computation | async-start | bytes 1179648 | tf_op jit(solution)/shard_map/all_to_all | solution.py:289
  19.9 3.7 %collective-permute-start.11 = (bf16[128,1152]{1,0:T(8,128)(2,1)}, bf16[128,1152]{1,0:T(8,128)(2,1)}, u32[]{:S(2)}, u32[]{:S(2)}) collective-permute-start(bf16[128,1152]{1,0:T(8,128)(2,1)} %get-tuple-element.22.refs_2_.refs_5_.refs_6_), channel_id=1, source_target_pairs={{0,112},{16,0},{32,16},{48,32},{64,48},{80,64},{96,80},{112,96},{1... | collective-permute-start | bytes 884744 | tf_op jit(solution)/shard_map/ppermute | solution.py:22
  24.3 5.8 %collective-permute-done.11.refs_8_ = bf16[128,1152]{1,0:T(8,128)(2,1)} collective-permute-done((bf16[128,1152]{1,0:T(8,128)(2,1)}, bf16[128,1152]{1,0:T(8,128)(2,1)}, u32[]{:S(2)}, u32[]{:S(2)}) %collective-permute-start.11) | collective-permute-done | bytes 294944 | tf_op jit(solution)/shard_map/ppermute | solution.py:22
  30.1 3.4 %collective-permute-start.13 = (bf16[128,1152]{1,0:T(8,128)(2,1)}, bf16[128,1152]{1,0:T(8,128)(2,1)}, u32[]{:S(2)}, u32[]{:S(2)}) collective-permute-start(bf16[128,1152]{1,0:T(8,128)(2,1)} %collective-permute-done.11.refs_8_), channel_id=1, source_target_pairs={{0,112},{16,0},{32,16},{48,32},{64,48},{80,64},{96,80},{112,96},{1... | collective-permute-start | bytes 884744 | tf_op jit(solution)/shard_map/ppermute | solution.py:22
  33.7 3.3 %arrive.1 = (bf16[96,1152]{1,0:T(8,128)(2,1)}, bf16[128,1152]{1,0:T(8,128)(2,1)}, bf16[128,1152]{1,0:T(8,128)(2,1)}) custom-call(s32[4]{0:T(128)} %pad_add_fusion.refs_0_, bf16[16,16,1152]{2,1,0:T(8,128)(2,1)} %all-to-all-done.refs_1_, s32[16,96]{1,0:T(8,128)} %bitcast.25, bf16[128,1152]{1,0:T(8,128)(2,1)} %bitcast.20, bf16[128,1152]{1,0:T(8,128)(2,1)} %bitcast.22), custom_call_target="tpu_custom_call" | custom-call | tf_op jit(solution)/shard_map/arrive/pallas_call | solution.py:59
  37.0 2.7 %collective-permute-start.1 = (bf16[96,1152]{1,0:T(8,128)(2,1)}, bf16[96,1152]{1,0:T(8,128)(2,1)}, u32[]{:S(2)}, u32[]{:S(2)}) collective-permute-start(bf16[96,1152]{1,0:T(8,128)(2,1)} %get-tuple-element.24.refs_5_.refs_6_.refs_2_), channel_id=1, source_target_pairs={{0,112},{16,0},{32,16},{48,32},{64,48},{80,64},{96,80},{112,96},{1... | collective-permute-start | bytes 663560 | tf_op jit(solution)/shard_map/ppermute | solution.py:22
  39.7 2.8 %collective-permute-start.15 = (bf16[128,1152]{1,0:T(8,128)(2,1)}, bf16[128,1152]{1,0:T(8,128)(2,1)}, u32[]{:S(2)}, u32[]{:S(2)}) collective-permute-start(bf16[128,1152]{1,0:T(8,128)(2,1)} %collective-permute-done.13.refs_10_), channel_id=1, source_target_pairs={{0,112},{16,0},{32,16},{48,32},{64,48},{80,64},{96,80},{112,96},{1... | collective-permute-start | bytes 884744 | tf_op jit(solution)/shard_map/ppermute | solution.py:22
  43.3 4.5 %collective-permute-start.18 = (bf16[128,1152]{1,0:T(8,128)(2,1)}, bf16[128,1152]{1,0:T(8,128)(2,1)}, u32[]{:S(2)}, u32[]{:S(2)}) collective-permute-start(bf16[128,1152]{1,0:T(8,128)(2,1)} %get-tuple-element.36), channel_id=1, source_target_pairs={{0,1},{1,0},{2,3},{3,2},{4,5},{5,4},{6,7},{7,6},{8,9},{9,8},{10,11... | collective-permute-start | bytes 884744 | tf_op jit(solution)/shard_map/ppermute | solution.py:22
  47.9 3.4 %collective-permute-start.3 = (bf16[96,1152]{1,0:T(8,128)(2,1)}, bf16[96,1152]{1,0:T(8,128)(2,1)}, u32[]{:S(2)}, u32[]{:S(2)}) collective-permute-start(bf16[96,1152]{1,0:T(8,128)(2,1)} %collective-permute-done.1.refs_7_), channel_id=1, source_target_pairs={{0,112},{16,0},{32,16},{48,32},{64,48},{80,64},{96,80},{112,96},{1... | collective-permute-start | bytes 663560 | tf_op jit(solution)/shard_map/ppermute | solution.py:22
  51.2 2.9 %collective-permute-start.19 = (bf16[128,1152]{1,0:T(8,128)(2,1)}, bf16[128,1152]{1,0:T(8,128)(2,1)}, u32[]{:S(2)}, u32[]{:S(2)}) collective-permute-start(bf16[128,1152]{1,0:T(8,128)(2,1)} %get-tuple-element.35.refs_0_), channel_id=1, source_target_pairs={{0,2},{2,0},{1,3},{3,1},{4,6},{6,4},{5,7},{7,5},{8,10},{10,8},{9,1... | collective-permute-start | bytes 884744 | tf_op jit(solution)/shard_map/ppermute | solution.py:22
  54.1 4.1 %collective-permute-start.20 = (bf16[128,1152]{1,0:T(8,128)(2,1)}, bf16[128,1152]{1,0:T(8,128)(2,1)}, u32[]{:S(2)}, u32[]{:S(2)}) collective-permute-start(bf16[128,1152]{1,0:T(8,128)(2,1)} %get-tuple-element.36), channel_id=1, source_target_pairs={{0,3},{1,2},{2,1},{3,0},{4,7},{5,6},{6,5},{7,4},{8,11},{9,10},{10,... | collective-permute-start | bytes 884744 | tf_op jit(solution)/shard_map/ppermute | solution.py:306
  59.6 5.2 %image_sums.1 = (f32[96,1152]{1,0:T(8,128)}, bf16[96,1152]{1,0:T(8,128)(2,1)}) custom-call(f32[1]{0:T(128)S(6)} %copy.12.refs_0_.refs_1_, f32[1]{0:T(128)S(6)} %copy.13.refs_1_, bf16[96,1152]{1,0:T(8,128)(2,1)} %get-tuple-element.24.refs_5_.refs_6_.refs_2_, bf16[96,1152]{1,0:T(8,128)(2,1)} %collective-permute-done.9.refs_3_, s32[1,128]{1,0:T(1,128)} %refs_4_.5, ...), custom_call_target="tpu_custom_call" | custom-call | tf_op jit(solution)/shard_map/image_sums/pallas_call | solution.py:59
  65.3 2.7 %collective-permute-start.5 = (bf16[96,1152]{1,0:T(8,128)(2,1)}, bf16[96,1152]{1,0:T(8,128)(2,1)}, u32[]{:S(2)}, u32[]{:S(2)}) collective-permute-start(bf16[96,1152]{1,0:T(8,128)(2,1)} %collective-permute-done.3.refs_9_), channel_id=1, source_target_pairs={{0,112},{16,0},{32,16},{48,32},{64,48},{80,64},{96,80},{112,96},{1... | collective-permute-start | bytes 663560 | tf_op jit(solution)/shard_map/ppermute | solution.py:22
  68.4 2.3 %joined.1 = (bf16[256,1152]{1,0:T(8,128)(2,1)}, bf16[256,1152]{1,0:T(8,128)(2,1)}) custom-call(bf16[128,1152]{1,0:T(8,128)(2,1)} %get-tuple-element.35.refs_0_, bf16[128,1152]{1,0:T(8,128)(2,1)} %collective-permute-done.18.refs_1_, bf16[128,1152]{1,0:T(8,128)(2,1)} %collective-permute-done.19.refs_2_, bf16[128,1152]{1,0:T(8,128)(2,1)} %collective-permute-done.20.refs_3_), custom_call_target="tpu_custom_call" | custom-call | tf_op jit(solution)/shard_map/joined/pallas_call | solution.py:59
  74.2 3.0 %image_back.1 = bf16[16,16,1152]{2,1,0:T(8,128)(2,1)} custom-call(s32[4]{0:T(128)} %pad_add_fusion.refs_0_, f32[1]{0:T(128)S(6)} %copy.12.refs_0_.refs_1_, f32[96,1152]{1,0:T(8,128)} %get-tuple-element.29.refs_2_, bf16[96,1152]{1,0:T(8,128)(2,1)} %collective-permute-done.17.refs_3_, s32[16,96]{1,0:T(8,128)} %bitcast.26), custom_call_target="tpu_custom_call" | custom-call | tf_op jit(solution)/shard_map/image_back/pallas_call | solution.py:59
  77.2 6.8 %all-to-all-start.1 = ((bf16[16,16,1152]{2,1,0:T(8,128)(2,1)}), bf16[16,16,1152]{2,1,0:T(8,128)(2,1)}, u32[]{:S(2)}, u32[]{:S(2)}) async-start(bf16[16,16,1152]{2,1,0:T(8,128)(2,1)} %image_back.1), calls=%async_computation.1 | async-start | bytes 1179648 | tf_op jit(solution)/shard_map/all_to_all | solution.py:326
  86.8 5.7 %collective-permute-done.6.refs_12_ = bf16[96,1152]{1,0:T(8,128)(2,1)} collective-permute-done((bf16[96,1152]{1,0:T(8,128)(2,1)}, bf16[96,1152]{1,0:T(8,128)(2,1)}, u32[]{:S(2)}, u32[]{:S(2)}) %collective-permute-start.6) | collective-permute-done | bytes 221216 | tf_op jit(solution)/shard_map/ppermute | solution.py:22
  92.5 5.5 %text_sums.1 = (f32[128,1152]{1,0:T(8,128)}, bf16[128,1152]{1,0:T(8,128)(2,1)}) custom-call(f32[1]{0:T(128)S(6)} %copy.12.refs_0_.refs_1_, f32[1]{0:T(128)S(6)} %copy.13.refs_1_, bf16[128,1152]{1,0:T(8,128)(2,1)} %get-tuple-element.22.refs_2_.refs_5_.refs_6_, bf16[128,1152]{1,0:T(8,128)(2,1)} %collective-permute-done.refs_3_, s32[1,128]{1,0:T(1,128)} %refs_4_.5, ...), custom_call_target="tpu_custom_call" | custom-call | tf_op jit(solution)/shard_map/text_sums/pallas_call | solution.py:59
  101.6 2.7 %collective-permute-start.26 = (bf16[256,1152]{1,0:T(8,128)(2,1)}, bf16[256,1152]{1,0:T(8,128)(2,1)}, u32[]{:S(2)}, u32[]{:S(2)}) collective-permute-start(bf16[256,1152]{1,0:T(8,128)(2,1)} %collective-permute-done.24.refs_7_), channel_id=1, source_target_pairs={{0,12},{4,0},{8,4},{12,8},{1,13},{5,1},{9,5},{13,9},{2,14},{6,2},{... | collective-permute-start | bytes 1769480 | tf_op jit(solution)/shard_map/ppermute | solution.py:22
  105.9 2.3 %text_back.1.refs_4_ = bf16[128,1152]{1,0:T(8,128)(2,1)} custom-call(f32[1]{0:T(128)S(6)} %copy.12.refs_0_.refs_1_, f32[128,1152]{1,0:T(8,128)} %get-tuple-element.25.refs_1_, bf16[128,1152]{1,0:T(8,128)(2,1)} %collective-permute-done.8.refs_2_, f32[128,1152]{1,0:T(8,128)} %get-tuple-element.27.refs_3_, f32[128,1]{1,0:T(8,128)} %get-tuple-element.28.refs_4_), custom_call_target="tpu_custom_call" | custom-call | tf_op jit(solution)/shard_map/text_back/pallas_call | solution.py:59
  108.3 2.8 %pool_back.1 = (bf16[128,1152]{1,0:T(8,128)(2,1)}, bf16[8,2,144,128]{3,2,1,0:T(8,128)(2,1)}) custom-call(bf16[16,16,1152]{2,1,0:T(8,128)(2,1)} %all-to-all-done.1.refs_0_, bf16[256,128]{1,0:T(8,128)(2,1)} %get-tuple-element.31.refs_1_, f32[128,1152]{1,0:T(8,128)} %get-tuple-element.32.refs_2_, f32[128,1]{1,0:T(8,128)} %get-tuple-element.21.refs_2_.refs_3_, ...), custom_call_target="tpu_custom_call" | custom-call | tf_op jit(solution)/shard_map/pool_back/pallas_call | solution.py:59
  111.1 8.5 %all-to-all-start.2 = ((bf16[16,144,128]{2,1,0:T(8,128)(2,1)}), bf16[16,144,128]{2,1,0:T(8,128)(2,1)}, u32[]{:S(2)}, u32[]{:S(2)}) async-start(bf16[16,144,128]{2,1,0:T(8,128)(2,1)} %bitcast.23), calls=%async_computation.2 | async-start | bytes 1179648 | tf_op jit(solution)/shard_map/all_to_all | solution.py:345
  119.7 7.0 %collective-permute-done.25.refs_8_ = bf16[256,1152]{1,0:T(8,128)(2,1)} collective-permute-done((bf16[256,1152]{1,0:T(8,128)(2,1)}, bf16[256,1152]{1,0:T(8,128)(2,1)}, u32[]{:S(2)}, u32[]{:S(2)}) %collective-permute-start.25) | collective-permute-done | bytes 589856 | tf_op jit(solution)/shard_map/ppermute | solution.py:22
  126.7 10.9 %all-to-all-done.2.refs_1_ = bf16[16,144,128]{2,1,0:T(8,128)(2,1)} async-done(((bf16[16,144,128]{2,1,0:T(8,128)(2,1)}), bf16[16,144,128]{2,1,0:T(8,128)(2,1)}, u32[]{:S(2)}, u32[]{:S(2)}) %all-to-all-start.2) | async-done | bytes 589856 | tf_op jit(solution)/shard_map/all_to_all | solution.py:345
  137.6 6.0 %head_terms.1 = bf16[128,16,128]{2,1,0:T(8,128)(2,1)} custom-call(s32[4]{0:T(128)} %pad_add_fusion.refs_0_, bf16[16,144,128]{2,1,0:T(8,128)(2,1)} %all-to-all-done.2.refs_1_, bf16[256,1152]{1,0:T(8,128)(2,1)} %get-tuple-element.37.refs_2_, bf16[256,1152]{1,0:T(8,128)(2,1)} %get-tuple-element.38.refs_3_, bf16[256,1152]{1,0:T(8,128)(2,1)} %collective-permute-done.21.refs_4_, ...), custom_call_target="tpu_custom_call" | custom-call | tf_op jit(solution)/shard_map/head_terms/pallas_call | solution.py:59
  143.6 9.8 %all-to-all-start.3 = ((bf16[256,8,128]{2,1,0:T(8,128)(2,1)}), bf16[256,8,128]{2,1,0:T(8,128)(2,1)}, u32[]{:S(2)}, u32[]{:S(2)}) async-start(bf16[256,8,128]{2,1,0:T(8,128)(2,1)} %bitcast.18), calls=%async_computation.3 | async-start | bytes 1048576 | tf_op jit(solution)/shard_map/all_to_all | solution.py:353
  153.4 3.5 %fusion = bf16[1,128,1152]{2,1,0:T(8,128)(2,1)} fusion(bf16[128,1152]{1,0:T(8,128)(2,1)} %text_back.1.refs_4_, bf16[1152,1152]{1,0:T(8,128)(2,1)} %refs_1_.4), kind=kOutput, calls=%fused_computation.2 | convolution fusion | flops 339886080 | bytes 3244032 | tf_op jit(solution)/shard_map/dot_general | solution.py:72
  158.5 14.8 %all-to-all-done.3 = bf16[256,8,128]{2,1,0:T(8,128)(2,1)} async-done(((bf16[256,8,128]{2,1,0:T(8,128)(2,1)}), bf16[256,8,128]{2,1,0:T(8,128)(2,1)}, u32[]{:S(2)}, u32[]{:S(2)}) %all-to-all-start.3) | async-done | bytes 524320 | tf_op jit(solution)/shard_map/all_to_all | solution.py:353
  173.3 3.1 %head_sums.1 = f32[9,1152]{1,0:T(8,128)} custom-call(s32[4]{0:T(128)} %pad_add_fusion.refs_0_, bf16[128,16,128]{2,1,0:T(8,128)(2,1)} %bitcast.11.refs_1_), custom_call_target="tpu_custom_call" | custom-call | tf_op jit(solution)/shard_map/head_sums/pallas_call | solution.py:59
  (50 shorter events, 16.6 us)
Async XLA Ops:
  9.4 14.1 %collective-permute-start.10 = (bf16[128,1152]{1,0:T(8,128)(2,1)}, bf16[128,1152]{1,0:T(8,128)(2,1)S(1)}, u32[]{:S(2)}, u32[]{:S(2)}) collective-permute-start(bf16[128,1152]{1,0:T(8,128)(2,1)} %get-tuple-element.22.refs_2_.refs_5_.refs_6_), channel_id=1, source_target_pairs={{0,16},{16,32},{32,48},{48,64},{64,80},{80,96},{96,112},{112,0},{1... | collective-permute-start | bytes 884744 | tf_op jit(solution)/shard_map/ppermute | solution.py:22
  12.0 21.7 %all-to-all-start = ((bf16[16,16,1152]{2,1,0:T(8,128)(2,1)}), bf16[16,16,1152]{2,1,0:T(8,128)(2,1)}, u32[]{:S(2)}, u32[]{:S(2)}) async-start(bf16[16,16,1152]{2,1,0:T(8,128)(2,1)} %get-tuple-element.23), calls=%async_computation | async-start | bytes 1179648 | tf_op jit(solution)/shard_map/all_to_all | solution.py:289
  19.9 10.2 %collective-permute-start.11 = (bf16[128,1152]{1,0:T(8,128)(2,1)}, bf16[128,1152]{1,0:T(8,128)(2,1)}, u32[]{:S(2)}, u32[]{:S(2)}) collective-permute-start(bf16[128,1152]{1,0:T(8,128)(2,1)} %get-tuple-element.22.refs_2_.refs_5_.refs_6_), channel_id=1, source_target_pairs={{0,112},{16,0},{32,16},{48,32},{64,48},{80,64},{96,80},{112,96},{1... | collective-permute-start | bytes 884744 | tf_op jit(solution)/shard_map/ppermute | solution.py:22
  24.3 9.4 %collective-permute-start.12 = (bf16[128,1152]{1,0:T(8,128)(2,1)S(1)}, bf16[128,1152]{1,0:T(8,128)(2,1)}, u32[]{:S(2)}, u32[]{:S(2)}) collective-permute-start(bf16[128,1152]{1,0:T(8,128)(2,1)S(1)} %collective-permute-done.10.refs_7_), channel_id=1, source_target_pairs={{0,16},{16,32},{32,48},{48,64},{64,80},{80,96},{96,112},{112,0},{1... | collective-permute-start | bytes 884744 | tf_op jit(solution)/shard_map/ppermute | solution.py:22
  30.1 9.6 %collective-permute-start.13 = (bf16[128,1152]{1,0:T(8,128)(2,1)}, bf16[128,1152]{1,0:T(8,128)(2,1)}, u32[]{:S(2)}, u32[]{:S(2)}) collective-permute-start(bf16[128,1152]{1,0:T(8,128)(2,1)} %collective-permute-done.11.refs_8_), channel_id=1, source_target_pairs={{0,112},{16,0},{32,16},{48,32},{64,48},{80,64},{96,80},{112,96},{1... | collective-permute-start | bytes 884744 | tf_op jit(solution)/shard_map/ppermute | solution.py:22
  33.7 8.8 %collective-permute-start.14 = (bf16[128,1152]{1,0:T(8,128)(2,1)}, bf16[128,1152]{1,0:T(8,128)(2,1)}, u32[]{:S(2)}, u32[]{:S(2)}) collective-permute-start(bf16[128,1152]{1,0:T(8,128)(2,1)} %collective-permute-done.12.refs_9_), channel_id=1, source_target_pairs={{0,16},{16,32},{32,48},{48,64},{64,80},{80,96},{96,112},{112,0},{1... | collective-permute-start | bytes 884744 | tf_op jit(solution)/shard_map/ppermute | solution.py:22
  37.0 6.3 %collective-permute-start.1 = (bf16[96,1152]{1,0:T(8,128)(2,1)}, bf16[96,1152]{1,0:T(8,128)(2,1)}, u32[]{:S(2)}, u32[]{:S(2)}) collective-permute-start(bf16[96,1152]{1,0:T(8,128)(2,1)} %get-tuple-element.24.refs_5_.refs_6_.refs_2_), channel_id=1, source_target_pairs={{0,112},{16,0},{32,16},{48,32},{64,48},{80,64},{96,80},{112,96},{1... | collective-permute-start | bytes 663560 | tf_op jit(solution)/shard_map/ppermute | solution.py:22
  39.7 11.5 %collective-permute-start.15 = (bf16[128,1152]{1,0:T(8,128)(2,1)}, bf16[128,1152]{1,0:T(8,128)(2,1)}, u32[]{:S(2)}, u32[]{:S(2)}) collective-permute-start(bf16[128,1152]{1,0:T(8,128)(2,1)} %collective-permute-done.13.refs_10_), channel_id=1, source_target_pairs={{0,112},{16,0},{32,16},{48,32},{64,48},{80,64},{96,80},{112,96},{1... | collective-permute-start | bytes 884744 | tf_op jit(solution)/shard_map/ppermute | solution.py:22
  42.5 11.6 %collective-permute-start.16 = (bf16[128,1152]{1,0:T(8,128)(2,1)}, bf16[128,1152]{1,0:T(8,128)(2,1)}, u32[]{:S(2)}, u32[]{:S(2)}) collective-permute-start(bf16[128,1152]{1,0:T(8,128)(2,1)} %collective-permute-done.14.refs_11_), channel_id=1, source_target_pairs={{0,16},{16,32},{32,48},{48,64},{64,80},{80,96},{96,112},{112,0},{1... | collective-permute-start | bytes 884744 | tf_op jit(solution)/shard_map/ppermute | solution.py:22
  42.5 5.4 %collective-permute-start.9 = (bf16[96,1152]{1,0:T(8,128)(2,1)}, bf16[96,1152]{1,0:T(8,128)(2,1)}, u32[]{:S(2)}, u32[]{:S(2)}) collective-permute-start(bf16[96,1152]{1,0:T(8,128)(2,1)} %get-tuple-element.24.refs_5_.refs_6_.refs_2_), channel_id=1, source_target_pairs={{0,128},{128,0},{1,129},{129,1},{2,130},{130,2},{3,131},{131,3},{4... | collective-permute-start | bytes 663560 | tf_op jit(solution)/shard_map/ppermute | solution.py:22
  42.9 21.9 %collective-permute-start.2 = (bf16[96,1152]{1,0:T(8,128)(2,1)}, bf16[96,1152]{1,0:T(8,128)(2,1)}, u32[]{:S(2)}, u32[]{:S(2)}) collective-permute-start(bf16[96,1152]{1,0:T(8,128)(2,1)} %get-tuple-element.24.refs_5_.refs_6_.refs_2_), channel_id=1, source_target_pairs={{0,16},{16,32},{32,48},{48,64},{64,80},{80,96},{96,112},{112,0},{1... | collective-permute-start | bytes 663560 | tf_op jit(solution)/shard_map/ppermute | solution.py:22
  43.3 22.0 %collective-permute-start.18 = (bf16[128,1152]{1,0:T(8,128)(2,1)}, bf16[128,1152]{1,0:T(8,128)(2,1)}, u32[]{:S(2)}, u32[]{:S(2)}) collective-permute-start(bf16[128,1152]{1,0:T(8,128)(2,1)} %get-tuple-element.36), channel_id=1, source_target_pairs={{0,1},{1,0},{2,3},{3,2},{4,5},{5,4},{6,7},{7,6},{8,9},{9,8},{10,11... | collective-permute-start | bytes 884744 | tf_op jit(solution)/shard_map/ppermute | solution.py:22
  47.9 17.4 %collective-permute-start.3 = (bf16[96,1152]{1,0:T(8,128)(2,1)}, bf16[96,1152]{1,0:T(8,128)(2,1)}, u32[]{:S(2)}, u32[]{:S(2)}) collective-permute-start(bf16[96,1152]{1,0:T(8,128)(2,1)} %collective-permute-done.1.refs_7_), channel_id=1, source_target_pairs={{0,112},{16,0},{32,16},{48,32},{64,48},{80,64},{96,80},{112,96},{1... | collective-permute-start | bytes 663560 | tf_op jit(solution)/shard_map/ppermute | solution.py:22
  51.2 16.7 %collective-permute-start.19 = (bf16[128,1152]{1,0:T(8,128)(2,1)}, bf16[128,1152]{1,0:T(8,128)(2,1)}, u32[]{:S(2)}, u32[]{:S(2)}) collective-permute-start(bf16[128,1152]{1,0:T(8,128)(2,1)} %get-tuple-element.35.refs_0_), channel_id=1, source_target_pairs={{0,2},{2,0},{1,3},{3,1},{4,6},{6,4},{5,7},{7,5},{8,10},{10,8},{9,1... | collective-permute-start | bytes 884744 | tf_op jit(solution)/shard_map/ppermute | solution.py:22
  54.1 14.3 %collective-permute-start.20 = (bf16[128,1152]{1,0:T(8,128)(2,1)}, bf16[128,1152]{1,0:T(8,128)(2,1)}, u32[]{:S(2)}, u32[]{:S(2)}) collective-permute-start(bf16[128,1152]{1,0:T(8,128)(2,1)} %get-tuple-element.36), channel_id=1, source_target_pairs={{0,3},{1,2},{2,1},{3,0},{4,7},{5,6},{6,5},{7,4},{8,11},{9,10},{10,... | collective-permute-start | bytes 884744 | tf_op jit(solution)/shard_map/ppermute | solution.py:306
  64.8 8.7 %collective-permute-start.17 = (bf16[96,1152]{1,0:T(8,128)(2,1)}, bf16[96,1152]{1,0:T(8,128)(2,1)}, u32[]{:S(2)}, u32[]{:S(2)}) collective-permute-start(bf16[96,1152]{1,0:T(8,128)(2,1)} %get-tuple-element.30), channel_id=1, source_target_pairs={{0,128},{128,0},{1,129},{129,1},{2,130},{130,2},{3,131},{131,3},{4... | collective-permute-start | bytes 663560 | tf_op jit(solution)/shard_map/ppermute | solution.py:22
  65.3 18.7 %collective-permute-start.4 = (bf16[96,1152]{1,0:T(8,128)(2,1)}, bf16[96,1152]{1,0:T(8,128)(2,1)}, u32[]{:S(2)}, u32[]{:S(2)}) collective-permute-start(bf16[96,1152]{1,0:T(8,128)(2,1)} %collective-permute-done.2.refs_8_), channel_id=1, source_target_pairs={{0,16},{16,32},{32,48},{48,64},{64,80},{80,96},{96,112},{112,0},{1... | collective-permute-start | bytes 663560 | tf_op jit(solution)/shard_map/ppermute | solution.py:22
  65.3 19.8 %collective-permute-start.5 = (bf16[96,1152]{1,0:T(8,128)(2,1)}, bf16[96,1152]{1,0:T(8,128)(2,1)}, u32[]{:S(2)}, u32[]{:S(2)}) collective-permute-start(bf16[96,1152]{1,0:T(8,128)(2,1)} %collective-permute-done.3.refs_9_), channel_id=1, source_target_pairs={{0,112},{16,0},{32,16},{48,32},{64,48},{80,64},{96,80},{112,96},{1... | collective-permute-start | bytes 663560 | tf_op jit(solution)/shard_map/ppermute | solution.py:22
  70.8 30.8 %collective-permute-start.21 = (bf16[256,1152]{1,0:T(8,128)(2,1)}, bf16[256,1152]{1,0:T(8,128)(2,1)}, u32[]{:S(2)}, u32[]{:S(2)}) collective-permute-start(bf16[256,1152]{1,0:T(8,128)(2,1)} %get-tuple-element.37.refs_2_), channel_id=1, source_target_pairs={{0,4},{4,8},{8,12},{12,0},{1,5},{5,9},{9,13},{13,1},{2,6},{6,10},{... | collective-permute-start | bytes 1769480 | tf_op jit(solution)/shard_map/ppermute | solution.py:22
  72.1 29.5 %collective-permute-start.24 = (bf16[256,1152]{1,0:T(8,128)(2,1)}, bf16[256,1152]{1,0:T(8,128)(2,1)}, u32[]{:S(2)}, u32[]{:S(2)}) collective-permute-start(bf16[256,1152]{1,0:T(8,128)(2,1)} %get-tuple-element.38.refs_3_), channel_id=1, source_target_pairs={{0,12},{4,0},{8,4},{12,8},{1,13},{5,1},{9,5},{13,9},{2,14},{6,2},{... | collective-permute-start | bytes 1769480 | tf_op jit(solution)/shard_map/ppermute | solution.py:22
  73.5 13.3 %collective-permute-start = (bf16[128,1152]{1,0:T(8,128)(2,1)}, bf16[128,1152]{1,0:T(8,128)(2,1)}, u32[]{:S(2)}, u32[]{:S(2)}) collective-permute-start(bf16[128,1152]{1,0:T(8,128)(2,1)} %get-tuple-element.22.refs_2_.refs_5_.refs_6_), channel_id=1, source_target_pairs={{0,128},{128,0},{1,129},{129,1},{2,130},{130,2},{3,131},{131,3},{4... | collective-permute-start | bytes 884744 | tf_op jit(solution)/shard_map/ppermute | solution.py:22
  77.2 31.1 %all-to-all-start.1 = ((bf16[16,16,1152]{2,1,0:T(8,128)(2,1)}), bf16[16,16,1152]{2,1,0:T(8,128)(2,1)}, u32[]{:S(2)}, u32[]{:S(2)}) async-start(bf16[16,16,1152]{2,1,0:T(8,128)(2,1)} %image_back.1), calls=%async_computation.1 | async-start | bytes 1179648 | tf_op jit(solution)/shard_map/all_to_all | solution.py:326
  84.0 8.5 %collective-permute-start.6 = (bf16[96,1152]{1,0:T(8,128)(2,1)}, bf16[96,1152]{1,0:T(8,128)(2,1)}, u32[]{:S(2)}, u32[]{:S(2)}) collective-permute-start(bf16[96,1152]{1,0:T(8,128)(2,1)} %collective-permute-done.4.refs_10_), channel_id=1, source_target_pairs={{0,16},{16,32},{32,48},{48,64},{64,80},{80,96},{96,112},{112,0},{1... | collective-permute-start | bytes 663560 | tf_op jit(solution)/shard_map/ppermute | solution.py:22
  85.1 7.4 %collective-permute-start.7 = (bf16[96,1152]{1,0:T(8,128)(2,1)}, bf16[96,1152]{1,0:T(8,128)(2,1)}, u32[]{:S(2)}, u32[]{:S(2)}) collective-permute-start(bf16[96,1152]{1,0:T(8,128)(2,1)} %collective-permute-done.5.refs_11_), channel_id=1, source_target_pairs={{0,112},{16,0},{32,16},{48,32},{64,48},{80,64},{96,80},{112,96},{1... | collective-permute-start | bytes 663560 | tf_op jit(solution)/shard_map/ppermute | solution.py:22
  98.0 7.9 %collective-permute-start.8 = (bf16[128,1152]{1,0:T(8,128)(2,1)}, bf16[128,1152]{1,0:T(8,128)(2,1)}, u32[]{:S(2)}, u32[]{:S(2)}) collective-permute-start(bf16[128,1152]{1,0:T(8,128)(2,1)} %get-tuple-element.26), channel_id=1, source_target_pairs={{0,128},{128,0},{1,129},{129,1},{2,130},{130,2},{3,131},{131,3},{4... | collective-permute-start | bytes 884744 | tf_op jit(solution)/shard_map/ppermute | solution.py:22
  98.9 20.8 %collective-permute-start.22 = (bf16[256,1152]{1,0:T(8,128)(2,1)}, bf16[256,1152]{1,0:T(8,128)(2,1)}, u32[]{:S(2)}, u32[]{:S(2)}) collective-permute-start(bf16[256,1152]{1,0:T(8,128)(2,1)} %get-tuple-element.38.refs_3_), channel_id=1, source_target_pairs={{0,4},{4,8},{8,12},{12,0},{1,5},{5,9},{9,13},{13,1},{2,6},{6,10},{... | collective-permute-start | bytes 1769480 | tf_op jit(solution)/shard_map/ppermute | solution.py:22
  100.1 19.6 %collective-permute-start.23 = (bf16[256,1152]{1,0:T(8,128)(2,1)}, bf16[256,1152]{1,0:T(8,128)(2,1)}, u32[]{:S(2)}, u32[]{:S(2)}) collective-permute-start(bf16[256,1152]{1,0:T(8,128)(2,1)} %get-tuple-element.37.refs_2_), channel_id=1, source_target_pairs={{0,12},{4,0},{8,4},{12,8},{1,13},{5,1},{9,5},{13,9},{2,14},{6,2},{... | collective-permute-start | bytes 1769480 | tf_op jit(solution)/shard_map/ppermute | solution.py:22
  101.6 25.1 %collective-permute-start.25 = (bf16[256,1152]{1,0:T(8,128)(2,1)}, bf16[256,1152]{1,0:T(8,128)(2,1)}, u32[]{:S(2)}, u32[]{:S(2)}) collective-permute-start(bf16[256,1152]{1,0:T(8,128)(2,1)} %collective-permute-done.21.refs_4_), channel_id=1, source_target_pairs={{0,4},{4,8},{8,12},{12,0},{1,5},{5,9},{9,13},{13,1},{2,6},{6,10},{... | collective-permute-start | bytes 1769480 | tf_op jit(solution)/shard_map/ppermute | solution.py:22
  101.6 25.1 %collective-permute-start.26 = (bf16[256,1152]{1,0:T(8,128)(2,1)}, bf16[256,1152]{1,0:T(8,128)(2,1)}, u32[]{:S(2)}, u32[]{:S(2)}) collective-permute-start(bf16[256,1152]{1,0:T(8,128)(2,1)} %collective-permute-done.24.refs_7_), channel_id=1, source_target_pairs={{0,12},{4,0},{8,4},{12,8},{1,13},{5,1},{9,5},{13,9},{2,14},{6,2},{... | collective-permute-start | bytes 1769480 | tf_op jit(solution)/shard_map/ppermute | solution.py:22
  111.1 26.4 %all-to-all-start.2 = ((bf16[16,144,128]{2,1,0:T(8,128)(2,1)}), bf16[16,144,128]{2,1,0:T(8,128)(2,1)}, u32[]{:S(2)}, u32[]{:S(2)}) async-start(bf16[16,144,128]{2,1,0:T(8,128)(2,1)} %bitcast.23), calls=%async_computation.2 | async-start | bytes 1179648 | tf_op jit(solution)/shard_map/all_to_all | solution.py:345
  143.6 13.3 %copy-start = (bf16[1152,1152]{1,0:T(8,128)(2,1)S(1)}, bf16[1152,1152]{1,0:T(8,128)(2,1)}, u32[]{:S(2)}) copy-start(bf16[1152,1152]{1,0:T(8,128)(2,1)} %refs_2_.1) | copy-start | bytes 7962628
  143.6 29.7 %all-to-all-start.3 = ((bf16[256,8,128]{2,1,0:T(8,128)(2,1)}), bf16[256,8,128]{2,1,0:T(8,128)(2,1)}, u32[]{:S(2)}, u32[]{:S(2)}) async-start(bf16[256,8,128]{2,1,0:T(8,128)(2,1)} %bitcast.18), calls=%async_computation.3 | async-start | bytes 1048576 | tf_op jit(solution)/shard_map/all_to_all | solution.py:353
  (2 other events, 14.1 us)

commit v5 on v4

--- a/solution.py
+++ b/solution.py
@@ -30,14 +30,14 @@
     return found + [shifted(ahead, "z", way)]
 
 
-def call(body, outs, name, scalars, arrays):
+def call(body, outs, name, scalars, arrays, after=()):
     shapes = [jax.ShapeDtypeStruct(shape, dtype) for shape, dtype in outs]
     count, total = len(arrays), len(arrays) + len(outs)
 
     def kernel(*refs):
         head = refs[: len(scalars)]
-        far = refs[len(scalars) : len(scalars) + total]
-        near = refs[len(scalars) + total : -1]
+        far = refs[len(scalars) :][:count] + refs[len(scalars) + count + len(after) :][: len(outs)]
+        near = refs[len(scalars) + len(after) + total : -1]
         sems = refs[-1]
         copies = [
             pltpu.make_async_copy(far[i], near[i], sems.at[i])
@@ -59,13 +59,13 @@
     return pl.pallas_call(
         kernel,
         out_shape=shapes,
-        in_specs=[SMEM] * len(scalars) + [FAR] * count,
+        in_specs=[SMEM] * len(scalars) + [FAR] * (count + len(after)),
         out_specs=[FAR] * len(outs),
         scratch_shapes=[pltpu.VMEM(s, d) for s, d in everything]
         + [pltpu.SemaphoreType.DMA((total,))],
         compiler_params=pltpu.CompilerParams(vmem_limit_bytes=64 * 2**20),
         name=name,
-    )(*scalars, *arrays)
+    )(*scalars, *arrays, *after)
 
 
 def dot(a, b, left=1, right=0):
@@ -78,12 +78,6 @@
 
 def one_hot(condition):
     return jnp.where(condition, 1.0, 0.0).astype(BF)
-
-
-def project(features, head):
-    projected = dot(features, head)
-    norm = jnp.sqrt(jnp.sum(projected * projected, axis=-1, keepdims=True) + 1e-06)
-    return projected / norm, norm
 
 
 def pull_back(unit, norm, gradient):
@@ -91,37 +85,78 @@
     return (gradient - unit * radial) / norm
 
 
-def text_front(feats_ref, head_ref, after_ref, unit_ref, norm_ref, emb_ref):
-    unit, norm = project(feats_ref[...], head_ref[...])
-    unit_ref[...] = unit
-    norm_ref[...] = norm
-    emb_ref[...] = unit.astype(BF)
-
-
-def pool_front(
-    place_ref, feats_ref, head_ref, owners_ref, slots_ref, unit_ref, norm_ref, out_ref, select_ref
+def front(
+    place_ref, owners_far, slots_far, pool_far, image_head_far, captions_far, text_head_far,
+    pool_unit_far, pool_norm_far, out_far, select_far, text_unit_far, text_norm_far, emb_far,
+    owners_ref, slots_ref, pool_ref, image_head_ref, captions_ref, text_head_ref,
+    pool_unit_ref, pool_norm_ref, out_ref, select_ref, text_unit_ref, text_norm_ref, emb_ref, sems,
 ):
-    rank = place_ref[0]
+    width = pool_ref.shape[1]
+    depth = width // 3
+    used = [0]
+
+    def moved(source, target):
+        copy = pltpu.make_async_copy(source, target, sems.at[used[0]])
+        used[0] += 1
+        copy.start()
+        return copy
+
+    def cut(far, ref):
+        rows = [pl.ds(i * depth, depth) for i in range(3)]
+        return [moved(far.at[r], ref.at[r]) for r in rows]
+
+    small = [moved(owners_far, owners_ref), moved(slots_far, slots_ref)]
+    pool_in = moved(pool_far, pool_ref)
+    image_head_in = cut(image_head_far, image_head_ref)
+    captions_in = moved(captions_far, captions_ref)
+    text_head_in = cut(text_head_far, text_head_ref)
+
+    def projected(feats_ref, head_ref, head_in):
+        total = jnp.zeros((feats_ref.shape[0], width), F32)
+        for i in range(3):
+            head_in[i].wait()
+            rows = pl.ds(i * depth, depth)
+            total += dot(feats_ref[:, rows], head_ref[rows])
+        norm = jnp.sqrt(jnp.sum(total * total, axis=-1, keepdims=True) + 1e-06)
+        return total / norm, norm
+
+    for copy in small:
+        copy.wait()
     owners = owners_ref[...]
     groups, images = owners.shape
     rows = groups * SLOTS
-    unit, norm = project(feats_ref[...], head_ref[...])
-    unit_ref[...] = unit
-    norm_ref[...] = norm
-
-    row, lane = iota((images, images), 0), iota((images, images), 1)
-    owned = owners == rank
-    place = dot(one_hot(owned), one_hot(row < lane))
+    owned = owners == place_ref[0]
+    place = dot(one_hot(owned), one_hot(iota((images, images), 0) < iota((images, images), 1)))
     code = jnp.where(owned, place, -1.0)
     spread = one_hot(lax.div(iota((rows, groups), 0), SLOTS) == iota((rows, groups), 1))
     code_rows = dot(spread, code.astype(BF))
     slot_rows = dot(spread, slots_ref[...].astype(F32).astype(BF))
     at = lax.rem(iota((rows, images), 0), SLOTS).astype(F32)
     slot = jnp.sum(jnp.where(code_rows == at, slot_rows + 1.0, 0.0), axis=1, keepdims=True) - 1.0
-    pool_rows = unit.shape[0]
-    select = one_hot(slot == iota((rows, pool_rows), 1).astype(F32))
+    select = one_hot(slot == iota((rows, pool_ref.shape[0]), 1).astype(F32))
     select_ref[...] = select
+    outs = [moved(select_ref, select_far)]
+
+    pool_in.wait()
+    unit, norm = projected(pool_ref, image_head_ref, image_head_in)
+    pool_unit_ref[...] = unit
+    pool_norm_ref[...] = norm
     out_ref[...] = dot(select, unit.astype(BF)).astype(BF).reshape(out_ref.shape)
+    outs += [
+        moved(out_ref, out_far),
+        moved(pool_unit_ref, pool_unit_far),
+        moved(pool_norm_ref, pool_norm_far),
+    ]
+
+    captions_in.wait()
+    unit, norm = projected(captions_ref, text_head_ref, text_head_in)
+    emb_ref[...] = unit.astype(BF)
+    outs += [moved(emb_ref, emb_far)]
+    text_unit_ref[...] = unit
+    text_norm_ref[...] = norm
+    outs += [moved(text_unit_ref, text_unit_far), moved(text_norm_ref, text_norm_far)]
+    for copy in outs:
+        copy.wait()
 
 
 def requested(place_ref, owners_ref, turned):
@@ -143,34 +178,31 @@
     return one_hot(mine_t * SLOTS + before == iota((images, groups * SLOTS), 1).astype(F32))
 
 
-def arrive(place_ref, arrived_ref, owners_ref, captions_ref, pool_ref, emb_ref, keep_ref, give_ref):
+def sorted_kinds(place_ref, captions_ref, pool_ref, keep_ref, give_ref):
+    first = place_ref[1] == 0
+    keep_ref[...] = jnp.where(first, captions_ref[...], pool_ref[...])
+    give_ref[...] = jnp.where(first, pool_ref[...], captions_ref[...])
+
+
+def arrive(place_ref, arrived_ref, owners_ref, emb_ref):
     hit = requested(place_ref, owners_ref, False)
     emb_ref[...] = dot(hit, arrived_ref[...].reshape(hit.shape[1], -1)).astype(BF)
 
-    @pl.when(place_ref[1] == 0)
-    def _():
-        keep_ref[...] = captions_ref[...]
-        give_ref[...] = pool_ref[...]
-
-    @pl.when(place_ref[1] != 0)
-    def _():
-        keep_ref[...] = pool_ref[...]
-        give_ref[...] = captions_ref[...]
-
-
-def joined(a_ref, b_ref, c_ref, d_ref, ab_ref, cd_ref):
+
+def joined(a_ref, b_ref, c_ref, d_ref, out_ref):
     rows = a_ref.shape[0]
-    ab_ref[:rows] = a_ref[...]
-    ab_ref[rows:] = b_ref[...]
-    cd_ref[:rows] = c_ref[...]
-    cd_ref[rows:] = d_ref[...]
+    for i, ref in enumerate((a_ref, b_ref, c_ref, d_ref)):
+        out_ref[i * rows : (i + 1) * rows] = ref[...]
 
 
 def pair_sums(turned, scale_ref, bias_ref, own_ref, other_ref, targets_ref, partners_ref, *refs):
     *block_refs, mine_ref, rest_ref = refs
     resident = jnp.concatenate([own_ref[...], other_ref[...]], axis=0)
     total = jnp.zeros(resident.shape, F32)
-    groups = [block_refs[:1]] + [block_refs[i : i + 2] for i in range(1, len(block_refs), 2)]
+    if len(block_refs) == 1:
+        groups = [[block_refs[0].at[pl.ds(i, 256)]] for i in range(0, block_refs[0].shape[0], 256)]
+    else:
+        groups = [block_refs[i : i + 2] for i in range(0, len(block_refs), 2)]
     for group in groups:
         moving = jnp.concatenate([ref[...] for ref in group], axis=0)
         logits = dot(resident, moving, 1, 1) * scale_ref[0] + bias_ref[0]
@@ -205,21 +237,19 @@
     strips_ref[:, 1] = turned.reshape(columns, strip, rows)
 
 
-def head_terms(place_ref, strips_ref, *refs):
-    x, yhi, core = place_ref[2], place_ref[3], place_ref[1]
-    *feats_refs, out_ref = refs
-    _, strip, lanes = strips_ref.shape
+def head_terms(place_ref, strips_ref, feats_ref, out_ref):
+    yhi, core = place_ref[2], place_ref[1]
+    sources, strip, lanes = strips_ref.shape
     extra = strip - lanes
-    terms = jnp.zeros((2 * lanes, feats_refs[0].shape[1]), F32)
-    for i, feats_ref in enumerate(feats_refs):
-        along, across = (0, 3, 1, 2)[i // 2], i % 2
-        blocks = []
-        for dc in range(2):
-            source = lax.rem(x + along, 4) * 4 + lax.rem(yhi + across, 2) * 2 + lax.rem(core + dc, 2)
-            blocks.append(strips_ref[source])
-        block = jnp.concatenate(blocks, axis=1)
-        block = jnp.concatenate([block[:lanes]] + [block[lanes:]] * (lanes // extra), axis=0)
-        terms += dot(block, feats_ref[...])
+    blocks = []
+    for x in range(sources // 4):
+        for dy in range(2):
+            for dc in range(2):
+                source = 4 * x + lax.rem(yhi + dy, 2) * 2 + lax.rem(core + dc, 2)
+                blocks.append(strips_ref[source])
+    block = jnp.concatenate(blocks, axis=1)
+    block = jnp.concatenate([block[:lanes]] + [block[lanes:]] * (lanes // extra), axis=0)
+    terms = dot(block, feats_ref[...])
     turned = terms.T
     turned = jnp.concatenate([turned, jnp.zeros((8, 2 * lanes), F32)], axis=0)
     row, lane = iota((8, lanes), 0), iota((8, lanes), 1)
@@ -274,43 +304,48 @@
     groups, images = owners.shape
     texts, width = captions.shape
     pool_rows = pool.shape[0]
-    place = jnp.stack([lax.axis_index(REP_AXES)] + [lax.axis_index(a) for a in ("core", "x", "yhi")])
-
-    pool_unit, pool_norm, outgoing, select = call(
-        pool_front,
-        [
-            ((pool_rows, width), F32),
-            ((pool_rows, 1), F32),
-            ((groups, SLOTS, width), BF),
-            ((groups * SLOTS, pool_rows), BF),
-        ],
-        "pool_front", [place], [pool, image_head, owners, image_slot],
-    )
+    place = jnp.stack([lax.axis_index(a) for a in (REP_AXES, "core", "yhi")])
+
+    outs = [
+        ((pool_rows, width), F32),
+        ((pool_rows, 1), F32),
+        ((groups, SLOTS, width), BF),
+        ((groups * SLOTS, pool_rows), BF),
+        ((texts, width), F32),
+        ((texts, 1), F32),
+        ((texts, width), BF),
+    ]
+    arrays = [owners, image_slot, pool, image_head, captions, text_head]
+    pool_unit, pool_norm, outgoing, select, text_unit, text_norm, text_emb = pl.pallas_call(
+        front,
+        out_shape=[jax.ShapeDtypeStruct(s, d) for s, d in outs],
+        in_specs=[SMEM] + [FAR] * len(arrays),
+        out_specs=[FAR] * len(outs),
+        scratch_shapes=[pltpu.VMEM(s, d) for s, d in [(a.shape, a.dtype) for a in arrays] + outs]
+        + [pltpu.SemaphoreType.DMA((17,))],
+        compiler_params=pltpu.CompilerParams(vmem_limit_bytes=64 * 2**20),
+        name="front",
+    )(place, *arrays)
+    text_blocks = [lax.all_gather(text_emb, "z", axis=0, tiled=True)]
     arrived = lax.all_to_all(outgoing, REP_AXES, 0, 0, tiled=True)
-    text_unit, text_norm, text_emb = call(
-        text_front,
-        [((texts, width), F32), ((texts, 1), F32), ((texts, width), BF)],
-        "text_front", [], [captions, text_head, pool_norm],
-    )
     other_text = shifted(text_emb, "ylo", 1)
-    text_blocks = gathered_along_z(text_emb, 1)
-    image_emb, keep, give = call(
-        arrive, [((images, width), BF), ((texts, width), BF), ((texts, width), BF)],
-        "arrive", [place], [arrived, owners, captions, pool],
-    )
-    other_image = shifted(image_emb, "ylo", 1)
-    image_blocks = gathered_along_z(image_emb, -1)
-
+    keep, give = call(
+        sorted_kinds, [((texts, width), BF)] * 2, "sorted_kinds", [place], [captions, pool],
+        [other_text],
+    )
     given = shifted(give, "core", 1)
     far_keep = shifted(keep, "yhi", 1)
     far_given = lax.ppermute(give, ("yhi", "core"), [(i, 3 - i) for i in range(4)])
-    home, far = call(
-        joined, [((2 * texts, width), BF)] * 2, "joined", [], [keep, given, far_keep, far_given]
-    )
-    feats = [home, far]
-    feats += [shifted(home, "x", 1), shifted(far, "x", 1)]
-    feats += [shifted(home, "x", -1), shifted(far, "x", -1)]
-    feats += [shifted(feats[2], "x", 1), shifted(feats[5], "x", -1)]
+    (image_emb,) = call(
+        arrive, [((images, width), BF)], "arrive", [place], [arrived, owners]
+    )
+    other_image = shifted(image_emb, "ylo", 1)
+    image_blocks = gathered_along_z(image_emb, -1)
+    (feats,) = call(
+        joined, [((4 * texts, width), BF)], "joined", [], [keep, given, far_keep, far_given],
+        [image_blocks[3]],
+    )
+    feats = lax.all_gather(feats, "x", axis=0, tiled=True)
 
     scalars = [logit_scale, logit_bias]
     image_mine, image_rest = call(
@@ -318,7 +353,7 @@
         [((images, width), F32), ((images, width), BF)],
         "image_sums", scalars, [image_emb, other_image, caption_image, text_emb, *text_blocks],
     )
-    image_rest = shifted(image_rest, "ylo", 1)
+    image_sent, image_rest = image_rest, shifted(image_rest, "ylo", 1)
     (send_back,) = call(
         image_back, [((groups, SLOTS, width), BF)], "image_back",
         [place, logit_scale], [image_mine, image_rest, owners],
@@ -329,6 +364,7 @@
         functools.partial(pair_sums, True),
         [((texts, width), F32), ((texts, width), BF)],
         "text_sums", scalars, [text_emb, other_text, caption_image, image_emb, *image_blocks],
+        [image_sent],
     )
     text_rest = shifted(text_rest, "ylo", 1)
     (text_grad,) = call(
@@ -348,7 +384,7 @@
 
     (terms,) = call(
         head_terms, [((128, 16, 128), BF)], "head_terms", [place],
-        [strips, *feats],
+        [strips, feats],
     )
     terms = lax.all_to_all(terms.reshape(256, 8, 128), CAP_AXES + REP_AXES, 0, 0, tiled=True)
     (head_share,) = call(

time: 177 us -> 186 us (1.051)
  starting transfers between devices: 79.2 us -> 48.5 us
  blocking collectives: 0 us -> 21.2 us
  between operations: 2.29 us -> 15.5 us
  waiting for transfers between devices: 46.8 us -> 53.7 us
    all_to_all x0 -> x1, blocking collectives: none -> 21.2 us  [per_device(): lax.all_to_all(strips.reshape(groups, strip, texts), REP_AXES, 0, 0, tile...]
    ppermute x26 -> x13, starting transfers between devices: 42 us -> 21.1 us  [shifted(): lax.ppermute(block, axis, [(i, (i + distance) % size) for i in range(size)])]
    all_to_all x1, waiting for transfers between devices: 0.01 us -> 11.2 us  [per_device(): arrived = lax.all_to_all(outgoing, REP_AXES, 0, 0, tiled=True)]
    all_to_all x1 -> x0, waiting for transfers between devices: 10.9 us -> none  [per_device(): lax.all_to_all(strips.reshape(groups, strip, texts), REP_AXES, 0, 0, tile...]
    all_to_all x1 -> x0, starting transfers between devices: 8.54 us -> none  [per_device(): lax.all_to_all(strips.reshape(groups, strip, texts), REP_AXES, 0, 0, tile...]
    pallas_call x11 -> x10, Pallas kernels: 41.8 us -> 35.1 us  [call(): pl.pallas_call(kernel, out_shape=shapes, in_specs=[SMEM] * len(scalars) +...]
    ppermute x1, waiting for transfers between devices: 0.46 us -> 6.5 us  [per_device(): lax.ppermute(give, ('yhi', 'core'), [(i, 3 - i) for i in range(4)])]
    pallas_call x0 -> x1, Pallas kernels: none -> 5.6 us  [per_device(): pl.pallas_call(front, out_shape=[jax.ShapeDtypeStruct(s, d) for s, d in o...]
  transfers between devices with their start and end apart: 31 -> 19, of which waited for: 10 -> 9; matrix products, arithmetic and copies ran while one was open for 3% -> 3% of each run, Pallas kernels for 14% -> 14%
where the time goes in v5:
time: 186 us; the launch traced here: 185 us
  waiting for transfers between devices  53.7 us (29%)
  starting transfers between devices  48.5 us (26%)
  Pallas kernels  40.7 us (22%)
  blocking collectives  21.2 us (11%)
  between operations  15.5 us (8%)
  matrix products  5.11 us (3%)
    pallas_call x10, Pallas kernels, call(): pl.pallas_call(kernel, out_shape=shapes, in_specs=[SMEM] * len(scalars) +...  35.1 us
    all_to_all x1, blocking collectives, per_device(): lax.all_to_all(strips.reshape(groups, strip, texts), REP_AXES, 0, 0, tile...  21.2 us
    ppermute x13, waiting for transfers between devices, shifted(): lax.ppermute(block, axis, [(i, (i + distance) % size) for i in range(size)])  21.2 us
    ppermute x13, starting transfers between devices, shifted(): lax.ppermute(block, axis, [(i, (i + distance) % size) for i in range(size)])  21.1 us
    all_to_all x1, waiting for transfers between devices, per_device(): lax.all_to_all(terms.reshape(256, 8, 128), CAP_AXES + REP_AXES, 0, 0, til...  14.8 us
    all_to_all x1, waiting for transfers between devices, per_device(): arrived = lax.all_to_all(outgoing, REP_AXES, 0, 0, tiled=True)  11.2 us
    all_to_all x1, starting transfers between devices, per_device(): arrived = lax.all_to_all(outgoing, REP_AXES, 0, 0, tiled=True)  8.46 us
    all_to_all x1, starting transfers between devices, per_device(): received = lax.all_to_all(send_back, REP_AXES, 0, 0, tiled=True)  8.25 us
  transfers between devices with their start and end apart: 19, of which 9 were waited for; matrix products, arithmetic and copies ran while one was open for 3% of the time, Pallas kernels for 14%

profile of v5, /device:TPU:1, one launch (start us, length us, event | category | flops | bytes accessed | tf_op | source)
XLA Modules:
  0.0 185.3 jit_solution(17375280695602736243)
XLA Ops:
  7.9 5.6 %front.1 = (f32[128,1152]{1,0:T(8,128)}, f32[128,1]{1,0:T(8,128)}, bf16[16,16,1152]{2,1,0:T(8,128)(2,1)}, bf16[256,128]{1,0:T(8,128)(2,1)}, f32[128,1152]{1,0:T(...) custom-call(s32[3]{0:T(128)} %pad_add_fusion.place_ref.refs_0_, s32[16,96]{1,0:T(8,128)} %bitcast.23, ...), custom_call_target="tpu_custom_call" | custom-call | tf_op jit(solution)/shard_map/front/pallas_call | solution.py:319
  13.5 8.5 %all-to-all-start = ((bf16[16,16,1152]{2,1,0:T(8,128)(2,1)}), bf16[16,16,1152]{2,1,0:T(8,128)(2,1)}, u32[]{:S(2)}, u32[]{:S(2)}) async-start(bf16[16,16,1152]{2,1,0:T(8,128)(2,1)} %get-tuple-element.19), calls=%async_computation | async-start | bytes 1179648 | tf_op jit(solution)/shard_map/all_to_all | solution.py:330
  22.5 11.2 %all-to-all-done.refs_1_ = bf16[16,16,1152]{2,1,0:T(8,128)(2,1)} async-done(((bf16[16,16,1152]{2,1,0:T(8,128)(2,1)}), bf16[16,16,1152]{2,1,0:T(8,128)(2,1)}, u32[]{:S(2)}, u32[]{:S(2)}) %all-to-all-start) | async-done | bytes 589856 | tf_op jit(solution)/shard_map/all_to_all | solution.py:330
  33.7 2.8 %arrive.1.refs_2_.refs_5_.refs_6_ = bf16[96,1152]{1,0:T(8,128)(2,1)} custom-call(s32[3]{0:T(128)} %pad_add_fusion.place_ref.refs_0_, bf16[16,16,1152]{2,1,0:T(8,128)(2,1)} %all-to-all-done.refs_1_, s32[16,96]{1,0:T(8,128)} %bitcast.24), custom_call_target="tpu_custom_call" | custom-call | tf_op jit(solution)/shard_map/arrive/pallas_call | solution.py:59
  36.6 5.6 %collective-permute-start.1 = (bf16[96,1152]{1,0:T(8,128)(2,1)}, bf16[96,1152]{1,0:T(8,128)(2,1)}, u32[]{:S(2)}, u32[]{:S(2)}) collective-permute-start(bf16[96,1152]{1,0:T(8,128)(2,1)} %arrive.1.refs_2_.refs_5_.refs_6_), channel_id=1, source_target_pairs={{0,112},{16,0},{32,16},{48,32},{64,48},{80,64},{96,80},{112,96},{1... | collective-permute-start | bytes 663560 | tf_op jit(solution)/shard_map/ppermute | solution.py:22
  42.2 2.6 %sorted_kinds.1 = (bf16[128,1152]{1,0:T(8,128)(2,1)}, bf16[128,1152]{1,0:T(8,128)(2,1)}) custom-call(s32[3]{0:T(128)} %pad_add_fusion.place_ref.refs_0_, bf16[128,1152]{1,0:T(8,128)(2,1)} %bitcast.21, bf16[128,1152]{1,0:T(8,128)(2,1)} %bitcast.19, bf16[128,1152]{1,0:T(8,128)(2,1)} %collective-permute-done.refs_3_), custom_call_target="tpu_custom_call" | custom-call | tf_op jit(solution)/shard_map/sorted_kinds/pallas_call | solution.py:59
  44.8 1.9 %collective-permute-start.11 = (bf16[128,1152]{1,0:T(8,128)(2,1)}, bf16[128,1152]{1,0:T(8,128)(2,1)}, u32[]{:S(2)}, u32[]{:S(2)}) collective-permute-start(bf16[128,1152]{1,0:T(8,128)(2,1)} %get-tuple-element.32), channel_id=1, source_target_pairs={{0,1},{1,0},{2,3},{3,2},{4,5},{5,4},{6,7},{7,6},{8,9},{9,8},{10,11... | collective-permute-start | bytes 884744 | tf_op jit(solution)/shard_map/ppermute | solution.py:22
  46.8 3.1 %collective-permute-start.13 = (bf16[128,1152]{1,0:T(8,128)(2,1)}, bf16[128,1152]{1,0:T(8,128)(2,1)}, u32[]{:S(2)}, u32[]{:S(2)}) collective-permute-start(bf16[128,1152]{1,0:T(8,128)(2,1)} %get-tuple-element.32), channel_id=1, source_target_pairs={{0,3},{1,2},{2,1},{3,0},{4,7},{5,6},{6,5},{7,4},{8,11},{9,10},{10,... | collective-permute-start | bytes 884744 | tf_op jit(solution)/shard_map/ppermute | solution.py:338
  50.0 1.4 collective-permute-done.1.refs_7_
  51.3 3.4 %collective-permute-start.3 = (bf16[96,1152]{1,0:T(8,128)(2,1)}, bf16[96,1152]{1,0:T(8,128)(2,1)}, u32[]{:S(2)}, u32[]{:S(2)}) collective-permute-start(bf16[96,1152]{1,0:T(8,128)(2,1)} %collective-permute-done.1.refs_7_), channel_id=1, source_target_pairs={{0,112},{16,0},{32,16},{48,32},{64,48},{80,64},{96,80},{112,96},{1... | collective-permute-start | bytes 663560 | tf_op jit(solution)/shard_map/ppermute | solution.py:22
  54.8 2.3 %collective-permute-done.12.refs_2_ = bf16[128,1152]{1,0:T(8,128)(2,1)} collective-permute-done((bf16[128,1152]{1,0:T(8,128)(2,1)}, bf16[128,1152]{1,0:T(8,128)(2,1)}, u32[]{:S(2)}, u32[]{:S(2)}) %collective-permute-start.12) | collective-permute-done | bytes 294944 | tf_op jit(solution)/shard_map/ppermute | solution.py:22
  57.1 6.5 %collective-permute-done.13.refs_3_ = bf16[128,1152]{1,0:T(8,128)(2,1)} collective-permute-done((bf16[128,1152]{1,0:T(8,128)(2,1)}, bf16[128,1152]{1,0:T(8,128)(2,1)}, u32[]{:S(2)}, u32[]{:S(2)}) %collective-permute-start.13) | collective-permute-done | bytes 294944 | tf_op jit(solution)/shard_map/ppermute | solution.py:338
  63.6 2.5 %joined.1 = bf16[512,1152]{1,0:T(8,128)(2,1)} custom-call(bf16[128,1152]{1,0:T(8,128)(2,1)} %get-tuple-element.31.refs_0_, bf16[128,1152]{1,0:T(8,128)(2,1)} %collective-permute-done.11.refs_1_, bf16[128,1152]{1,0:T(8,128)(2,1)} %collective-permute-done.12.refs_2_, bf16[128,1152]{1,0:T(8,128)(2,1)} %collective-permute-done.13.refs_3_, ...), custom_call_target="tpu_custom_call" | custom-call | tf_op jit(solution)/shard_map/joined/pallas_call | solution.py:59
  68.2 3.1 %collective-permute-done.8.refs_3_ = bf16[96,1152]{1,0:T(8,128)(2,1)} collective-permute-done((bf16[96,1152]{1,0:T(8,128)(2,1)}, bf16[96,1152]{1,0:T(8,128)(2,1)}, u32[]{:S(2)}, u32[]{:S(2)}) %collective-permute-start.8) | collective-permute-done | bytes 221216 | tf_op jit(solution)/shard_map/ppermute | solution.py:22
  71.3 5.0 %image_sums.1 = (f32[96,1152]{1,0:T(8,128)}, bf16[96,1152]{1,0:T(8,128)(2,1)}) custom-call(f32[1]{0:T(128)S(6)} %copy.12.refs_0_.refs_1_, f32[1]{0:T(128)S(6)} %copy.13.refs_1_, bf16[96,1152]{1,0:T(8,128)(2,1)} %arrive.1.refs_2_.refs_5_.refs_6_, bf16[96,1152]{1,0:T(8,128)(2,1)} %collective-permute-done.8.refs_3_, s32[1,128]{1,0:T(1,128)} %refs_4_.3, ...), custom_call_target="tpu_custom_call" | custom-call | tf_op jit(solution)/shard_map/image_sums/pallas_call | solution.py:59
  76.3 1.6 collective-permute-start.10
  77.9 2.7 %collective-permute-start.5 = (bf16[96,1152]{1,0:T(8,128)(2,1)}, bf16[96,1152]{1,0:T(8,128)(2,1)}, u32[]{:S(2)}, u32[]{:S(2)}) collective-permute-start(bf16[96,1152]{1,0:T(8,128)(2,1)} %collective-permute-done.3.refs_9_.refs_4_), channel_id=1, source_target_pairs={{0,112},{16,0},{32,16},{48,32},{64,48},{80,64},{96,80},{112,96},{1... | collective-permute-start | bytes 663560 | tf_op jit(solution)/shard_map/ppermute | solution.py:22
  81.6 3.0 %image_back.1 = bf16[16,16,1152]{2,1,0:T(8,128)(2,1)} custom-call(s32[3]{0:T(128)} %pad_add_fusion.place_ref.refs_0_, f32[1]{0:T(128)S(6)} %copy.12.refs_0_.refs_1_, f32[96,1152]{1,0:T(8,128)} %get-tuple-element.25.refs_2_, bf16[96,1152]{1,0:T(8,128)(2,1)} %collective-permute-done.10.refs_3_, s32[16,96]{1,0:T(8,128)} %bitcast.25), custom_call_target="tpu_custom_call" | custom-call | tf_op jit(solution)/shard_map/image_back/pallas_call | solution.py:59
  84.6 8.2 %all-to-all-start.1 = ((bf16[16,16,1152]{2,1,0:T(8,128)(2,1)}), bf16[16,16,1152]{2,1,0:T(8,128)(2,1)}, u32[]{:S(2)}, u32[]{:S(2)}) async-start(bf16[16,16,1152]{2,1,0:T(8,128)(2,1)} %image_back.1), calls=%async_computation.1 | async-start | bytes 1179648 | tf_op jit(solution)/shard_map/all_to_all | solution.py:361
  93.1 3.5 %collective-permute-start.7 = (bf16[96,1152]{1,0:T(8,128)(2,1)}, bf16[96,1152]{1,0:T(8,128)(2,1)}, u32[]{:S(2)}, u32[]{:S(2)}) collective-permute-start(bf16[96,1152]{1,0:T(8,128)(2,1)} %collective-permute-done.5.refs_11_), channel_id=1, source_target_pairs={{0,112},{16,0},{32,16},{48,32},{64,48},{80,64},{96,80},{112,96},{1... | collective-permute-start | bytes 663560 | tf_op jit(solution)/shard_map/ppermute | solution.py:22
  96.6 5.9 %collective-permute-done.6.refs_12_ = bf16[96,1152]{1,0:T(8,128)(2,1)} collective-permute-done((bf16[96,1152]{1,0:T(8,128)(2,1)}, bf16[96,1152]{1,0:T(8,128)(2,1)}, u32[]{:S(2)}, u32[]{:S(2)}) %collective-permute-start.6) | collective-permute-done | bytes 221216 | tf_op jit(solution)/shard_map/ppermute | solution.py:22
  102.5 5.0 %text_sums.1 = (f32[128,1152]{1,0:T(8,128)}, bf16[128,1152]{1,0:T(8,128)(2,1)}) custom-call(f32[1]{0:T(128)S(6)} %copy.12.refs_0_.refs_1_, f32[1]{0:T(128)S(6)} %copy.13.refs_1_, bf16[128,1152]{1,0:T(8,128)(2,1)} %get-tuple-element.18.refs_5_.refs_2_, bf16[128,1152]{1,0:T(8,128)(2,1)} %collective-permute-done.refs_3_, s32[1,128]{1,0:T(1,128)} %refs_4_.3, ...), custom_call_target="tpu_custom_call" | custom-call | tf_op jit(solution)/shard_map/text_sums/pallas_call | solution.py:59
  108.3 7.5 %collective-permute-done.9.refs_2_ = bf16[128,1152]{1,0:T(8,128)(2,1)} collective-permute-done((bf16[128,1152]{1,0:T(8,128)(2,1)}, bf16[128,1152]{1,0:T(8,128)(2,1)}, u32[]{:S(2)}, u32[]{:S(2)}) %collective-permute-start.9) | collective-permute-done | bytes 294944 | tf_op jit(solution)/shard_map/ppermute | solution.py:22
  115.7 2.4 %text_back.1.refs_4_ = bf16[128,1152]{1,0:T(8,128)(2,1)} custom-call(f32[1]{0:T(128)S(6)} %copy.12.refs_0_.refs_1_, f32[128,1152]{1,0:T(8,128)} %get-tuple-element.21.refs_1_, bf16[128,1152]{1,0:T(8,128)(2,1)} %collective-permute-done.9.refs_2_, f32[128,1152]{1,0:T(8,128)} %get-tuple-element.23.refs_3_, f32[128,1]{1,0:T(8,128)} %get-tuple-element.24.refs_4_), custom_call_target="tpu_custom_call" | custom-call | tf_op jit(solution)/shard_map/text_back/pallas_call | solution.py:59
  118.1 2.8 %pool_back.1 = (bf16[128,1152]{1,0:T(8,128)(2,1)}, bf16[8,2,144,128]{3,2,1,0:T(8,128)(2,1)}) custom-call(bf16[16,16,1152]{2,1,0:T(8,128)(2,1)} %all-to-all-done.1.refs_0_, bf16[256,128]{1,0:T(8,128)(2,1)} %get-tuple-element.26.refs_1_, f32[128,1152]{1,0:T(8,128)} %get-tuple-element.27.refs_2_, f32[128,1]{1,0:T(8,128)} %get-tuple-element.28.refs_3_, ...), custom_call_target="tpu_custom_call" | custom-call | tf_op jit(solution)/shard_map/pool_back/pallas_call | solution.py:59
  121.0 21.2 %all_to_all.20.refs_1_ = bf16[16,144,128]{2,1,0:T(8,128)(2,1)} all-to-all(bf16[16,144,128]{2,1,0:T(8,128)(2,1)} %bitcast.22), channel_id=1, replica_groups=mesh['ylo'=2,'z'=8,'x'=4,'yhi'=2,'core'=2] {'x','yhi','core'}, dimensions={0} | all-to-all | bytes 1179648 | tf_op jit(solution)/shard_map/all_to_all | solution.py:381
  142.2 5.8 %head_terms.1 = bf16[128,16,128]{2,1,0:T(8,128)(2,1)} custom-call(s32[3]{0:T(128)} %pad_add_fusion.place_ref.refs_0_, bf16[16,144,128]{2,1,0:T(8,128)(2,1)} %all_to_all.20.refs_1_, bf16[2048,1152]{1,0:T(8,128)(2,1)} %all-gather.5.cloned.1.call-done.refs_2_), custom_call_target="tpu_custom_call" | custom-call | tf_op jit(solution)/shard_map/head_terms/pallas_call | solution.py:59
  148.0 7.5 %all-to-all-start.3 = ((bf16[256,8,128]{2,1,0:T(8,128)(2,1)}), bf16[256,8,128]{2,1,0:T(8,128)(2,1)}, u32[]{:S(2)}, u32[]{:S(2)}) async-start(bf16[256,8,128]{2,1,0:T(8,128)(2,1)} %bitcast.17), calls=%async_computation.3 | async-start | bytes 1048576 | tf_op jit(solution)/shard_map/all_to_all | solution.py:389
  155.5 3.5 %fusion = bf16[1,128,1152]{2,1,0:T(8,128)(2,1)} fusion(bf16[128,1152]{1,0:T(8,128)(2,1)} %text_back.1.refs_4_, bf16[1152,1152]{1,0:T(8,128)(2,1)} %text_head_far.1), kind=kOutput, calls=%fused_computation.2 | convolution fusion | flops 339886080 | bytes 3244032 | tf_op jit(solution)/shard_map/dot_general | solution.py:72
  158.9 1.6 fusion.1
  160.6 14.8 %all-to-all-done.3 = bf16[256,8,128]{2,1,0:T(8,128)(2,1)} async-done(((bf16[256,8,128]{2,1,0:T(8,128)(2,1)}), bf16[256,8,128]{2,1,0:T(8,128)(2,1)}, u32[]{:S(2)}, u32[]{:S(2)}) %all-to-all-start.3) | async-done | bytes 524320 | tf_op jit(solution)/shard_map/all_to_all | solution.py:389
  175.3 3.1 %head_sums.1 = f32[9,1152]{1,0:T(8,128)} custom-call(s32[3]{0:T(128)} %pad_add_fusion.place_ref.refs_0_, bf16[128,16,128]{2,1,0:T(8,128)(2,1)} %bitcast.10.refs_1_), custom_call_target="tpu_custom_call" | custom-call | tf_op jit(solution)/shard_map/head_sums/pallas_call | solution.py:59
  (27 shorter events, 4.2 us)
Async XLA Ops:
  7.2 64.1 %all-gather.3.cloned.1.call-start = ((), (), s32[]{:S(2)}) async-start(), calls=%async_computation.4 | async-start | bytes 2654208 | tf_op jit(solution)/shard_map/all_gather | solution.py:329
  13.5 20.2 %all-to-all-start = ((bf16[16,16,1152]{2,1,0:T(8,128)(2,1)}), bf16[16,16,1152]{2,1,0:T(8,128)(2,1)}, u32[]{:S(2)}, u32[]{:S(2)}) async-start(bf16[16,16,1152]{2,1,0:T(8,128)(2,1)} %get-tuple-element.19), calls=%async_computation | async-start | bytes 1179648 | tf_op jit(solution)/shard_map/all_to_all | solution.py:330
  22.0 120.2 %all-gather.5.cloned.1.call-start = ((), (), s32[]{:S(2)}) async-start(), calls=%async_computation.5 | async-start | bytes 5898240 | tf_op jit(solution)/shard_map/all_gather | solution.py:348
  22.0 20.2 %collective-permute-start = (bf16[128,1152]{1,0:T(8,128)(2,1)}, bf16[128,1152]{1,0:T(8,128)(2,1)}, u32[]{:S(2)}, u32[]{:S(2)}) collective-permute-start(bf16[128,1152]{1,0:T(8,128)(2,1)} %get-tuple-element.18.refs_5_.refs_2_), channel_id=1, source_target_pairs={{0,128},{128,0},{1,129},{129,1},{2,130},{130,2},{3,131},{131,3},{4... | collective-permute-start | bytes 884744 | tf_op jit(solution)/shard_map/ppermute | solution.py:22
  36.6 14.8 %collective-permute-start.1 = (bf16[96,1152]{1,0:T(8,128)(2,1)}, bf16[96,1152]{1,0:T(8,128)(2,1)}, u32[]{:S(2)}, u32[]{:S(2)}) collective-permute-start(bf16[96,1152]{1,0:T(8,128)(2,1)} %arrive.1.refs_2_.refs_5_.refs_6_), channel_id=1, source_target_pairs={{0,112},{16,0},{32,16},{48,32},{64,48},{80,64},{96,80},{112,96},{1... | collective-permute-start | bytes 663560 | tf_op jit(solution)/shard_map/ppermute | solution.py:22
  44.8 9.9 %collective-permute-start.11 = (bf16[128,1152]{1,0:T(8,128)(2,1)}, bf16[128,1152]{1,0:T(8,128)(2,1)}, u32[]{:S(2)}, u32[]{:S(2)}) collective-permute-start(bf16[128,1152]{1,0:T(8,128)(2,1)} %get-tuple-element.32), channel_id=1, source_target_pairs={{0,1},{1,0},{2,3},{3,2},{4,5},{5,4},{6,7},{7,6},{8,9},{9,8},{10,11... | collective-permute-start | bytes 884744 | tf_op jit(solution)/shard_map/ppermute | solution.py:22
  46.7 10.4 %collective-permute-start.12 = (bf16[128,1152]{1,0:T(8,128)(2,1)}, bf16[128,1152]{1,0:T(8,128)(2,1)}, u32[]{:S(2)}, u32[]{:S(2)}) collective-permute-start(bf16[128,1152]{1,0:T(8,128)(2,1)} %get-tuple-element.31.refs_0_), channel_id=1, source_target_pairs={{0,2},{2,0},{1,3},{3,1},{4,6},{6,4},{5,7},{7,5},{8,10},{10,8},{9,1... | collective-permute-start | bytes 884744 | tf_op jit(solution)/shard_map/ppermute | solution.py:22
  46.8 16.8 %collective-permute-start.13 = (bf16[128,1152]{1,0:T(8,128)(2,1)}, bf16[128,1152]{1,0:T(8,128)(2,1)}, u32[]{:S(2)}, u32[]{:S(2)}) collective-permute-start(bf16[128,1152]{1,0:T(8,128)(2,1)} %get-tuple-element.32), channel_id=1, source_target_pairs={{0,3},{1,2},{2,1},{3,0},{4,7},{5,6},{6,5},{7,4},{8,11},{9,10},{10,... | collective-permute-start | bytes 884744 | tf_op jit(solution)/shard_map/ppermute | solution.py:338
  51.3 12.3 %collective-permute-start.3 = (bf16[96,1152]{1,0:T(8,128)(2,1)}, bf16[96,1152]{1,0:T(8,128)(2,1)}, u32[]{:S(2)}, u32[]{:S(2)}) collective-permute-start(bf16[96,1152]{1,0:T(8,128)(2,1)} %collective-permute-done.1.refs_7_), channel_id=1, source_target_pairs={{0,112},{16,0},{32,16},{48,32},{64,48},{80,64},{96,80},{112,96},{1... | collective-permute-start | bytes 663560 | tf_op jit(solution)/shard_map/ppermute | solution.py:22
  66.1 5.2 %collective-permute-start.8 = (bf16[96,1152]{1,0:T(8,128)(2,1)}, bf16[96,1152]{1,0:T(8,128)(2,1)}, u32[]{:S(2)}, u32[]{:S(2)}) collective-permute-start(bf16[96,1152]{1,0:T(8,128)(2,1)} %arrive.1.refs_2_.refs_5_.refs_6_), channel_id=1, source_target_pairs={{0,128},{128,0},{1,129},{129,1},{2,130},{130,2},{3,131},{131,3},{4... | collective-permute-start | bytes 663560 | tf_op jit(solution)/shard_map/ppermute | solution.py:22
  66.9 11.1 %collective-permute-start.2 = (bf16[96,1152]{1,0:T(8,128)(2,1)}, bf16[96,1152]{1,0:T(8,128)(2,1)}, u32[]{:S(2)}, u32[]{:S(2)}) collective-permute-start(bf16[96,1152]{1,0:T(8,128)(2,1)} %arrive.1.refs_2_.refs_5_.refs_6_), channel_id=1, source_target_pairs={{0,16},{16,32},{32,48},{48,64},{64,80},{80,96},{96,112},{112,0},{1... | collective-permute-start | bytes 663560 | tf_op jit(solution)/shard_map/ppermute | solution.py:22
  76.3 5.2 %collective-permute-start.10 = (bf16[96,1152]{1,0:T(8,128)(2,1)}, bf16[96,1152]{1,0:T(8,128)(2,1)}, u32[]{:S(2)}, u32[]{:S(2)}) collective-permute-start(bf16[96,1152]{1,0:T(8,128)(2,1)} %get-tuple-element.20.refs_14_), channel_id=1, source_target_pairs={{0,128},{128,0},{1,129},{129,1},{2,130},{130,2},{3,131},{131,3},{4... | collective-permute-start | bytes 663560 | tf_op jit(solution)/shard_map/ppermute | solution.py:22
  77.9 14.9 %collective-permute-start.4 = (bf16[96,1152]{1,0:T(8,128)(2,1)}, bf16[96,1152]{1,0:T(8,128)(2,1)}, u32[]{:S(2)}, u32[]{:S(2)}) collective-permute-start(bf16[96,1152]{1,0:T(8,128)(2,1)} %collective-permute-done.2.refs_8_), channel_id=1, source_target_pairs={{0,16},{16,32},{32,48},{48,64},{64,80},{80,96},{96,112},{112,0},{1... | collective-permute-start | bytes 663560 | tf_op jit(solution)/shard_map/ppermute | solution.py:22
  77.9 15.2 %collective-permute-start.5 = (bf16[96,1152]{1,0:T(8,128)(2,1)}, bf16[96,1152]{1,0:T(8,128)(2,1)}, u32[]{:S(2)}, u32[]{:S(2)}) collective-permute-start(bf16[96,1152]{1,0:T(8,128)(2,1)} %collective-permute-done.3.refs_9_.refs_4_), channel_id=1, source_target_pairs={{0,112},{16,0},{32,16},{48,32},{64,48},{80,64},{96,80},{112,96},{1... | collective-permute-start | bytes 663560 | tf_op jit(solution)/shard_map/ppermute | solution.py:22
  84.6 33.5 %all-to-all-start.1 = ((bf16[16,16,1152]{2,1,0:T(8,128)(2,1)}), bf16[16,16,1152]{2,1,0:T(8,128)(2,1)}, u32[]{:S(2)}, u32[]{:S(2)}) async-start(bf16[16,16,1152]{2,1,0:T(8,128)(2,1)} %image_back.1), calls=%async_computation.1 | async-start | bytes 1179648 | tf_op jit(solution)/shard_map/all_to_all | solution.py:361
  92.8 9.6 %collective-permute-start.6 = (bf16[96,1152]{1,0:T(8,128)(2,1)}, bf16[96,1152]{1,0:T(8,128)(2,1)}, u32[]{:S(2)}, u32[]{:S(2)}) collective-permute-start(bf16[96,1152]{1,0:T(8,128)(2,1)} %collective-permute-done.4.refs_10_), channel_id=1, source_target_pairs={{0,16},{16,32},{32,48},{48,64},{64,80},{80,96},{96,112},{112,0},{1... | collective-permute-start | bytes 663560 | tf_op jit(solution)/shard_map/ppermute | solution.py:22
  93.1 9.3 %collective-permute-start.7 = (bf16[96,1152]{1,0:T(8,128)(2,1)}, bf16[96,1152]{1,0:T(8,128)(2,1)}, u32[]{:S(2)}, u32[]{:S(2)}) collective-permute-start(bf16[96,1152]{1,0:T(8,128)(2,1)} %collective-permute-done.5.refs_11_), channel_id=1, source_target_pairs={{0,112},{16,0},{32,16},{48,32},{64,48},{80,64},{96,80},{112,96},{1... | collective-permute-start | bytes 663560 | tf_op jit(solution)/shard_map/ppermute | solution.py:22
  107.5 8.3 %collective-permute-start.9 = (bf16[128,1152]{1,0:T(8,128)(2,1)}, bf16[128,1152]{1,0:T(8,128)(2,1)}, u32[]{:S(2)}, u32[]{:S(2)}) collective-permute-start(bf16[128,1152]{1,0:T(8,128)(2,1)} %get-tuple-element.22), channel_id=1, source_target_pairs={{0,128},{128,0},{1,129},{129,1},{2,130},{130,2},{3,131},{131,3},{4... | collective-permute-start | bytes 884744 | tf_op jit(solution)/shard_map/ppermute | solution.py:22
  148.0 11.0 %copy-start = (bf16[1152,1152]{1,0:T(8,128)(2,1)S(1)}, bf16[1152,1152]{1,0:T(8,128)(2,1)}, u32[]{:S(2)}) copy-start(bf16[1152,1152]{1,0:T(8,128)(2,1)} %image_head_far.1) | copy-start | bytes 7962628
  148.0 11.0 %copy-start.1 = (bf16[128,1152]{1,0:T(8,128)(2,1)S(1)}, bf16[128,1152]{1,0:T(8,128)(2,1)}, u32[]{:S(2)}) copy-start(bf16[128,1152]{1,0:T(8,128)(2,1)} %get-tuple-element.29) | copy-start | bytes 884740
  148.0 27.4 %all-to-all-start.3 = ((bf16[256,8,128]{2,1,0:T(8,128)(2,1)}), bf16[256,8,128]{2,1,0:T(8,128)(2,1)}, u32[]{:S(2)}, u32[]{:S(2)}) async-start(bf16[256,8,128]{2,1,0:T(8,128)(2,1)} %bitcast.17), calls=%async_computation.3 | async-start | bytes 1048576 | tf_op jit(solution)/shard_map/all_to_all | solution.py:389
Sparse Core Ops, SparseCore 0:
  13.6 51.2 all-gather.2
  66.7 61.4 all-gather.4

commit v6 on v5

--- a/solution.py
+++ b/solution.py
@@ -28,6 +28,10 @@
         ahead, behind = shifted(ahead, "z", way), shifted(behind, "z", -way)
         found += [ahead, behind]
     return found + [shifted(ahead, "z", way)]
+
+
+def together(*arrays):
+    return lax.optimization_barrier(arrays)
 
 
 def call(body, outs, name, scalars, arrays, after=()):
@@ -86,10 +90,12 @@
 
 
 def front(
-    place_ref, owners_far, slots_far, pool_far, image_head_far, captions_far, text_head_far,
+    owners_far, slots_far, pool_far, image_head_far, captions_far, text_head_far,
     pool_unit_far, pool_norm_far, out_far, select_far, text_unit_far, text_norm_far, emb_far,
+    keep_far, give_far,
     owners_ref, slots_ref, pool_ref, image_head_ref, captions_ref, text_head_ref,
-    pool_unit_ref, pool_norm_ref, out_ref, select_ref, text_unit_ref, text_norm_ref, emb_ref, sems,
+    pool_unit_ref, pool_norm_ref, out_ref, select_ref, text_unit_ref, text_norm_ref, emb_ref,
+    keep_ref, give_ref, sems,
 ):
     width = pool_ref.shape[1]
     depth = width // 3
@@ -125,7 +131,7 @@
     owners = owners_ref[...]
     groups, images = owners.shape
     rows = groups * SLOTS
-    owned = owners == place_ref[0]
+    owned = owners == lax.axis_index(REP_AXES)
     place = dot(one_hot(owned), one_hot(iota((images, images), 0) < iota((images, images), 1)))
     code = jnp.where(owned, place, -1.0)
     spread = one_hot(lax.div(iota((rows, groups), 0), SLOTS) == iota((rows, groups), 1))
@@ -149,6 +155,10 @@
     ]
 
     captions_in.wait()
+    first = lax.axis_index("core") == 0
+    keep_ref[...] = jnp.where(first, captions_ref[...], pool_ref[...])
+    give_ref[...] = jnp.where(first, pool_ref[...], captions_ref[...])
+    outs += [moved(keep_ref, keep_far), moved(give_ref, give_far)]
     unit, norm = projected(captions_ref, text_head_ref, text_head_in)
     emb_ref[...] = unit.astype(BF)
     outs += [moved(emb_ref, emb_far)]
@@ -159,12 +169,12 @@
         copy.wait()
 
 
-def requested(place_ref, owners_ref, turned):
+def requested(owners_ref, turned):
     owners = owners_ref[...]
     groups, images = owners.shape
     row, lane = iota((images, images), 0), iota((images, images), 1)
     mine = jnp.sum(
-        jnp.where(iota((groups, images), 0) == place_ref[0], owners.astype(F32), 0.0),
+        jnp.where(iota((groups, images), 0) == lax.axis_index(REP_AXES), owners.astype(F32), 0.0),
         axis=0,
         keepdims=True,
     )
@@ -178,21 +188,17 @@
     return one_hot(mine_t * SLOTS + before == iota((images, groups * SLOTS), 1).astype(F32))
 
 
-def sorted_kinds(place_ref, captions_ref, pool_ref, keep_ref, give_ref):
-    first = place_ref[1] == 0
-    keep_ref[...] = jnp.where(first, captions_ref[...], pool_ref[...])
-    give_ref[...] = jnp.where(first, pool_ref[...], captions_ref[...])
-
-
-def arrive(place_ref, arrived_ref, owners_ref, emb_ref):
-    hit = requested(place_ref, owners_ref, False)
+def arrive(arrived_ref, owners_ref, emb_ref):
+    hit = requested(owners_ref, False)
     emb_ref[...] = dot(hit, arrived_ref[...].reshape(hit.shape[1], -1)).astype(BF)
 
 
-def joined(a_ref, b_ref, c_ref, d_ref, out_ref):
+def joined(a_ref, b_ref, c_ref, d_ref, ab_ref, cd_ref):
     rows = a_ref.shape[0]
-    for i, ref in enumerate((a_ref, b_ref, c_ref, d_ref)):
-        out_ref[i * rows : (i + 1) * rows] = ref[...]
+    ab_ref[:rows] = a_ref[...]
+    ab_ref[rows:] = b_ref[...]
+    cd_ref[:rows] = c_ref[...]
+    cd_ref[rows:] = d_ref[...]
 
 
 def pair_sums(turned, scale_ref, bias_ref, own_ref, other_ref, targets_ref, partners_ref, *refs):
@@ -215,41 +221,44 @@
     rest_ref[...] = total[own_rows:].astype(BF)
 
 
-def image_back(place_ref, scale_ref, mine_ref, rest_ref, owners_ref, out_ref):
+def image_back(scale_ref, mine_ref, rest_ref, owners_ref, out_ref):
     gradient = (scale_ref[0] * (mine_ref[...] + rest_ref[...].astype(F32))).astype(BF)
-    out_ref[...] = dot(requested(place_ref, owners_ref, True), gradient).astype(BF).reshape(out_ref.shape)
-
-
-def text_back(scale_ref, mine_ref, rest_ref, unit_ref, norm_ref, grad_ref):
+    out_ref[...] = dot(requested(owners_ref, True), gradient).astype(BF).reshape(out_ref.shape)
+
+
+def both_back(
+    scale_ref, mine_ref, rest_ref, text_unit_ref, text_norm_ref,
+    received_ref, select_ref, pool_unit_ref, pool_norm_ref,
+    text_grad_ref, pool_grad_ref, strips_ref,
+):
+    columns, _, strip, rows = strips_ref.shape
     gradient = scale_ref[0] * (mine_ref[...] + rest_ref[...].astype(F32))
-    grad_ref[...] = pull_back(unit_ref[...], norm_ref[...], gradient).astype(BF)
-
-
-def pool_back(received_ref, select_ref, unit_ref, norm_ref, text_ref, grad_ref, strips_ref):
+    gradient = pull_back(text_unit_ref[...], text_norm_ref[...], gradient)
+    text_grad_ref[...] = gradient.astype(BF)
+    strips_ref[:, 0] = gradient.T.astype(BF).reshape(columns, strip, rows)
+
     received = received_ref[...].reshape(select_ref.shape[0], -1)
     choose = select_ref[...].astype(F32).T.astype(BF)
-    gradient = pull_back(unit_ref[...], norm_ref[...], dot(choose, received))
-    grad_ref[...] = gradient.astype(BF)
-    columns, _, strip, rows = strips_ref.shape
-    turned = text_ref[...].astype(F32).T.astype(BF)
-    strips_ref[:, 0] = turned.reshape(columns, strip, rows)
-    turned = gradient.T.astype(BF)
-    strips_ref[:, 1] = turned.reshape(columns, strip, rows)
-
-
-def head_terms(place_ref, strips_ref, feats_ref, out_ref):
-    yhi, core = place_ref[2], place_ref[1]
-    sources, strip, lanes = strips_ref.shape
+    gradient = pull_back(pool_unit_ref[...], pool_norm_ref[...], dot(choose, received))
+    pool_grad_ref[...] = gradient.astype(BF)
+    strips_ref[:, 1] = gradient.T.astype(BF).reshape(columns, strip, rows)
+
+
+def head_terms(strips_ref, *refs):
+    x, yhi, core = (lax.axis_index(axis) for axis in REP_AXES)
+    *feats_refs, out_ref = refs
+    _, strip, lanes = strips_ref.shape
     extra = strip - lanes
-    blocks = []
-    for x in range(sources // 4):
-        for dy in range(2):
-            for dc in range(2):
-                source = 4 * x + lax.rem(yhi + dy, 2) * 2 + lax.rem(core + dc, 2)
-                blocks.append(strips_ref[source])
-    block = jnp.concatenate(blocks, axis=1)
-    block = jnp.concatenate([block[:lanes]] + [block[lanes:]] * (lanes // extra), axis=0)
-    terms = dot(block, feats_ref[...])
+    terms = jnp.zeros((2 * lanes, feats_refs[0].shape[1]), F32)
+    for i, feats_ref in enumerate(feats_refs):
+        along, across = (0, 3, 1, 2)[i // 2], i % 2
+        blocks = []
+        for dc in range(2):
+            source = lax.rem(x + along, 4) * 4 + lax.rem(yhi + across, 2) * 2 + lax.rem(core + dc, 2)
+            blocks.append(strips_ref[source])
+        block = jnp.concatenate(blocks, axis=1)
+        block = jnp.concatenate([block[:lanes]] + [block[lanes:]] * (lanes // extra), axis=0)
+        terms += dot(block, feats_ref[...])
     turned = terms.T
     turned = jnp.concatenate([turned, jnp.zeros((8, 2 * lanes), F32)], axis=0)
     row, lane = iota((8, lanes), 0), iota((8, lanes), 1)
@@ -264,8 +273,8 @@
         out_ref[pair] = jnp.concatenate(halves, axis=0).astype(BF)
 
 
-def head_sums(place_ref, terms_ref, out_ref):
-    core = place_ref[1]
+def head_sums(terms_ref, out_ref):
+    core = lax.axis_index("core")
     lanes = terms_ref.shape[2]
     extra = out_ref.shape[1] // 8 - lanes
     row, lane = iota((16, lanes), 0), iota((16, lanes), 1)
@@ -304,8 +313,6 @@
     groups, images = owners.shape
     texts, width = captions.shape
     pool_rows = pool.shape[0]
-    place = jnp.stack([lax.axis_index(a) for a in (REP_AXES, "core", "yhi")])
-
     outs = [
         ((pool_rows, width), F32),
         ((pool_rows, 1), F32),
@@ -314,49 +321,57 @@
         ((texts, width), F32),
         ((texts, 1), F32),
         ((texts, width), BF),
+        ((texts, width), BF),
+        ((texts, width), BF),
     ]
     arrays = [owners, image_slot, pool, image_head, captions, text_head]
-    pool_unit, pool_norm, outgoing, select, text_unit, text_norm, text_emb = pl.pallas_call(
+    pool_unit, pool_norm, outgoing, select, text_unit, text_norm, text_emb, keep, give = pl.pallas_call(
         front,
         out_shape=[jax.ShapeDtypeStruct(s, d) for s, d in outs],
-        in_specs=[SMEM] + [FAR] * len(arrays),
+        in_specs=[FAR] * len(arrays),
         out_specs=[FAR] * len(outs),
         scratch_shapes=[pltpu.VMEM(s, d) for s, d in [(a.shape, a.dtype) for a in arrays] + outs]
-        + [pltpu.SemaphoreType.DMA((17,))],
+        + [pltpu.SemaphoreType.DMA((19,))],
         compiler_params=pltpu.CompilerParams(vmem_limit_bytes=64 * 2**20),
         name="front",
-    )(place, *arrays)
-    text_blocks = [lax.all_gather(text_emb, "z", axis=0, tiled=True)]
+    )(*arrays)
+    text_blocks = gathered_along_z(text_emb, 1)
     arrived = lax.all_to_all(outgoing, REP_AXES, 0, 0, tiled=True)
     other_text = shifted(text_emb, "ylo", 1)
-    keep, give = call(
-        sorted_kinds, [((texts, width), BF)] * 2, "sorted_kinds", [place], [captions, pool],
-        [other_text],
-    )
     given = shifted(give, "core", 1)
     far_keep = shifted(keep, "yhi", 1)
     far_given = lax.ppermute(give, ("yhi", "core"), [(i, 3 - i) for i in range(4)])
     (image_emb,) = call(
-        arrive, [((images, width), BF)], "arrive", [place], [arrived, owners]
+        arrive, [((images, width), BF)], "arrive", [], [arrived, owners], [given]
     )
     other_image = shifted(image_emb, "ylo", 1)
-    image_blocks = gathered_along_z(image_emb, -1)
-    (feats,) = call(
-        joined, [((4 * texts, width), BF)], "joined", [], [keep, given, far_keep, far_given],
-        [image_blocks[3]],
-    )
-    feats = lax.all_gather(feats, "x", axis=0, tiled=True)
+    image_blocks = [image_emb]
+    ahead = behind = image_emb
+    for step in range(3):
+        ahead, behind = shifted(ahead, "z", -1), shifted(behind, "z", 1)
+        ahead, behind = together(ahead, behind)
+        image_blocks += [ahead, behind]
+    image_blocks += [shifted(ahead, "z", -1)]
+    home, far = call(
+        joined, [((2 * texts, width), BF)] * 2, "joined", [], [keep, given, far_keep, far_given],
+    )
+    feats = [home, far]
+    feats += [shifted(home, "x", 1), shifted(far, "x", 1)]
+    feats += [shifted(home, "x", -1), shifted(far, "x", -1)]
+    feats += [shifted(feats[2], "x", 1), shifted(feats[5], "x", -1)]
 
     scalars = [logit_scale, logit_bias]
     image_mine, image_rest = call(
         functools.partial(pair_sums, False),
         [((images, width), F32), ((images, width), BF)],
         "image_sums", scalars, [image_emb, other_image, caption_image, text_emb, *text_blocks],
+        [home],
     )
     image_sent, image_rest = image_rest, shifted(image_rest, "ylo", 1)
     (send_back,) = call(
         image_back, [((groups, SLOTS, width), BF)], "image_back",
-        [place, logit_scale], [image_mine, image_rest, owners],
+        [logit_scale], [image_mine, image_rest, owners],
+        [feats[2], feats[4], *image_blocks[6:]],
     )
     received = lax.all_to_all(send_back, REP_AXES, 0, 0, tiled=True)
 
@@ -364,31 +379,28 @@
         functools.partial(pair_sums, True),
         [((texts, width), F32), ((texts, width), BF)],
         "text_sums", scalars, [text_emb, other_text, caption_image, image_emb, *image_blocks],
-        [image_sent],
+        [send_back, feats[3], feats[5]],
     )
     text_rest = shifted(text_rest, "ylo", 1)
-    (text_grad,) = call(
-        text_back, [((texts, width), BF)], "text_back", scalars[:1],
-        [text_mine, text_rest, text_unit, text_norm],
-    )
     columns = groups // 2
     strip = width // columns
-    pool_proj_grad, strips = call(
-        pool_back,
-        [((pool_rows, width), BF), ((columns, 2, strip, texts), BF)],
-        "pool_back", [], [received, select, pool_unit, pool_norm, text_grad],
+    text_grad, pool_proj_grad, strips = call(
+        both_back,
+        [((texts, width), BF), ((pool_rows, width), BF), ((columns, 2, strip, texts), BF)],
+        "both_back", scalars[:1],
+        [text_mine, text_rest, text_unit, text_norm, received, select, pool_unit, pool_norm],
     )
     strips = lax.all_to_all(strips.reshape(groups, strip, texts), REP_AXES, 0, 0, tiled=True)
     text_feat_grad = dot(text_grad, text_head, 1, 1).astype(BF)
     pool_grad = dot(pool_proj_grad, image_head, 1, 1).astype(BF)
 
     (terms,) = call(
-        head_terms, [((128, 16, 128), BF)], "head_terms", [place],
-        [strips, feats],
+        head_terms, [((128, 16, 128), BF)], "head_terms", [],
+        [strips, *feats],
     )
     terms = lax.all_to_all(terms.reshape(256, 8, 128), CAP_AXES + REP_AXES, 0, 0, tiled=True)
     (head_share,) = call(
-        head_sums, [((9, width), F32)], "head_sums", [place], [terms.reshape(128, 16, 128)]
+        head_sums, [((9, width), F32)], "head_sums", [], [terms.reshape(128, 16, 128)]
     )
     return text_feat_grad[None], pool_grad[None], head_share
 

time: 186 us -> 168 us (0.903)
  blocking collectives: 21.2 us -> 0 us
  starting transfers between devices: 48.5 us -> 66 us
  between operations: 15.5 us -> 2.27 us
  Pallas kernels: 40.7 us -> 33.3 us
  waiting for transfers between devices: 53.7 us -> 60.6 us
    all_to_all x1 -> x0, blocking collectives: 21.2 us -> none  [per_device(): lax.all_to_all(strips.reshape(groups, strip, texts), REP_AXES, 0, 0, tile...]
    all_to_all x0 -> x1, waiting for transfers between devices: none -> 11.8 us  [per_device(): lax.all_to_all(strips.reshape(groups, strip, texts), REP_AXES, 0, 0, tile...]
    all_to_all x1, waiting for transfers between devices: 11.2 us -> 0.01 us  [per_device(): arrived = lax.all_to_all(outgoing, REP_AXES, 0, 0, tiled=True)]
    ppermute x13 -> x26, waiting for transfers between devices: 21.2 us -> 32.4 us  [shifted(): lax.ppermute(block, axis, [(i, (i + distance) % size) for i in range(size)])]
    ppermute x13 -> x26, starting transfers between devices: 21.1 us -> 31.2 us  [shifted(): lax.ppermute(block, axis, [(i, (i + distance) % size) for i in range(size)])]
    pallas_call x10 -> x8, Pallas kernels: 35.1 us -> 28.3 us  [call(): pl.pallas_call(kernel, out_shape=shapes, in_specs=[SMEM] * len(scalars) +...]
    all_to_all x0 -> x1, starting transfers between devices: none -> 6.05 us  [per_device(): lax.all_to_all(strips.reshape(groups, strip, texts), REP_AXES, 0, 0, tile...]
    ppermute x1, waiting for transfers between devices: 6.5 us -> 1.5 us  [per_device(): lax.ppermute(give, ('yhi', 'core'), [(i, 3 - i) for i in range(4)])]
  transfers between devices with their start and end apart: 19 -> 31, of which waited for: 9 -> 13; matrix products, arithmetic and copies ran while one was open for 3% -> 3% of each run, Pallas kernels for 14% -> 12%
where the time goes in v6:
time: 168 us; the launch traced here: 167 us
  starting transfers between devices  66 us (39%)
  waiting for transfers between devices  60.6 us (36%)
  Pallas kernels  33.3 us (20%)
  matrix products  5.12 us (3%)
  between operations  2.27 us (1%)
    ppermute x26, waiting for transfers between devices, shifted(): lax.ppermute(block, axis, [(i, (i + distance) % size) for i in range(size)])  32.4 us
    ppermute x26, starting transfers between devices, shifted(): lax.ppermute(block, axis, [(i, (i + distance) % size) for i in range(size)])  31.2 us
    pallas_call x8, Pallas kernels, call(): pl.pallas_call(kernel, out_shape=shapes, in_specs=[SMEM] * len(scalars) +...  28.3 us
    all_to_all x1, waiting for transfers between devices, per_device(): lax.all_to_all(terms.reshape(256, 8, 128), CAP_AXES + REP_AXES, 0, 0, til...  14.9 us
    all_to_all x1, waiting for transfers between devices, per_device(): lax.all_to_all(strips.reshape(groups, strip, texts), REP_AXES, 0, 0, tile...  11.8 us
    all_to_all x1, starting transfers between devices, per_device(): received = lax.all_to_all(send_back, REP_AXES, 0, 0, tiled=True)  8.5 us
    all_to_all x1, starting transfers between devices, per_device(): arrived = lax.all_to_all(outgoing, REP_AXES, 0, 0, tiled=True)  8.46 us
    all_to_all x1, starting transfers between devices, per_device(): lax.all_to_all(terms.reshape(256, 8, 128), CAP_AXES + REP_AXES, 0, 0, til...  8.32 us
  transfers between devices with their start and end apart: 31, of which 13 were waited for; matrix products, arithmetic and copies ran while one was open for 3% of the time, Pallas kernels for 12%

profile of v6, /device:TPU:1, one launch (start us, length us, event | category | flops | bytes accessed | tf_op | source)
XLA Modules:
  0.0 167.3 jit_solution(8866884848492623955)
XLA Ops:
  0.6 5.0 %front.1 = (f32[128,1152]{1,0:T(8,128)}, f32[128,1]{1,0:T(8,128)}, bf16[16,16,1152]{2,1,0:T(8,128)(2,1)}, bf16[256,128]{1,0:T(8,128)(2,1)}, f32[128,1152]{1,0:T(...) custom-call(s32[16,96]{1,0:T(8,128)} %bitcast.18, ...), custom_call_target="tpu_custom_call" | custom-call | tf_op jit(solution)/shard_map/front/pallas_call | solution.py:328
  5.7 8.5 %all-to-all-start = ((bf16[16,16,1152]{2,1,0:T(8,128)(2,1)}), bf16[16,16,1152]{2,1,0:T(8,128)(2,1)}, u32[]{:S(2)}, u32[]{:S(2)}) async-start(bf16[16,16,1152]{2,1,0:T(8,128)(2,1)} %get-tuple-element.28), calls=%async_computation | async-start | bytes 1179648 | tf_op jit(solution)/shard_map/all_to_all | solution.py:339
  14.1 1.7 collective-permute-start.10
  16.3 3.7 %collective-permute-start.11 = (bf16[128,1152]{1,0:T(8,128)(2,1)}, bf16[128,1152]{1,0:T(8,128)(2,1)}, u32[]{:S(2)}, u32[]{:S(2)}) collective-permute-start(bf16[128,1152]{1,0:T(8,128)(2,1)} %get-tuple-element.27.refs_5_.refs_6_.refs_2_), channel_id=1, source_target_pairs={{0,112},{16,0},{32,16},{48,32},{64,48},{80,64},{96,80},{112,96},{1... | collective-permute-start | bytes 884744 | tf_op jit(solution)/shard_map/ppermute | solution.py:22
  20.0 7.2 %collective-permute-done.10.refs_7_ = bf16[128,1152]{1,0:T(8,128)(2,1)} collective-permute-done((bf16[128,1152]{1,0:T(8,128)(2,1)}, bf16[128,1152]{1,0:T(8,128)(2,1)}, u32[]{:S(2)}, u32[]{:S(2)}) %collective-permute-start.10) | collective-permute-done | bytes 294944 | tf_op jit(solution)/shard_map/ppermute | solution.py:22
  27.3 2.2 %arrive.1.refs_2_.refs_5_.refs_6_ = bf16[96,1152]{1,0:T(8,128)(2,1)} custom-call(bf16[16,16,1152]{2,1,0:T(8,128)(2,1)} %all-to-all-done.refs_0_, s32[16,96]{1,0:T(8,128)} %bitcast.19, bf16[128,1152]{1,0:T(8,128)(2,1)} %collective-permute-done.1.refs_2_.refs_1_), custom_call_target="tpu_custom_call" | custom-call | tf_op jit(solution)/shard_map/arrive/pallas_call | solution.py:63
  29.5 4.3 %collective-permute-start.2 = (bf16[96,1152]{1,0:T(8,128)(2,1)}, bf16[96,1152]{1,0:T(8,128)(2,1)}, u32[]{:S(2)}, u32[]{:S(2)}) collective-permute-start(bf16[96,1152]{1,0:T(8,128)(2,1)} %arrive.1.refs_2_.refs_5_.refs_6_), channel_id=1, source_target_pairs={{0,112},{16,0},{32,16},{48,32},{64,48},{80,64},{96,80},{112,96},{1... | collective-permute-start | bytes 663560 | tf_op jit(solution)/shard_map/ppermute | solution.py:22
  35.1 3.5 %collective-permute-start.18 = (bf16[128,1152]{1,0:T(8,128)(2,1)}, bf16[128,1152]{1,0:T(8,128)(2,1)}, u32[]{:S(2)}, u32[]{:S(2)}) collective-permute-start(bf16[128,1152]{1,0:T(8,128)(2,1)} %get-tuple-element.29), channel_id=1, source_target_pairs={{0,3},{1,2},{2,1},{3,0},{4,7},{5,6},{6,5},{7,4},{8,11},{9,10},{10,... | collective-permute-start | bytes 884744 | tf_op jit(solution)/shard_map/ppermute | solution.py:343
  38.7 2.7 %collective-permute-start.13 = (bf16[128,1152]{1,0:T(8,128)(2,1)}, bf16[128,1152]{1,0:T(8,128)(2,1)}, u32[]{:S(2)}, u32[]{:S(2)}) collective-permute-start(bf16[128,1152]{1,0:T(8,128)(2,1)} %collective-permute-done.11.refs_8_), channel_id=1, source_target_pairs={{0,112},{16,0},{32,16},{48,32},{64,48},{80,64},{96,80},{112,96},{1... | collective-permute-start | bytes 884744 | tf_op jit(solution)/shard_map/ppermute | solution.py:22
  41.3 6.3 %collective-permute-done.3.refs_8_ = bf16[96,1152]{1,0:T(8,128)(2,1)} collective-permute-done((bf16[96,1152]{1,0:T(8,128)(2,1)}, bf16[96,1152]{1,0:T(8,128)(2,1)}, u32[]{:S(2)}, u32[]{:S(2)}) %collective-permute-start.3) | collective-permute-done | bytes 221216 | tf_op jit(solution)/shard_map/ppermute | solution.py:22
  47.6 1.5 collective-permute-start.5
  49.1 1.5 collective-permute-done.18.refs_3_
  50.6 2.4 %joined.1 = (bf16[256,1152]{1,0:T(8,128)(2,1)}, bf16[256,1152]{1,0:T(8,128)(2,1)}) custom-call(bf16[128,1152]{1,0:T(8,128)(2,1)} %get-tuple-element.36.refs_0_, bf16[128,1152]{1,0:T(8,128)(2,1)} %collective-permute-done.1.refs_2_.refs_1_, bf16[128,1152]{1,0:T(8,128)(2,1)} %collective-permute-done.17.refs_2_, bf16[128,1152]{1,0:T(8,128)(2,1)} %collective-permute-done.18.refs_3_), custom_call_target="tpu_custom_call" | custom-call | tf_op jit(solution)/shard_map/joined/pallas_call | solution.py:63
  55.6 2.0 %collective-permute-done.5.refs_10_ = bf16[96,1152]{1,0:T(8,128)(2,1)} collective-permute-done((bf16[96,1152]{1,0:T(8,128)(2,1)}, bf16[96,1152]{1,0:T(8,128)(2,1)}, u32[]{:S(2)}, u32[]{:S(2)}) %collective-permute-start.5) | collective-permute-done | bytes 221216 | tf_op jit(solution)/shard_map/ppermute | solution.py:22
  59.0 2.0 %collective-permute-done.9.refs_3_ = bf16[96,1152]{1,0:T(8,128)(2,1)} collective-permute-done((bf16[96,1152]{1,0:T(8,128)(2,1)}, bf16[96,1152]{1,0:T(8,128)(2,1)}, u32[]{:S(2)}, u32[]{:S(2)}) %collective-permute-start.9) | collective-permute-done | bytes 221216 | tf_op jit(solution)/shard_map/ppermute | solution.py:22
  61.7 1.6 collective-permute-done.15.refs_12_
  64.6 3.0 %collective-permute-start.23 = (bf16[256,1152]{1,0:T(8,128)(2,1)}, bf16[256,1152]{1,0:T(8,128)(2,1)}, u32[]{:S(2)}, u32[]{:S(2)}) collective-permute-start(bf16[256,1152]{1,0:T(8,128)(2,1)} %get-tuple-element.40.refs_2_), channel_id=1, source_target_pairs={{0,12},{4,0},{8,4},{12,8},{1,13},{5,1},{9,5},{13,9},{2,14},{6,2},{... | collective-permute-start | bytes 1769480 | tf_op jit(solution)/shard_map/ppermute | solution.py:22
  70.4 5.0 %image_sums.1 = (f32[96,1152]{1,0:T(8,128)}, bf16[96,1152]{1,0:T(8,128)(2,1)}) custom-call(f32[1]{0:T(128)S(6)} %copy.12.refs_0_, f32[1]{0:T(128)S(6)} %copy.13.refs_1_, bf16[96,1152]{1,0:T(8,128)(2,1)} %arrive.1.refs_2_.refs_5_.refs_6_, bf16[96,1152]{1,0:T(8,128)(2,1)} %collective-permute-done.9.refs_3_, s32[1,128]{1,0:T(1,128)} %refs_4_.3, ...), custom_call_target="tpu_custom_call" | custom-call | tf_op jit(solution)/shard_map/image_sums/pallas_call | solution.py:63
  78.7 2.5 %collective-permute-done.19.refs_2_ = bf16[96,1152]{1,0:T(8,128)(2,1)} collective-permute-done((bf16[96,1152]{1,0:T(8,128)(2,1)}, bf16[96,1152]{1,0:T(8,128)(2,1)}, u32[]{:S(2)}, u32[]{:S(2)}) %collective-permute-start.19) | collective-permute-done | bytes 221216 | tf_op jit(solution)/shard_map/ppermute | solution.py:22
  82.0 2.4 %image_back.1.refs_14_ = bf16[16,16,1152]{2,1,0:T(8,128)(2,1)} custom-call(f32[1]{0:T(128)S(6)} %copy.12.refs_0_, f32[96,1152]{1,0:T(8,128)} %get-tuple-element.38.refs_1_, bf16[96,1152]{1,0:T(8,128)(2,1)} %collective-permute-done.19.refs_2_, s32[16,96]{1,0:T(8,128)} %bitcast.20, bf16[256,1152]{1,0:T(8,128)(2,1)} %collective-permute-done.20.refs_4_.refs_3_, ...), custom_call_target="tpu_custom_call" | custom-call | tf_op jit(solution)/shard_map/image_back/pallas_call | solution.py:63
  84.4 8.5 %all-to-all-start.1 = ((bf16[16,16,1152]{2,1,0:T(8,128)(2,1)}), bf16[16,16,1152]{2,1,0:T(8,128)(2,1)}, u32[]{:S(2)}, u32[]{:S(2)}) async-start(bf16[16,16,1152]{2,1,0:T(8,128)(2,1)} %image_back.1.refs_14_), calls=%async_computation.1 | async-start | bytes 1179648 | tf_op jit(solution)/shard_map/all_to_all | solution.py:376
  92.9 5.0 %text_sums.1 = (f32[128,1152]{1,0:T(8,128)}, bf16[128,1152]{1,0:T(8,128)(2,1)}) custom-call(f32[1]{0:T(128)S(6)} %copy.12.refs_0_, f32[1]{0:T(128)S(6)} %copy.13.refs_1_, bf16[128,1152]{1,0:T(8,128)(2,1)} %get-tuple-element.27.refs_5_.refs_6_.refs_2_, bf16[128,1152]{1,0:T(8,128)(2,1)} %collective-permute-done.refs_3_, s32[1,128]{1,0:T(1,128)} %refs_4_.3, ...), custom_call_target="tpu_custom_call" | custom-call | tf_op jit(solution)/shard_map/text_sums/pallas_call | solution.py:63
  101.1 8.4 %collective-permute-done.24.refs_2_ = bf16[128,1152]{1,0:T(8,128)(2,1)} collective-permute-done((bf16[128,1152]{1,0:T(8,128)(2,1)}, bf16[128,1152]{1,0:T(8,128)(2,1)}, u32[]{:S(2)}, u32[]{:S(2)}) %collective-permute-start.24) | collective-permute-done | bytes 294944 | tf_op jit(solution)/shard_map/ppermute | solution.py:22
  109.5 3.5 %both_back.1 = (bf16[128,1152]{1,0:T(8,128)(2,1)}, bf16[128,1152]{1,0:T(8,128)(2,1)}, bf16[8,2,144,128]{3,2,1,0:T(8,128)(2,1)}) custom-call(f32[1]{0:T(128)S(6)} %copy.12.refs_0_, f32[128,1152]{1,0:T(8,128)} %get-tuple-element.41.refs_1_, bf16[128,1152]{1,0:T(8,128)(2,1)} %collective-permute-done.24.refs_2_, f32[128,1152]{1,0:T(8,128)} %get-tuple-element.43.refs_3_, ...), custom_call_target="tpu_custom_call" | custom-call | tf_op jit(solution)/shard_map/both_back/pallas_call | solution.py:63
  113.1 6.1 %all-to-all-start.2 = ((bf16[16,144,128]{2,1,0:T(8,128)(2,1)}), bf16[16,144,128]{2,1,0:T(8,128)(2,1)}, u32[]{:S(2)}, u32[]{:S(2)}) async-start(bf16[16,144,128]{2,1,0:T(8,128)(2,1)} %bitcast.15), calls=%async_computation.2 | async-start | bytes 1179648 | tf_op jit(solution)/shard_map/all_to_all | solution.py:393
  119.1 11.8 %all-to-all-done.2.refs_0_ = bf16[16,144,128]{2,1,0:T(8,128)(2,1)} async-done(((bf16[16,144,128]{2,1,0:T(8,128)(2,1)}), bf16[16,144,128]{2,1,0:T(8,128)(2,1)}, u32[]{:S(2)}, u32[]{:S(2)}) %all-to-all-start.2) | async-done | bytes 589856 | tf_op jit(solution)/shard_map/all_to_all | solution.py:393
  130.9 5.3 %head_terms.1 = bf16[128,16,128]{2,1,0:T(8,128)(2,1)} custom-call(bf16[16,144,128]{2,1,0:T(8,128)(2,1)} %all-to-all-done.2.refs_0_, bf16[256,1152]{1,0:T(8,128)(2,1)} %get-tuple-element.37.refs_14_.refs_1_, bf16[256,1152]{1,0:T(8,128)(2,1)} %get-tuple-element.40.refs_2_, bf16[256,1152]{1,0:T(8,128)(2,1)} %collective-permute-done.20.refs_4_.refs_3_, ...), custom_call_target="tpu_custom_call" | custom-call | tf_op jit(solution)/shard_map/head_terms/pallas_call | solution.py:63
  136.3 8.3 %all-to-all-start.3 = ((bf16[256,8,128]{2,1,0:T(8,128)(2,1)}), bf16[256,8,128]{2,1,0:T(8,128)(2,1)}, u32[]{:S(2)}, u32[]{:S(2)}) async-start(bf16[256,8,128]{2,1,0:T(8,128)(2,1)} %bitcast.14), calls=%async_computation.3 | async-start | bytes 1048576 | tf_op jit(solution)/shard_map/all_to_all | solution.py:401
  144.6 3.5 %fusion = bf16[1,128,1152]{2,1,0:T(8,128)(2,1)} fusion(bf16[128,1152]{1,0:T(8,128)(2,1)} %get-tuple-element.48, bf16[1152,1152]{1,0:T(8,128)(2,1)} %text_head_far.1), kind=kOutput, calls=%fused_computation.2 | convolution fusion | flops 339886080 | bytes 3244032 | tf_op jit(solution)/shard_map/dot_general | solution.py:76
  148.1 1.6 fusion.1
  149.7 14.9 %all-to-all-done.3 = bf16[256,8,128]{2,1,0:T(8,128)(2,1)} async-done(((bf16[256,8,128]{2,1,0:T(8,128)(2,1)}), bf16[256,8,128]{2,1,0:T(8,128)(2,1)}, u32[]{:S(2)}, u32[]{:S(2)}) %all-to-all-start.3) | async-done | bytes 524320 | tf_op jit(solution)/shard_map/all_to_all | solution.py:401
  164.6 2.5 %head_sums.1 = f32[9,1152]{1,0:T(8,128)} custom-call(bf16[128,16,128]{2,1,0:T(8,128)(2,1)} %bitcast.7.refs_0_), custom_call_target="tpu_custom_call" | custom-call | tf_op jit(solution)/shard_map/head_sums/pallas_call | solution.py:63
  (45 shorter events, 16.7 us)
Async XLA Ops:
  5.7 21.6 %all-to-all-start = ((bf16[16,16,1152]{2,1,0:T(8,128)(2,1)}), bf16[16,16,1152]{2,1,0:T(8,128)(2,1)}, u32[]{:S(2)}, u32[]{:S(2)}) async-start(bf16[16,16,1152]{2,1,0:T(8,128)(2,1)} %get-tuple-element.28), calls=%async_computation | async-start | bytes 1179648 | tf_op jit(solution)/shard_map/all_to_all | solution.py:339
  14.1 13.1 %collective-permute-start.10 = (bf16[128,1152]{1,0:T(8,128)(2,1)}, bf16[128,1152]{1,0:T(8,128)(2,1)}, u32[]{:S(2)}, u32[]{:S(2)}) collective-permute-start(bf16[128,1152]{1,0:T(8,128)(2,1)} %get-tuple-element.27.refs_5_.refs_6_.refs_2_), channel_id=1, source_target_pairs={{0,16},{16,32},{32,48},{48,64},{64,80},{80,96},{96,112},{112,0},{1... | collective-permute-start | bytes 884744 | tf_op jit(solution)/shard_map/ppermute | solution.py:22
  15.8 11.5 %collective-permute-start.1 = (bf16[128,1152]{1,0:T(8,128)(2,1)}, bf16[128,1152]{1,0:T(8,128)(2,1)}, u32[]{:S(2)}, u32[]{:S(2)}) collective-permute-start(bf16[128,1152]{1,0:T(8,128)(2,1)} %get-tuple-element.29), channel_id=1, source_target_pairs={{0,1},{1,0},{2,3},{3,2},{4,5},{5,4},{6,7},{7,6},{8,9},{9,8},{10,11... | collective-permute-start | bytes 884744 | tf_op jit(solution)/shard_map/ppermute | solution.py:22
  16.3 22.4 %collective-permute-start.11 = (bf16[128,1152]{1,0:T(8,128)(2,1)}, bf16[128,1152]{1,0:T(8,128)(2,1)}, u32[]{:S(2)}, u32[]{:S(2)}) collective-permute-start(bf16[128,1152]{1,0:T(8,128)(2,1)} %get-tuple-element.27.refs_5_.refs_6_.refs_2_), channel_id=1, source_target_pairs={{0,112},{16,0},{32,16},{48,32},{64,48},{80,64},{96,80},{112,96},{1... | collective-permute-start | bytes 884744 | tf_op jit(solution)/shard_map/ppermute | solution.py:22
  27.3 11.4 %collective-permute-start.12 = (bf16[128,1152]{1,0:T(8,128)(2,1)}, bf16[128,1152]{1,0:T(8,128)(2,1)}, u32[]{:S(2)}, u32[]{:S(2)}) collective-permute-start(bf16[128,1152]{1,0:T(8,128)(2,1)} %collective-permute-done.10.refs_7_), channel_id=1, source_target_pairs={{0,16},{16,32},{32,48},{48,64},{64,80},{80,96},{96,112},{112,0},{1... | collective-permute-start | bytes 884744 | tf_op jit(solution)/shard_map/ppermute | solution.py:22
  29.5 11.9 %collective-permute-start.2 = (bf16[96,1152]{1,0:T(8,128)(2,1)}, bf16[96,1152]{1,0:T(8,128)(2,1)}, u32[]{:S(2)}, u32[]{:S(2)}) collective-permute-start(bf16[96,1152]{1,0:T(8,128)(2,1)} %arrive.1.refs_2_.refs_5_.refs_6_), channel_id=1, source_target_pairs={{0,112},{16,0},{32,16},{48,32},{64,48},{80,64},{96,80},{112,96},{1... | collective-permute-start | bytes 663560 | tf_op jit(solution)/shard_map/ppermute | solution.py:22
  33.7 13.9 %collective-permute-start.17 = (bf16[128,1152]{1,0:T(8,128)(2,1)}, bf16[128,1152]{1,0:T(8,128)(2,1)}, u32[]{:S(2)}, u32[]{:S(2)}) collective-permute-start(bf16[128,1152]{1,0:T(8,128)(2,1)} %get-tuple-element.36.refs_0_), channel_id=1, source_target_pairs={{0,2},{2,0},{1,3},{3,1},{4,6},{6,4},{5,7},{7,5},{8,10},{10,8},{9,1... | collective-permute-start | bytes 884744 | tf_op jit(solution)/shard_map/ppermute | solution.py:22
  35.1 15.5 %collective-permute-start.18 = (bf16[128,1152]{1,0:T(8,128)(2,1)}, bf16[128,1152]{1,0:T(8,128)(2,1)}, u32[]{:S(2)}, u32[]{:S(2)}) collective-permute-start(bf16[128,1152]{1,0:T(8,128)(2,1)} %get-tuple-element.29), channel_id=1, source_target_pairs={{0,3},{1,2},{2,1},{3,0},{4,7},{5,6},{6,5},{7,4},{8,11},{9,10},{10,... | collective-permute-start | bytes 884744 | tf_op jit(solution)/shard_map/ppermute | solution.py:343
  38.7 9.0 %collective-permute-start.3 = (bf16[96,1152]{1,0:T(8,128)(2,1)}, bf16[96,1152]{1,0:T(8,128)(2,1)}, u32[]{:S(2)}, u32[]{:S(2)}) collective-permute-start(bf16[96,1152]{1,0:T(8,128)(2,1)} %arrive.1.refs_2_.refs_5_.refs_6_), channel_id=1, source_target_pairs={{0,16},{16,32},{32,48},{48,64},{64,80},{80,96},{96,112},{112,0},{1... | collective-permute-start | bytes 663560 | tf_op jit(solution)/shard_map/ppermute | solution.py:22
  38.7 14.8 %collective-permute-start.13 = (bf16[128,1152]{1,0:T(8,128)(2,1)}, bf16[128,1152]{1,0:T(8,128)(2,1)}, u32[]{:S(2)}, u32[]{:S(2)}) collective-permute-start(bf16[128,1152]{1,0:T(8,128)(2,1)} %collective-permute-done.11.refs_8_), channel_id=1, source_target_pairs={{0,112},{16,0},{32,16},{48,32},{64,48},{80,64},{96,80},{112,96},{1... | collective-permute-start | bytes 884744 | tf_op jit(solution)/shard_map/ppermute | solution.py:22
  41.3 12.8 %collective-permute-start.14 = (bf16[128,1152]{1,0:T(8,128)(2,1)}, bf16[128,1152]{1,0:T(8,128)(2,1)}, u32[]{:S(2)}, u32[]{:S(2)}) collective-permute-start(bf16[128,1152]{1,0:T(8,128)(2,1)} %collective-permute-done.12.refs_9_), channel_id=1, source_target_pairs={{0,16},{16,32},{32,48},{48,64},{64,80},{80,96},{96,112},{112,0},{1... | collective-permute-start | bytes 884744 | tf_op jit(solution)/shard_map/ppermute | solution.py:22
  47.6 7.1 %collective-permute-start.4 = (bf16[96,1152]{1,0:T(8,128)(2,1)}, bf16[96,1152]{1,0:T(8,128)(2,1)}, u32[]{:S(2)}, u32[]{:S(2)}) collective-permute-start(bf16[96,1152]{1,0:T(8,128)(2,1)} %collective-permute-done.2.refs_7_), channel_id=1, source_target_pairs={{0,112},{16,0},{32,16},{48,32},{64,48},{80,64},{96,80},{112,96},{1... | collective-permute-start | bytes 663560 | tf_op jit(solution)/shard_map/ppermute | solution.py:22
  47.6 10.0 %collective-permute-start.5 = (bf16[96,1152]{1,0:T(8,128)(2,1)}, bf16[96,1152]{1,0:T(8,128)(2,1)}, u32[]{:S(2)}, u32[]{:S(2)}) collective-permute-start(bf16[96,1152]{1,0:T(8,128)(2,1)} %collective-permute-done.3.refs_8_), channel_id=1, source_target_pairs={{0,16},{16,32},{32,48},{48,64},{64,80},{80,96},{96,112},{112,0},{1... | collective-permute-start | bytes 663560 | tf_op jit(solution)/shard_map/ppermute | solution.py:22
  53.0 23.3 %collective-permute-start.20 = (bf16[256,1152]{1,0:T(8,128)(2,1)}, bf16[256,1152]{1,0:T(8,128)(2,1)}, u32[]{:S(2)}, u32[]{:S(2)}) collective-permute-start(bf16[256,1152]{1,0:T(8,128)(2,1)} %get-tuple-element.37.refs_14_.refs_1_), channel_id=1, source_target_pairs={{0,4},{4,8},{8,12},{12,0},{1,5},{5,9},{9,13},{13,1},{2,6},{6,10},{... | collective-permute-start | bytes 1769480 | tf_op jit(solution)/shard_map/ppermute | solution.py:22
  53.4 7.6 %collective-permute-start.9 = (bf16[96,1152]{1,0:T(8,128)(2,1)}, bf16[96,1152]{1,0:T(8,128)(2,1)}, u32[]{:S(2)}, u32[]{:S(2)}) collective-permute-start(bf16[96,1152]{1,0:T(8,128)(2,1)} %arrive.1.refs_2_.refs_5_.refs_6_), channel_id=1, source_target_pairs={{0,128},{128,0},{1,129},{129,1},{2,130},{130,2},{3,131},{131,3},{4... | collective-permute-start | bytes 663560 | tf_op jit(solution)/shard_map/ppermute | solution.py:22
  54.1 9.2 %collective-permute-start.15 = (bf16[128,1152]{1,0:T(8,128)(2,1)}, bf16[128,1152]{1,0:T(8,128)(2,1)}, u32[]{:S(2)}, u32[]{:S(2)}) collective-permute-start(bf16[128,1152]{1,0:T(8,128)(2,1)} %collective-permute-done.13.refs_10_), channel_id=1, source_target_pairs={{0,112},{16,0},{32,16},{48,32},{64,48},{80,64},{96,80},{112,96},{1... | collective-permute-start | bytes 884744 | tf_op jit(solution)/shard_map/ppermute | solution.py:22
  54.8 9.9 %collective-permute-start.16 = (bf16[128,1152]{1,0:T(8,128)(2,1)}, bf16[128,1152]{1,0:T(8,128)(2,1)}, u32[]{:S(2)}, u32[]{:S(2)}) collective-permute-start(bf16[128,1152]{1,0:T(8,128)(2,1)} %collective-permute-done.14.refs_11_), channel_id=1, source_target_pairs={{0,16},{16,32},{32,48},{48,64},{64,80},{80,96},{96,112},{112,0},{1... | collective-permute-start | bytes 884744 | tf_op jit(solution)/shard_map/ppermute | solution.py:22
  57.6 20.0 %collective-permute-start.21 = (bf16[256,1152]{1,0:T(8,128)(2,1)}, bf16[256,1152]{1,0:T(8,128)(2,1)}, u32[]{:S(2)}, u32[]{:S(2)}) collective-permute-start(bf16[256,1152]{1,0:T(8,128)(2,1)} %get-tuple-element.37.refs_14_.refs_1_), channel_id=1, source_target_pairs={{0,12},{4,0},{8,4},{12,8},{1,13},{5,1},{9,5},{13,9},{2,14},{6,2},{... | collective-permute-start | bytes 1769480 | tf_op jit(solution)/shard_map/ppermute | solution.py:22
  61.0 6.7 %collective-permute-start.6 = (bf16[96,1152]{1,0:T(8,128)(2,1)}, bf16[96,1152]{1,0:T(8,128)(2,1)}, u32[]{:S(2)}, u32[]{:S(2)}) collective-permute-start(bf16[96,1152]{1,0:T(8,128)(2,1)} %collective-permute-done.4.refs_9_), channel_id=1, source_target_pairs={{0,112},{16,0},{32,16},{48,32},{64,48},{80,64},{96,80},{112,96},{1... | collective-permute-start | bytes 663560 | tf_op jit(solution)/shard_map/ppermute | solution.py:22
  63.3 12.1 %collective-permute-start.7 = (bf16[96,1152]{1,0:T(8,128)(2,1)}, bf16[96,1152]{1,0:T(8,128)(2,1)}, u32[]{:S(2)}, u32[]{:S(2)}) collective-permute-start(bf16[96,1152]{1,0:T(8,128)(2,1)} %collective-permute-done.5.refs_10_), channel_id=1, source_target_pairs={{0,16},{16,32},{32,48},{48,64},{64,80},{80,96},{96,112},{112,0},{1... | collective-permute-start | bytes 663560 | tf_op jit(solution)/shard_map/ppermute | solution.py:22
  64.6 28.3 %collective-permute-start.23 = (bf16[256,1152]{1,0:T(8,128)(2,1)}, bf16[256,1152]{1,0:T(8,128)(2,1)}, u32[]{:S(2)}, u32[]{:S(2)}) collective-permute-start(bf16[256,1152]{1,0:T(8,128)(2,1)} %get-tuple-element.40.refs_2_), channel_id=1, source_target_pairs={{0,12},{4,0},{8,4},{12,8},{1,13},{5,1},{9,5},{13,9},{2,14},{6,2},{... | collective-permute-start | bytes 1769480 | tf_op jit(solution)/shard_map/ppermute | solution.py:22
  67.7 25.2 %collective-permute-start.22 = (bf16[256,1152]{1,0:T(8,128)(2,1)}, bf16[256,1152]{1,0:T(8,128)(2,1)}, u32[]{:S(2)}, u32[]{:S(2)}) collective-permute-start(bf16[256,1152]{1,0:T(8,128)(2,1)} %get-tuple-element.40.refs_2_), channel_id=1, source_target_pairs={{0,4},{4,8},{8,12},{12,0},{1,5},{5,9},{9,13},{13,1},{2,6},{6,10},{... | collective-permute-start | bytes 1769480 | tf_op jit(solution)/shard_map/ppermute | solution.py:22
  75.4 5.8 %collective-permute-start.19 = (bf16[96,1152]{1,0:T(8,128)(2,1)}, bf16[96,1152]{1,0:T(8,128)(2,1)}, u32[]{:S(2)}, u32[]{:S(2)}) collective-permute-start(bf16[96,1152]{1,0:T(8,128)(2,1)} %get-tuple-element.39), channel_id=1, source_target_pairs={{0,128},{128,0},{1,129},{129,1},{2,130},{130,2},{3,131},{131,3},{4... | collective-permute-start | bytes 663560 | tf_op jit(solution)/shard_map/ppermute | solution.py:22
  76.3 5.7 %collective-permute-start.8 = (bf16[96,1152]{1,0:T(8,128)(2,1)}, bf16[96,1152]{1,0:T(8,128)(2,1)}, u32[]{:S(2)}, u32[]{:S(2)}) collective-permute-start(bf16[96,1152]{1,0:T(8,128)(2,1)} %collective-permute-done.6.refs_11_), channel_id=1, source_target_pairs={{0,112},{16,0},{32,16},{48,32},{64,48},{80,64},{96,80},{112,96},{1... | collective-permute-start | bytes 663560 | tf_op jit(solution)/shard_map/ppermute | solution.py:22
  77.6 15.3 %collective-permute-start = (bf16[128,1152]{1,0:T(8,128)(2,1)}, bf16[128,1152]{1,0:T(8,128)(2,1)}, u32[]{:S(2)}, u32[]{:S(2)}) collective-permute-start(bf16[128,1152]{1,0:T(8,128)(2,1)} %get-tuple-element.27.refs_5_.refs_6_.refs_2_), channel_id=1, source_target_pairs={{0,128},{128,0},{1,129},{129,1},{2,130},{130,2},{3,131},{131,3},{4... | collective-permute-start | bytes 884744 | tf_op jit(solution)/shard_map/ppermute | solution.py:22
  84.4 25.1 %all-to-all-start.1 = ((bf16[16,16,1152]{2,1,0:T(8,128)(2,1)}), bf16[16,16,1152]{2,1,0:T(8,128)(2,1)}, u32[]{:S(2)}, u32[]{:S(2)}) async-start(bf16[16,16,1152]{2,1,0:T(8,128)(2,1)} %image_back.1.refs_14_), calls=%async_computation.1 | async-start | bytes 1179648 | tf_op jit(solution)/shard_map/all_to_all | solution.py:376
  97.9 11.6 %collective-permute-start.24 = (bf16[128,1152]{1,0:T(8,128)(2,1)}, bf16[128,1152]{1,0:T(8,128)(2,1)}, u32[]{:S(2)}, u32[]{:S(2)}) collective-permute-start(bf16[128,1152]{1,0:T(8,128)(2,1)} %get-tuple-element.42), channel_id=1, source_target_pairs={{0,128},{128,0},{1,129},{129,1},{2,130},{130,2},{3,131},{131,3},{4... | collective-permute-start | bytes 884744 | tf_op jit(solution)/shard_map/ppermute | solution.py:22
  98.5 20.7 %collective-permute-start.25 = (bf16[256,1152]{1,0:T(8,128)(2,1)}, bf16[256,1152]{1,0:T(8,128)(2,1)}, u32[]{:S(2)}, u32[]{:S(2)}) collective-permute-start(bf16[256,1152]{1,0:T(8,128)(2,1)} %collective-permute-done.20.refs_4_.refs_3_), channel_id=1, source_target_pairs={{0,4},{4,8},{8,12},{12,0},{1,5},{5,9},{9,13},{13,1},{2,6},{6,10},{... | collective-permute-start | bytes 1769480 | tf_op jit(solution)/shard_map/ppermute | solution.py:22
  99.8 19.3 %collective-permute-start.26 = (bf16[256,1152]{1,0:T(8,128)(2,1)}, bf16[256,1152]{1,0:T(8,128)(2,1)}, u32[]{:S(2)}, u32[]{:S(2)}) collective-permute-start(bf16[256,1152]{1,0:T(8,128)(2,1)} %collective-permute-done.23.refs_16_.refs_6_), channel_id=1, source_target_pairs={{0,12},{4,0},{8,4},{12,8},{1,13},{5,1},{9,5},{13,9},{2,14},{6,2},{... | collective-permute-start | bytes 1769480 | tf_op jit(solution)/shard_map/ppermute | solution.py:22
  113.1 17.8 %all-to-all-start.2 = ((bf16[16,144,128]{2,1,0:T(8,128)(2,1)}), bf16[16,144,128]{2,1,0:T(8,128)(2,1)}, u32[]{:S(2)}, u32[]{:S(2)}) async-start(bf16[16,144,128]{2,1,0:T(8,128)(2,1)} %bitcast.15), calls=%async_computation.2 | async-start | bytes 1179648 | tf_op jit(solution)/shard_map/all_to_all | solution.py:393
  136.2 11.8 %copy-start = (bf16[1152,1152]{1,0:T(8,128)(2,1)S(1)}, bf16[1152,1152]{1,0:T(8,128)(2,1)}, u32[]{:S(2)}) copy-start(bf16[1152,1152]{1,0:T(8,128)(2,1)} %image_head_far.1) | copy-start | bytes 7962628
  136.3 28.4 %all-to-all-start.3 = ((bf16[256,8,128]{2,1,0:T(8,128)(2,1)}), bf16[256,8,128]{2,1,0:T(8,128)(2,1)}, u32[]{:S(2)}, u32[]{:S(2)}) async-start(bf16[256,8,128]{2,1,0:T(8,128)(2,1)} %bitcast.14), calls=%async_computation.3 | async-start | bytes 1048576 | tf_op jit(solution)/shard_map/all_to_all | solution.py:401
  (1 other events, 11.8 us)

commit v7 on v6

--- a/solution.py
+++ b/solution.py
@@ -201,24 +201,63 @@
     cd_ref[rows:] = d_ref[...]
 
 
-def pair_sums(turned, scale_ref, bias_ref, own_ref, other_ref, targets_ref, partners_ref, *refs):
-    *block_refs, mine_ref, rest_ref = refs
-    resident = jnp.concatenate([own_ref[...], other_ref[...]], axis=0)
-    total = jnp.zeros(resident.shape, F32)
-    if len(block_refs) == 1:
-        groups = [[block_refs[0].at[pl.ds(i, 256)]] for i in range(0, block_refs[0].shape[0], 256)]
-    else:
-        groups = [block_refs[i : i + 2] for i in range(0, len(block_refs), 2)]
-    for group in groups:
-        moving = jnp.concatenate([ref[...] for ref in group], axis=0)
-        logits = dot(resident, moving, 1, 1) * scale_ref[0] + bias_ref[0]
-        total += dot(jax.nn.sigmoid(logits).astype(BF), moving)
-    own_rows, partner_rows = own_ref.shape[0], partners_ref.shape[0]
+def pair_sums(turned, count, scale_ref, bias_ref, targets_far, own_far, other_far, *refs):
+    blocks_far = refs[:count]
+    mine_far, rest_far, targets_ref, resident_ref, moving_ref, mine_ref, rest_ref, sems = refs[-8:]
+    used = 0
+    copies = []
+    for far, ref in ((own_far, resident_ref), (other_far, resident_ref), (targets_far, targets_ref)):
+        part = ref.at[pl.ds(own_far.shape[0], own_far.shape[0])] if far is other_far else ref
+        part = ref.at[pl.ds(0, own_far.shape[0])] if far is own_far else part
+        copies.append(pltpu.make_async_copy(far, part, sems.at[len(copies)]))
+        copies[-1].start()
+    for far in blocks_far:
+        rows = far.shape[0]
+        part = moving_ref.at[pl.ds(used, rows)]
+        copies.append(pltpu.make_async_copy(far, part, sems.at[len(copies)]))
+        copies[-1].start()
+        used += rows
+    for copy in copies:
+        copy.wait()
+    resident, moving = resident_ref[...], moving_ref[...]
+    logits = dot(resident, moving, 1, 1) * scale_ref[0] + bias_ref[0]
+    total = dot(jax.nn.sigmoid(logits).astype(BF), moving)
+    own_rows, partner_rows = mine_ref.shape[0], blocks_far[0].shape[0]
     images, texts = (partner_rows, own_rows) if turned else (own_rows, partner_rows)
     hits = jnp.where(targets_ref[...] == iota((images, texts), 0), 1.0, 0.0)
     hits = hits.T if turned else hits
-    mine_ref[...] = total[:own_rows] - dot(hits.astype(BF), partners_ref[...])
+    mine_ref[...] = total[:own_rows] - dot(hits.astype(BF), moving_ref[:partner_rows])
     rest_ref[...] = total[own_rows:].astype(BF)
+    outs = [
+        pltpu.make_async_copy(mine_ref, mine_far, sems.at[len(copies)]),
+        pltpu.make_async_copy(rest_ref, rest_far, sems.at[len(copies) + 1]),
+    ]
+    for copy in outs:
+        copy.start()
+    for copy in outs:
+        copy.wait()
+
+
+def pair_call(turned, name, scalars, targets, own, other, blocks, after):
+    rows, width = own.shape
+    moving = (sum(block.shape[0] for block in blocks), width)
+    arrays = [targets, own, other, *blocks]
+    return pl.pallas_call(
+        functools.partial(pair_sums, turned, len(blocks)),
+        out_shape=[jax.ShapeDtypeStruct((rows, width), d) for d in (F32, BF)],
+        in_specs=[SMEM] * 2 + [FAR] * (len(arrays) + len(after)),
+        out_specs=[FAR] * 2,
+        scratch_shapes=[
+            pltpu.VMEM(targets.shape, targets.dtype),
+            pltpu.VMEM((2 * rows, width), BF),
+            pltpu.VMEM(moving, BF),
+            pltpu.VMEM((rows, width), F32),
+            pltpu.VMEM((rows, width), BF),
+            pltpu.SemaphoreType.DMA((len(arrays) + 2,)),
+        ],
+        compiler_params=pltpu.CompilerParams(vmem_limit_bytes=64 * 2**20),
+        name=name,
+    )(*scalars, *arrays, *after)
 
 
 def image_back(scale_ref, mine_ref, rest_ref, owners_ref, out_ref):
@@ -361,11 +400,8 @@
     feats += [shifted(feats[2], "x", 1), shifted(feats[5], "x", -1)]
 
     scalars = [logit_scale, logit_bias]
-    image_mine, image_rest = call(
-        functools.partial(pair_sums, False),
-        [((images, width), F32), ((images, width), BF)],
-        "image_sums", scalars, [image_emb, other_image, caption_image, text_emb, *text_blocks],
-        [home],
+    image_mine, image_rest = pair_call(
+        False, "image_sums", scalars, caption_image, image_emb, other_image, text_blocks, [home]
     )
     image_sent, image_rest = image_rest, shifted(image_rest, "ylo", 1)
     (send_back,) = call(
@@ -375,10 +411,8 @@
     )
     received = lax.all_to_all(send_back, REP_AXES, 0, 0, tiled=True)
 
-    text_mine, text_rest = call(
-        functools.partial(pair_sums, True),
-        [((texts, width), F32), ((texts, width), BF)],
-        "text_sums", scalars, [text_emb, other_text, caption_image, image_emb, *image_blocks],
+    text_mine, text_rest = pair_call(
+        True, "text_sums", scalars, caption_image, text_emb, other_text, image_blocks,
         [send_back, feats[3], feats[5]],
     )
     text_rest = shifted(text_rest, "ylo", 1)

time: 168 us -> 167 us (level)
    pallas_call x8 -> x6, Pallas kernels: 28.3 us -> 18.3 us  [call(): pl.pallas_call(kernel, out_shape=shapes, in_specs=[SMEM] * len(scalars) +...]
    pallas_call x0 -> x2, Pallas kernels: none -> 8.47 us  [pair_call(): pl.pallas_call(functools.partial(pair_sums, turned, len(blocks)), out_sha...]
  transfers between devices with their start and end apart: 31 -> 31, of which waited for: 13 -> 13; matrix products, arithmetic and copies ran while one was open for 3% -> 3% of each run, Pallas kernels for 12% -> 11%
where the time goes in v7:
time: 167 us; the launch traced here: 166 us
  starting transfers between devices  66.3 us (40%)
  waiting for transfers between devices  61 us (37%)
  Pallas kernels  31.8 us (19%)
  matrix products  5.11 us (3%)
  between operations  2.27 us (1%)
    ppermute x26, waiting for transfers between devices, shifted(): lax.ppermute(block, axis, [(i, (i + distance) % size) for i in range(size)])  32.8 us
    ppermute x26, starting transfers between devices, shifted(): lax.ppermute(block, axis, [(i, (i + distance) % size) for i in range(size)])  31.2 us
    pallas_call x6, Pallas kernels, call(): pl.pallas_call(kernel, out_shape=shapes, in_specs=[SMEM] * len(scalars) +...  18.3 us
    all_to_all x1, waiting for transfers between devices, per_device(): lax.all_to_all(terms.reshape(256, 8, 128), CAP_AXES + REP_AXES, 0, 0, til...  14.9 us
    all_to_all x1, waiting for transfers between devices, per_device(): lax.all_to_all(strips.reshape(groups, strip, texts), REP_AXES, 0, 0, tile...  11.8 us
    all_to_all x1, starting transfers between devices, per_device(): received = lax.all_to_all(send_back, REP_AXES, 0, 0, tiled=True)  8.5 us
    pallas_call x2, Pallas kernels, pair_call(): pl.pallas_call(functools.partial(pair_sums, turned, len(blocks)), out_sha...  8.47 us
    all_to_all x1, starting transfers between devices, per_device(): arrived = lax.all_to_all(outgoing, REP_AXES, 0, 0, tiled=True)  8.46 us
  transfers between devices with their start and end apart: 31, of which 13 were waited for; matrix products, arithmetic and copies ran while one was open for 3% of the time, Pallas kernels for 11%

profile of v7, /device:TPU:1, one launch (start us, length us, event | category | flops | bytes accessed | tf_op | source)
XLA Modules:
  0.0 166.4 jit_solution(1508598008571621947)
XLA Ops:
  0.6 5.0 %front.1 = (f32[128,1152]{1,0:T(8,128)}, f32[128,1]{1,0:T(8,128)}, bf16[16,16,1152]{2,1,0:T(8,128)(2,1)}, bf16[256,128]{1,0:T(8,128)(2,1)}, f32[128,1152]{1,0:T(...) custom-call(s32[16,96]{1,0:T(8,128)} %bitcast.18, ...), custom_call_target="tpu_custom_call" | custom-call | tf_op jit(solution)/shard_map/front/pallas_call | solution.py:367
  5.7 8.5 %all-to-all-start = ((bf16[16,16,1152]{2,1,0:T(8,128)(2,1)}), bf16[16,16,1152]{2,1,0:T(8,128)(2,1)}, u32[]{:S(2)}, u32[]{:S(2)}) async-start(bf16[16,16,1152]{2,1,0:T(8,128)(2,1)} %get-tuple-element.28), calls=%async_computation | async-start | bytes 1179648 | tf_op jit(solution)/shard_map/all_to_all | solution.py:378
  14.1 1.7 collective-permute-start.10
  16.3 3.7 %collective-permute-start.11 = (bf16[128,1152]{1,0:T(8,128)(2,1)}, bf16[128,1152]{1,0:T(8,128)(2,1)}, u32[]{:S(2)}, u32[]{:S(2)}) collective-permute-start(bf16[128,1152]{1,0:T(8,128)(2,1)} %get-tuple-element.27.refs_0_.own_far), channel_id=1, source_target_pairs={{0,112},{16,0},{32,16},{48,32},{64,48},{80,64},{96,80},{112,96},{1... | collective-permute-start | bytes 884744 | tf_op jit(solution)/shard_map/ppermute | solution.py:22
  20.0 7.2 %collective-permute-done.10.refs_1_ = bf16[128,1152]{1,0:T(8,128)(2,1)} collective-permute-done((bf16[128,1152]{1,0:T(8,128)(2,1)}, bf16[128,1152]{1,0:T(8,128)(2,1)}, u32[]{:S(2)}, u32[]{:S(2)}) %collective-permute-start.10) | collective-permute-done | bytes 294944 | tf_op jit(solution)/shard_map/ppermute | solution.py:22
  27.3 2.2 %arrive.1.own_far.refs_0_ = bf16[96,1152]{1,0:T(8,128)(2,1)} custom-call(bf16[16,16,1152]{2,1,0:T(8,128)(2,1)} %all-to-all-done.refs_0_, s32[16,96]{1,0:T(8,128)} %bitcast.19, bf16[128,1152]{1,0:T(8,128)(2,1)} %collective-permute-done.1.refs_2_.refs_1_), custom_call_target="tpu_custom_call" | custom-call | tf_op jit(solution)/shard_map/arrive/pallas_call | solution.py:63
  29.5 4.3 %collective-permute-start.2 = (bf16[96,1152]{1,0:T(8,128)(2,1)}, bf16[96,1152]{1,0:T(8,128)(2,1)}, u32[]{:S(2)}, u32[]{:S(2)}) collective-permute-start(bf16[96,1152]{1,0:T(8,128)(2,1)} %arrive.1.own_far.refs_0_), channel_id=1, source_target_pairs={{0,112},{16,0},{32,16},{48,32},{64,48},{80,64},{96,80},{112,96},{1... | collective-permute-start | bytes 663560 | tf_op jit(solution)/shard_map/ppermute | solution.py:22
  35.1 3.5 %collective-permute-start.18 = (bf16[128,1152]{1,0:T(8,128)(2,1)}, bf16[128,1152]{1,0:T(8,128)(2,1)}, u32[]{:S(2)}, u32[]{:S(2)}) collective-permute-start(bf16[128,1152]{1,0:T(8,128)(2,1)} %get-tuple-element.29), channel_id=1, source_target_pairs={{0,3},{1,2},{2,1},{3,0},{4,7},{5,6},{6,5},{7,4},{8,11},{9,10},{10,... | collective-permute-start | bytes 884744 | tf_op jit(solution)/shard_map/ppermute | solution.py:382
  38.7 2.7 %collective-permute-start.13 = (bf16[128,1152]{1,0:T(8,128)(2,1)}, bf16[128,1152]{1,0:T(8,128)(2,1)}, u32[]{:S(2)}, u32[]{:S(2)}) collective-permute-start(bf16[128,1152]{1,0:T(8,128)(2,1)} %collective-permute-done.11.refs_2_), channel_id=1, source_target_pairs={{0,112},{16,0},{32,16},{48,32},{64,48},{80,64},{96,80},{112,96},{1... | collective-permute-start | bytes 884744 | tf_op jit(solution)/shard_map/ppermute | solution.py:22
  41.3 6.3 %collective-permute-done.3.refs_2_ = bf16[96,1152]{1,0:T(8,128)(2,1)} collective-permute-done((bf16[96,1152]{1,0:T(8,128)(2,1)}, bf16[96,1152]{1,0:T(8,128)(2,1)}, u32[]{:S(2)}, u32[]{:S(2)}) %collective-permute-start.3) | collective-permute-done | bytes 221216 | tf_op jit(solution)/shard_map/ppermute | solution.py:22
  47.6 1.5 collective-permute-start.5
  49.1 1.5 collective-permute-done.18.refs_3_
  50.6 2.4 %joined.1 = (bf16[256,1152]{1,0:T(8,128)(2,1)}, bf16[256,1152]{1,0:T(8,128)(2,1)}) custom-call(bf16[128,1152]{1,0:T(8,128)(2,1)} %get-tuple-element.36.refs_0_, bf16[128,1152]{1,0:T(8,128)(2,1)} %collective-permute-done.1.refs_2_.refs_1_, bf16[128,1152]{1,0:T(8,128)(2,1)} %collective-permute-done.17.refs_2_, bf16[128,1152]{1,0:T(8,128)(2,1)} %collective-permute-done.18.refs_3_), custom_call_target="tpu_custom_call" | custom-call | tf_op jit(solution)/shard_map/joined/pallas_call | solution.py:63
  55.6 2.0 %collective-permute-done.5.refs_4_ = bf16[96,1152]{1,0:T(8,128)(2,1)} collective-permute-done((bf16[96,1152]{1,0:T(8,128)(2,1)}, bf16[96,1152]{1,0:T(8,128)(2,1)}, u32[]{:S(2)}, u32[]{:S(2)}) %collective-permute-start.5) | collective-permute-done | bytes 221216 | tf_op jit(solution)/shard_map/ppermute | solution.py:22
  59.0 2.0 %collective-permute-done.9.other_far = bf16[96,1152]{1,0:T(8,128)(2,1)} collective-permute-done((bf16[96,1152]{1,0:T(8,128)(2,1)}, bf16[96,1152]{1,0:T(8,128)(2,1)}, u32[]{:S(2)}, u32[]{:S(2)}) %collective-permute-start.9) | collective-permute-done | bytes 221216 | tf_op jit(solution)/shard_map/ppermute | solution.py:22
  61.7 1.6 collective-permute-done.15.refs_6_
  64.6 3.0 %collective-permute-start.23 = (bf16[256,1152]{1,0:T(8,128)(2,1)}, bf16[256,1152]{1,0:T(8,128)(2,1)}, u32[]{:S(2)}, u32[]{:S(2)}) collective-permute-start(bf16[256,1152]{1,0:T(8,128)(2,1)} %get-tuple-element.40.refs_2_), channel_id=1, source_target_pairs={{0,12},{4,0},{8,4},{12,8},{1,13},{5,1},{9,5},{13,9},{2,14},{6,2},{... | collective-permute-start | bytes 1769480 | tf_op jit(solution)/shard_map/ppermute | solution.py:22
  70.4 4.3 %image_sums.1 = (f32[96,1152]{1,0:T(8,128)}, bf16[96,1152]{1,0:T(8,128)(2,1)}) custom-call(f32[1]{0:T(128)S(6)} %copy.12.scale_ref.refs_0_, f32[1]{0:T(128)S(6)} %copy.13.bias_ref, s32[1,128]{1,0:T(1,128)} %targets_far.3, bf16[96,1152]{1,0:T(8,128)(2,1)} %arrive.1.own_far.refs_0_, bf16[96,1152]{1,0:T(8,128)(2,1)} %collective-permute-done.9.other_far, ...), custom_call_target="tpu_custom_call" | custom-call | tf_op jit(solution)/shard_map/image_sums/pallas_call | solution.py:245
  78.0 2.5 %collective-permute-done.19.refs_2_ = bf16[96,1152]{1,0:T(8,128)(2,1)} collective-permute-done((bf16[96,1152]{1,0:T(8,128)(2,1)}, bf16[96,1152]{1,0:T(8,128)(2,1)}, u32[]{:S(2)}, u32[]{:S(2)}) %collective-permute-start.19) | collective-permute-done | bytes 221216 | tf_op jit(solution)/shard_map/ppermute | solution.py:22
  81.3 2.4 %image_back.1.refs_8_ = bf16[16,16,1152]{2,1,0:T(8,128)(2,1)} custom-call(f32[1]{0:T(128)S(6)} %copy.12.scale_ref.refs_0_, f32[96,1152]{1,0:T(8,128)} %get-tuple-element.38.refs_1_, bf16[96,1152]{1,0:T(8,128)(2,1)} %collective-permute-done.19.refs_2_, s32[16,96]{1,0:T(8,128)} %bitcast.20, bf16[256,1152]{1,0:T(8,128)(2,1)} %collective-permute-done.20.refs_4_.refs_3_, ...), custom_call_target="tpu_custom_call" | custom-call | tf_op jit(solution)/shard_map/image_back/pallas_call | solution.py:63
  83.7 8.5 %all-to-all-start.1 = ((bf16[16,16,1152]{2,1,0:T(8,128)(2,1)}), bf16[16,16,1152]{2,1,0:T(8,128)(2,1)}, u32[]{:S(2)}, u32[]{:S(2)}) async-start(bf16[16,16,1152]{2,1,0:T(8,128)(2,1)} %image_back.1.refs_8_), calls=%async_computation.1 | async-start | bytes 1179648 | tf_op jit(solution)/shard_map/all_to_all | solution.py:412
  92.2 4.2 %text_sums.1 = (f32[128,1152]{1,0:T(8,128)}, bf16[128,1152]{1,0:T(8,128)(2,1)}) custom-call(f32[1]{0:T(128)S(6)} %copy.12.scale_ref.refs_0_, f32[1]{0:T(128)S(6)} %copy.13.bias_ref, s32[1,128]{1,0:T(1,128)} %targets_far.3, bf16[128,1152]{1,0:T(8,128)(2,1)} %get-tuple-element.27.refs_0_.own_far, bf16[128,1152]{1,0:T(8,128)(2,1)} %collective-permute-done.other_far, ...), custom_call_target="tpu_custom_call" | custom-call | tf_op jit(solution)/shard_map/text_sums/pallas_call | solution.py:245
  99.6 8.8 %collective-permute-done.24.refs_2_ = bf16[128,1152]{1,0:T(8,128)(2,1)} collective-permute-done((bf16[128,1152]{1,0:T(8,128)(2,1)}, bf16[128,1152]{1,0:T(8,128)(2,1)}, u32[]{:S(2)}, u32[]{:S(2)}) %collective-permute-start.24) | collective-permute-done | bytes 294944 | tf_op jit(solution)/shard_map/ppermute | solution.py:22
  108.4 3.5 %both_back.1 = (bf16[128,1152]{1,0:T(8,128)(2,1)}, bf16[128,1152]{1,0:T(8,128)(2,1)}, bf16[8,2,144,128]{3,2,1,0:T(8,128)(2,1)}) custom-call(f32[1]{0:T(128)S(6)} %copy.12.scale_ref.refs_0_, f32[128,1152]{1,0:T(8,128)} %get-tuple-element.41.refs_1_, bf16[128,1152]{1,0:T(8,128)(2,1)} %collective-permute-done.24.refs_2_, ...), custom_call_target="tpu_custom_call" | custom-call | tf_op jit(solution)/shard_map/both_back/pallas_call | solution.py:63
  112.0 6.3 %all-to-all-start.2 = ((bf16[16,144,128]{2,1,0:T(8,128)(2,1)}), bf16[16,144,128]{2,1,0:T(8,128)(2,1)}, u32[]{:S(2)}, u32[]{:S(2)}) async-start(bf16[16,144,128]{2,1,0:T(8,128)(2,1)} %bitcast.15), calls=%async_computation.2 | async-start | bytes 1179648 | tf_op jit(solution)/shard_map/all_to_all | solution.py:427
  118.3 11.8 %all-to-all-done.2.refs_0_ = bf16[16,144,128]{2,1,0:T(8,128)(2,1)} async-done(((bf16[16,144,128]{2,1,0:T(8,128)(2,1)}), bf16[16,144,128]{2,1,0:T(8,128)(2,1)}, u32[]{:S(2)}, u32[]{:S(2)}) %all-to-all-start.2) | async-done | bytes 589856 | tf_op jit(solution)/shard_map/all_to_all | solution.py:427
  130.0 5.3 %head_terms.1 = bf16[128,16,128]{2,1,0:T(8,128)(2,1)} custom-call(bf16[16,144,128]{2,1,0:T(8,128)(2,1)} %all-to-all-done.2.refs_0_, bf16[256,1152]{1,0:T(8,128)(2,1)} %get-tuple-element.37.refs_8_.refs_1_, bf16[256,1152]{1,0:T(8,128)(2,1)} %get-tuple-element.40.refs_2_, bf16[256,1152]{1,0:T(8,128)(2,1)} %collective-permute-done.20.refs_4_.refs_3_, ...), custom_call_target="tpu_custom_call" | custom-call | tf_op jit(solution)/shard_map/head_terms/pallas_call | solution.py:63
  135.4 8.3 %all-to-all-start.3 = ((bf16[256,8,128]{2,1,0:T(8,128)(2,1)}), bf16[256,8,128]{2,1,0:T(8,128)(2,1)}, u32[]{:S(2)}, u32[]{:S(2)}) async-start(bf16[256,8,128]{2,1,0:T(8,128)(2,1)} %bitcast.14), calls=%async_computation.3 | async-start | bytes 1048576 | tf_op jit(solution)/shard_map/all_to_all | solution.py:435
  143.7 3.5 %fusion = bf16[1,128,1152]{2,1,0:T(8,128)(2,1)} fusion(bf16[128,1152]{1,0:T(8,128)(2,1)} %get-tuple-element.48, bf16[1152,1152]{1,0:T(8,128)(2,1)} %text_head_far.1), kind=kOutput, calls=%fused_computation.2 | convolution fusion | flops 339886080 | bytes 3244032 | tf_op jit(solution)/shard_map/dot_general | solution.py:76
  147.2 1.6 fusion.1
  148.8 14.9 %all-to-all-done.3 = bf16[256,8,128]{2,1,0:T(8,128)(2,1)} async-done(((bf16[256,8,128]{2,1,0:T(8,128)(2,1)}), bf16[256,8,128]{2,1,0:T(8,128)(2,1)}, u32[]{:S(2)}, u32[]{:S(2)}) %all-to-all-start.3) | async-done | bytes 524320 | tf_op jit(solution)/shard_map/all_to_all | solution.py:435
  163.7 2.5 %head_sums.1 = f32[9,1152]{1,0:T(8,128)} custom-call(bf16[128,16,128]{2,1,0:T(8,128)(2,1)} %bitcast.7.refs_0_), custom_call_target="tpu_custom_call" | custom-call | tf_op jit(solution)/shard_map/head_sums/pallas_call | solution.py:63
  (45 shorter events, 16.7 us)
Async XLA Ops:
  5.7 21.6 %all-to-all-start = ((bf16[16,16,1152]{2,1,0:T(8,128)(2,1)}), bf16[16,16,1152]{2,1,0:T(8,128)(2,1)}, u32[]{:S(2)}, u32[]{:S(2)}) async-start(bf16[16,16,1152]{2,1,0:T(8,128)(2,1)} %get-tuple-element.28), calls=%async_computation | async-start | bytes 1179648 | tf_op jit(solution)/shard_map/all_to_all | solution.py:378
  14.1 13.1 %collective-permute-start.10 = (bf16[128,1152]{1,0:T(8,128)(2,1)}, bf16[128,1152]{1,0:T(8,128)(2,1)}, u32[]{:S(2)}, u32[]{:S(2)}) collective-permute-start(bf16[128,1152]{1,0:T(8,128)(2,1)} %get-tuple-element.27.refs_0_.own_far), channel_id=1, source_target_pairs={{0,16},{16,32},{32,48},{48,64},{64,80},{80,96},{96,112},{112,0},{1... | collective-permute-start | bytes 884744 | tf_op jit(solution)/shard_map/ppermute | solution.py:22
  15.8 11.5 %collective-permute-start.1 = (bf16[128,1152]{1,0:T(8,128)(2,1)}, bf16[128,1152]{1,0:T(8,128)(2,1)}, u32[]{:S(2)}, u32[]{:S(2)}) collective-permute-start(bf16[128,1152]{1,0:T(8,128)(2,1)} %get-tuple-element.29), channel_id=1, source_target_pairs={{0,1},{1,0},{2,3},{3,2},{4,5},{5,4},{6,7},{7,6},{8,9},{9,8},{10,11... | collective-permute-start | bytes 884744 | tf_op jit(solution)/shard_map/ppermute | solution.py:22
  16.3 22.4 %collective-permute-start.11 = (bf16[128,1152]{1,0:T(8,128)(2,1)}, bf16[128,1152]{1,0:T(8,128)(2,1)}, u32[]{:S(2)}, u32[]{:S(2)}) collective-permute-start(bf16[128,1152]{1,0:T(8,128)(2,1)} %get-tuple-element.27.refs_0_.own_far), channel_id=1, source_target_pairs={{0,112},{16,0},{32,16},{48,32},{64,48},{80,64},{96,80},{112,96},{1... | collective-permute-start | bytes 884744 | tf_op jit(solution)/shard_map/ppermute | solution.py:22
  27.3 11.4 %collective-permute-start.12 = (bf16[128,1152]{1,0:T(8,128)(2,1)}, bf16[128,1152]{1,0:T(8,128)(2,1)}, u32[]{:S(2)}, u32[]{:S(2)}) collective-permute-start(bf16[128,1152]{1,0:T(8,128)(2,1)} %collective-permute-done.10.refs_1_), channel_id=1, source_target_pairs={{0,16},{16,32},{32,48},{48,64},{64,80},{80,96},{96,112},{112,0},{1... | collective-permute-start | bytes 884744 | tf_op jit(solution)/shard_map/ppermute | solution.py:22
  29.5 11.9 %collective-permute-start.2 = (bf16[96,1152]{1,0:T(8,128)(2,1)}, bf16[96,1152]{1,0:T(8,128)(2,1)}, u32[]{:S(2)}, u32[]{:S(2)}) collective-permute-start(bf16[96,1152]{1,0:T(8,128)(2,1)} %arrive.1.own_far.refs_0_), channel_id=1, source_target_pairs={{0,112},{16,0},{32,16},{48,32},{64,48},{80,64},{96,80},{112,96},{1... | collective-permute-start | bytes 663560 | tf_op jit(solution)/shard_map/ppermute | solution.py:22
  33.7 13.9 %collective-permute-start.17 = (bf16[128,1152]{1,0:T(8,128)(2,1)}, bf16[128,1152]{1,0:T(8,128)(2,1)}, u32[]{:S(2)}, u32[]{:S(2)}) collective-permute-start(bf16[128,1152]{1,0:T(8,128)(2,1)} %get-tuple-element.36.refs_0_), channel_id=1, source_target_pairs={{0,2},{2,0},{1,3},{3,1},{4,6},{6,4},{5,7},{7,5},{8,10},{10,8},{9,1... | collective-permute-start | bytes 884744 | tf_op jit(solution)/shard_map/ppermute | solution.py:22
  35.1 15.5 %collective-permute-start.18 = (bf16[128,1152]{1,0:T(8,128)(2,1)}, bf16[128,1152]{1,0:T(8,128)(2,1)}, u32[]{:S(2)}, u32[]{:S(2)}) collective-permute-start(bf16[128,1152]{1,0:T(8,128)(2,1)} %get-tuple-element.29), channel_id=1, source_target_pairs={{0,3},{1,2},{2,1},{3,0},{4,7},{5,6},{6,5},{7,4},{8,11},{9,10},{10,... | collective-permute-start | bytes 884744 | tf_op jit(solution)/shard_map/ppermute | solution.py:382
  38.7 9.0 %collective-permute-start.3 = (bf16[96,1152]{1,0:T(8,128)(2,1)}, bf16[96,1152]{1,0:T(8,128)(2,1)}, u32[]{:S(2)}, u32[]{:S(2)}) collective-permute-start(bf16[96,1152]{1,0:T(8,128)(2,1)} %arrive.1.own_far.refs_0_), channel_id=1, source_target_pairs={{0,16},{16,32},{32,48},{48,64},{64,80},{80,96},{96,112},{112,0},{1... | collective-permute-start | bytes 663560 | tf_op jit(solution)/shard_map/ppermute | solution.py:22
  38.7 14.8 %collective-permute-start.13 = (bf16[128,1152]{1,0:T(8,128)(2,1)}, bf16[128,1152]{1,0:T(8,128)(2,1)}, u32[]{:S(2)}, u32[]{:S(2)}) collective-permute-start(bf16[128,1152]{1,0:T(8,128)(2,1)} %collective-permute-done.11.refs_2_), channel_id=1, source_target_pairs={{0,112},{16,0},{32,16},{48,32},{64,48},{80,64},{96,80},{112,96},{1... | collective-permute-start | bytes 884744 | tf_op jit(solution)/shard_map/ppermute | solution.py:22
  41.3 12.8 %collective-permute-start.14 = (bf16[128,1152]{1,0:T(8,128)(2,1)}, bf16[128,1152]{1,0:T(8,128)(2,1)}, u32[]{:S(2)}, u32[]{:S(2)}) collective-permute-start(bf16[128,1152]{1,0:T(8,128)(2,1)} %collective-permute-done.12.refs_3_), channel_id=1, source_target_pairs={{0,16},{16,32},{32,48},{48,64},{64,80},{80,96},{96,112},{112,0},{1... | collective-permute-start | bytes 884744 | tf_op jit(solution)/shard_map/ppermute | solution.py:22
  47.6 7.1 %collective-permute-start.4 = (bf16[96,1152]{1,0:T(8,128)(2,1)}, bf16[96,1152]{1,0:T(8,128)(2,1)}, u32[]{:S(2)}, u32[]{:S(2)}) collective-permute-start(bf16[96,1152]{1,0:T(8,128)(2,1)} %collective-permute-done.2.refs_1_), channel_id=1, source_target_pairs={{0,112},{16,0},{32,16},{48,32},{64,48},{80,64},{96,80},{112,96},{1... | collective-permute-start | bytes 663560 | tf_op jit(solution)/shard_map/ppermute | solution.py:22
  47.6 10.0 %collective-permute-start.5 = (bf16[96,1152]{1,0:T(8,128)(2,1)}, bf16[96,1152]{1,0:T(8,128)(2,1)}, u32[]{:S(2)}, u32[]{:S(2)}) collective-permute-start(bf16[96,1152]{1,0:T(8,128)(2,1)} %collective-permute-done.3.refs_2_), channel_id=1, source_target_pairs={{0,16},{16,32},{32,48},{48,64},{64,80},{80,96},{96,112},{112,0},{1... | collective-permute-start | bytes 663560 | tf_op jit(solution)/shard_map/ppermute | solution.py:22
  53.0 22.6 %collective-permute-start.20 = (bf16[256,1152]{1,0:T(8,128)(2,1)}, bf16[256,1152]{1,0:T(8,128)(2,1)}, u32[]{:S(2)}, u32[]{:S(2)}) collective-permute-start(bf16[256,1152]{1,0:T(8,128)(2,1)} %get-tuple-element.37.refs_8_.refs_1_), channel_id=1, source_target_pairs={{0,4},{4,8},{8,12},{12,0},{1,5},{5,9},{9,13},{13,1},{2,6},{6,10},{... | collective-permute-start | bytes 1769480 | tf_op jit(solution)/shard_map/ppermute | solution.py:22
  53.4 7.6 %collective-permute-start.9 = (bf16[96,1152]{1,0:T(8,128)(2,1)}, bf16[96,1152]{1,0:T(8,128)(2,1)}, u32[]{:S(2)}, u32[]{:S(2)}) collective-permute-start(bf16[96,1152]{1,0:T(8,128)(2,1)} %arrive.1.own_far.refs_0_), channel_id=1, source_target_pairs={{0,128},{128,0},{1,129},{129,1},{2,130},{130,2},{3,131},{131,3},{4... | collective-permute-start | bytes 663560 | tf_op jit(solution)/shard_map/ppermute | solution.py:22
  54.1 9.2 %collective-permute-start.15 = (bf16[128,1152]{1,0:T(8,128)(2,1)}, bf16[128,1152]{1,0:T(8,128)(2,1)}, u32[]{:S(2)}, u32[]{:S(2)}) collective-permute-start(bf16[128,1152]{1,0:T(8,128)(2,1)} %collective-permute-done.13.refs_4_), channel_id=1, source_target_pairs={{0,112},{16,0},{32,16},{48,32},{64,48},{80,64},{96,80},{112,96},{1... | collective-permute-start | bytes 884744 | tf_op jit(solution)/shard_map/ppermute | solution.py:22
  54.8 9.9 %collective-permute-start.16 = (bf16[128,1152]{1,0:T(8,128)(2,1)}, bf16[128,1152]{1,0:T(8,128)(2,1)}, u32[]{:S(2)}, u32[]{:S(2)}) collective-permute-start(bf16[128,1152]{1,0:T(8,128)(2,1)} %collective-permute-done.14.refs_5_), channel_id=1, source_target_pairs={{0,16},{16,32},{32,48},{48,64},{64,80},{80,96},{96,112},{112,0},{1... | collective-permute-start | bytes 884744 | tf_op jit(solution)/shard_map/ppermute | solution.py:22
  57.6 19.3 %collective-permute-start.21 = (bf16[256,1152]{1,0:T(8,128)(2,1)}, bf16[256,1152]{1,0:T(8,128)(2,1)}, u32[]{:S(2)}, u32[]{:S(2)}) collective-permute-start(bf16[256,1152]{1,0:T(8,128)(2,1)} %get-tuple-element.37.refs_8_.refs_1_), channel_id=1, source_target_pairs={{0,12},{4,0},{8,4},{12,8},{1,13},{5,1},{9,5},{13,9},{2,14},{6,2},{... | collective-permute-start | bytes 1769480 | tf_op jit(solution)/shard_map/ppermute | solution.py:22
  61.0 6.7 %collective-permute-start.6 = (bf16[96,1152]{1,0:T(8,128)(2,1)}, bf16[96,1152]{1,0:T(8,128)(2,1)}, u32[]{:S(2)}, u32[]{:S(2)}) collective-permute-start(bf16[96,1152]{1,0:T(8,128)(2,1)} %collective-permute-done.4.refs_3_), channel_id=1, source_target_pairs={{0,112},{16,0},{32,16},{48,32},{64,48},{80,64},{96,80},{112,96},{1... | collective-permute-start | bytes 663560 | tf_op jit(solution)/shard_map/ppermute | solution.py:22
  63.3 11.4 %collective-permute-start.7 = (bf16[96,1152]{1,0:T(8,128)(2,1)}, bf16[96,1152]{1,0:T(8,128)(2,1)}, u32[]{:S(2)}, u32[]{:S(2)}) collective-permute-start(bf16[96,1152]{1,0:T(8,128)(2,1)} %collective-permute-done.5.refs_4_), channel_id=1, source_target_pairs={{0,16},{16,32},{32,48},{48,64},{64,80},{80,96},{96,112},{112,0},{1... | collective-permute-start | bytes 663560 | tf_op jit(solution)/shard_map/ppermute | solution.py:22
  64.6 27.5 %collective-permute-start.23 = (bf16[256,1152]{1,0:T(8,128)(2,1)}, bf16[256,1152]{1,0:T(8,128)(2,1)}, u32[]{:S(2)}, u32[]{:S(2)}) collective-permute-start(bf16[256,1152]{1,0:T(8,128)(2,1)} %get-tuple-element.40.refs_2_), channel_id=1, source_target_pairs={{0,12},{4,0},{8,4},{12,8},{1,13},{5,1},{9,5},{13,9},{2,14},{6,2},{... | collective-permute-start | bytes 1769480 | tf_op jit(solution)/shard_map/ppermute | solution.py:22
  67.7 24.5 %collective-permute-start.22 = (bf16[256,1152]{1,0:T(8,128)(2,1)}, bf16[256,1152]{1,0:T(8,128)(2,1)}, u32[]{:S(2)}, u32[]{:S(2)}) collective-permute-start(bf16[256,1152]{1,0:T(8,128)(2,1)} %get-tuple-element.40.refs_2_), channel_id=1, source_target_pairs={{0,4},{4,8},{8,12},{12,0},{1,5},{5,9},{9,13},{13,1},{2,6},{6,10},{... | collective-permute-start | bytes 1769480 | tf_op jit(solution)/shard_map/ppermute | solution.py:22
  74.7 5.8 %collective-permute-start.19 = (bf16[96,1152]{1,0:T(8,128)(2,1)}, bf16[96,1152]{1,0:T(8,128)(2,1)}, u32[]{:S(2)}, u32[]{:S(2)}) collective-permute-start(bf16[96,1152]{1,0:T(8,128)(2,1)} %get-tuple-element.39), channel_id=1, source_target_pairs={{0,128},{128,0},{1,129},{129,1},{2,130},{130,2},{3,131},{131,3},{4... | collective-permute-start | bytes 663560 | tf_op jit(solution)/shard_map/ppermute | solution.py:22
  75.6 5.7 %collective-permute-start.8 = (bf16[96,1152]{1,0:T(8,128)(2,1)}, bf16[96,1152]{1,0:T(8,128)(2,1)}, u32[]{:S(2)}, u32[]{:S(2)}) collective-permute-start(bf16[96,1152]{1,0:T(8,128)(2,1)} %collective-permute-done.6.refs_5_), channel_id=1, source_target_pairs={{0,112},{16,0},{32,16},{48,32},{64,48},{80,64},{96,80},{112,96},{1... | collective-permute-start | bytes 663560 | tf_op jit(solution)/shard_map/ppermute | solution.py:22
  76.9 15.3 %collective-permute-start = (bf16[128,1152]{1,0:T(8,128)(2,1)}, bf16[128,1152]{1,0:T(8,128)(2,1)}, u32[]{:S(2)}, u32[]{:S(2)}) collective-permute-start(bf16[128,1152]{1,0:T(8,128)(2,1)} %get-tuple-element.27.refs_0_.own_far), channel_id=1, source_target_pairs={{0,128},{128,0},{1,129},{129,1},{2,130},{130,2},{3,131},{131,3},{4... | collective-permute-start | bytes 884744 | tf_op jit(solution)/shard_map/ppermute | solution.py:22
  83.7 24.7 %all-to-all-start.1 = ((bf16[16,16,1152]{2,1,0:T(8,128)(2,1)}), bf16[16,16,1152]{2,1,0:T(8,128)(2,1)}, u32[]{:S(2)}, u32[]{:S(2)}) async-start(bf16[16,16,1152]{2,1,0:T(8,128)(2,1)} %image_back.1.refs_8_), calls=%async_computation.1 | async-start | bytes 1179648 | tf_op jit(solution)/shard_map/all_to_all | solution.py:412
  96.4 12.0 %collective-permute-start.24 = (bf16[128,1152]{1,0:T(8,128)(2,1)}, bf16[128,1152]{1,0:T(8,128)(2,1)}, u32[]{:S(2)}, u32[]{:S(2)}) collective-permute-start(bf16[128,1152]{1,0:T(8,128)(2,1)} %get-tuple-element.42), channel_id=1, source_target_pairs={{0,128},{128,0},{1,129},{129,1},{2,130},{130,2},{3,131},{131,3},{4... | collective-permute-start | bytes 884744 | tf_op jit(solution)/shard_map/ppermute | solution.py:22
  96.9 21.3 %collective-permute-start.25 = (bf16[256,1152]{1,0:T(8,128)(2,1)}, bf16[256,1152]{1,0:T(8,128)(2,1)}, u32[]{:S(2)}, u32[]{:S(2)}) collective-permute-start(bf16[256,1152]{1,0:T(8,128)(2,1)} %collective-permute-done.20.refs_4_.refs_3_), channel_id=1, source_target_pairs={{0,4},{4,8},{8,12},{12,0},{1,5},{5,9},{9,13},{13,1},{2,6},{6,10},{... | collective-permute-start | bytes 1769480 | tf_op jit(solution)/shard_map/ppermute | solution.py:22
  98.3 20.0 %collective-permute-start.26 = (bf16[256,1152]{1,0:T(8,128)(2,1)}, bf16[256,1152]{1,0:T(8,128)(2,1)}, u32[]{:S(2)}, u32[]{:S(2)}) collective-permute-start(bf16[256,1152]{1,0:T(8,128)(2,1)} %collective-permute-done.23.refs_10_.refs_6_), channel_id=1, source_target_pairs={{0,12},{4,0},{8,4},{12,8},{1,13},{5,1},{9,5},{13,9},{2,14},{6,2},{... | collective-permute-start | bytes 1769480 | tf_op jit(solution)/shard_map/ppermute | solution.py:22
  112.0 18.1 %all-to-all-start.2 = ((bf16[16,144,128]{2,1,0:T(8,128)(2,1)}), bf16[16,144,128]{2,1,0:T(8,128)(2,1)}, u32[]{:S(2)}, u32[]{:S(2)}) async-start(bf16[16,144,128]{2,1,0:T(8,128)(2,1)} %bitcast.15), calls=%async_computation.2 | async-start | bytes 1179648 | tf_op jit(solution)/shard_map/all_to_all | solution.py:427
  135.4 11.8 %copy-start = (bf16[1152,1152]{1,0:T(8,128)(2,1)S(1)}, bf16[1152,1152]{1,0:T(8,128)(2,1)}, u32[]{:S(2)}) copy-start(bf16[1152,1152]{1,0:T(8,128)(2,1)} %image_head_far.1) | copy-start | bytes 7962628
  135.4 28.4 %all-to-all-start.3 = ((bf16[256,8,128]{2,1,0:T(8,128)(2,1)}), bf16[256,8,128]{2,1,0:T(8,128)(2,1)}, u32[]{:S(2)}, u32[]{:S(2)}) async-start(bf16[256,8,128]{2,1,0:T(8,128)(2,1)} %bitcast.14), calls=%async_computation.3 | async-start | bytes 1048576 | tf_op jit(solution)/shard_map/all_to_all | solution.py:435
  (1 other events, 11.8 us)

commit v8 on v7

--- a/solution.py
+++ b/solution.py
@@ -413,7 +413,7 @@
 
     text_mine, text_rest = pair_call(
         True, "text_sums", scalars, caption_image, text_emb, other_text, image_blocks,
-        [send_back, feats[3], feats[5]],
+        [send_back],
     )
     text_rest = shifted(text_rest, "ylo", 1)
     columns = groups // 2
@@ -423,6 +423,7 @@
         [((texts, width), BF), ((pool_rows, width), BF), ((columns, 2, strip, texts), BF)],
         "both_back", scalars[:1],
         [text_mine, text_rest, text_unit, text_norm, received, select, pool_unit, pool_norm],
+        [feats[3], feats[5]],
     )
     strips = lax.all_to_all(strips.reshape(groups, strip, texts), REP_AXES, 0, 0, tiled=True)
     text_feat_grad = dot(text_grad, text_head, 1, 1).astype(BF)

time: 167 us -> 165 us (0.988)
  waiting for transfers between devices: 61 us -> 52.1 us
  starting transfers between devices: 66.3 us -> 72.8 us
    ppermute x26, waiting for transfers between devices: 32.8 us -> 22.3 us  [shifted(): lax.ppermute(block, axis, [(i, (i + distance) % size) for i in range(size)])]
    ppermute x26, starting transfers between devices: 31.2 us -> 35 us  [shifted(): lax.ppermute(block, axis, [(i, (i + distance) % size) for i in range(size)])]
    ppermute x1, waiting for transfers between devices: 1.5 us -> 3.34 us  [per_device(): lax.ppermute(give, ('yhi', 'core'), [(i, 3 - i) for i in range(4)])]
  transfers between devices with their start and end apart: 31 -> 31, of which waited for: 13 -> 8; matrix products, arithmetic and copies ran while one was open for 3% -> 3% of each run, Pallas kernels for 11% -> 11%
where the time goes in v8:
time: 165 us; the launch traced here: 164 us
  starting transfers between devices  72.8 us (44%)
  waiting for transfers between devices  52.1 us (32%)
  Pallas kernels  31.7 us (19%)
  matrix products  5.11 us (3%)
  between operations  2.26 us (1%)
    ppermute x26, starting transfers between devices, shifted(): lax.ppermute(block, axis, [(i, (i + distance) % size) for i in range(size)])  35 us
    ppermute x26, waiting for transfers between devices, shifted(): lax.ppermute(block, axis, [(i, (i + distance) % size) for i in range(size)])  22.3 us
    pallas_call x6, Pallas kernels, call(): pl.pallas_call(kernel, out_shape=shapes, in_specs=[SMEM] * len(scalars) +...  18.2 us
    all_to_all x1, waiting for transfers between devices, per_device(): lax.all_to_all(terms.reshape(256, 8, 128), CAP_AXES + REP_AXES, 0, 0, til...  14.8 us
    all_to_all x1, waiting for transfers between devices, per_device(): lax.all_to_all(strips.reshape(groups, strip, texts), REP_AXES, 0, 0, tile...  11.8 us
    all_to_all x1, starting transfers between devices, per_device(): received = lax.all_to_all(send_back, REP_AXES, 0, 0, tiled=True)  9.83 us
    all_to_all x1, starting transfers between devices, per_device(): lax.all_to_all(terms.reshape(256, 8, 128), CAP_AXES + REP_AXES, 0, 0, til...  9.04 us
    pallas_call x2, Pallas kernels, pair_call(): pl.pallas_call(functools.partial(pair_sums, turned, len(blocks)), out_sha...  8.46 us
  transfers between devices with their start and end apart: 31, of which 8 were waited for; matrix products, arithmetic and copies ran while one was open for 3% of the time, Pallas kernels for 11%

profile of v8, /device:TPU:1, one launch (start us, length us, event | category | flops | bytes accessed | tf_op | source)
XLA Modules:
  0.0 164.0 jit_solution(9495516491570366586)
XLA Ops:
  0.6 5.0 %front.1 = (f32[128,1152]{1,0:T(8,128)}, f32[128,1]{1,0:T(8,128)}, bf16[16,16,1152]{2,1,0:T(8,128)(2,1)}, bf16[256,128]{1,0:T(8,128)(2,1)}, f32[128,1152]{1,0:T(...) custom-call(s32[16,96]{1,0:T(8,128)} %bitcast.18, ...), custom_call_target="tpu_custom_call" | custom-call | tf_op jit(solution)/shard_map/front/pallas_call | solution.py:367
  5.7 8.5 %all-to-all-start = ((bf16[16,16,1152]{2,1,0:T(8,128)(2,1)}), bf16[16,16,1152]{2,1,0:T(8,128)(2,1)}, u32[]{:S(2)}, u32[]{:S(2)}) async-start(bf16[16,16,1152]{2,1,0:T(8,128)(2,1)} %get-tuple-element.28), calls=%async_computation | async-start | bytes 1179648 | tf_op jit(solution)/shard_map/all_to_all | solution.py:378
  14.1 1.7 %collective-permute-start.10 = (bf16[128,1152]{1,0:T(8,128)(2,1)}, bf16[128,1152]{1,0:T(8,128)(2,1)}, u32[]{:S(2)}, u32[]{:S(2)}) collective-permute-start(bf16[128,1152]{1,0:T(8,128)(2,1)} %get-tuple-element.27.refs_0_.own_far), channel_id=1, source_target_pairs={{0,16},{16,32},{32,48},{48,64},{64,80},{80,96},{96,112},{112,0},{1... | collective-permute-start | bytes 884744 | tf_op jit(solution)/shard_map/ppermute | solution.py:22
  16.3 3.7 %collective-permute-start.11 = (bf16[128,1152]{1,0:T(8,128)(2,1)}, bf16[128,1152]{1,0:T(8,128)(2,1)}, u32[]{:S(2)}, u32[]{:S(2)}) collective-permute-start(bf16[128,1152]{1,0:T(8,128)(2,1)} %get-tuple-element.27.refs_0_.own_far), channel_id=1, source_target_pairs={{0,112},{16,0},{32,16},{48,32},{64,48},{80,64},{96,80},{112,96},{1... | collective-permute-start | bytes 884744 | tf_op jit(solution)/shard_map/ppermute | solution.py:22
  20.0 7.2 %collective-permute-done.10.refs_1_ = bf16[128,1152]{1,0:T(8,128)(2,1)} collective-permute-done((bf16[128,1152]{1,0:T(8,128)(2,1)}, bf16[128,1152]{1,0:T(8,128)(2,1)}, u32[]{:S(2)}, u32[]{:S(2)}) %collective-permute-start.10) | collective-permute-done | bytes 294944 | tf_op jit(solution)/shard_map/ppermute | solution.py:22
  27.3 2.2 %arrive.1.own_far.refs_0_ = bf16[96,1152]{1,0:T(8,128)(2,1)} custom-call(bf16[16,16,1152]{2,1,0:T(8,128)(2,1)} %all-to-all-done.refs_0_, s32[16,96]{1,0:T(8,128)} %bitcast.19, bf16[128,1152]{1,0:T(8,128)(2,1)} %collective-permute-done.1.refs_2_.refs_1_), custom_call_target="tpu_custom_call" | custom-call | tf_op jit(solution)/shard_map/arrive/pallas_call | solution.py:63
  29.5 4.3 %collective-permute-start.2 = (bf16[96,1152]{1,0:T(8,128)(2,1)}, bf16[96,1152]{1,0:T(8,128)(2,1)}, u32[]{:S(2)}, u32[]{:S(2)}) collective-permute-start(bf16[96,1152]{1,0:T(8,128)(2,1)} %arrive.1.own_far.refs_0_), channel_id=1, source_target_pairs={{0,112},{16,0},{32,16},{48,32},{64,48},{80,64},{96,80},{112,96},{1... | collective-permute-start | bytes 663560 | tf_op jit(solution)/shard_map/ppermute | solution.py:22
  35.1 2.7 %collective-permute-start.13 = (bf16[128,1152]{1,0:T(8,128)(2,1)}, bf16[128,1152]{1,0:T(8,128)(2,1)}, u32[]{:S(2)}, u32[]{:S(2)}) collective-permute-start(bf16[128,1152]{1,0:T(8,128)(2,1)} %collective-permute-done.11.refs_2_), channel_id=1, source_target_pairs={{0,112},{16,0},{32,16},{48,32},{64,48},{80,64},{96,80},{112,96},{1... | collective-permute-start | bytes 884744 | tf_op jit(solution)/shard_map/ppermute | solution.py:22
  37.8 4.1 %collective-permute-start.18 = (bf16[128,1152]{1,0:T(8,128)(2,1)}, bf16[128,1152]{1,0:T(8,128)(2,1)}, u32[]{:S(2)}, u32[]{:S(2)}) collective-permute-start(bf16[128,1152]{1,0:T(8,128)(2,1)} %get-tuple-element.29), channel_id=1, source_target_pairs={{0,3},{1,2},{2,1},{3,0},{4,7},{5,6},{6,5},{7,4},{8,11},{9,10},{10,... | collective-permute-start | bytes 884744 | tf_op jit(solution)/shard_map/ppermute | solution.py:382
  42.0 2.7 %collective-permute-start.4 = (bf16[96,1152]{1,0:T(8,128)(2,1)}, bf16[96,1152]{1,0:T(8,128)(2,1)}, u32[]{:S(2)}, u32[]{:S(2)}) collective-permute-start(bf16[96,1152]{1,0:T(8,128)(2,1)} %collective-permute-done.2.refs_1_), channel_id=1, source_target_pairs={{0,112},{16,0},{32,16},{48,32},{64,48},{80,64},{96,80},{112,96},{1... | collective-permute-start | bytes 663560 | tf_op jit(solution)/shard_map/ppermute | solution.py:22
  44.7 2.7 %collective-permute-start.15 = (bf16[128,1152]{1,0:T(8,128)(2,1)}, bf16[128,1152]{1,0:T(8,128)(2,1)}, u32[]{:S(2)}, u32[]{:S(2)}) collective-permute-start(bf16[128,1152]{1,0:T(8,128)(2,1)} %collective-permute-done.13.refs_4_), channel_id=1, source_target_pairs={{0,112},{16,0},{32,16},{48,32},{64,48},{80,64},{96,80},{112,96},{1... | collective-permute-start | bytes 884744 | tf_op jit(solution)/shard_map/ppermute | solution.py:22
  47.4 3.3 %collective-permute-done.18.refs_3_ = bf16[128,1152]{1,0:T(8,128)(2,1)} collective-permute-done((bf16[128,1152]{1,0:T(8,128)(2,1)}, bf16[128,1152]{1,0:T(8,128)(2,1)}, u32[]{:S(2)}, u32[]{:S(2)}) %collective-permute-start.18) | collective-permute-done | bytes 294944 | tf_op jit(solution)/shard_map/ppermute | solution.py:382
  51.3 2.3 %joined.1 = (bf16[256,1152]{1,0:T(8,128)(2,1)}, bf16[256,1152]{1,0:T(8,128)(2,1)}) custom-call(bf16[128,1152]{1,0:T(8,128)(2,1)} %get-tuple-element.36.refs_0_, bf16[128,1152]{1,0:T(8,128)(2,1)} %collective-permute-done.1.refs_2_.refs_1_, bf16[128,1152]{1,0:T(8,128)(2,1)} %collective-permute-done.17.refs_2_, bf16[128,1152]{1,0:T(8,128)(2,1)} %collective-permute-done.18.refs_3_), custom_call_target="tpu_custom_call" | custom-call | tf_op jit(solution)/shard_map/joined/pallas_call | solution.py:63
  54.0 2.4 %collective-permute-start.21 = (bf16[256,1152]{1,0:T(8,128)(2,1)}, bf16[256,1152]{1,0:T(8,128)(2,1)}, u32[]{:S(2)}, u32[]{:S(2)}) collective-permute-start(bf16[256,1152]{1,0:T(8,128)(2,1)} %get-tuple-element.37.refs_8_.refs_1_), channel_id=1, source_target_pairs={{0,12},{4,0},{8,4},{12,8},{1,13},{5,1},{9,5},{13,9},{2,14},{6,2},{... | collective-permute-start | bytes 1769480 | tf_op jit(solution)/shard_map/ppermute | solution.py:22
  57.6 2.9 %collective-permute-start.6 = (bf16[96,1152]{1,0:T(8,128)(2,1)}, bf16[96,1152]{1,0:T(8,128)(2,1)}, u32[]{:S(2)}, u32[]{:S(2)}) collective-permute-start(bf16[96,1152]{1,0:T(8,128)(2,1)} %collective-permute-done.4.refs_3_), channel_id=1, source_target_pairs={{0,112},{16,0},{32,16},{48,32},{64,48},{80,64},{96,80},{112,96},{1... | collective-permute-start | bytes 663560 | tf_op jit(solution)/shard_map/ppermute | solution.py:22
  61.8 3.6 %collective-permute-done.16.refs_7_ = bf16[128,1152]{1,0:T(8,128)(2,1)} collective-permute-done((bf16[128,1152]{1,0:T(8,128)(2,1)}, bf16[128,1152]{1,0:T(8,128)(2,1)}, u32[]{:S(2)}, u32[]{:S(2)}) %collective-permute-start.16) | collective-permute-done | bytes 294944 | tf_op jit(solution)/shard_map/ppermute | solution.py:22
  65.4 4.3 %image_sums.1 = (f32[96,1152]{1,0:T(8,128)}, bf16[96,1152]{1,0:T(8,128)(2,1)}) custom-call(f32[1]{0:T(128)S(6)} %copy.12.scale_ref.refs_0_, f32[1]{0:T(128)S(6)} %copy.13.bias_ref, s32[1,128]{1,0:T(1,128)} %targets_far.3, bf16[96,1152]{1,0:T(8,128)(2,1)} %arrive.1.own_far.refs_0_, bf16[96,1152]{1,0:T(8,128)(2,1)} %collective-permute-done.9.other_far, ...), custom_call_target="tpu_custom_call" | custom-call | tf_op jit(solution)/shard_map/image_sums/pallas_call | solution.py:245
  70.5 2.8 %collective-permute-start.8 = (bf16[96,1152]{1,0:T(8,128)(2,1)}, bf16[96,1152]{1,0:T(8,128)(2,1)}, u32[]{:S(2)}, u32[]{:S(2)}) collective-permute-start(bf16[96,1152]{1,0:T(8,128)(2,1)} %collective-permute-done.6.refs_5_), channel_id=1, source_target_pairs={{0,112},{16,0},{32,16},{48,32},{64,48},{80,64},{96,80},{112,96},{1... | collective-permute-start | bytes 663560 | tf_op jit(solution)/shard_map/ppermute | solution.py:22
  74.3 1.5 collective-permute-start.23
  77.1 2.3 %image_back.1.refs_8_ = bf16[16,16,1152]{2,1,0:T(8,128)(2,1)} custom-call(f32[1]{0:T(128)S(6)} %copy.12.scale_ref.refs_0_, f32[96,1152]{1,0:T(8,128)} %get-tuple-element.38.refs_1_, bf16[96,1152]{1,0:T(8,128)(2,1)} %collective-permute-done.19.refs_2_, s32[16,96]{1,0:T(8,128)} %bitcast.20, bf16[256,1152]{1,0:T(8,128)(2,1)} %collective-permute-done.20.refs_4_.refs_3_, ...), custom_call_target="tpu_custom_call" | custom-call | tf_op jit(solution)/shard_map/image_back/pallas_call | solution.py:63
  79.4 9.8 %all-to-all-start.1 = ((bf16[16,16,1152]{2,1,0:T(8,128)(2,1)}), bf16[16,16,1152]{2,1,0:T(8,128)(2,1)}, u32[]{:S(2)}, u32[]{:S(2)}) async-start(bf16[16,16,1152]{2,1,0:T(8,128)(2,1)} %image_back.1.refs_8_), calls=%async_computation.1 | async-start | bytes 1179648 | tf_op jit(solution)/shard_map/all_to_all | solution.py:412
  89.3 4.2 %text_sums.1 = (f32[128,1152]{1,0:T(8,128)}, bf16[128,1152]{1,0:T(8,128)(2,1)}) custom-call(f32[1]{0:T(128)S(6)} %copy.12.scale_ref.refs_0_, f32[1]{0:T(128)S(6)} %copy.13.bias_ref, s32[1,128]{1,0:T(1,128)} %targets_far.3, bf16[128,1152]{1,0:T(8,128)(2,1)} %get-tuple-element.27.refs_0_.own_far, bf16[128,1152]{1,0:T(8,128)(2,1)} %collective-permute-done.other_far, ...), custom_call_target="tpu_custom_call" | custom-call | tf_op jit(solution)/shard_map/text_sums/pallas_call | solution.py:245
  96.6 8.8 %collective-permute-done.22.refs_2_ = bf16[128,1152]{1,0:T(8,128)(2,1)} collective-permute-done((bf16[128,1152]{1,0:T(8,128)(2,1)}, bf16[128,1152]{1,0:T(8,128)(2,1)}, u32[]{:S(2)}, u32[]{:S(2)}) %collective-permute-start.22) | collective-permute-done | bytes 294944 | tf_op jit(solution)/shard_map/ppermute | solution.py:22
  105.5 3.5 %both_back.1 = (bf16[128,1152]{1,0:T(8,128)(2,1)}, bf16[128,1152]{1,0:T(8,128)(2,1)}, bf16[8,2,144,128]{3,2,1,0:T(8,128)(2,1)}) custom-call(f32[1]{0:T(128)S(6)} %copy.12.scale_ref.refs_0_, f32[128,1152]{1,0:T(8,128)} %get-tuple-element.40.refs_1_, bf16[128,1152]{1,0:T(8,128)(2,1)} %collective-permute-done.22.refs_2_, ...), custom_call_target="tpu_custom_call" | custom-call | tf_op jit(solution)/shard_map/both_back/pallas_call | solution.py:63
  109.0 6.3 %all-to-all-start.2 = ((bf16[16,144,128]{2,1,0:T(8,128)(2,1)}), bf16[16,144,128]{2,1,0:T(8,128)(2,1)}, u32[]{:S(2)}, u32[]{:S(2)}) async-start(bf16[16,144,128]{2,1,0:T(8,128)(2,1)} %bitcast.15), calls=%async_computation.2 | async-start | bytes 1179648 | tf_op jit(solution)/shard_map/all_to_all | solution.py:428
  115.3 11.8 %all-to-all-done.2.refs_0_ = bf16[16,144,128]{2,1,0:T(8,128)(2,1)} async-done(((bf16[16,144,128]{2,1,0:T(8,128)(2,1)}), bf16[16,144,128]{2,1,0:T(8,128)(2,1)}, u32[]{:S(2)}, u32[]{:S(2)}) %all-to-all-start.2) | async-done | bytes 589856 | tf_op jit(solution)/shard_map/all_to_all | solution.py:428
  127.0 5.4 %head_terms.1 = bf16[128,16,128]{2,1,0:T(8,128)(2,1)} custom-call(bf16[16,144,128]{2,1,0:T(8,128)(2,1)} %all-to-all-done.2.refs_0_, bf16[256,1152]{1,0:T(8,128)(2,1)} %get-tuple-element.37.refs_8_.refs_1_, bf16[256,1152]{1,0:T(8,128)(2,1)} %get-tuple-element.47.refs_2_, bf16[256,1152]{1,0:T(8,128)(2,1)} %collective-permute-done.20.refs_4_.refs_3_, ...), custom_call_target="tpu_custom_call" | custom-call | tf_op jit(solution)/shard_map/head_terms/pallas_call | solution.py:63
  132.4 9.0 %all-to-all-start.3 = ((bf16[256,8,128]{2,1,0:T(8,128)(2,1)}), bf16[256,8,128]{2,1,0:T(8,128)(2,1)}, u32[]{:S(2)}, u32[]{:S(2)}) async-start(bf16[256,8,128]{2,1,0:T(8,128)(2,1)} %bitcast.14), calls=%async_computation.3 | async-start | bytes 1048576 | tf_op jit(solution)/shard_map/all_to_all | solution.py:436
  141.4 3.5 %fusion = bf16[1,128,1152]{2,1,0:T(8,128)(2,1)} fusion(bf16[128,1152]{1,0:T(8,128)(2,1)} %get-tuple-element.48, bf16[1152,1152]{1,0:T(8,128)(2,1)} %text_head_far.1), kind=kOutput, calls=%fused_computation.2 | convolution fusion | flops 339886080 | bytes 3244032 | tf_op jit(solution)/shard_map/dot_general | solution.py:76
  144.9 1.6 fusion.1
  146.6 14.8 %all-to-all-done.3 = bf16[256,8,128]{2,1,0:T(8,128)(2,1)} async-done(((bf16[256,8,128]{2,1,0:T(8,128)(2,1)}), bf16[256,8,128]{2,1,0:T(8,128)(2,1)}, u32[]{:S(2)}, u32[]{:S(2)}) %all-to-all-start.3) | async-done | bytes 524320 | tf_op jit(solution)/shard_map/all_to_all | solution.py:436
  161.3 2.5 %head_sums.1 = f32[9,1152]{1,0:T(8,128)} custom-call(bf16[128,16,128]{2,1,0:T(8,128)(2,1)} %bitcast.7.refs_0_), custom_call_target="tpu_custom_call" | custom-call | tf_op jit(solution)/shard_map/head_sums/pallas_call | solution.py:63
  (45 shorter events, 10.3 us)
Async XLA Ops:
  5.7 21.6 %all-to-all-start = ((bf16[16,16,1152]{2,1,0:T(8,128)(2,1)}), bf16[16,16,1152]{2,1,0:T(8,128)(2,1)}, u32[]{:S(2)}, u32[]{:S(2)}) async-start(bf16[16,16,1152]{2,1,0:T(8,128)(2,1)} %get-tuple-element.28), calls=%async_computation | async-start | bytes 1179648 | tf_op jit(solution)/shard_map/all_to_all | solution.py:378
  14.1 13.1 %collective-permute-start.10 = (bf16[128,1152]{1,0:T(8,128)(2,1)}, bf16[128,1152]{1,0:T(8,128)(2,1)}, u32[]{:S(2)}, u32[]{:S(2)}) collective-permute-start(bf16[128,1152]{1,0:T(8,128)(2,1)} %get-tuple-element.27.refs_0_.own_far), channel_id=1, source_target_pairs={{0,16},{16,32},{32,48},{48,64},{64,80},{80,96},{96,112},{112,0},{1... | collective-permute-start | bytes 884744 | tf_op jit(solution)/shard_map/ppermute | solution.py:22
  15.8 11.5 %collective-permute-start.1 = (bf16[128,1152]{1,0:T(8,128)(2,1)}, bf16[128,1152]{1,0:T(8,128)(2,1)}, u32[]{:S(2)}, u32[]{:S(2)}) collective-permute-start(bf16[128,1152]{1,0:T(8,128)(2,1)} %get-tuple-element.29), channel_id=1, source_target_pairs={{0,1},{1,0},{2,3},{3,2},{4,5},{5,4},{6,7},{7,6},{8,9},{9,8},{10,11... | collective-permute-start | bytes 884744 | tf_op jit(solution)/shard_map/ppermute | solution.py:22
  16.3 18.8 %collective-permute-start.11 = (bf16[128,1152]{1,0:T(8,128)(2,1)}, bf16[128,1152]{1,0:T(8,128)(2,1)}, u32[]{:S(2)}, u32[]{:S(2)}) collective-permute-start(bf16[128,1152]{1,0:T(8,128)(2,1)} %get-tuple-element.27.refs_0_.own_far), channel_id=1, source_target_pairs={{0,112},{16,0},{32,16},{48,32},{64,48},{80,64},{96,80},{112,96},{1... | collective-permute-start | bytes 884744 | tf_op jit(solution)/shard_map/ppermute | solution.py:22
  27.3 10.5 %collective-permute-start.12 = (bf16[128,1152]{1,0:T(8,128)(2,1)}, bf16[128,1152]{1,0:T(8,128)(2,1)}, u32[]{:S(2)}, u32[]{:S(2)}) collective-permute-start(bf16[128,1152]{1,0:T(8,128)(2,1)} %collective-permute-done.10.refs_1_), channel_id=1, source_target_pairs={{0,16},{16,32},{32,48},{48,64},{64,80},{80,96},{96,112},{112,0},{1... | collective-permute-start | bytes 884744 | tf_op jit(solution)/shard_map/ppermute | solution.py:22
  29.5 12.5 %collective-permute-start.2 = (bf16[96,1152]{1,0:T(8,128)(2,1)}, bf16[96,1152]{1,0:T(8,128)(2,1)}, u32[]{:S(2)}, u32[]{:S(2)}) collective-permute-start(bf16[96,1152]{1,0:T(8,128)(2,1)} %arrive.1.own_far.refs_0_), channel_id=1, source_target_pairs={{0,112},{16,0},{32,16},{48,32},{64,48},{80,64},{96,80},{112,96},{1... | collective-permute-start | bytes 663560 | tf_op jit(solution)/shard_map/ppermute | solution.py:22
  33.7 8.2 %collective-permute-start.3 = (bf16[96,1152]{1,0:T(8,128)(2,1)}, bf16[96,1152]{1,0:T(8,128)(2,1)}, u32[]{:S(2)}, u32[]{:S(2)}) collective-permute-start(bf16[96,1152]{1,0:T(8,128)(2,1)} %arrive.1.own_far.refs_0_), channel_id=1, source_target_pairs={{0,16},{16,32},{32,48},{48,64},{64,80},{80,96},{96,112},{112,0},{1... | collective-permute-start | bytes 663560 | tf_op jit(solution)/shard_map/ppermute | solution.py:22
  33.7 10.9 %collective-permute-start.17 = (bf16[128,1152]{1,0:T(8,128)(2,1)}, bf16[128,1152]{1,0:T(8,128)(2,1)}, u32[]{:S(2)}, u32[]{:S(2)}) collective-permute-start(bf16[128,1152]{1,0:T(8,128)(2,1)} %get-tuple-element.36.refs_0_), channel_id=1, source_target_pairs={{0,2},{2,0},{1,3},{3,1},{4,6},{6,4},{5,7},{7,5},{8,10},{10,8},{9,1... | collective-permute-start | bytes 884744 | tf_op jit(solution)/shard_map/ppermute | solution.py:22
  35.1 9.5 %collective-permute-start.13 = (bf16[128,1152]{1,0:T(8,128)(2,1)}, bf16[128,1152]{1,0:T(8,128)(2,1)}, u32[]{:S(2)}, u32[]{:S(2)}) collective-permute-start(bf16[128,1152]{1,0:T(8,128)(2,1)} %collective-permute-done.11.refs_2_), channel_id=1, source_target_pairs={{0,112},{16,0},{32,16},{48,32},{64,48},{80,64},{96,80},{112,96},{1... | collective-permute-start | bytes 884744 | tf_op jit(solution)/shard_map/ppermute | solution.py:22
  37.8 12.9 %collective-permute-start.18 = (bf16[128,1152]{1,0:T(8,128)(2,1)}, bf16[128,1152]{1,0:T(8,128)(2,1)}, u32[]{:S(2)}, u32[]{:S(2)}) collective-permute-start(bf16[128,1152]{1,0:T(8,128)(2,1)} %get-tuple-element.29), channel_id=1, source_target_pairs={{0,3},{1,2},{2,1},{3,0},{4,7},{5,6},{6,5},{7,4},{8,11},{9,10},{10,... | collective-permute-start | bytes 884744 | tf_op jit(solution)/shard_map/ppermute | solution.py:382
  42.0 11.7 %collective-permute-start.14 = (bf16[128,1152]{1,0:T(8,128)(2,1)}, bf16[128,1152]{1,0:T(8,128)(2,1)}, u32[]{:S(2)}, u32[]{:S(2)}) collective-permute-start(bf16[128,1152]{1,0:T(8,128)(2,1)} %collective-permute-done.12.refs_3_), channel_id=1, source_target_pairs={{0,16},{16,32},{32,48},{48,64},{64,80},{80,96},{96,112},{112,0},{1... | collective-permute-start | bytes 884744 | tf_op jit(solution)/shard_map/ppermute | solution.py:22
  42.0 12.0 %collective-permute-start.4 = (bf16[96,1152]{1,0:T(8,128)(2,1)}, bf16[96,1152]{1,0:T(8,128)(2,1)}, u32[]{:S(2)}, u32[]{:S(2)}) collective-permute-start(bf16[96,1152]{1,0:T(8,128)(2,1)} %collective-permute-done.2.refs_1_), channel_id=1, source_target_pairs={{0,112},{16,0},{32,16},{48,32},{64,48},{80,64},{96,80},{112,96},{1... | collective-permute-start | bytes 663560 | tf_op jit(solution)/shard_map/ppermute | solution.py:22
  44.6 11.8 %collective-permute-start.5 = (bf16[96,1152]{1,0:T(8,128)(2,1)}, bf16[96,1152]{1,0:T(8,128)(2,1)}, u32[]{:S(2)}, u32[]{:S(2)}) collective-permute-start(bf16[96,1152]{1,0:T(8,128)(2,1)} %collective-permute-done.3.refs_2_), channel_id=1, source_target_pairs={{0,16},{16,32},{32,48},{48,64},{64,80},{80,96},{96,112},{112,0},{1... | collective-permute-start | bytes 663560 | tf_op jit(solution)/shard_map/ppermute | solution.py:22
  44.7 15.8 %collective-permute-start.15 = (bf16[128,1152]{1,0:T(8,128)(2,1)}, bf16[128,1152]{1,0:T(8,128)(2,1)}, u32[]{:S(2)}, u32[]{:S(2)}) collective-permute-start(bf16[128,1152]{1,0:T(8,128)(2,1)} %collective-permute-done.13.refs_4_), channel_id=1, source_target_pairs={{0,112},{16,0},{32,16},{48,32},{64,48},{80,64},{96,80},{112,96},{1... | collective-permute-start | bytes 884744 | tf_op jit(solution)/shard_map/ppermute | solution.py:22
  50.7 6.9 %collective-permute-start.9 = (bf16[96,1152]{1,0:T(8,128)(2,1)}, bf16[96,1152]{1,0:T(8,128)(2,1)}, u32[]{:S(2)}, u32[]{:S(2)}) collective-permute-start(bf16[96,1152]{1,0:T(8,128)(2,1)} %arrive.1.own_far.refs_0_), channel_id=1, source_target_pairs={{0,128},{128,0},{1,129},{129,1},{2,130},{130,2},{3,131},{131,3},{4... | collective-permute-start | bytes 663560 | tf_op jit(solution)/shard_map/ppermute | solution.py:22
  53.7 19.6 %collective-permute-start.20 = (bf16[256,1152]{1,0:T(8,128)(2,1)}, bf16[256,1152]{1,0:T(8,128)(2,1)}, u32[]{:S(2)}, u32[]{:S(2)}) collective-permute-start(bf16[256,1152]{1,0:T(8,128)(2,1)} %get-tuple-element.37.refs_8_.refs_1_), channel_id=1, source_target_pairs={{0,4},{4,8},{8,12},{12,0},{1,5},{5,9},{9,13},{13,1},{2,6},{6,10},{... | collective-permute-start | bytes 1769480 | tf_op jit(solution)/shard_map/ppermute | solution.py:22
  54.0 20.3 %collective-permute-start.21 = (bf16[256,1152]{1,0:T(8,128)(2,1)}, bf16[256,1152]{1,0:T(8,128)(2,1)}, u32[]{:S(2)}, u32[]{:S(2)}) collective-permute-start(bf16[256,1152]{1,0:T(8,128)(2,1)} %get-tuple-element.37.refs_8_.refs_1_), channel_id=1, source_target_pairs={{0,12},{4,0},{8,4},{12,8},{1,13},{5,1},{9,5},{13,9},{2,14},{6,2},{... | collective-permute-start | bytes 1769480 | tf_op jit(solution)/shard_map/ppermute | solution.py:22
  56.4 9.0 %collective-permute-start.16 = (bf16[128,1152]{1,0:T(8,128)(2,1)}, bf16[128,1152]{1,0:T(8,128)(2,1)}, u32[]{:S(2)}, u32[]{:S(2)}) collective-permute-start(bf16[128,1152]{1,0:T(8,128)(2,1)} %collective-permute-done.14.refs_5_), channel_id=1, source_target_pairs={{0,16},{16,32},{32,48},{48,64},{64,80},{80,96},{96,112},{112,0},{1... | collective-permute-start | bytes 884744 | tf_op jit(solution)/shard_map/ppermute | solution.py:22
  57.6 12.8 %collective-permute-start.6 = (bf16[96,1152]{1,0:T(8,128)(2,1)}, bf16[96,1152]{1,0:T(8,128)(2,1)}, u32[]{:S(2)}, u32[]{:S(2)}) collective-permute-start(bf16[96,1152]{1,0:T(8,128)(2,1)} %collective-permute-done.4.refs_3_), channel_id=1, source_target_pairs={{0,112},{16,0},{32,16},{48,32},{64,48},{80,64},{96,80},{112,96},{1... | collective-permute-start | bytes 663560 | tf_op jit(solution)/shard_map/ppermute | solution.py:22
  60.5 9.9 %collective-permute-start.7 = (bf16[96,1152]{1,0:T(8,128)(2,1)}, bf16[96,1152]{1,0:T(8,128)(2,1)}, u32[]{:S(2)}, u32[]{:S(2)}) collective-permute-start(bf16[96,1152]{1,0:T(8,128)(2,1)} %collective-permute-done.5.refs_4_), channel_id=1, source_target_pairs={{0,16},{16,32},{32,48},{48,64},{64,80},{80,96},{96,112},{112,0},{1... | collective-permute-start | bytes 663560 | tf_op jit(solution)/shard_map/ppermute | solution.py:22
  69.7 6.1 %collective-permute-start.19 = (bf16[96,1152]{1,0:T(8,128)(2,1)}, bf16[96,1152]{1,0:T(8,128)(2,1)}, u32[]{:S(2)}, u32[]{:S(2)}) collective-permute-start(bf16[96,1152]{1,0:T(8,128)(2,1)} %get-tuple-element.39), channel_id=1, source_target_pairs={{0,128},{128,0},{1,129},{129,1},{2,130},{130,2},{3,131},{131,3},{4... | collective-permute-start | bytes 663560 | tf_op jit(solution)/shard_map/ppermute | solution.py:22
  70.5 6.6 %collective-permute-start.8 = (bf16[96,1152]{1,0:T(8,128)(2,1)}, bf16[96,1152]{1,0:T(8,128)(2,1)}, u32[]{:S(2)}, u32[]{:S(2)}) collective-permute-start(bf16[96,1152]{1,0:T(8,128)(2,1)} %collective-permute-done.6.refs_5_), channel_id=1, source_target_pairs={{0,112},{16,0},{32,16},{48,32},{64,48},{80,64},{96,80},{112,96},{1... | collective-permute-start | bytes 663560 | tf_op jit(solution)/shard_map/ppermute | solution.py:22
  73.3 22.0 %collective-permute-start.24 = (bf16[256,1152]{1,0:T(8,128)(2,1)}, bf16[256,1152]{1,0:T(8,128)(2,1)}, u32[]{:S(2)}, u32[]{:S(2)}) collective-permute-start(bf16[256,1152]{1,0:T(8,128)(2,1)} %get-tuple-element.47.refs_2_), channel_id=1, source_target_pairs={{0,12},{4,0},{8,4},{12,8},{1,13},{5,1},{9,5},{13,9},{2,14},{6,2},{... | collective-permute-start | bytes 1769480 | tf_op jit(solution)/shard_map/ppermute | solution.py:22
  73.3 16.0 %collective-permute-start = (bf16[128,1152]{1,0:T(8,128)(2,1)}, bf16[128,1152]{1,0:T(8,128)(2,1)}, u32[]{:S(2)}, u32[]{:S(2)}) collective-permute-start(bf16[128,1152]{1,0:T(8,128)(2,1)} %get-tuple-element.27.refs_0_.own_far), channel_id=1, source_target_pairs={{0,128},{128,0},{1,129},{129,1},{2,130},{130,2},{3,131},{131,3},{4... | collective-permute-start | bytes 884744 | tf_op jit(solution)/shard_map/ppermute | solution.py:22
  74.3 22.3 %collective-permute-start.23 = (bf16[256,1152]{1,0:T(8,128)(2,1)}, bf16[256,1152]{1,0:T(8,128)(2,1)}, u32[]{:S(2)}, u32[]{:S(2)}) collective-permute-start(bf16[256,1152]{1,0:T(8,128)(2,1)} %get-tuple-element.47.refs_2_), channel_id=1, source_target_pairs={{0,4},{4,8},{8,12},{12,0},{1,5},{5,9},{9,13},{13,1},{2,6},{6,10},{... | collective-permute-start | bytes 1769480 | tf_op jit(solution)/shard_map/ppermute | solution.py:22
  79.4 26.0 %all-to-all-start.1 = ((bf16[16,16,1152]{2,1,0:T(8,128)(2,1)}), bf16[16,16,1152]{2,1,0:T(8,128)(2,1)}, u32[]{:S(2)}, u32[]{:S(2)}) async-start(bf16[16,16,1152]{2,1,0:T(8,128)(2,1)} %image_back.1.refs_8_), calls=%async_computation.1 | async-start | bytes 1179648 | tf_op jit(solution)/shard_map/all_to_all | solution.py:412
  93.5 12.0 %collective-permute-start.22 = (bf16[128,1152]{1,0:T(8,128)(2,1)}, bf16[128,1152]{1,0:T(8,128)(2,1)}, u32[]{:S(2)}, u32[]{:S(2)}) collective-permute-start(bf16[128,1152]{1,0:T(8,128)(2,1)} %get-tuple-element.41), channel_id=1, source_target_pairs={{0,128},{128,0},{1,129},{129,1},{2,130},{130,2},{3,131},{131,3},{4... | collective-permute-start | bytes 884744 | tf_op jit(solution)/shard_map/ppermute | solution.py:22
  93.9 21.3 %collective-permute-start.25 = (bf16[256,1152]{1,0:T(8,128)(2,1)}, bf16[256,1152]{1,0:T(8,128)(2,1)}, u32[]{:S(2)}, u32[]{:S(2)}) collective-permute-start(bf16[256,1152]{1,0:T(8,128)(2,1)} %collective-permute-done.20.refs_4_.refs_3_), channel_id=1, source_target_pairs={{0,4},{4,8},{8,12},{12,0},{1,5},{5,9},{9,13},{13,1},{2,6},{6,10},{... | collective-permute-start | bytes 1769480 | tf_op jit(solution)/shard_map/ppermute | solution.py:22
  95.3 19.9 %collective-permute-start.26 = (bf16[256,1152]{1,0:T(8,128)(2,1)}, bf16[256,1152]{1,0:T(8,128)(2,1)}, u32[]{:S(2)}, u32[]{:S(2)}) collective-permute-start(bf16[256,1152]{1,0:T(8,128)(2,1)} %collective-permute-done.24.refs_10_.refs_6_), channel_id=1, source_target_pairs={{0,12},{4,0},{8,4},{12,8},{1,13},{5,1},{9,5},{13,9},{2,14},{6,2},{... | collective-permute-start | bytes 1769480 | tf_op jit(solution)/shard_map/ppermute | solution.py:22
  109.0 18.1 %all-to-all-start.2 = ((bf16[16,144,128]{2,1,0:T(8,128)(2,1)}), bf16[16,144,128]{2,1,0:T(8,128)(2,1)}, u32[]{:S(2)}, u32[]{:S(2)}) async-start(bf16[16,144,128]{2,1,0:T(8,128)(2,1)} %bitcast.15), calls=%async_computation.2 | async-start | bytes 1179648 | tf_op jit(solution)/shard_map/all_to_all | solution.py:428
  132.4 12.6 %copy-start = (bf16[1152,1152]{1,0:T(8,128)(2,1)S(1)}, bf16[1152,1152]{1,0:T(8,128)(2,1)}, u32[]{:S(2)}) copy-start(bf16[1152,1152]{1,0:T(8,128)(2,1)} %image_head_far.1) | copy-start | bytes 7962628
  132.4 28.9 %all-to-all-start.3 = ((bf16[256,8,128]{2,1,0:T(8,128)(2,1)}), bf16[256,8,128]{2,1,0:T(8,128)(2,1)}, u32[]{:S(2)}, u32[]{:S(2)}) async-start(bf16[256,8,128]{2,1,0:T(8,128)(2,1)} %bitcast.14), calls=%async_computation.3 | async-start | bytes 1048576 | tf_op jit(solution)/shard_map/all_to_all | solution.py:436
  (1 other events, 12.6 us)

commit v9 on v8

--- a/solution.py
+++ b/solution.py
@@ -407,13 +407,13 @@
     (send_back,) = call(
         image_back, [((groups, SLOTS, width), BF)], "image_back",
         [logit_scale], [image_mine, image_rest, owners],
-        [feats[2], feats[4], *image_blocks[6:]],
+        [home, *image_blocks[6:]],
     )
     received = lax.all_to_all(send_back, REP_AXES, 0, 0, tiled=True)
 
     text_mine, text_rest = pair_call(
         True, "text_sums", scalars, caption_image, text_emb, other_text, image_blocks,
-        [send_back],
+        [send_back, feats[2], feats[4]],
     )
     text_rest = shifted(text_rest, "ylo", 1)
     columns = groups // 2

time: 165 us -> 169 us (1.024)
  waiting for transfers between devices: 52.1 us -> 58.1 us
  starting transfers between devices: 72.8 us -> 70.3 us
    ppermute x1, waiting for transfers between devices: 3.34 us -> 6.65 us  [per_device(): lax.ppermute(give, ('yhi', 'core'), [(i, 3 - i) for i in range(4)])]
    ppermute x26, waiting for transfers between devices: 22.3 us -> 24.9 us  [shifted(): lax.ppermute(block, axis, [(i, (i + distance) % size) for i in range(size)])]
    ppermute x26, starting transfers between devices: 35 us -> 32.4 us  [shifted(): lax.ppermute(block, axis, [(i, (i + distance) % size) for i in range(size)])]
  transfers between devices with their start and end apart: 31 -> 31, of which waited for: 8 -> 10; matrix products, arithmetic and copies ran while one was open for 3% -> 3% of each run, Pallas kernels for 11% -> 11%
where the time goes in v9:
time: 169 us; the launch traced here: 168 us
  starting transfers between devices  70.3 us (42%)
  waiting for transfers between devices  58.1 us (34%)
  Pallas kernels  31.7 us (19%)
  matrix products  5.12 us (3%)
  between operations  2.28 us (1%)
    ppermute x26, starting transfers between devices, shifted(): lax.ppermute(block, axis, [(i, (i + distance) % size) for i in range(size)])  32.4 us
    ppermute x26, waiting for transfers between devices, shifted(): lax.ppermute(block, axis, [(i, (i + distance) % size) for i in range(size)])  24.9 us
    pallas_call x6, Pallas kernels, call(): pl.pallas_call(kernel, out_shape=shapes, in_specs=[SMEM] * len(scalars) +...  18.2 us
    all_to_all x1, waiting for transfers between devices, per_device(): lax.all_to_all(terms.reshape(256, 8, 128), CAP_AXES + REP_AXES, 0, 0, til...  14.8 us
    all_to_all x1, waiting for transfers between devices, per_device(): lax.all_to_all(strips.reshape(groups, strip, texts), REP_AXES, 0, 0, tile...  11.8 us
    all_to_all x1, starting transfers between devices, per_device(): received = lax.all_to_all(send_back, REP_AXES, 0, 0, tiled=True)  10 us
    all_to_all x1, starting transfers between devices, per_device(): lax.all_to_all(terms.reshape(256, 8, 128), CAP_AXES + REP_AXES, 0, 0, til...  8.72 us
    pallas_call x2, Pallas kernels, pair_call(): pl.pallas_call(functools.partial(pair_sums, turned, len(blocks)), out_sha...  8.47 us
  transfers between devices with their start and end apart: 31, of which 10 were waited for; matrix products, arithmetic and copies ran while one was open for 3% of the time, Pallas kernels for 11%

profile of v9, /device:TPU:1, one launch (start us, length us, event | category | flops | bytes accessed | tf_op | source)
XLA Modules:
  0.0 168.2 jit_solution(5666187687103300178)
XLA Ops:
  0.6 5.0 %front.1 = (f32[128,1152]{1,0:T(8,128)}, f32[128,1]{1,0:T(8,128)}, bf16[16,16,1152]{2,1,0:T(8,128)(2,1)}, bf16[256,128]{1,0:T(8,128)(2,1)}, f32[128,1152]{1,0:T(...) custom-call(s32[16,96]{1,0:T(8,128)} %bitcast.18, ...), custom_call_target="tpu_custom_call" | custom-call | tf_op jit(solution)/shard_map/front/pallas_call | solution.py:367
  5.7 8.5 %all-to-all-start = ((bf16[16,16,1152]{2,1,0:T(8,128)(2,1)}), bf16[16,16,1152]{2,1,0:T(8,128)(2,1)}, u32[]{:S(2)}, u32[]{:S(2)}) async-start(bf16[16,16,1152]{2,1,0:T(8,128)(2,1)} %get-tuple-element.28), calls=%async_computation | async-start | bytes 1179648 | tf_op jit(solution)/shard_map/all_to_all | solution.py:378
  14.1 1.7 collective-permute-start.10
  15.8 4.0 %collective-permute-start.11 = (bf16[128,1152]{1,0:T(8,128)(2,1)}, bf16[128,1152]{1,0:T(8,128)(2,1)}, u32[]{:S(2)}, u32[]{:S(2)}) collective-permute-start(bf16[128,1152]{1,0:T(8,128)(2,1)} %get-tuple-element.27.refs_0_.own_far), channel_id=1, source_target_pairs={{0,112},{16,0},{32,16},{48,32},{64,48},{80,64},{96,80},{112,96},{1... | collective-permute-start | bytes 884744 | tf_op jit(solution)/shard_map/ppermute | solution.py:22
  20.3 7.0 %collective-permute-done.10.refs_1_ = bf16[128,1152]{1,0:T(8,128)(2,1)} collective-permute-done((bf16[128,1152]{1,0:T(8,128)(2,1)}, bf16[128,1152]{1,0:T(8,128)(2,1)}, u32[]{:S(2)}, u32[]{:S(2)}) %collective-permute-start.10) | collective-permute-done | bytes 294944 | tf_op jit(solution)/shard_map/ppermute | solution.py:22
  27.3 2.7 %collective-permute-start.13 = (bf16[128,1152]{1,0:T(8,128)(2,1)}, bf16[128,1152]{1,0:T(8,128)(2,1)}, u32[]{:S(2)}, u32[]{:S(2)}) collective-permute-start(bf16[128,1152]{1,0:T(8,128)(2,1)} %collective-permute-done.11.refs_2_), channel_id=1, source_target_pairs={{0,112},{16,0},{32,16},{48,32},{64,48},{80,64},{96,80},{112,96},{1... | collective-permute-start | bytes 884744 | tf_op jit(solution)/shard_map/ppermute | solution.py:22
  29.9 2.2 %arrive.1.own_far.refs_0_ = bf16[96,1152]{1,0:T(8,128)(2,1)} custom-call(bf16[16,16,1152]{2,1,0:T(8,128)(2,1)} %all-to-all-done.refs_0_, s32[16,96]{1,0:T(8,128)} %bitcast.19, bf16[128,1152]{1,0:T(8,128)(2,1)} %collective-permute-done.1.refs_2_.refs_1_), custom_call_target="tpu_custom_call" | custom-call | tf_op jit(solution)/shard_map/arrive/pallas_call | solution.py:63
  33.7 2.9 %collective-permute-done.12.refs_3_ = bf16[128,1152]{1,0:T(8,128)(2,1)} collective-permute-done((bf16[128,1152]{1,0:T(8,128)(2,1)}, bf16[128,1152]{1,0:T(8,128)(2,1)}, u32[]{:S(2)}, u32[]{:S(2)}) %collective-permute-start.12) | collective-permute-done | bytes 294944 | tf_op jit(solution)/shard_map/ppermute | solution.py:22
  36.6 3.7 %collective-permute-done.2.refs_1_ = bf16[96,1152]{1,0:T(8,128)(2,1)S(1)} collective-permute-done((bf16[96,1152]{1,0:T(8,128)(2,1)}, bf16[96,1152]{1,0:T(8,128)(2,1)S(1)}, u32[]{:S(2)}, u32[]{:S(2)}) %collective-permute-start.2) | collective-permute-done | bytes 221216 | tf_op jit(solution)/shard_map/ppermute | solution.py:22
  41.0 3.3 %collective-permute-start.4 = (bf16[96,1152]{1,0:T(8,128)(2,1)S(1)}, bf16[96,1152]{1,0:T(8,128)(2,1)}, u32[]{:S(2)}, u32[]{:S(2)}) collective-permute-start(bf16[96,1152]{1,0:T(8,128)(2,1)S(1)} %collective-permute-done.2.refs_1_), channel_id=1, source_target_pairs={{0,112},{16,0},{32,16},{48,32},{64,48},{80,64},{96,80},{112,96},{1... | collective-permute-start | bytes 663560 | tf_op jit(solution)/shard_map/ppermute | solution.py:22
  44.3 2.6 %collective-permute-start.17 = (bf16[128,1152]{1,0:T(8,128)(2,1)}, bf16[128,1152]{1,0:T(8,128)(2,1)}, u32[]{:S(2)}, u32[]{:S(2)}) collective-permute-start(bf16[128,1152]{1,0:T(8,128)(2,1)} %get-tuple-element.36.refs_0_), channel_id=1, source_target_pairs={{0,2},{2,0},{1,3},{3,1},{4,6},{6,4},{5,7},{7,5},{8,10},{10,8},{9,1... | collective-permute-start | bytes 884744 | tf_op jit(solution)/shard_map/ppermute | solution.py:22
  46.9 3.2 %collective-permute-start.18 = (bf16[128,1152]{1,0:T(8,128)(2,1)}, bf16[128,1152]{1,0:T(8,128)(2,1)}, u32[]{:S(2)}, u32[]{:S(2)}) collective-permute-start(bf16[128,1152]{1,0:T(8,128)(2,1)} %get-tuple-element.29), channel_id=1, source_target_pairs={{0,3},{1,2},{2,1},{3,0},{4,7},{5,6},{6,5},{7,4},{8,11},{9,10},{10,... | collective-permute-start | bytes 884744 | tf_op jit(solution)/shard_map/ppermute | solution.py:382
  50.1 2.5 %collective-permute-start.15 = (bf16[128,1152]{1,0:T(8,128)(2,1)}, bf16[128,1152]{1,0:T(8,128)(2,1)}, u32[]{:S(2)}, u32[]{:S(2)}) collective-permute-start(bf16[128,1152]{1,0:T(8,128)(2,1)} %collective-permute-done.13.refs_4_), channel_id=1, source_target_pairs={{0,112},{16,0},{32,16},{48,32},{64,48},{80,64},{96,80},{112,96},{1... | collective-permute-start | bytes 884744 | tf_op jit(solution)/shard_map/ppermute | solution.py:22
  53.5 2.2 %collective-permute-start.6 = (bf16[96,1152]{1,0:T(8,128)(2,1)}, bf16[96,1152]{1,0:T(8,128)(2,1)}, u32[]{:S(2)}, u32[]{:S(2)}) collective-permute-start(bf16[96,1152]{1,0:T(8,128)(2,1)} %collective-permute-done.4.refs_3_), channel_id=1, source_target_pairs={{0,112},{16,0},{32,16},{48,32},{64,48},{80,64},{96,80},{112,96},{1... | collective-permute-start | bytes 663560 | tf_op jit(solution)/shard_map/ppermute | solution.py:22
  55.7 6.7 %collective-permute-done.18.refs_3_ = bf16[128,1152]{1,0:T(8,128)(2,1)} collective-permute-done((bf16[128,1152]{1,0:T(8,128)(2,1)}, bf16[128,1152]{1,0:T(8,128)(2,1)}, u32[]{:S(2)}, u32[]{:S(2)}) %collective-permute-start.18) | collective-permute-done | bytes 294944 | tf_op jit(solution)/shard_map/ppermute | solution.py:382
  62.3 2.3 %joined.1 = (bf16[256,1152]{1,0:T(8,128)(2,1)}, bf16[256,1152]{1,0:T(8,128)(2,1)}) custom-call(bf16[128,1152]{1,0:T(8,128)(2,1)} %get-tuple-element.36.refs_0_, bf16[128,1152]{1,0:T(8,128)(2,1)} %collective-permute-done.1.refs_2_.refs_1_, bf16[128,1152]{1,0:T(8,128)(2,1)} %collective-permute-done.17.refs_2_, bf16[128,1152]{1,0:T(8,128)(2,1)} %collective-permute-done.18.refs_3_), custom_call_target="tpu_custom_call" | custom-call | tf_op jit(solution)/shard_map/joined/pallas_call | solution.py:63
  65.7 1.7 %collective-permute-start.21 = (bf16[256,1152]{1,0:T(8,128)(2,1)}, bf16[256,1152]{1,0:T(8,128)(2,1)}, u32[]{:S(2)}, u32[]{:S(2)}) collective-permute-start(bf16[256,1152]{1,0:T(8,128)(2,1)} %get-tuple-element.37.refs_8_.refs_4_.refs_1_), channel_id=1, source_target_pairs={{0,12},{4,0},{8,4},{12,8},{1,13},{5,1},{9,5},{13,9},{2,14},{6,2},{... | collective-permute-start | bytes 1769480 | tf_op jit(solution)/shard_map/ppermute | solution.py:22
  68.8 4.3 %image_sums.1 = (f32[96,1152]{1,0:T(8,128)}, bf16[96,1152]{1,0:T(8,128)(2,1)}) custom-call(f32[1]{0:T(128)S(6)} %copy.12.scale_ref.refs_0_, f32[1]{0:T(128)S(6)} %copy.13.bias_ref, s32[1,128]{1,0:T(1,128)} %targets_far.3, bf16[96,1152]{1,0:T(8,128)(2,1)} %arrive.1.own_far.refs_0_, bf16[96,1152]{1,0:T(8,128)(2,1)} %collective-permute-done.9.other_far, ...), custom_call_target="tpu_custom_call" | custom-call | tf_op jit(solution)/shard_map/image_sums/pallas_call | solution.py:245
  73.9 2.7 %collective-permute-start.8 = (bf16[96,1152]{1,0:T(8,128)(2,1)}, bf16[96,1152]{1,0:T(8,128)(2,1)}, u32[]{:S(2)}, u32[]{:S(2)}) collective-permute-start(bf16[96,1152]{1,0:T(8,128)(2,1)} %collective-permute-done.6.refs_5_), channel_id=1, source_target_pairs={{0,112},{16,0},{32,16},{48,32},{64,48},{80,64},{96,80},{112,96},{1... | collective-permute-start | bytes 663560 | tf_op jit(solution)/shard_map/ppermute | solution.py:22
  80.0 2.3 %image_back.1.refs_8_ = bf16[16,16,1152]{2,1,0:T(8,128)(2,1)} custom-call(f32[1]{0:T(128)S(6)} %copy.12.scale_ref.refs_0_, f32[96,1152]{1,0:T(8,128)} %get-tuple-element.38.refs_1_, bf16[96,1152]{1,0:T(8,128)(2,1)} %collective-permute-done.19.refs_2_, s32[16,96]{1,0:T(8,128)} %bitcast.20, bf16[256,1152]{1,0:T(8,128)(2,1)} %get-tuple-element.37.refs_8_.refs_4_.refs_1_, ...), custom_call_target="tpu_custom_call" | custom-call | tf_op jit(solution)/shard_map/image_back/pallas_call | solution.py:63
  82.3 10.0 %all-to-all-start.1 = ((bf16[16,16,1152]{2,1,0:T(8,128)(2,1)}), bf16[16,16,1152]{2,1,0:T(8,128)(2,1)}, u32[]{:S(2)}, u32[]{:S(2)}) async-start(bf16[16,16,1152]{2,1,0:T(8,128)(2,1)} %image_back.1.refs_8_), calls=%async_computation.1 | async-start | bytes 1179648 | tf_op jit(solution)/shard_map/all_to_all | solution.py:412
  92.4 4.2 %text_sums.1 = (f32[128,1152]{1,0:T(8,128)}, bf16[128,1152]{1,0:T(8,128)(2,1)}) custom-call(f32[1]{0:T(128)S(6)} %copy.12.scale_ref.refs_0_, f32[1]{0:T(128)S(6)} %copy.13.bias_ref, s32[1,128]{1,0:T(1,128)} %targets_far.3, bf16[128,1152]{1,0:T(8,128)(2,1)} %get-tuple-element.27.refs_0_.own_far, bf16[128,1152]{1,0:T(8,128)(2,1)} %collective-permute-done.other_far, ...), custom_call_target="tpu_custom_call" | custom-call | tf_op jit(solution)/shard_map/text_sums/pallas_call | solution.py:245
  99.8 8.9 %collective-permute-done.22.refs_2_ = bf16[128,1152]{1,0:T(8,128)(2,1)} collective-permute-done((bf16[128,1152]{1,0:T(8,128)(2,1)}, bf16[128,1152]{1,0:T(8,128)(2,1)}, u32[]{:S(2)}, u32[]{:S(2)}) %collective-permute-start.22) | collective-permute-done | bytes 294944 | tf_op jit(solution)/shard_map/ppermute | solution.py:22
  108.7 3.5 %both_back.1 = (bf16[128,1152]{1,0:T(8,128)(2,1)}, bf16[128,1152]{1,0:T(8,128)(2,1)}, bf16[8,2,144,128]{3,2,1,0:T(8,128)(2,1)}) custom-call(f32[1]{0:T(128)S(6)} %copy.12.scale_ref.refs_0_, f32[128,1152]{1,0:T(8,128)} %get-tuple-element.40.refs_1_, bf16[128,1152]{1,0:T(8,128)(2,1)} %collective-permute-done.22.refs_2_, ...), custom_call_target="tpu_custom_call" | custom-call | tf_op jit(solution)/shard_map/both_back/pallas_call | solution.py:63
  112.2 7.5 %all-to-all-start.2 = ((bf16[16,144,128]{2,1,0:T(8,128)(2,1)}), bf16[16,144,128]{2,1,0:T(8,128)(2,1)}, u32[]{:S(2)}, u32[]{:S(2)}) async-start(bf16[16,144,128]{2,1,0:T(8,128)(2,1)} %bitcast.15), calls=%async_computation.2 | async-start | bytes 1179648 | tf_op jit(solution)/shard_map/all_to_all | solution.py:428
  119.7 11.8 %all-to-all-done.2.refs_0_ = bf16[16,144,128]{2,1,0:T(8,128)(2,1)} async-done(((bf16[16,144,128]{2,1,0:T(8,128)(2,1)}), bf16[16,144,128]{2,1,0:T(8,128)(2,1)}, u32[]{:S(2)}, u32[]{:S(2)}) %all-to-all-start.2) | async-done | bytes 589856 | tf_op jit(solution)/shard_map/all_to_all | solution.py:428
  131.5 5.3 %head_terms.1 = bf16[128,16,128]{2,1,0:T(8,128)(2,1)} custom-call(bf16[16,144,128]{2,1,0:T(8,128)(2,1)} %all-to-all-done.2.refs_0_, bf16[256,1152]{1,0:T(8,128)(2,1)} %get-tuple-element.37.refs_8_.refs_4_.refs_1_, bf16[256,1152]{1,0:T(8,128)(2,1)} %get-tuple-element.47.refs_2_, bf16[256,1152]{1,0:T(8,128)(2,1)} %collective-permute-done.20.refs_9_.refs_3_, ...), custom_call_target="tpu_custom_call" | custom-call | tf_op jit(solution)/shard_map/head_terms/pallas_call | solution.py:63
  136.9 8.7 %all-to-all-start.3 = ((bf16[256,8,128]{2,1,0:T(8,128)(2,1)}), bf16[256,8,128]{2,1,0:T(8,128)(2,1)}, u32[]{:S(2)}, u32[]{:S(2)}) async-start(bf16[256,8,128]{2,1,0:T(8,128)(2,1)} %bitcast.14), calls=%async_computation.3 | async-start | bytes 1048576 | tf_op jit(solution)/shard_map/all_to_all | solution.py:436
  145.6 3.5 %fusion = bf16[1,128,1152]{2,1,0:T(8,128)(2,1)} fusion(bf16[128,1152]{1,0:T(8,128)(2,1)} %get-tuple-element.48, bf16[1152,1152]{1,0:T(8,128)(2,1)} %text_head_far.1), kind=kOutput, calls=%fused_computation.2 | convolution fusion | flops 339886080 | bytes 3244032 | tf_op jit(solution)/shard_map/dot_general | solution.py:76
  149.1 1.6 fusion.1
  150.7 14.8 %all-to-all-done.3 = bf16[256,8,128]{2,1,0:T(8,128)(2,1)} async-done(((bf16[256,8,128]{2,1,0:T(8,128)(2,1)}), bf16[256,8,128]{2,1,0:T(8,128)(2,1)}, u32[]{:S(2)}, u32[]{:S(2)}) %all-to-all-start.3) | async-done | bytes 524320 | tf_op jit(solution)/shard_map/all_to_all | solution.py:436
  165.5 2.5 %head_sums.1 = f32[9,1152]{1,0:T(8,128)} custom-call(bf16[128,16,128]{2,1,0:T(8,128)(2,1)} %bitcast.7.refs_0_), custom_call_target="tpu_custom_call" | custom-call | tf_op jit(solution)/shard_map/head_sums/pallas_call | solution.py:63
  (49 shorter events, 12.3 us)
Async XLA Ops:
  5.7 24.3 %all-to-all-start = ((bf16[16,16,1152]{2,1,0:T(8,128)(2,1)}), bf16[16,16,1152]{2,1,0:T(8,128)(2,1)}, u32[]{:S(2)}, u32[]{:S(2)}) async-start(bf16[16,16,1152]{2,1,0:T(8,128)(2,1)} %get-tuple-element.28), calls=%async_computation | async-start | bytes 1179648 | tf_op jit(solution)/shard_map/all_to_all | solution.py:378
  14.1 13.1 %collective-permute-start.10 = (bf16[128,1152]{1,0:T(8,128)(2,1)}, bf16[128,1152]{1,0:T(8,128)(2,1)}, u32[]{:S(2)}, u32[]{:S(2)}) collective-permute-start(bf16[128,1152]{1,0:T(8,128)(2,1)} %get-tuple-element.27.refs_0_.own_far), channel_id=1, source_target_pairs={{0,16},{16,32},{32,48},{48,64},{64,80},{80,96},{96,112},{112,0},{1... | collective-permute-start | bytes 884744 | tf_op jit(solution)/shard_map/ppermute | solution.py:22
  15.8 11.5 %collective-permute-start.11 = (bf16[128,1152]{1,0:T(8,128)(2,1)}, bf16[128,1152]{1,0:T(8,128)(2,1)}, u32[]{:S(2)}, u32[]{:S(2)}) collective-permute-start(bf16[128,1152]{1,0:T(8,128)(2,1)} %get-tuple-element.27.refs_0_.own_far), channel_id=1, source_target_pairs={{0,112},{16,0},{32,16},{48,32},{64,48},{80,64},{96,80},{112,96},{1... | collective-permute-start | bytes 884744 | tf_op jit(solution)/shard_map/ppermute | solution.py:22
  19.8 10.2 %collective-permute-start.1 = (bf16[128,1152]{1,0:T(8,128)(2,1)}, bf16[128,1152]{1,0:T(8,128)(2,1)}, u32[]{:S(2)}, u32[]{:S(2)}) collective-permute-start(bf16[128,1152]{1,0:T(8,128)(2,1)} %get-tuple-element.29), channel_id=1, source_target_pairs={{0,1},{1,0},{2,3},{3,2},{4,5},{5,4},{6,7},{7,6},{8,9},{9,8},{10,11... | collective-permute-start | bytes 884744 | tf_op jit(solution)/shard_map/ppermute | solution.py:22
  27.3 9.4 %collective-permute-start.12 = (bf16[128,1152]{1,0:T(8,128)(2,1)}, bf16[128,1152]{1,0:T(8,128)(2,1)}, u32[]{:S(2)}, u32[]{:S(2)}) collective-permute-start(bf16[128,1152]{1,0:T(8,128)(2,1)} %collective-permute-done.10.refs_1_), channel_id=1, source_target_pairs={{0,16},{16,32},{32,48},{48,64},{64,80},{80,96},{96,112},{112,0},{1... | collective-permute-start | bytes 884744 | tf_op jit(solution)/shard_map/ppermute | solution.py:22
  27.3 19.6 %collective-permute-start.13 = (bf16[128,1152]{1,0:T(8,128)(2,1)}, bf16[128,1152]{1,0:T(8,128)(2,1)}, u32[]{:S(2)}, u32[]{:S(2)}) collective-permute-start(bf16[128,1152]{1,0:T(8,128)(2,1)} %collective-permute-done.11.refs_2_), channel_id=1, source_target_pairs={{0,112},{16,0},{32,16},{48,32},{64,48},{80,64},{96,80},{112,96},{1... | collective-permute-start | bytes 884744 | tf_op jit(solution)/shard_map/ppermute | solution.py:22
  32.1 8.2 %collective-permute-start.2 = (bf16[96,1152]{1,0:T(8,128)(2,1)}, bf16[96,1152]{1,0:T(8,128)(2,1)S(1)}, u32[]{:S(2)}, u32[]{:S(2)}) collective-permute-start(bf16[96,1152]{1,0:T(8,128)(2,1)} %arrive.1.own_far.refs_0_), channel_id=1, source_target_pairs={{0,112},{16,0},{32,16},{48,32},{64,48},{80,64},{96,80},{112,96},{1... | collective-permute-start | bytes 663560 | tf_op jit(solution)/shard_map/ppermute | solution.py:22
  33.7 6.6 %collective-permute-start.3 = (bf16[96,1152]{1,0:T(8,128)(2,1)}, bf16[96,1152]{1,0:T(8,128)(2,1)S(1)}, u32[]{:S(2)}, u32[]{:S(2)}) collective-permute-start(bf16[96,1152]{1,0:T(8,128)(2,1)} %arrive.1.own_far.refs_0_), channel_id=1, source_target_pairs={{0,16},{16,32},{32,48},{48,64},{64,80},{80,96},{96,112},{112,0},{1... | collective-permute-start | bytes 663560 | tf_op jit(solution)/shard_map/ppermute | solution.py:22
  36.6 13.4 %collective-permute-start.14 = (bf16[128,1152]{1,0:T(8,128)(2,1)}, bf16[128,1152]{1,0:T(8,128)(2,1)}, u32[]{:S(2)}, u32[]{:S(2)}) collective-permute-start(bf16[128,1152]{1,0:T(8,128)(2,1)} %collective-permute-done.12.refs_3_), channel_id=1, source_target_pairs={{0,16},{16,32},{32,48},{48,64},{64,80},{80,96},{96,112},{112,0},{1... | collective-permute-start | bytes 884744 | tf_op jit(solution)/shard_map/ppermute | solution.py:22
  41.0 11.6 %collective-permute-start.4 = (bf16[96,1152]{1,0:T(8,128)(2,1)S(1)}, bf16[96,1152]{1,0:T(8,128)(2,1)}, u32[]{:S(2)}, u32[]{:S(2)}) collective-permute-start(bf16[96,1152]{1,0:T(8,128)(2,1)S(1)} %collective-permute-done.2.refs_1_), channel_id=1, source_target_pairs={{0,112},{16,0},{32,16},{48,32},{64,48},{80,64},{96,80},{112,96},{1... | collective-permute-start | bytes 663560 | tf_op jit(solution)/shard_map/ppermute | solution.py:22
  44.3 9.2 %collective-permute-start.17 = (bf16[128,1152]{1,0:T(8,128)(2,1)}, bf16[128,1152]{1,0:T(8,128)(2,1)}, u32[]{:S(2)}, u32[]{:S(2)}) collective-permute-start(bf16[128,1152]{1,0:T(8,128)(2,1)} %get-tuple-element.36.refs_0_), channel_id=1, source_target_pairs={{0,2},{2,0},{1,3},{3,1},{4,6},{6,4},{5,7},{7,5},{8,10},{10,8},{9,1... | collective-permute-start | bytes 884744 | tf_op jit(solution)/shard_map/ppermute | solution.py:22
  46.9 6.4 %collective-permute-start.5 = (bf16[96,1152]{1,0:T(8,128)(2,1)S(1)}, bf16[96,1152]{1,0:T(8,128)(2,1)}, u32[]{:S(2)}, u32[]{:S(2)}) collective-permute-start(bf16[96,1152]{1,0:T(8,128)(2,1)S(1)} %collective-permute-done.3.refs_2_), channel_id=1, source_target_pairs={{0,16},{16,32},{32,48},{48,64},{64,80},{80,96},{96,112},{112,0},{1... | collective-permute-start | bytes 663560 | tf_op jit(solution)/shard_map/ppermute | solution.py:22
  46.9 15.5 %collective-permute-start.18 = (bf16[128,1152]{1,0:T(8,128)(2,1)}, bf16[128,1152]{1,0:T(8,128)(2,1)}, u32[]{:S(2)}, u32[]{:S(2)}) collective-permute-start(bf16[128,1152]{1,0:T(8,128)(2,1)} %get-tuple-element.29), channel_id=1, source_target_pairs={{0,3},{1,2},{2,1},{3,0},{4,7},{5,6},{6,5},{7,4},{8,11},{9,10},{10,... | collective-permute-start | bytes 884744 | tf_op jit(solution)/shard_map/ppermute | solution.py:382
  50.1 15.7 %collective-permute-start.15 = (bf16[128,1152]{1,0:T(8,128)(2,1)}, bf16[128,1152]{1,0:T(8,128)(2,1)}, u32[]{:S(2)}, u32[]{:S(2)}) collective-permute-start(bf16[128,1152]{1,0:T(8,128)(2,1)} %collective-permute-done.13.refs_4_), channel_id=1, source_target_pairs={{0,112},{16,0},{32,16},{48,32},{64,48},{80,64},{96,80},{112,96},{1... | collective-permute-start | bytes 884744 | tf_op jit(solution)/shard_map/ppermute | solution.py:22
  52.6 16.2 %collective-permute-start.16 = (bf16[128,1152]{1,0:T(8,128)(2,1)}, bf16[128,1152]{1,0:T(8,128)(2,1)}, u32[]{:S(2)}, u32[]{:S(2)}) collective-permute-start(bf16[128,1152]{1,0:T(8,128)(2,1)} %collective-permute-done.14.refs_5_), channel_id=1, source_target_pairs={{0,16},{16,32},{32,48},{48,64},{64,80},{80,96},{96,112},{112,0},{1... | collective-permute-start | bytes 884744 | tf_op jit(solution)/shard_map/ppermute | solution.py:22
  53.3 11.4 %collective-permute-start.9 = (bf16[96,1152]{1,0:T(8,128)(2,1)}, bf16[96,1152]{1,0:T(8,128)(2,1)}, u32[]{:S(2)}, u32[]{:S(2)}) collective-permute-start(bf16[96,1152]{1,0:T(8,128)(2,1)} %arrive.1.own_far.refs_0_), channel_id=1, source_target_pairs={{0,128},{128,0},{1,129},{129,1},{2,130},{130,2},{3,131},{131,3},{4... | collective-permute-start | bytes 663560 | tf_op jit(solution)/shard_map/ppermute | solution.py:22
  53.5 20.3 %collective-permute-start.6 = (bf16[96,1152]{1,0:T(8,128)(2,1)}, bf16[96,1152]{1,0:T(8,128)(2,1)}, u32[]{:S(2)}, u32[]{:S(2)}) collective-permute-start(bf16[96,1152]{1,0:T(8,128)(2,1)} %collective-permute-done.4.refs_3_), channel_id=1, source_target_pairs={{0,112},{16,0},{32,16},{48,32},{64,48},{80,64},{96,80},{112,96},{1... | collective-permute-start | bytes 663560 | tf_op jit(solution)/shard_map/ppermute | solution.py:22
  62.3 11.5 %collective-permute-start.7 = (bf16[96,1152]{1,0:T(8,128)(2,1)}, bf16[96,1152]{1,0:T(8,128)(2,1)}, u32[]{:S(2)}, u32[]{:S(2)}) collective-permute-start(bf16[96,1152]{1,0:T(8,128)(2,1)} %collective-permute-done.5.refs_4_), channel_id=1, source_target_pairs={{0,16},{16,32},{32,48},{48,64},{64,80},{80,96},{96,112},{112,0},{1... | collective-permute-start | bytes 663560 | tf_op jit(solution)/shard_map/ppermute | solution.py:22
  64.7 27.6 %collective-permute-start.20 = (bf16[256,1152]{1,0:T(8,128)(2,1)}, bf16[256,1152]{1,0:T(8,128)(2,1)}, u32[]{:S(2)}, u32[]{:S(2)}) collective-permute-start(bf16[256,1152]{1,0:T(8,128)(2,1)} %get-tuple-element.37.refs_8_.refs_4_.refs_1_), channel_id=1, source_target_pairs={{0,4},{4,8},{8,12},{12,0},{1,5},{5,9},{9,13},{13,1},{2,6},{6,10},{... | collective-permute-start | bytes 1769480 | tf_op jit(solution)/shard_map/ppermute | solution.py:22
  65.7 26.6 %collective-permute-start.21 = (bf16[256,1152]{1,0:T(8,128)(2,1)}, bf16[256,1152]{1,0:T(8,128)(2,1)}, u32[]{:S(2)}, u32[]{:S(2)}) collective-permute-start(bf16[256,1152]{1,0:T(8,128)(2,1)} %get-tuple-element.37.refs_8_.refs_4_.refs_1_), channel_id=1, source_target_pairs={{0,12},{4,0},{8,4},{12,8},{1,13},{5,1},{9,5},{13,9},{2,14},{6,2},{... | collective-permute-start | bytes 1769480 | tf_op jit(solution)/shard_map/ppermute | solution.py:22
  73.1 5.5 %collective-permute-start.19 = (bf16[96,1152]{1,0:T(8,128)(2,1)}, bf16[96,1152]{1,0:T(8,128)(2,1)}, u32[]{:S(2)}, u32[]{:S(2)}) collective-permute-start(bf16[96,1152]{1,0:T(8,128)(2,1)} %get-tuple-element.39), channel_id=1, source_target_pairs={{0,128},{128,0},{1,129},{129,1},{2,130},{130,2},{3,131},{131,3},{4... | collective-permute-start | bytes 663560 | tf_op jit(solution)/shard_map/ppermute | solution.py:22
  73.9 6.1 %collective-permute-start.8 = (bf16[96,1152]{1,0:T(8,128)(2,1)}, bf16[96,1152]{1,0:T(8,128)(2,1)}, u32[]{:S(2)}, u32[]{:S(2)}) collective-permute-start(bf16[96,1152]{1,0:T(8,128)(2,1)} %collective-permute-done.6.refs_5_), channel_id=1, source_target_pairs={{0,112},{16,0},{32,16},{48,32},{64,48},{80,64},{96,80},{112,96},{1... | collective-permute-start | bytes 663560 | tf_op jit(solution)/shard_map/ppermute | solution.py:22
  76.5 22.0 %collective-permute-start.24 = (bf16[256,1152]{1,0:T(8,128)(2,1)}, bf16[256,1152]{1,0:T(8,128)(2,1)}, u32[]{:S(2)}, u32[]{:S(2)}) collective-permute-start(bf16[256,1152]{1,0:T(8,128)(2,1)} %get-tuple-element.47.refs_2_), channel_id=1, source_target_pairs={{0,12},{4,0},{8,4},{12,8},{1,13},{5,1},{9,5},{13,9},{2,14},{6,2},{... | collective-permute-start | bytes 1769480 | tf_op jit(solution)/shard_map/ppermute | solution.py:22
  78.5 13.8 %collective-permute-start = (bf16[128,1152]{1,0:T(8,128)(2,1)}, bf16[128,1152]{1,0:T(8,128)(2,1)}, u32[]{:S(2)}, u32[]{:S(2)}) collective-permute-start(bf16[128,1152]{1,0:T(8,128)(2,1)} %get-tuple-element.27.refs_0_.own_far), channel_id=1, source_target_pairs={{0,128},{128,0},{1,129},{129,1},{2,130},{130,2},{3,131},{131,3},{4... | collective-permute-start | bytes 884744 | tf_op jit(solution)/shard_map/ppermute | solution.py:22
  80.0 19.9 %collective-permute-start.23 = (bf16[256,1152]{1,0:T(8,128)(2,1)}, bf16[256,1152]{1,0:T(8,128)(2,1)}, u32[]{:S(2)}, u32[]{:S(2)}) collective-permute-start(bf16[256,1152]{1,0:T(8,128)(2,1)} %get-tuple-element.47.refs_2_), channel_id=1, source_target_pairs={{0,4},{4,8},{8,12},{12,0},{1,5},{5,9},{9,13},{13,1},{2,6},{6,10},{... | collective-permute-start | bytes 1769480 | tf_op jit(solution)/shard_map/ppermute | solution.py:22
  82.3 26.4 %all-to-all-start.1 = ((bf16[16,16,1152]{2,1,0:T(8,128)(2,1)}), bf16[16,16,1152]{2,1,0:T(8,128)(2,1)}, u32[]{:S(2)}, u32[]{:S(2)}) async-start(bf16[16,16,1152]{2,1,0:T(8,128)(2,1)} %image_back.1.refs_8_), calls=%async_computation.1 | async-start | bytes 1179648 | tf_op jit(solution)/shard_map/all_to_all | solution.py:412
  96.6 12.2 %collective-permute-start.22 = (bf16[128,1152]{1,0:T(8,128)(2,1)}, bf16[128,1152]{1,0:T(8,128)(2,1)}, u32[]{:S(2)}, u32[]{:S(2)}) collective-permute-start(bf16[128,1152]{1,0:T(8,128)(2,1)} %get-tuple-element.41), channel_id=1, source_target_pairs={{0,128},{128,0},{1,129},{129,1},{2,130},{130,2},{3,131},{131,3},{4... | collective-permute-start | bytes 884744 | tf_op jit(solution)/shard_map/ppermute | solution.py:22
  97.1 22.6 %collective-permute-start.25 = (bf16[256,1152]{1,0:T(8,128)(2,1)}, bf16[256,1152]{1,0:T(8,128)(2,1)}, u32[]{:S(2)}, u32[]{:S(2)}) collective-permute-start(bf16[256,1152]{1,0:T(8,128)(2,1)} %collective-permute-done.20.refs_9_.refs_3_), channel_id=1, source_target_pairs={{0,4},{4,8},{8,12},{12,0},{1,5},{5,9},{9,13},{13,1},{2,6},{6,10},{... | collective-permute-start | bytes 1769480 | tf_op jit(solution)/shard_map/ppermute | solution.py:22
  98.5 21.2 %collective-permute-start.26 = (bf16[256,1152]{1,0:T(8,128)(2,1)}, bf16[256,1152]{1,0:T(8,128)(2,1)}, u32[]{:S(2)}, u32[]{:S(2)}) collective-permute-start(bf16[256,1152]{1,0:T(8,128)(2,1)} %collective-permute-done.24.refs_10_.refs_6_), channel_id=1, source_target_pairs={{0,12},{4,0},{8,4},{12,8},{1,13},{5,1},{9,5},{13,9},{2,14},{6,2},{... | collective-permute-start | bytes 1769480 | tf_op jit(solution)/shard_map/ppermute | solution.py:22
  112.2 19.3 %all-to-all-start.2 = ((bf16[16,144,128]{2,1,0:T(8,128)(2,1)}), bf16[16,144,128]{2,1,0:T(8,128)(2,1)}, u32[]{:S(2)}, u32[]{:S(2)}) async-start(bf16[16,144,128]{2,1,0:T(8,128)(2,1)} %bitcast.15), calls=%async_computation.2 | async-start | bytes 1179648 | tf_op jit(solution)/shard_map/all_to_all | solution.py:428
  136.9 12.2 %copy-start = (bf16[1152,1152]{1,0:T(8,128)(2,1)S(1)}, bf16[1152,1152]{1,0:T(8,128)(2,1)}, u32[]{:S(2)}) copy-start(bf16[1152,1152]{1,0:T(8,128)(2,1)} %image_head_far.1) | copy-start | bytes 7962628
  136.9 28.6 %all-to-all-start.3 = ((bf16[256,8,128]{2,1,0:T(8,128)(2,1)}), bf16[256,8,128]{2,1,0:T(8,128)(2,1)}, u32[]{:S(2)}, u32[]{:S(2)}) async-start(bf16[256,8,128]{2,1,0:T(8,128)(2,1)} %bitcast.14), calls=%async_computation.3 | async-start | bytes 1048576 | tf_op jit(solution)/shard_map/all_to_all | solution.py:436
  (3 other events, 24.5 us)
